TPU v7x, 32 devices: a whole 2x2x4 slice. The times are simulated.
32 devices in a mesh: dp: 16 (over z, x, core), tensor: 2 (over y).
Axes of the slice: x: 2, y: 2, z: 4, core: 2. Of those that a mesh axis runs over, the one named last changes fastest.
Arguments:
- layer_input: bfloat16 [8192, 2048], P(('dp', 'tensor')), may hold values from -12 to 12
- doc_lengths: int32 [16, 3], P('dp'), may hold values from 63 to 384, as said below
- ln1_gain: float32 [2048], P(('dp', 'tensor')), may hold values from 0.1 to 1.9
- ln1_bias: float32 [2048], P(('dp', 'tensor')), may hold values from -1.75 to 1.75
- ln2_gain: float32 [2048], P(('dp', 'tensor')), may hold values from 0.1 to 1.9
- ln2_bias: float32 [2048], P(('dp', 'tensor')), may hold values from -1.75 to 1.75
- w_qkv: bfloat16 [2048, 6144], P('dp', 'tensor'), may hold values from -0.125 to 0.125
- b_qkv: bfloat16 [6144], P(('tensor', 'dp')), may hold values from -1.75 to 1.75
- w_dense: bfloat16 [2048, 2048], P('tensor', 'dp'), may hold values from -0.5 to 0.5
- b_dense: float32 [2048], P(('dp', 'tensor')), may hold values from -1.75 to 1.75
- w_fc1: bfloat16 [2048, 8192], P('dp', 'tensor'), may hold values from -0.125 to 0.125
- b_fc1: bfloat16 [8192], P(('tensor', 'dp')), may hold values from -1.75 to 1.75
- w_fc2: bfloat16 [8192, 2048], P('tensor', 'dp'), may hold values from -0.0625 to 0.0625
- b_fc2: float32 [2048], P(('dp', 'tensor')), may hold values from -1.75 to 1.75
- cotangent: bfloat16 [8192, 2048], P(('dp', 'tensor')), may hold values from -12 to 12
Outputs:
- output: bfloat16 [8192, 2048], P(('dp', 'tensor'))
- input_grad: bfloat16 [8192, 2048], P(('dp', 'tensor'))
- ln1_gain_grad: float32 [2048], P(('dp', 'tensor'))
- ln1_bias_grad: float32 [2048], P(('dp', 'tensor'))
- ln2_gain_grad: float32 [2048], P(('dp', 'tensor'))
- ln2_bias_grad: float32 [2048], P(('dp', 'tensor'))
- w_qkv_grad: float32 [2048, 6144], P('dp', 'tensor')
- b_qkv_grad: float32 [6144], P(('tensor', 'dp'))
- w_dense_grad: float32 [2048, 2048], P('tensor', 'dp')
- b_dense_grad: float32 [2048], P(('dp', 'tensor'))
- w_fc1_grad: float32 [2048, 8192], P('dp', 'tensor')
- b_fc1_grad: float32 [8192], P(('tensor', 'dp'))
- w_fc2_grad: float32 [8192, 2048], P('tensor', 'dp')
- b_fc2_grad: float32 [2048], P(('dp', 'tensor'))
Inputs may be any that keep to these rules, and one draw needn't show every extreme that they name: `doc_lengths`: row d gives the lengths of the 3 documents packed in order from the first row of group d; their sum lies above 256 and at most 512, and equals 512 for some group; the rows after it are padding.
All inputs are finite; a program needn't handle non-finite values.
Results may differ from a plain program's by a relative error of at most 0.0091.
Values may be sent and summed in bfloat16 or wider, within the bound.
No kernel may reach another device: no remote copies, remote signals or barrier semaphores. Data moves between devices by JAX's collectives and lax.ppermute only.
A program may use at most 320 MiB of HBM per device.

v0:
```python
from functools import partial
import math

import jax
import jax.numpy as jnp
from jax import lax
from jax.sharding import PartitionSpec as P

HD = 256
ROT = 64
DOCS = 3


EPSILON = 1e-05


def layer_norm(rows, gain, shift):
    mean = jnp.mean(rows, axis=-1, keepdims=True)
    centred = rows - mean
    spread = jnp.mean(centred * centred, axis=-1, keepdims=True)
    return centred * lax.rsqrt(spread + EPSILON) * gain + shift


def both_norms(rows, gain_one, shift_one, gain_two, shift_two):
    return (layer_norm(rows, gain_one, shift_one), layer_norm(rows, gain_two, shift_two))


def layout(lengths, count):
    places = jnp.arange(count, dtype=jnp.int32)
    ends = jnp.cumsum(lengths)
    segment = jnp.sum((places[:, None] >= ends[None, :]).astype(jnp.int32), axis=1)
    starts = jnp.concatenate([jnp.zeros((1,), jnp.int32), ends])
    slots = jnp.arange(starts.shape[0], dtype=jnp.int32)
    start = jnp.sum(jnp.where(segment[:, None] == slots[None, :], starts[None, :], 0), axis=1)
    return (segment, places - start)


def angles(position, width):
    half = width // 2
    freq = 10000.0 ** (-(2.0 * jnp.arange(half, dtype=jnp.float32)) / width)
    turn = position.astype(jnp.float32)[:, None] * freq[None, :]
    turn = jnp.concatenate([turn, turn], axis=1)
    return (jnp.cos(turn)[:, None, :], jnp.sin(turn)[:, None, :])


def rotate(field, cosine, sine):
    width = cosine.shape[-1]
    half = width // 2
    part = field[..., :width]
    turned = jnp.concatenate([-part[..., half:], part[..., :half]], axis=-1)
    return jnp.concatenate([part * cosine + turned * sine, field[..., width:]], axis=-1)


def visibility(segment):
    places = jnp.arange(segment.shape[0], dtype=jnp.int32)
    same = segment[:, None] == segment[None, :]
    causal = places[None, :] <= places[:, None]
    live = (segment[:, None] < DOCS) | (places[:, None] == places[None, :])
    return same & causal & live


def masked_scores(query, key, visible, scale):
    raw = jnp.einsum("qhd,khd->hqk", query, key, preferred_element_type=jnp.float32) * scale
    return jnp.where(visible[None], raw, -1e30)


def per_device(
    layer_input,
    doc_lengths,
    ln1_gain,
    ln1_bias,
    ln2_gain,
    ln2_bias,
    w_qkv,
    b_qkv,
    w_dense,
    b_dense,
    w_fc1,
    b_fc1,
    w_fc2,
    b_fc2,
    cotangent,
):
    own_rows = layer_input.shape[0]
    rows = own_rows * lax.axis_size("tensor")
    gain_one, shift_one, gain_two, shift_two, bias_dense, bias_fc2 = (
        lax.all_gather(ln1_gain, ("dp", "tensor"), axis=0, tiled=True),
        lax.all_gather(ln1_bias, ("dp", "tensor"), axis=0, tiled=True),
        lax.all_gather(ln2_gain, ("dp", "tensor"), axis=0, tiled=True),
        lax.all_gather(ln2_bias, ("dp", "tensor"), axis=0, tiled=True),
        lax.all_gather(b_dense, ("dp", "tensor"), axis=0, tiled=True),
        lax.all_gather(b_fc2, ("dp", "tensor"), axis=0, tiled=True),
    )
    w_qkv_all, b_qkv_all, w_dense_all = (
        lax.all_gather(w_qkv, "dp", axis=0, tiled=True),
        lax.all_gather(b_qkv, "dp", axis=0, tiled=True),
        lax.all_gather(w_dense, "dp", axis=1, tiled=True),
    )
    w_fc1_all, b_fc1_all, w_fc2_all = (
        lax.all_gather(w_fc1, "dp", axis=0, tiled=True),
        lax.all_gather(b_fc1, "dp", axis=0, tiled=True),
        lax.all_gather(w_fc2, "dp", axis=1, tiled=True),
    )
    input_own = layer_input.astype(jnp.float32)
    own_one = layer_norm(input_own, gain_one, shift_one).astype(jnp.bfloat16)
    own_two = layer_norm(input_own, gain_two, shift_two).astype(jnp.bfloat16)
    normed_one, normed_two = (
        lax.all_gather(own_one, "tensor", axis=0, tiled=True),
        lax.all_gather(own_two, "tensor", axis=0, tiled=True),
    )
    segment, position = layout(doc_lengths[0], rows)
    visible = visibility(segment)
    cosine, sine = angles(position, ROT)
    heads = w_qkv_all.shape[1] // (3 * HD)
    scale = 1.0 / math.sqrt(HD)
    qkv = (jnp.dot(normed_one, w_qkv_all, preferred_element_type=jnp.float32) + b_qkv_all).reshape(
        rows, heads, 3, HD
    )
    query = rotate(qkv[:, :, 0], cosine, sine).astype(jnp.bfloat16)
    key = rotate(qkv[:, :, 1], cosine, sine).astype(jnp.bfloat16)
    value = qkv[:, :, 2].astype(jnp.bfloat16)
    scores = masked_scores(query, key, visible, scale)
    peak = jnp.max(scores, axis=-1, keepdims=True)
    expo = jnp.exp(scores - peak)
    total = jnp.sum(expo, axis=-1, keepdims=True)
    log_total = peak + jnp.log(total)
    probs = expo / total
    mixed = jnp.einsum(
        "hqk,khd->qhd", probs.astype(jnp.bfloat16), value, preferred_element_type=jnp.float32
    )
    mixed = mixed.astype(jnp.bfloat16).reshape(rows, heads * HD)
    attention = jnp.dot(mixed, w_dense_all, preferred_element_type=jnp.float32)
    pre = jnp.dot(normed_two, w_fc1_all, preferred_element_type=jnp.float32) + b_fc1_all
    hidden = jax.nn.gelu(pre, approximate=False).astype(jnp.bfloat16)
    feed = jnp.dot(hidden, w_fc2_all, preferred_element_type=jnp.float32)
    summed = lax.psum_scatter(attention + feed, "tensor", scatter_dimension=0, tiled=True)
    output = (input_own + summed + bias_dense + bias_fc2).astype(jnp.bfloat16)
    cot_all = lax.all_gather(cotangent, "tensor", axis=0, tiled=True)
    w_fc1_all, b_fc1_all, w_fc2_all = (
        lax.all_gather(w_fc1, "dp", axis=0, tiled=True),
        lax.all_gather(b_fc1, "dp", axis=0, tiled=True),
        lax.all_gather(w_fc2, "dp", axis=1, tiled=True),
    )
    w_qkv_all, b_qkv_all, w_dense_all = (
        lax.all_gather(w_qkv, "dp", axis=0, tiled=True),
        lax.all_gather(b_qkv, "dp", axis=0, tiled=True),
        lax.all_gather(w_dense, "dp", axis=1, tiled=True),
    )
    hidden_grad = jnp.einsum("rd,fd->rf", cot_all, w_fc2_all, preferred_element_type=jnp.float32)
    gelu_pull = jax.vjp(partial(jax.nn.gelu, approximate=False), pre)[1]
    pre_grad = gelu_pull(hidden_grad)[0].astype(jnp.bfloat16)
    fc1_bias_grad = jnp.sum(pre_grad, axis=0, dtype=jnp.float32)
    normed_two_grad = jnp.einsum(
        "rf,df->rd", pre_grad, w_fc1_all, preferred_element_type=jnp.float32
    )
    fc2_grad = jnp.einsum("rf,rd->fd", hidden, cot_all, preferred_element_type=jnp.float32)
    fc1_grad = jnp.einsum("rd,rf->df", normed_two, pre_grad, preferred_element_type=jnp.float32)
    fc1_share, fc1_bias_share, fc2_share = (
        lax.psum_scatter(fc1_grad, "dp", scatter_dimension=0, tiled=True),
        lax.psum_scatter(fc1_bias_grad, "dp", scatter_dimension=0, tiled=True),
        lax.psum_scatter(fc2_grad, "dp", scatter_dimension=1, tiled=True),
    )
    mixed_grad = jnp.einsum("rd,cd->rc", cot_all, w_dense_all, preferred_element_type=jnp.float32)
    mixed_grad = mixed_grad.astype(jnp.bfloat16).reshape(rows, heads, HD)
    probs_again = jnp.exp(masked_scores(query, key, visible, scale) - log_total)
    value_grad = jnp.einsum(
        "hqk,qhd->khd",
        probs_again.astype(jnp.bfloat16),
        mixed_grad,
        preferred_element_type=jnp.float32,
    )
    probs_grad = jnp.einsum("qhd,khd->hqk", mixed_grad, value, preferred_element_type=jnp.float32)
    inner = jnp.sum(probs_again * probs_grad, axis=-1, keepdims=True)
    score_grad = (probs_again * (probs_grad - inner)).astype(jnp.bfloat16)
    query_turned = (
        jnp.einsum("hqk,khd->qhd", score_grad, key, preferred_element_type=jnp.float32) * scale
    )
    key_turned = (
        jnp.einsum("hqk,qhd->khd", score_grad, query, preferred_element_type=jnp.float32) * scale
    )
    unturn = jax.vjp(partial(rotate, cosine=cosine, sine=sine), qkv[:, :, 0])[1]
    qkv_grad = jnp.stack([unturn(query_turned)[0], unturn(key_turned)[0], value_grad], axis=2)
    qkv_grad = qkv_grad.astype(jnp.bfloat16).reshape(rows, heads * 3 * HD)
    qkv_bias_grad = jnp.sum(qkv_grad, axis=0, dtype=jnp.float32)
    normed_one_grad = jnp.einsum(
        "rc,dc->rd", qkv_grad, w_qkv_all, preferred_element_type=jnp.float32
    )
    dense_grad = jnp.einsum("rc,rd->cd", mixed, cot_all, preferred_element_type=jnp.float32)
    qkv_weight_grad = jnp.einsum(
        "rd,rc->dc", normed_one, qkv_grad, preferred_element_type=jnp.float32
    )
    qkv_share, qkv_bias_share, dense_share = (
        lax.psum_scatter(qkv_weight_grad, "dp", scatter_dimension=0, tiled=True),
        lax.psum_scatter(qkv_bias_grad, "dp", scatter_dimension=0, tiled=True),
        lax.psum_scatter(dense_grad, "dp", scatter_dimension=1, tiled=True),
    )
    one_grad, two_grad = (
        lax.psum_scatter(normed_one_grad, "tensor", scatter_dimension=0, tiled=True),
        lax.psum_scatter(normed_two_grad, "tensor", scatter_dimension=0, tiled=True),
    )
    norm_pull = jax.vjp(both_norms, input_own, gain_one, shift_one, gain_two, shift_two)[1]
    input_term, term_g1, term_s1, term_g2, term_s2 = norm_pull((one_grad, two_grad))
    input_grad = (cotangent.astype(jnp.float32) + input_term).astype(jnp.bfloat16)
    bias_out = jnp.sum(cotangent, axis=0, dtype=jnp.float32)
    vector_sums = (
        lax.psum_scatter(term_g1, ("dp", "tensor"), scatter_dimension=0, tiled=True),
        lax.psum_scatter(term_s1, ("dp", "tensor"), scatter_dimension=0, tiled=True),
        lax.psum_scatter(term_g2, ("dp", "tensor"), scatter_dimension=0, tiled=True),
        lax.psum_scatter(term_s2, ("dp", "tensor"), scatter_dimension=0, tiled=True),
        lax.psum_scatter(bias_out, ("dp", "tensor"), scatter_dimension=0, tiled=True),
    )
    return (
        output,
        input_grad,
        vector_sums[0],
        vector_sums[1],
        vector_sums[2],
        vector_sums[3],
        qkv_share,
        qkv_bias_share,
        dense_share,
        vector_sums[4],
        fc1_share,
        fc1_bias_share,
        fc2_share,
        vector_sums[4],
    )


def solution(mesh):
    placed = (
        P(("dp", "tensor"), None),
        P("dp", None),
        P(("dp", "tensor")),
        P(("dp", "tensor")),
        P(("dp", "tensor")),
        P(("dp", "tensor")),
        P("dp", "tensor"),
        P(("tensor", "dp")),
        P("tensor", "dp"),
        P(("dp", "tensor")),
        P("dp", "tensor"),
        P(("tensor", "dp")),
        P("tensor", "dp"),
        P(("dp", "tensor")),
        P(("dp", "tensor"), None),
    )
    return jax.shard_map(
        per_device,
        mesh=mesh,
        in_specs=placed,
        out_specs=(
            P(("dp", "tensor"), None),
            P(("dp", "tensor"), None),
            P(("dp", "tensor")),
            P(("dp", "tensor")),
            P(("dp", "tensor")),
            P(("dp", "tensor")),
            P("dp", "tensor"),
            P(("tensor", "dp")),
            P("tensor", "dp"),
            P(("dp", "tensor")),
            P("dp", "tensor"),
            P(("tensor", "dp")),
            P("tensor", "dp"),
            P(("dp", "tensor")),
        ),
        check_vma=False,
    )
```

profile of v0, /device:TPU:8, one launch (start us, length us, event | category | flops | bytes accessed | tf_op | source)
XLA Modules:
  0.0 1737.8 jit_solution(15888626177040818360)
XLA Ops:
  7.2 0.7 all-gather.21.cloned.1.call-update
  8.0 0.7 all-gather.13.cloned.1.call-update
  8.7 0.9 dynamic-update-slice.3
  9.6 0.9 dynamic-update-slice.4
  10.5 0.9 dynamic-update-slice
  11.3 0.9 dynamic-update-slice.1
  12.2 41.0 %all-reduce.23 = (f32[2048]{0:T(1024)S(1)}, f32[2048]{0:T(1024)S(1)}, f32[2048]{0:T(1024)S(1)}, f32[2048]{0:T(1024)S(1)}) all-reduce(f32[2048]{0:T(1024)S(1)} %dynamic-update-slice.1, f32[2048]{0:T(1024)S(1)} %dynamic-update-slice, f32[2048]{0:T(1024)S(1)} %dynamic-update-slice.4, ...), channel_id=1, replica_groups=mesh['dp'=16,'tensor'=2] {'dp','tensor'}, use_global_device_ids=true, to_apply=%add.9 | all-reduce | flops 8192 | bytes 65536
  53.2 1.5 convert_reduce_fusion.2
  54.7 1.7 fusion.25
  57.0 2.0 fusion.22
  60.9 0.7 all-gather.19.cloned.1.call-update
  63.2 24.5 %all-reduce.10 = bf16[3072]{0:T(1024)(128)(2,1)S(1)} all-reduce(bf16[3072]{0:T(1024)(128)(2,1)S(1)} %dynamic-update-slice.2), channel_id=1, replica_groups=mesh['dp'=16,'tensor'=2] {'dp'}, use_global_device_ids=true, to_apply=%add.10 | all-reduce | flops 3072 | bytes 12288
  87.7 22.3 %all-gather = bf16[16,1,256]{2,1,0:T(2,128)(2,1)S(1)} all-gather(bf16[1,1,256]{2,1,0:T(2,128)(2,1)S(1)} %reshape.286), channel_id=1, replica_groups=mesh['dp'=16,'tensor'=2] {'dp'}, dimensions={0}, use_global_device_ids=true | all-gather | bytes 8704 | tf_op jit(solution)/shard_map/all_gather | solution.py:101
  110.6 1.8 fusion.51
  112.3 0.9 fusion.45
  113.3 5.2 convolution_convert_fusion
  119.0 15.1 all-gather.9.cloned.1.call-done
  134.1 101.6 %all-gather.11.cloned.1.call-done = bf16[2048,3072]{1,0:T(8,128)(2,1)} async-done(((bf16[128,3072]{1,0:T(8,128)(2,1)}), bf16[2048,3072]{1,0:T(8,128)(2,1)}) %all-gather.11.cloned.1.call-update) | async-done | bytes 12582928 | tf_op jit(solution)/shard_map/all_gather | solution.py:95
  235.7 11.9 convolution_add_fusion
  247.6 6.5 copy.79
  254.1 4.7 fusion.61
  258.8 1.9 copy.107
  260.7 1.3 slice.77
  262.1 3.1 copy.108
  265.2 2.0 slice.76
  267.2 2.4 slice_negate_fusion.2
  269.6 0.8 fusion.43
  270.9 1.6 fusion.65
  273.1 1.0 copy-done.21
  274.1 2.6 multiply_reduce_fusion
  276.7 1.2 multiply_convert_fusion.1
  278.0 1.2 multiply_bitcast_fusion.1
  279.8 0.8 multiply_bitcast_fusion
  282.1 0.7 pad_add_fusion.1
  283.9 11.5 fusion.35
  295.3 1.3 convert_reduce_fusion.1
  296.6 2.8 copy.95
  299.5 12.0 fusion.69
  311.6 85.8 %all-gather.17.cloned.1.call-done = bf16[2048,4096]{1,0:T(8,128)(2,1)} async-done(((bf16[128,4096]{1,0:T(8,128)(2,1)}), bf16[2048,4096]{1,0:T(8,128)(2,1)}) %all-gather.17.cloned.1.call-update) | async-done | bytes 16777232 | tf_op jit(solution)/shard_map/all_gather | solution.py:100
  397.4 15.0 fusion.67
  412.4 115.8 %all-gather.19.cloned.1.call-done = bf16[4096,2048]{1,0:T(8,128)(2,1)} async-done(((bf16[4096,128]{1,0:T(8,128)(2,1)}), bf16[4096,2048]{1,0:T(8,128)(2,1)}) %all-gather.19.cloned.1.call-update) | async-done | bytes 16777232 | tf_op jit(solution)/shard_map/all_gather | solution.py:102
  528.1 32.3 %convert_reduce_fusion = (f32[4096]{0:T(1024)S(1)}, bf16[512,4096]{1,0:T(8,128)(2,1)S(1)}, f32[512,4096]{1,0:T(8,128)}) fusion(f32[512,4096]{1,0:T(8,128)} %fusion.67, f32[4096]{0:T(1024)S(1)} %bitcast.74, bf16[512,2048]{1,0:T(8,128)(2,1)S(1)} %copy-done.28, bf16[4096,2048]{1,0:T(8,128)(2,1)} %all-gather.19.cloned.1.call-done), kind=kOutput, calls=%fused_computation.2 | convolution fusion | flops 8747216896 | bytes 39878656 | tf_op jit(solution)/shard_map/rd,fd->rf/dot_general | solution.py:149
  560.5 1.9 copy-done.37
  562.4 14.1 fusion.68
  577.2 4.0 fusion.38
  581.3 2.5 fusion.66
  583.8 9.9 multiply_convert_fusion
  593.7 15.4 convolution_add_fusion.1
  609.2 7.2 fusion.71
  616.5 1.8 copy-done.9
  618.3 13.7 fusion.70
  632.1 1.5 copy-done.29
  633.6 18.3 %fusion.73 = f32[4096,2048]{1,0:T(8,128)} fusion(bf16[512,4096]{1,0:T(8,128)(2,1)} %multiply_convert_fusion, bf16[512,2048]{1,0:T(8,128)(2,1)S(1)} %copy-done.29), kind=kOutput, calls=%fused_computation.138 | convolution fusion | flops 8589934592 | bytes 39845888 | tf_op jit(solution)/shard_map/rf,rd->fd/dot_general | solution.py:156
  652.0 1.5 copy-done.30
  653.5 17.9 %fusion.72 = f32[2048,4096]{1,0:T(8,128)} fusion(bf16[512,2048]{1,0:T(8,128)(2,1)S(1)} %copy-done.30, bf16[512,4096]{1,0:T(8,128)(2,1)} %copy-done.37), kind=kOutput, calls=%fused_computation.137 | convolution fusion | flops 8589934592 | bytes 39845888 | tf_op jit(solution)/shard_map/rd,rf->df/dot_general | solution.py:157
  673.7 53.7 %all-reduce.24 = (f32[3072]{0:T(1024)S(1)}, f32[4096]{0:T(1024)S(1)}) all-reduce(f32[3072]{0:T(1024)S(1)} %reduce_sum.177, f32[4096]{0:T(1024)S(1)} %get-tuple-element.37), channel_id=10, replica_groups=mesh['dp'=16,'tensor'=2] {'dp'}, use_global_device_ids=true, to_apply=%region_25.26.clone | all-reduce | flops 7168 | bytes 57344
  728.7 3.2 fusion.59
  732.2 1.7 fusion.24
  733.8 49.9 %all-reduce.22 = (f32[2048]{0:T(1024)S(1)}, f32[2048]{0:T(1024)S(1)}, f32[2048]{0:T(1024)S(1)}, f32[2048]{0:T(1024)S(1)}, f32[2048]{0:T(1024)S(1)}, /*index=5*/f32[2048]{0:T(1024)S(1)}, f32[2048]{0:T(1024)S(1)}) all-reduce(f32[2048]{0:T(1024)S(1)} %dynamic-update-slice.6, ...), channel_id=1, replica_groups=mesh['dp'=16,'tensor'=2] {'dp','tensor'}, use_global_device_ids=true, to_apply=%add.14 | all-reduce | flops 14336 | bytes 114688
  786.2 4.6 fusion.18
  790.8 18.3 %reduce-scatter.16.cloned.1.call-done = f32[1024,128]{1,0:T(8,128)} async-done(((f32[1024,2048]{1,0:T(8,128)}), f32[1024,128]{1,0:T(8,128)}) %reduce-scatter.16.cloned.1.call-update) | async-done | bytes 524304 | tf_op jit(solution)/shard_map/reduce_scatter | solution.py:195
  809.0 246.7 %reduce-scatter.14.cloned.1.call-done = f32[128,3072]{1,0:T(8,128)} async-done(((f32[2048,3072]{1,0:T(8,128)}), f32[128,3072]{1,0:T(8,128)}) %reduce-scatter.14.cloned.1.call-update) | async-done | bytes 1572880 | tf_op jit(solution)/shard_map/reduce_scatter | solution.py:193
  1055.7 337.7 %reduce-scatter.20.cloned.1.call-done = f32[4096,128]{1,0:T(8,128)} async-done(((f32[4096,2048]{1,0:T(8,128)}), f32[4096,128]{1,0:T(8,128)}) %reduce-scatter.20.cloned.1.call-update) | async-done | bytes 2097168 | tf_op jit(solution)/shard_map/reduce_scatter | solution.py:161
  1393.4 337.1 %reduce-scatter.18.cloned.1.call-done = f32[128,4096]{1,0:T(8,128)} async-done(((f32[2048,4096]{1,0:T(8,128)}), f32[128,4096]{1,0:T(8,128)}) %reduce-scatter.18.cloned.1.call-update) | async-done | bytes 2097168 | tf_op jit(solution)/shard_map/reduce_scatter | solution.py:159
  (151 shorter events, 15.0 us)
Async XLA Ops:
  7.2 49.8 %copy-start.1 = (bf16[256,2048]{1,0:T(8,128)(2,1)S(1)}, bf16[256,2048]{1,0:T(8,128)(2,1)}, u32[]{:S(2)}) copy-start(bf16[256,2048]{1,0:T(8,128)(2,1)} %param.15) | copy-start | bytes 3145732
  7.2 106.1 %all-gather.21.cloned.1.call-start = ((), (), s32[]{:S(2)}) async-start(), calls=%async_computation.14 | async-start | bytes 3145728 | tf_op jit(solution)/shard_map/all_gather | solution.py:138
  7.9 105.4 %all-gather.13.cloned.1.call-start = ((), (), s32[]{:S(2)}) async-start(), calls=%async_computation.9 | async-start | bytes 4456448 | tf_op jit(solution)/shard_map/all_gather | solution.py:97
  8.7 125.4 %all-gather.9.cloned.1.call-start = ((), (), s32[]{:S(2)}) async-start(), calls=%async_computation.7 | async-start | bytes 3145728 | tf_op jit(solution)/shard_map/all_gather | solution.py:108
  53.2 7.6 copy-start.12
  53.2 7.6 copy-start.14
  54.7 4.3 copy-start.17
  56.3 0.6 copy-start.25
  56.9 4.7 copy-start.31
  56.9 4.7 copy-start.27
  56.9 6.0 copy-start.32
  56.9 53.0 %copy-start.33 = (s32[1,3]{1,0:T(1,128)S(1)}, s32[1,3]{1,0:T(1,128)}, u32[]{:S(2)}) copy-start(s32[1,3]{1,0:T(1,128)} %param.16) | copy-start | bytes 40
  56.9 2.1 copy-start.23
  59.0 176.7 %all-gather.11.cloned.1.call-start = ((), (), s32[]{:S(2)}) async-start(), calls=%async_computation.8 | async-start | bytes 13369344 | tf_op jit(solution)/shard_map/all_gather | solution.py:95
  59.6 252.0 %all-gather.15.cloned.1.call-start = ((), (), s32[]{:S(2)}) async-start(), calls=%async_computation.10 | async-start | bytes 3145728 | tf_op jit(solution)/shard_map/all_gather | solution.py:109
  60.2 337.2 %all-gather.17.cloned.1.call-start = ((), (), s32[]{:S(2)}) async-start(), calls=%async_computation.11 | async-start | bytes 17825792 | tf_op jit(solution)/shard_map/all_gather | solution.py:100
  60.8 467.3 %all-gather.19.cloned.1.call-start = ((), (), s32[]{:S(2)}) async-start(), calls=%async_computation.12 | async-start | bytes 17825792 | tf_op jit(solution)/shard_map/all_gather | solution.py:102
  61.6 667.1 %reduce-scatter.12.cloned.1.call-start = ((), (), s32[]{:S(2)}) async-start(), calls=%async_computation.16 | async-start | bytes 6291456 | tf_op jit(solution)/shard_map/reduce_scatter | solution.py:198
  267.2 2.5 copy-start.5
  267.2 2.5 copy-start.10
  269.6 1.2 copy-start.8
  269.6 1.3 copy-start.11
  272.5 4.3 copy-start.19
  272.5 11.4 copy-start
  273.1 1.0 copy-start.21
  311.5 216.6 %copy-start.28 = (bf16[512,2048]{1,0:T(8,128)(2,1)S(1)}, bf16[512,2048]{1,0:T(8,128)(2,1)}, u32[]{:S(2)}) copy-start(bf16[512,2048]{1,0:T(8,128)(2,1)} %all-gather.21.cloned.1.call-done) | copy-start | bytes 6291460
  311.5 417.2 %reduce-scatter.10.cloned.1.call-start = ((), (), s32[]{:S(2)}) async-start(), calls=%async_computation.15 | async-start | bytes 6291456 | tf_op jit(solution)/shard_map/reduce_scatter | solution.py:199
  560.5 2.0 copy-start.37
  576.5 0.7 copy-start.20
  576.5 0.7 copy-start.22
  576.5 209.6 %reduce-scatter.8.cloned.1.call-start = ((), (), s32[]{:S(2)}) async-start(), calls=%async_computation.13 | async-start | bytes 6291456 | tf_op jit(solution)/shard_map/reduce_scatter | solution.py:136
  577.2 4.1 copy-start.6
  609.1 199.9 %reduce-scatter.16.cloned.1.call-start = ((), (), s32[]{:S(2)}) async-start(), calls=%async_computation.18 | async-start | bytes 8912896 | tf_op jit(solution)/shard_map/reduce_scatter | solution.py:195
  616.4 1.9 copy-start.9
  616.4 439.3 %reduce-scatter.14.cloned.1.call-start = ((), (), s32[]{:S(2)}) async-start(), calls=%async_computation.17 | async-start | bytes 26738688 | tf_op jit(solution)/shard_map/reduce_scatter | solution.py:193
  632.0 1.6 copy-start.29
  632.0 761.4 %reduce-scatter.20.cloned.1.call-start = ((), (), s32[]{:S(2)}) async-start(), calls=%async_computation.20 | async-start | bytes 35651584 | tf_op jit(solution)/shard_map/reduce_scatter | solution.py:161
  651.9 1.6 copy-start.30
  651.9 1078.6 %reduce-scatter.18.cloned.1.call-start = ((), (), s32[]{:S(2)}) async-start(), calls=%async_computation.19 | async-start | bytes 35651584 | tf_op jit(solution)/shard_map/reduce_scatter | solution.py:159
  671.4 1.5 copy-start.34
  671.4 1.8 copy-start.35
  671.4 2.1 copy-start.7
  671.4 2.3 copy-start.16
  671.4 57.3 %copy-start.2 = (bf16[256,2048]{1,0:T(8,128)(2,1)S(1)}, bf16[256,2048]{1,0:T(8,128)(2,1)}, u32[]{:S(2)}) copy-start(bf16[256,2048]{1,0:T(8,128)(2,1)} %param.15) | copy-start | bytes 3145732
  671.4 57.3 %copy-start.13 = (f32[2048]{0:T(1024)S(1)}, f32[2048]{0:T(1024)}, u32[]{:S(2)}) copy-start(f32[2048]{0:T(1024)} %copy-done.12) | copy-start | bytes 24580
  671.4 57.3 %copy-start.15 = (f32[2048]{0:T(1024)S(1)}, f32[2048]{0:T(1024)}, u32[]{:S(2)}) copy-start(f32[2048]{0:T(1024)} %copy-done.14) | copy-start | bytes 24580
  671.4 57.3 %copy-start.18 = (f32[256]{0:T(256)S(1)}, f32[256]{0:T(256)}, u32[]{:S(2)}) copy-start(f32[256]{0:T(256)} %copy-done.17) | copy-start | bytes 3076
  671.5 60.5 %copy-start.26 = (f32[256]{0:T(256)S(1)}, f32[256]{0:T(256)}, u32[]{:S(2)}) copy-start(f32[256]{0:T(256)} %copy-done.25) | copy-start | bytes 3076
  671.5 60.5 %copy-start.24 = (f32[256]{0:T(256)S(1)}, f32[256]{0:T(256)}, u32[]{:S(2)}) copy-start(f32[256]{0:T(256)} %copy-done.23) | copy-start | bytes 3076
  728.7 3.3 copy-start.3
  728.7 3.5 copy-start.4
  783.8 946.7 %copy-start.36 = (f32[64]{0:T(128)}, f32[64]{0:T(128)S(1)}, u32[]{:S(2)}) copy-start(f32[64]{0:T(128)S(1)} %dynamic-slice.7) | copy-start | bytes 772
Sparse Core Ops, SparseCore 0:
  9.6 34.7 all-gather.20
  46.5 52.1 all-gather.12
  100.8 33.2 all-gather.8
  136.3 99.4 all-gather.10
  237.7 32.6 all-gather.14
  272.4 125.0 all-gather.16
  399.6 128.5 all-gather.18
  530.4 54.3 reduce-scatter.11
  587.2 54.2 reduce-scatter.9
  643.7 54.3 reduce-scatter.7
  703.2 105.7 reduce-scatter.15
  814.1 241.5 reduce-scatter.13
  1061.2 332.2 reduce-scatter.19
  1398.7 331.7 reduce-scatter.17
where the time goes:
time: 1750 us; the launch traced here: 1740 us
  waiting for transfers between devices  1260 us (72%)
  blocking collectives  191 us (11%)
  matrix products  187 us (11%)
  local copies, waits for them, and re-layouts  43 us (2%)
  other arithmetic  37 us (2%)
    reduce_scatter x1, waiting for transfers between devices, per_device(): lax.psum_scatter(fc2_grad, 'dp', scatter_dimension=1, tiled=True)  338 us
    reduce_scatter x1, waiting for transfers between devices, per_device(): lax.psum_scatter(fc1_grad, 'dp', scatter_dimension=0, tiled=True)  337 us
    reduce_scatter x1, waiting for transfers between devices, per_device(): lax.psum_scatter(qkv_weight_grad, 'dp', scatter_dimension=0, tiled=True)  247 us
    unnamed x4, blocking collectives  169 us
    all_gather x1, waiting for transfers between devices, per_device(): lax.all_gather(w_fc2, 'dp', axis=1, tiled=True)  116 us
    all_gather x1, waiting for transfers between devices, per_device(): lax.all_gather(w_qkv, 'dp', axis=0, tiled=True)  102 us
    all_gather x1, waiting for transfers between devices, per_device(): lax.all_gather(w_fc1, 'dp', axis=0, tiled=True)  85.8 us
  transfers between devices with their start and end apart: 14, of which 8 were waited for; matrix products, arithmetic and copies ran while one was open for 15% of the time, Pallas kernels for 0%

commit v1 on v0

v1 whole, which is shorter than its diff:
```python
import functools
import math

import jax
import jax.numpy as jnp
from jax import lax
from jax.experimental import pallas as pl
from jax.experimental.pallas import tpu as pltpu
from jax.sharding import PartitionSpec as P

HD = 256
ROT = 64
DOCS = 3
EPSILON = 1e-05
INNER = 4
LANES = 128
FEED = (1, 1, 1, 1)
AXES = ("dp", "tensor")
BF = jnp.bfloat16
F32 = jnp.float32
NT = ((1,), (1,))
NN = ((1,), (0,))
TN = ((0,), (0,))
VMEM_LIMIT = 56 * 2**20


def dot(a, b, dims):
    return lax.dot_general(a, b, (dims, ((), ())), preferred_element_type=F32)


def take_weights(parts, gain_ref, w1, w2, cols):
    own, near, far_one, far_two, passed_one, passed_two = parts
    for b in range(16):
        lanes = slice(b * LANES, (b + 1) * LANES)
        k = b % 4
        if b < 4:
            block = own[k].astype(F32)
        elif b < 8:
            block = near[k].astype(F32)
        elif b < 12:
            block = far_one[k].astype(F32) + passed_one[k].astype(F32)
        else:
            block = far_two[k].astype(F32) + passed_two[k].astype(F32)
        w1[:, lanes] = (block[:cols] * gain_ref[:, lanes]).astype(BF)
        w2[:, lanes] = block[cols:].astype(BF)


def give_grads(acc1, acc2, col, gain_ref, shift_ref, w1, cols, own_ref, rest_ref, norm_ref):
    for b in range(16):
        lanes = slice(b * LANES, (b + 1) * LANES)
        gain = gain_ref[:, lanes]
        m = acc1[:, lanes]
        w = w1[:, lanes].astype(F32)
        to, k = (own_ref, b) if b < 4 else (rest_ref, b - 4)
        to[k, :cols] = (m * gain + col[...] * shift_ref[:, lanes]).astype(BF)
        to[k, cols:] = acc2[:, lanes].astype(BF)
        norm_ref[0:1, lanes] = jnp.sum(w * m, axis=0, keepdims=True) / gain
        norm_ref[1:2, lanes] = jnp.sum(w * col[...], axis=0, keepdims=True) / gain


def stream(step, sources, buffers, sems):
    steps = len(sources[0]) // 2

    def copies(s):
        made = []
        for blocks, buffer in zip(sources, buffers):
            for k in (2 * s, 2 * s + 1):
                at = 0
                for ref in blocks[k]:
                    rows, cols = ref.shape
                    to = buffer.at[s % 2, pl.ds((k % 2) * rows, rows), pl.ds(at, cols)]
                    made.append(pltpu.make_async_copy(ref, to, sems.at[s % 2, len(made)]))
                    at += cols
        return made

    def begin(s):
        for c in copies(s):
            c.start()

    def arrive():
        for s in range(steps):
            @pl.when(step == s)
            def _(s=s):
                if s + 1 < steps:
                    begin(s + 1)
                for c in copies(s):
                    c.wait()

    return begin, arrive


def split_refs(shape, refs):
    refs, arrays = list(refs), []
    for counts in shape:
        arrays.append([[refs.pop(0) for _ in range(n)] for n in counts])
    return arrays, refs


def feed_kernel(shape, cols, *refs):
    sources, refs = split_refs(shape, refs)
    p0, p1, p2, p3, p4, p5, gain_ref, shift_ref, ratio_ref, bias_ref = refs[:10]
    hidden_ref, pre_grad_ref, w1, w2, own_ref, rest_ref, norm_ref, sum_ref = refs[10:18]
    acc1, acc2, col, row, unit_buf, cot_buf, sems = refs[18:]
    step = pl.program_id(0)
    begin, arrive = stream(step, sources, (unit_buf, cot_buf), sems)

    @pl.when(step == 0)
    def _():
        begin(0)
        take_weights((p0, p1, p2, p3, p4, p5), gain_ref, w1, w2, cols)
        row[...] = jnp.sum(dot(ratio_ref[...], w1[...], NT), axis=0, keepdims=True) + bias_ref[...]
        acc1[...] = jnp.zeros_like(acc1)
        acc2[...] = jnp.zeros_like(acc2)
        col[...] = jnp.zeros_like(col)
        sum_ref[...] = jnp.zeros_like(sum_ref)

    arrive()
    slot = lax.rem(step, 2)
    unit = unit_buf[slot]
    cot = cot_buf[slot]
    pre = dot(unit, w1[...], NT) + row[...]
    back = dot(cot, w2[...], NT)
    phi = 0.5 * (1.0 + lax.erf(pre * (1.0 / math.sqrt(2.0))))
    slope = phi + pre * (jnp.exp(-0.5 * pre * pre) * (1.0 / math.sqrt(2.0 * math.pi)))
    hidden = (pre * phi).astype(BF)
    pre_grad = (back * slope).astype(BF)
    hidden_ref[...] = hidden
    pre_grad_ref[...] = pre_grad
    acc1[...] += dot(pre_grad, unit, TN)
    acc2[...] += dot(hidden, cot, TN)
    col[...] += dot(pre_grad, jnp.ones((pre_grad.shape[0], LANES), BF), TN)
    sum_ref[...] += jnp.sum(pre_grad.astype(F32), axis=0, keepdims=True)

    @pl.when(step == pl.num_programs(0) - 1)
    def _():
        give_grads(acc1, acc2, col, gain_ref, shift_ref, w1, cols, own_ref, rest_ref, norm_ref)


def whole(shape):
    return pl.BlockSpec(shape, lambda *_: (0,) * len(shape), pipeline_mode=pl.Buffered(1))


def flat(arrays):
    return [p for blocks in arrays for block in blocks for p in block]


def counts(arrays):
    return tuple(tuple(len(block) for block in blocks) for blocks in arrays)


def stream_scratch(rows, width):
    return [pltpu.VMEM((2, rows, width), BF), pltpu.VMEM((2, rows, width), BF), pltpu.SemaphoreType.DMA((2, 8))]


ANYWHERE = pl.BlockSpec(memory_space=pl.ANY)


def feed_call(arrays, weights, gain, shift, ratio, bias):
    own = arrays[0][0][0]
    block, rows, width = 2 * own.shape[0], 8 * own.shape[0], own.shape[1]
    cols = bias.shape[1]
    pieces = flat(arrays)
    cb = pl.BlockSpec((block, cols), lambda r: (r, 0))
    shapes = [
        jax.ShapeDtypeStruct((rows, cols), BF),
        jax.ShapeDtypeStruct((rows, cols), BF),
        jax.ShapeDtypeStruct((cols, width), BF),
        jax.ShapeDtypeStruct((cols, width), BF),
        jax.ShapeDtypeStruct((4, 2 * cols, LANES), BF),
        jax.ShapeDtypeStruct((12, 2 * cols, LANES), BF),
        jax.ShapeDtypeStruct((2, width), F32),
        jax.ShapeDtypeStruct((1, cols), F32),
    ]
    return pl.pallas_call(
        functools.partial(feed_kernel, counts(arrays), cols),
        grid=(rows // block,),
        out_shape=shapes,
        in_specs=[ANYWHERE] * len(pieces)
        + [whole(w.shape) for w in weights]
        + [whole(v.shape) for v in (gain, shift, ratio, bias)],
        out_specs=[cb, cb] + [whole(s.shape) for s in shapes[2:]],
        scratch_shapes=[
            pltpu.VMEM((cols, width), F32), pltpu.VMEM((cols, width), F32), pltpu.VMEM((cols, LANES), F32),
            pltpu.VMEM((1, cols), F32),
        ]
        + stream_scratch(block, width),
        compiler_params=pltpu.CompilerParams(vmem_limit_bytes=VMEM_LIMIT),
        cost_estimate=pl.CostEstimate(flops=8 * rows * width * cols, bytes_accessed=4 * rows * width, transcendentals=0),
        name="feed",
    )(*pieces, *weights, gain, shift, ratio, bias)


def attention_kernel(shape, cols, lengths, half_ref, *refs):
    sources, refs = split_refs(shape, refs)
    p0, p1, p2, p3, p4, p5, gain_ref, shift_ref, ratio_ref, bias_ref = refs[:10]
    cos_ref, sin_up_ref, sin_down_ref = refs[10:13]
    mixed_ref, qkv_grad_ref, w1, w2, own_ref, rest_ref, norm_ref, sum_ref = refs[13:21]
    acc1, acc2, col, row, unit_buf, cot_buf, sems = refs[21:]
    group = pl.program_id(0)
    begin, arrive = stream(group, sources, (unit_buf, cot_buf), sems)

    @pl.when(group == 0)
    def _():
        begin(0)
        take_weights((p0, p1, p2, p3, p4, p5), gain_ref, w1, w2, cols)
        row[...] = jnp.sum(dot(ratio_ref[...], w1[...], NT), axis=0, keepdims=True) + bias_ref[...]
        acc1[...] = jnp.zeros_like(acc1)
        acc2[...] = jnp.zeros_like(acc2)
        col[...] = jnp.zeros_like(col)
        sum_ref[...] = jnp.zeros_like(sum_ref)

    arrive()
    slot = lax.rem(group, 2)
    unit = unit_buf[slot]
    cot = cot_buf[slot]
    count = unit.shape[0]
    cosine, sin_up, sin_down = cos_ref[...], sin_up_ref[...], sin_down_ref[...]
    half = ROT // 2

    def turn(u):
        p = u[:, :LANES]
        p = p * cosine + pltpu.roll(p, LANES - half, 1) * sin_up + pltpu.roll(p, half, 1) * sin_down
        return jnp.concatenate([p, u[:, LANES:]], axis=1)

    def unturn(u):
        p = u[:, :LANES]
        p = p * cosine + pltpu.roll(p * sin_up, half, 1) + pltpu.roll(p * sin_down, LANES - half, 1)
        return jnp.concatenate([p, u[:, LANES:]], axis=1)

    qkv = dot(unit, w1[...], NT) + row[...]
    query = turn(qkv[:, :HD]).astype(BF)
    key = turn(qkv[:, HD : 2 * HD]).astype(BF)
    value = qkv[:, 2 * HD :].astype(BF)
    back = dot(cot, w2[...], NT).astype(BF)

    shift = half_ref[0]
    at = lax.broadcasted_iota(jnp.int32, (count, 1), 0) + shift
    at = jnp.where(at >= count, at - count, at)
    to = lax.broadcasted_iota(jnp.int32, (1, count), 1) + shift
    to = jnp.where(to >= count, to - count, to)
    end, seg_at, seg_to = 0, jnp.zeros_like(at), jnp.zeros_like(to)
    for k in range(DOCS):
        end = end + lengths[group, k]
        seg_at = seg_at + jnp.where(at >= end, 1, 0)
        seg_to = seg_to + jnp.where(to >= end, 1, 0)
    seg_at = jnp.where(seg_at == DOCS, DOCS + at, seg_at)
    seg_to = jnp.where(seg_to == DOCS, DOCS + to, seg_to)
    visible = (seg_at == seg_to) & (to <= at)

    scale = 1.0 / math.sqrt(HD)
    scores = jnp.where(visible, dot(query, key, NT) * scale, -1e30)
    expo = jnp.exp(scores - jnp.max(scores, axis=1, keepdims=True))
    probs = expo / jnp.sum(expo, axis=1, keepdims=True)
    low = probs.astype(BF)
    mixed = dot(low, value, NN).astype(BF)
    value_grad = dot(low, back, TN)
    probs_grad = dot(back, value, NT)
    inner = jnp.sum(probs * probs_grad, axis=1, keepdims=True)
    score_grad = (probs * (probs_grad - inner)).astype(BF)
    query_grad = unturn(dot(score_grad, key, NN) * scale)
    key_grad = unturn(dot(score_grad, query, TN) * scale)
    qkv_grad = jnp.concatenate([query_grad, key_grad, value_grad], axis=1).astype(BF)
    mixed_ref[...] = mixed
    qkv_grad_ref[...] = qkv_grad
    acc1[...] += dot(qkv_grad, unit, TN)
    acc2[...] += dot(mixed, cot, TN)
    col[...] += dot(qkv_grad, jnp.ones((count, LANES), BF), TN)
    sum_ref[...] += jnp.sum(qkv_grad.astype(F32), axis=0, keepdims=True)

    @pl.when(group == pl.num_programs(0) - 1)
    def _():
        give_grads(acc1, acc2, col, gain_ref, shift_ref, w1, cols, own_ref, rest_ref, norm_ref)


def attention_call(lengths, half, arrays, weights, gain, shift, ratio, bias, turns):
    own = arrays[0][0][0]
    count, rows, width = 2 * own.shape[0], 8 * own.shape[0], own.shape[1]
    cols, ctx = bias.shape[1], HD
    pieces = flat(arrays)
    smem = pl.BlockSpec(memory_space=pltpu.SMEM)
    shapes = [
        jax.ShapeDtypeStruct((rows, ctx), BF),
        jax.ShapeDtypeStruct((rows, cols), BF),
        jax.ShapeDtypeStruct((cols, width), BF),
        jax.ShapeDtypeStruct((ctx, width), BF),
        jax.ShapeDtypeStruct((4, cols + ctx, LANES), BF),
        jax.ShapeDtypeStruct((12, cols + ctx, LANES), BF),
        jax.ShapeDtypeStruct((2, width), F32),
        jax.ShapeDtypeStruct((1, cols), F32),
    ]
    return pl.pallas_call(
        functools.partial(attention_kernel, counts(arrays), cols),
        grid=(rows // count,),
        out_shape=shapes,
        in_specs=[smem, smem]
        + [ANYWHERE] * len(pieces)
        + [whole(w.shape) for w in weights]
        + [whole(v.shape) for v in (gain, shift, ratio, bias)]
        + [pl.BlockSpec((count, LANES), lambda r: (r, 0))] * 3,
        out_specs=[pl.BlockSpec((count, ctx), lambda r: (r, 0)), pl.BlockSpec((count, cols), lambda r: (r, 0))]
        + [whole(s.shape) for s in shapes[2:]],
        scratch_shapes=[
            pltpu.VMEM((cols, width), F32), pltpu.VMEM((ctx, width), F32), pltpu.VMEM((cols, LANES), F32),
            pltpu.VMEM((1, cols), F32),
        ]
        + stream_scratch(count, width),
        compiler_params=pltpu.CompilerParams(vmem_limit_bytes=VMEM_LIMIT),
        cost_estimate=pl.CostEstimate(
            flops=4 * rows * width * (cols + ctx), bytes_accessed=4 * rows * width, transcendentals=0
        ),
        name="attention",
    )(lengths, half, *pieces, *weights, gain, shift, ratio, bias, *turns)


def join_kernel(n, *refs):
    total = dot(refs[0][...], refs[n][...], NN)
    for j in range(1, n):
        total += dot(refs[j][...], refs[n + j][...], NN)
    refs[2 * n][...] = total.astype(BF)


def join_call(acts, weights, sent):
    rows, width = acts[0].shape[0], weights[0].shape[1]
    block = rows // 8
    place = (lambda r: 4 * (r // 2) + r % 2 + 2) if sent else (lambda r: 4 * (r // 2) + r % 2)
    flops = sum(rows * a.shape[1] * width for a in acts)
    return pl.pallas_call(
        functools.partial(join_kernel, len(acts)),
        grid=(4,),
        out_shape=jax.ShapeDtypeStruct((rows // 2, width), BF),
        in_specs=[pl.BlockSpec((block, a.shape[1]), lambda r: (place(r), 0)) for a in acts]
        + [whole(w.shape) for w in weights],
        out_specs=pl.BlockSpec((block, width), lambda r: (r, 0)),
        compiler_params=pltpu.CompilerParams(vmem_limit_bytes=VMEM_LIMIT),
        cost_estimate=pl.CostEstimate(flops=flops, bytes_accessed=2 * rows * width, transcendentals=0),
        name="join",
    )(*acts, *weights)


def after(v, *others):
    return lax.optimization_barrier((v, *others))[0]


def make(dp, tensor):
    outer = dp // INNER
    face = INNER * tensor
    total = dp * tensor
    short = outer == 4

    def permute(v, pairs):
        return lax.ppermute(v, AXES, pairs)

    def flip(v, k):
        return permute(v, [(l, l ^ k) for l in range(total)])

    def hop(v, moves):
        return permute(v, [(a * face + f, b * face + f) for a, b in moves for f in range(face)])

    column_groups = [[o * face + f for o in range(outer)] for f in range(face)]
    ring_groups = [[o * face + i * tensor + t for i in range(INNER)] for o in range(outer) for t in range(tensor)]

    order_table = [[0, 1, 2, 3], [1, 0, 2, 3], [2, 3, 1, 0], [3, 2, 1, 0]]
    back_table = [[0, 1, 2, 3], [1, 0, 2, 3], [3, 2, 0, 1], [3, 2, 1, 0]]

    def blocks(v, table, o):
        if not short:
            return v
        width = v.shape[-1] // outer
        row = jnp.array(table, jnp.int32)[o]
        return jnp.concatenate(
            [lax.dynamic_slice_in_dim(v, row[j] * width, width, axis=v.ndim - 1) for j in range(outer)], axis=-1
        )

    def swap_ring(v):
        return lax.all_to_all(v, AXES, split_axis=0, concat_axis=0, tiled=True, axis_index_groups=ring_groups)

    def gather_step(v, token):
        if not short:
            every = lax.all_gather(v, AXES, axis=0, tiled=True, axis_index_groups=column_groups)
            n = v.shape[1]
            every = every.transpose(1, 0, 2).reshape(n, 16, LANES).transpose(1, 0, 2)
            none = jnp.zeros_like(every[:4])
            return [every[:4], every[4:8], every[8:12], every[12:], none, none], token
        v = after(v, token[0])
        near = flip(v, face)
        far_one = hop(v, [(1, 2), (2, 1)])
        far_two = hop(near, [(1, 2), (2, 1)])
        ready_one = after(far_one, token[1])
        passed_one = hop(ready_one, [(1, 0), (2, 3)])
        ready_two = after(far_two, passed_one)
        passed_two = hop(ready_two, [(1, 0), (2, 3)])
        return [v, near, far_one, far_two, passed_one, passed_two], (near, passed_two)

    def reduce_outer(own, rest, tokens):
        if not short:
            v = jnp.concatenate([own, rest], axis=0)
            n = v.shape[1]
            v = v.transpose(1, 0, 2).reshape(n, dp, -1).transpose(1, 0, 2)
            return lax.psum_scatter(v, AXES, scatter_dimension=0, tiled=True, axis_index_groups=column_groups)
        first = hop(rest, [(0, 1), (3, 2)])
        if tokens[0] is not None:
            first = after(first, tokens[0])
        far = (rest[4:].astype(F32) + first[4:].astype(F32)).astype(BF)
        second = hop(far, [(1, 2), (2, 1)])
        if tokens[1] is not None:
            second = after(second, tokens[1])
        near = (rest[:4].astype(F32) + second[4:].astype(F32)).astype(BF)
        third = hop(near, [(1, 0), (2, 3)])
        if tokens[2] is not None:
            third = after(third, tokens[2])
        total = own.astype(F32) + first[:4].astype(F32) + second[:4].astype(F32) + third.astype(F32)
        return total.astype(BF)

    def reduce_face(kept, sent):
        m = kept.shape[0] // 4
        half = kept.shape[1] // 2
        other = flip(sent, 2)

        def part(k, left):
            cut = slice(0, half) if left else slice(half, 2 * half)
            rows = slice(k * m, (k + 1) * m)
            return kept[rows, cut].astype(F32) + other[rows, cut].astype(F32)

        x1 = flip(jnp.concatenate([part(3, True), part(2, True)], axis=1).astype(BF), 4)
        t1 = flip(jnp.concatenate([part(3, False), part(1, False)], axis=1).astype(BF), 1)
        t2 = flip((part(1, True) + x1[:, :half].astype(F32)).astype(BF), 1)
        x2 = flip((part(2, False) + t1[:, :half].astype(F32)).astype(BF), 4)
        left = part(0, True) + x1[:, half:].astype(F32) + t2.astype(F32)
        right = part(0, False) + t1[:, half:].astype(F32) + x2.astype(F32)
        return jnp.concatenate([left, right], axis=1)

    def per_device(
        layer_input, doc_lengths, ln1_gain, ln1_bias, ln2_gain, ln2_bias, w_qkv, b_qkv, w_dense, b_dense,
        w_fc1, b_fc1, w_fc2, b_fc2, cotangent,
    ):
        d, t = lax.axis_index("dp"), lax.axis_index("tensor")
        o, i = d // INNER, d % INNER
        own_rows, width = layer_input.shape
        group_rows = own_rows * tensor
        strip = width // dp
        ctx = w_dense.shape[0] // INNER
        hidden_own = w_fc1.shape[1] // INNER
        qkv_own = w_qkv.shape[1] // INNER
        unit_cols = hidden_own // sum(FEED)
        sizes = [n * unit_cols for n in FEED]
        starts = [sum(sizes[:c]) for c in range(len(sizes))]

        cot_own = blocks(cotangent, order_table, o)
        cot_t, cot_x, cot_c = flip(cot_own, 1), flip(cot_own, 4), flip(cot_own, 2)

        fc1 = w_fc1.T.reshape(INNER, hidden_own, strip)
        fc2 = w_fc2.reshape(INNER, hidden_own, strip)
        pieces = [
            jnp.concatenate([fc1[:, s : s + n], fc2[:, s : s + n]], axis=1) for s, n in zip(starts, sizes)
        ]
        qkv_piece = jnp.concatenate(
            [w_qkv.T.reshape(INNER, qkv_own, strip), w_dense.reshape(INNER, ctx, strip)], axis=1
        )
        ring = [swap_ring(pieces[0])]

        input_own = layer_input.astype(F32)
        mean = jnp.mean(input_own, axis=-1, keepdims=True)
        centred = input_own - mean
        rstd = lax.rsqrt(jnp.mean(centred * centred, axis=-1, keepdims=True) + EPSILON)
        unit_float = centred * rstd
        unit_own = blocks(unit_float.astype(BF), order_table, o)
        unit_t, unit_x, unit_c = flip(unit_own, 1), flip(unit_own, 4), flip(unit_own, 2)

        second = after(jnp.concatenate([pieces[1], qkv_piece], axis=1), unit_own, ring[0])
        second = swap_ring(second)
        n = pieces[1].shape[1]
        ring += [second[:, :n], second[:, n:]]

        cot_b = flip(cot_x, 1)
        cot_tc, cot_xc = flip(cot_t, 2), flip(cot_x, 2)
        cot_bc = flip(cot_b, 2)
        mid = width // 2
        unit_bl, unit_br = flip(unit_t[:, :mid], 4), flip(unit_x[:, mid:], 1)
        unit_tc, unit_xc = flip(unit_t, 2), flip(unit_x, 2)
        unit_blc, unit_brc = flip(unit_bl, 2), flip(unit_br, 2)
        arrays = [
            [[unit_own], [unit_t], [unit_c], [unit_tc], [unit_x], [unit_bl, unit_br], [unit_xc], [unit_blc, unit_brc]],
            [[cot_own], [cot_t], [cot_c], [cot_tc], [cot_x], [cot_b], [cot_xc], [cot_bc]],
        ]

        third = after(jnp.concatenate(pieces[2:], axis=1), second, unit_x)
        third = swap_ring(third)
        at = 0
        for p in pieces[2:]:
            ring.append(third[:, at : at + p.shape[1]])
            at += p.shape[1]

        full = []
        token = (pieces[0], pieces[0])
        for w in ring:
            got, token = gather_step(w, token)
            full.append(got)

        piece = width // total
        small = jnp.concatenate(
            [ln1_gain, ln1_bias, ln2_gain, ln2_bias, b_dense + b_fc2, b_qkv.astype(F32), b_fc1.astype(F32),
             doc_lengths[0].astype(F32), jnp.zeros((128 - DOCS,), F32)]
        )
        small = jnp.broadcast_to(after(small, unit_own, ring[0])[None], (total, small.shape[0]))
        small = lax.all_to_all(small, AXES, split_axis=0, concat_axis=0, tiled=True)
        small = after(small, second)
        vectors = small[:, : 5 * piece].reshape(total, 5, piece).transpose(1, 0, 2).reshape(5, width)
        vectors = blocks(vectors, order_table, o)
        gain_one, shift_one, gain_two, shift_two, bias_out = (vectors[j : j + 1] for j in range(5))
        nq, nf = b_qkv.shape[0], b_fc1.shape[0]
        mine = lax.dynamic_index_in_dim(small.reshape(dp, tensor, -1), t, 1, keepdims=False)
        at = 5 * piece
        bias_qkv = lax.dynamic_slice_in_dim(mine[:, at : at + nq].reshape(1, -1), i * qkv_own, qkv_own, axis=1)
        bias_fc1 = lax.dynamic_slice_in_dim(
            mine[:, at + nq : at + nq + nf].reshape(1, -1), i * hidden_own, hidden_own, axis=1
        )
        docs = mine[:, at + nq + nf : at + nq + nf + DOCS]
        docs = lax.dynamic_slice_in_dim(docs, o * INNER, INNER, axis=0)
        docs = jnp.concatenate([lax.dynamic_slice_in_dim(docs, i ^ g, 1, axis=0) for g in range(INNER)], axis=0)
        lengths = jnp.round(docs).astype(jnp.int32)

        def fine(v):
            high = v.astype(BF)
            low = (v - high.astype(F32)).astype(BF)
            return jnp.concatenate([high, low, jnp.zeros((14, v.shape[1]), BF)], axis=0)

        ratio_one = fine(shift_one / gain_one)
        ratio_two = fine(shift_two / gain_two)

        place = (jnp.arange(group_rows, dtype=jnp.int32) + t * own_rows) % group_rows
        ends = jnp.cumsum(lengths, axis=1)
        begin = jnp.zeros((INNER, group_rows), jnp.int32)
        for k in range(DOCS):
            begin = jnp.where(place[None] >= ends[:, k : k + 1], ends[:, k : k + 1], begin)
        position = (place[None] - begin).reshape(-1, 1).astype(F32)
        lane = jnp.arange(LANES)
        half = ROT // 2
        freq = 10000.0 ** (-(2.0 * (lane % half).astype(F32)) / ROT)
        angle = position * freq[None]
        cosine = jnp.where(lane < ROT, jnp.cos(angle), 1.0)
        sine = jnp.sin(angle)
        turns = (cosine, jnp.where(lane < half, -sine, 0.0), jnp.where((lane >= half) & (lane < ROT), sine, 0.0))

        def feed(c, weights):
            bias = bias_fc1[:, starts[c] : starts[c] + sizes[c]]
            return feed_call(arrays, weights, gain_two, shift_two, ratio_two, bias)

        shift = (t * own_rows).astype(jnp.int32).reshape(1)
        done = []
        for k, weights in enumerate(full):
            if done:
                weights = [after(weights[0], done[-1][7])] + weights[1:]
            if k == 2:
                p = attention_call(
                    lengths, shift, arrays, weights, gain_one, shift_one, ratio_one, bias_qkv, turns
                )
            else:
                p = feed(k if k < 2 else k - 1, weights)
            done.append(p)
        attn = done[2]
        feeds = done[:2] + done[3:]
        acts, outs = [p[0] for p in done], [p[3] for p in done]
        grads, ins = [p[1] for p in done], [p[2] for p in done]
        back = reduce_face(join_call(grads, ins, False), join_call(grads, ins, True))
        summed = reduce_face(join_call(acts, outs, False), join_call(acts, outs, True))
        names = [p[7] for p in done] + [None] * 8
        reduced = [reduce_outer(p[4], p[5], names[k + 2 : k + 5]) for k, p in enumerate(done)]

        output = (input_own + blocks(summed + bias_out, back_table, o)).astype(BF)
        pulled = blocks(back, back_table, o)
        along = jnp.mean(pulled * unit_float, axis=-1, keepdims=True)
        level = jnp.mean(pulled, axis=-1, keepdims=True)
        term = rstd * (pulled - level - unit_float * along)
        input_grad = (cotangent.astype(F32) + term).astype(BF)

        own_sums = jnp.concatenate([attn[6], sum(p[6] for p in feeds)], axis=0)
        own_sums = blocks(own_sums, back_table, o)
        own_sums = jnp.concatenate([own_sums, jnp.sum(cotangent, axis=0, dtype=F32)[None]], axis=0)
        own_sums = own_sums.reshape(5, total, piece).transpose(1, 0, 2).reshape(total, 5 * piece)
        share = dp // INNER

        def spread(v, n):
            held = jnp.zeros((dp, tensor, n), F32)
            return lax.dynamic_update_slice(held, v.reshape(share, 1, n), (i * share, t, 0)).reshape(total, n)

        tail = jnp.concatenate(
            [own_sums, spread(attn[7], nq), spread(jnp.concatenate([p[7] for p in feeds], axis=1), nf)], axis=1
        )
        pad = -tail.shape[1] % 128
        tail = jnp.concatenate([tail, jnp.zeros((total, pad), F32)], axis=1)
        tail = jnp.sum(lax.all_to_all(tail, AXES, split_axis=0, concat_axis=0, tiled=True), axis=0)
        cuts = [tail[j * piece : (j + 1) * piece] for j in range(5)]
        b_qkv_grad = tail[at : at + nq]
        b_fc1_grad = tail[at + nq : at + nq + nf]

        final = [swap_ring(r) for r in reduced]
        attn_grad = final[2]
        feed_grads = final[:2] + final[3:]
        w_qkv_grad = attn_grad[:, :qkv_own].reshape(INNER * qkv_own, strip).T.astype(F32)
        w_dense_grad = attn_grad[:, qkv_own:].reshape(INNER * ctx, strip).astype(F32)
        w_fc1_grad = jnp.concatenate([g[:, :n] for g, n in zip(feed_grads, sizes)], axis=1)
        w_fc1_grad = w_fc1_grad.reshape(INNER * hidden_own, strip).T.astype(F32)
        w_fc2_grad = jnp.concatenate([g[:, n:] for g, n in zip(feed_grads, sizes)], axis=1)
        w_fc2_grad = w_fc2_grad.reshape(INNER * hidden_own, strip).astype(F32)
        return (
            output, input_grad, cuts[0], cuts[1], cuts[2], cuts[3], w_qkv_grad, b_qkv_grad, w_dense_grad, cuts[4],
            w_fc1_grad, b_fc1_grad, w_fc2_grad, cuts[4],
        )

    return per_device


def solution(mesh):
    rows = P(("dp", "tensor"), None)
    vector = P(("dp", "tensor"))
    crossed = P(("tensor", "dp"))
    wide = P("dp", "tensor")
    tall = P("tensor", "dp")
    return jax.shard_map(
        make(mesh.shape["dp"], mesh.shape["tensor"]),
        mesh=mesh,
        in_specs=(rows, P("dp", None), vector, vector, vector, vector, wide, crossed, tall, vector, wide, crossed,
                  tall, vector, rows),
        out_specs=(rows, rows, vector, vector, vector, vector, wide, crossed, tall, vector, wide, crossed, tall,
                   vector),
        check_vma=False,
    )
```

time: 1750 us -> 665 us (0.38)
  waiting for transfers between devices: 1260 us -> 198 us
  blocking collectives: 191 us -> 0 us
  matrix products: 187 us -> 0 us
  starting transfers between devices: 0.56 us -> 168 us
  Pallas kernels: 0 us -> 160 us
  other arithmetic: 37 us -> 86.4 us
    reduce_scatter x7 -> x0, waiting for transfers between devices: 940 us -> none  [the longest x1 338 us: per_device(): lax.psum_scatter(fc2_grad, 'dp', scatter_dimension=1, tiled=True)]
    all_gather x7 -> x0, waiting for transfers between devices: 318 us -> none  [the longest x1 116 us: per_device(): lax.all_gather(w_fc2, 'dp', axis=1, tiled=True)]
    dot_general x18 -> x0, matrix products: 187 us -> none  [the longest x1 32.3 us: per_device(): jnp.einsum('rd,fd->rf', cot_all, w_fc2_all, preferred_element_type=jnp.fl...]
    ppermute x0 -> x66, waiting for transfers between devices: none -> 186 us  [permute(): return lax.ppermute(v, AXES, pairs)]
    unnamed x4 -> x0, blocking collectives: 169 us -> none
    pallas_call x0 -> x9, Pallas kernels: none -> 160 us  [the longest x4 74.5 us: feed_call(): pl.pallas_call(functools.partial(feed_kernel, counts(arrays), cols), grid...]
    ppermute x0 -> x66, starting transfers between devices: none -> 126 us  [permute(): return lax.ppermute(v, AXES, pairs)]
    all_to_all x0 -> x10, starting transfers between devices: none -> 41.5 us  [the longest x8 31.3 us: swap_ring(): lax.all_to_all(v, AXES, split_axis=0, concat_axis=0, tiled=True, axis_ind...]
  transfers between devices with their start and end apart: 14 -> 76, of which waited for: 8 -> 29; matrix products, arithmetic and copies ran while one was open for 15% -> 16% of each run, Pallas kernels for 0% -> 24%
where the time goes in v1:
time: 665 us; the launch traced here: 654 us
  waiting for transfers between devices  198 us (30%)
  starting transfers between devices  168 us (25%)
  Pallas kernels  160 us (24%)
  other arithmetic  86.4 us (13%)
  local copies, waits for them, and re-layouts  33.7 us (5%)
  between operations  7.98 us (1%)
    ppermute x66, waiting for transfers between devices, permute(): return lax.ppermute(v, AXES, pairs)  186 us
    ppermute x66, starting transfers between devices, permute(): return lax.ppermute(v, AXES, pairs)  126 us
    pallas_call x4, Pallas kernels, feed_call(): pl.pallas_call(functools.partial(feed_kernel, counts(arrays), cols), grid...  74.5 us
    pallas_call x4, Pallas kernels, join_call(): pl.pallas_call(functools.partial(join_kernel, len(acts)), grid=(4,), out_...  46.6 us
    pallas_call x1, Pallas kernels, attention_call(): pl.pallas_call(functools.partial(attention_kernel, counts(arrays), cols),...  38.7 us
    all_to_all x8, starting transfers between devices, swap_ring(): lax.all_to_all(v, AXES, split_axis=0, concat_axis=0, tiled=True, axis_ind...  31.3 us
  transfers between devices with their start and end apart: 76, of which 29 were waited for; matrix products, arithmetic and copies ran while one was open for 16% of the time, Pallas kernels for 24%

profile of v1, /device:TPU:8, one launch (start us, length us, event | category | flops | bytes accessed | tf_op | source)
XLA Modules:
  0.0 653.6 jit_solution(12772864322076787455)
XLA Ops:
  4.1 4.1 all-to-all-start
  21.8 4.6 collective-permute-start.17
  26.4 3.6 all-to-all-start.2
  31.4 7.4 %collective-permute-done.17.refs_20_ = bf16[4,512,128]{2,1,0:T(8,128)(2,1)} collective-permute-done((bf16[4,512,128]{2,1,0:T(8,128)(2,1)}, bf16[4,512,128]{2,1,0:T(8,128)(2,1)}, u32[]{:S(2)}, u32[]{:S(2)}) %collective-permute-start.17) | collective-permute-done | bytes 524320 | tf_op jit(solution)/shard_map/ppermute | solution.py:351
  40.9 3.6 collective-permute-start.18
  51.9 4.5 collective-permute-done.18.refs_21_
  60.2 5.3 all-to-all-start.1
  66.4 4.6 collective-permute-start.22
  79.0 4.2 collective-permute-done.22.refs_20_
  84.4 3.6 collective-permute-start.23
  90.5 9.2 %collective-permute-done.23.refs_21_ = bf16[4,512,128]{2,1,0:T(8,128)(2,1)S(1)} collective-permute-done((bf16[4,512,128]{2,1,0:T(8,128)(2,1)}, bf16[4,512,128]{2,1,0:T(8,128)(2,1)S(1)}, u32[]{:S(2)}, u32[]{:S(2)}) %collective-permute-start.23) | collective-permute-done | bytes 524320 | tf_op jit(solution)/shard_map/ppermute | solution.py:351
  99.7 3.3 collective-permute-start.27
  104.6 3.0 collective-permute-start.25
  108.3 6.8 %collective-permute-done.12.refs_14_ = bf16[256,2048]{1,0:T(8,128)(2,1)} collective-permute-done((bf16[256,2048]{1,0:T(8,128)(2,1)S(1)}, bf16[256,2048]{1,0:T(8,128)(2,1)}, u32[]{:S(2)}, u32[]{:S(2)}) %collective-permute-start.12) | collective-permute-done | bytes 1048608 | tf_op jit(solution)/shard_map/ppermute | solution.py:351
  116.7 3.5 all-to-all-start.3
  120.3 4.3 collective-permute-done.4.refs_5_
  127.4 5.2 collective-permute-done.25.refs_23_
  132.5 3.0 collective-permute-start.28
  137.9 5.8 fusion.11
  144.2 6.8 %collective-permute-done.13.refs_15_ = bf16[256,2048]{1,0:T(8,128)(2,1)} collective-permute-done((bf16[256,2048]{1,0:T(8,128)(2,1)}, bf16[256,2048]{1,0:T(8,128)(2,1)}, u32[]{:S(2)}, u32[]{:S(2)}) %collective-permute-start.13) | collective-permute-done | bytes 1048608 | tf_op jit(solution)/shard_map/ppermute | solution.py:351
  151.1 6.5 collective-permute-done.28.refs_21_
  160.8 5.3 collective-permute-start.30
  166.3 2.9 collective-permute-start.32
  169.2 18.6 %feed.4 = (bf16[2048,256]{1,0:T(8,128)(2,1)}, bf16[2048,256]{1,0:T(8,128)(2,1)}, bf16[256,2048]{1,0:T(8,128)(2,1)}, bf16[256,2048]{1,0:T(8,128)(2,1)}, bf16[4,51...) custom-call(bf16[256,2048]{1,0:T(8,128)(2,1)} %pad_maximum_fusion.2.refs_0_, ...), custom_call_target="tpu_custom_call" | custom-call | flops 8589934592 | bytes 16777216 | tf_op jit(solution)/shard_map/feed/pallas_call | solution.py:174
  189.1 9.6 %collective-permute-done.31.refs_19_ = bf16[4,512,128]{2,1,0:T(8,128)(2,1)S(1)} collective-permute-done((bf16[4,512,128]{2,1,0:T(8,128)(2,1)S(1)}, bf16[4,512,128]{2,1,0:T(8,128)(2,1)S(1)}, u32[]{:S(2)}, u32[]{:S(2)}) %collective-permute-start.31) | collective-permute-done | bytes 524320 | tf_op jit(solution)/shard_map/ppermute | solution.py:351
  205.2 18.6 %feed.5 = (bf16[2048,256]{1,0:T(8,128)(2,1)}, bf16[2048,256]{1,0:T(8,128)(2,1)}, bf16[256,2048]{1,0:T(8,128)(2,1)}, bf16[256,2048]{1,0:T(8,128)(2,1)}, bf16[4,51...) custom-call(bf16[256,2048]{1,0:T(8,128)(2,1)} %pad_maximum_fusion.2.refs_0_, ...), custom_call_target="tpu_custom_call" | custom-call | flops 8589934592 | bytes 16777216 | tf_op jit(solution)/shard_map/feed/pallas_call | solution.py:174
  225.2 3.1 collective-permute-start.37
  228.3 10.3 %collective-permute-done.36.refs_19_ = bf16[4,512,128]{2,1,0:T(8,128)(2,1)} collective-permute-done((bf16[4,512,128]{2,1,0:T(8,128)(2,1)S(1)}, bf16[4,512,128]{2,1,0:T(8,128)(2,1)}, u32[]{:S(2)}, u32[]{:S(2)}) %collective-permute-start.36) | collective-permute-done | bytes 524320 | tf_op jit(solution)/shard_map/ppermute | solution.py:351
  238.6 3.1 collective-permute-start.38
  244.3 38.7 %attention.1 = (bf16[2048,256]{1,0:T(8,128)(2,1)}, bf16[2048,768]{1,0:T(8,128)(2,1)}, bf16[768,2048]{1,0:T(8,128)(2,1)}, bf16[256,2048]{1,0:T(8,128)(2,1)}, bf16...) custom-call(s32[4,3]{1,0:T(4,128)} %copy-done.34, ...), custom_call_target="tpu_custom_call" | custom-call | flops 17179869184 | bytes 16777216 | tf_op jit(solution)/shard_map/attention/pallas_call | solution.py:291
  290.6 4.4 collective-permute-start.39
  295.0 18.7 %feed.6 = (bf16[2048,256]{1,0:T(8,128)(2,1)}, bf16[2048,256]{1,0:T(8,128)(2,1)}, bf16[256,2048]{1,0:T(8,128)(2,1)}, bf16[256,2048]{1,0:T(8,128)(2,1)}, bf16[4,51...) custom-call(bf16[256,2048]{1,0:T(8,128)(2,1)} %pad_maximum_fusion.2.refs_0_, ...), custom_call_target="tpu_custom_call" | custom-call | flops 8589934592 | bytes 16777216 | tf_op jit(solution)/shard_map/feed/pallas_call | solution.py:174
  315.1 6.5 collective-permute-start.40
  329.1 3.0 collective-permute-done.40.refs_23_
  332.0 18.5 %feed.7 = (bf16[2048,256]{1,0:T(8,128)(2,1)}, bf16[2048,256]{1,0:T(8,128)(2,1)}, bf16[256,2048]{1,0:T(8,128)(2,1)}, bf16[256,2048]{1,0:T(8,128)(2,1)}, bf16[4,51...) custom-call(bf16[256,2048]{1,0:T(8,128)(2,1)} %pad_maximum_fusion.2.refs_0_, ...), custom_call_target="tpu_custom_call" | custom-call | flops 8589934592 | bytes 16777216 | tf_op jit(solution)/shard_map/feed/pallas_call | solution.py:174
  352.1 13.0 %join.7 = bf16[1024,2048]{1,0:T(8,128)(2,1)} custom-call(bf16[2048,256]{1,0:T(8,128)(2,1)} %get-tuple-element.120.refs_0_, bf16[2048,256]{1,0:T(8,128)(2,1)} %get-tuple-element.121.refs_1_, bf16[2048,768]{1,0:T(8,128)(2,1)} %get-tuple-element.122.refs_2_, bf16[2048,256]{1,0:T(8,128)(2,1)} %get-tuple-element.123.refs_3_, ...), custom_call_target="tpu_custom_call" | custom-call | flops 7516192768 | bytes 8388608 | tf_op jit(solution)/shard_map/join/pallas_call | solution.py:327
  365.1 13.1 %join.6 = bf16[1024,2048]{1,0:T(8,128)(2,1)} custom-call(bf16[2048,256]{1,0:T(8,128)(2,1)} %get-tuple-element.120.refs_0_, bf16[2048,256]{1,0:T(8,128)(2,1)} %get-tuple-element.121.refs_1_, bf16[2048,768]{1,0:T(8,128)(2,1)} %get-tuple-element.122.refs_2_, bf16[2048,256]{1,0:T(8,128)(2,1)} %get-tuple-element.123.refs_3_, ...), custom_call_target="tpu_custom_call" | custom-call | flops 7516192768 | bytes 8388608 | tf_op jit(solution)/shard_map/join/pallas_call | solution.py:327
  378.4 10.2 %join.5 = bf16[1024,2048]{1,0:T(8,128)(2,1)} custom-call(bf16[2048,256]{1,0:T(8,128)(2,1)} %get-tuple-element.89.refs_0_, bf16[2048,256]{1,0:T(8,128)(2,1)} %get-tuple-element.95.refs_1_, bf16[2048,256]{1,0:T(8,128)(2,1)} %get-tuple-element.101.refs_2_, bf16[2048,256]{1,0:T(8,128)(2,1)} %get-tuple-element.108.refs_3_, ...), custom_call_target="tpu_custom_call" | custom-call | flops 5368709120 | bytes 8388608 | tf_op jit(solution)/shard_map/join/pallas_call | solution.py:327
  389.7 10.3 %join.4 = bf16[1024,2048]{1,0:T(8,128)(2,1)} custom-call(bf16[2048,256]{1,0:T(8,128)(2,1)} %get-tuple-element.89.refs_0_, bf16[2048,256]{1,0:T(8,128)(2,1)} %get-tuple-element.95.refs_1_, bf16[2048,256]{1,0:T(8,128)(2,1)} %get-tuple-element.101.refs_2_, bf16[2048,256]{1,0:T(8,128)(2,1)} %get-tuple-element.108.refs_3_, ...), custom_call_target="tpu_custom_call" | custom-call | flops 5368709120 | bytes 8388608 | tf_op jit(solution)/shard_map/join/pallas_call | solution.py:327
  400.3 6.7 %collective-permute-start.59 = (bf16[4,512,128]{2,1,0:T(8,128)(2,1)}, bf16[4,512,128]{2,1,0:T(8,128)(2,1)}, u32[]{:S(2)}, u32[]{:S(2)}) collective-permute-start(bf16[4,512,128]{2,1,0:T(8,128)(2,1)} %add_convert_fusion.12), channel_id=1, source_target_pairs={{8,0},{9,1},{10,2},{11,3},{12,4},{13,5},{14,6},{15,7},{16,24},{17,... | collective-permute-start | bytes 1572872 | tf_op jit(solution)/shard_map/ppermute | solution.py:351
  414.1 4.1 all-to-all-start.6
  424.7 3.5 add_convert_fusion
  428.1 3.0 collective-permute-start.52
  433.0 4.8 collective-permute-done.61
  444.3 4.1 all-to-all-start.7
  448.5 11.8 %collective-permute-done.64 = bf16[8,512,128]{2,1,0:T(8,128)(2,1)} collective-permute-done((bf16[8,512,128]{2,1,0:T(8,128)(2,1)}, bf16[8,512,128]{2,1,0:T(8,128)(2,1)}, u32[]{:S(2)}, u32[]{:S(2)}) %collective-permute-start.64) | collective-permute-done | bytes 1048608 | tf_op jit(solution)/shard_map/ppermute | solution.py:351
  467.1 4.1 all-to-all-start.8
  476.6 3.5 all-to-all-done.8
  480.1 4.1 all-to-all-start.9
  486.1 18.1 %collective-permute-done.52 = bf16[8,1024,128]{2,1,0:T(8,128)(2,1)S(1)} collective-permute-done((bf16[8,1024,128]{2,1,0:T(8,128)(2,1)}, bf16[8,1024,128]{2,1,0:T(8,128)(2,1)S(1)}, u32[]{:S(2)}, u32[]{:S(2)}) %collective-permute-start.52) | collective-permute-done | bytes 2097184 | tf_op jit(solution)/shard_map/ppermute | solution.py:351
  504.3 3.2 add_convert_fusion.6
  520.8 10.4 %collective-permute-done.53 = bf16[4,1024,128]{2,1,0:T(8,128)(2,1)} collective-permute-done((bf16[4,1024,128]{2,1,0:T(8,128)(2,1)}, bf16[4,1024,128]{2,1,0:T(8,128)(2,1)}, u32[]{:S(2)}, u32[]{:S(2)}) %collective-permute-start.53) | collective-permute-done | bytes 1048608 | tf_op jit(solution)/shard_map/ppermute | solution.py:351
  531.2 3.4 add_convert_fusion.5
  534.5 3.5 all-to-all-start.5
  543.1 3.6 add_convert_fusion.18
  554.5 20.6 %collective-permute-done.42 = bf16[256,2048]{1,0:T(8,128)(2,1)} collective-permute-done((bf16[256,2048]{1,0:T(8,128)(2,1)}, bf16[256,2048]{1,0:T(8,128)(2,1)}, u32[]{:S(2)}, u32[]{:S(2)}) %collective-permute-start.42) | collective-permute-done | bytes 1048608 | tf_op jit(solution)/shard_map/ppermute | solution.py:351
  575.1 3.7 add_convert_fusion.24
  581.9 3.3 collective-permute-done.48
  585.2 3.7 convert_add_fusion.3
  590.6 5.8 collective-permute-done.43
  596.5 21.4 %collective-permute-done.44 = bf16[256,2048]{1,0:T(8,128)(2,1)} collective-permute-done((bf16[256,2048]{1,0:T(8,128)(2,1)}, bf16[256,2048]{1,0:T(8,128)(2,1)}, u32[]{:S(2)}, u32[]{:S(2)}) %collective-permute-start.44) | collective-permute-done | bytes 1048608 | tf_op jit(solution)/shard_map/ppermute | solution.py:351
  624.1 9.4 %collective-permute-done.45 = bf16[256,1024]{1,0:T(8,128)(2,1)S(1)} collective-permute-done((bf16[256,1024]{1,0:T(8,128)(2,1)S(1)}, bf16[256,1024]{1,0:T(8,128)(2,1)S(1)}, u32[]{:S(2)}, u32[]{:S(2)}) %collective-permute-start.45) | collective-permute-done | bytes 524320 | tf_op jit(solution)/shard_map/ppermute | solution.py:351
  640.0 4.9 all-to-all-start.4
  645.7 5.1 all-to-all-done.4
  (370 shorter events, 164.9 us)
Async XLA Ops:
  4.1 17.3 %all-to-all-start = ((bf16[4,512,128]{2,1,0:T(8,128)(2,1)}), bf16[4,512,128]{2,1,0:T(8,128)(2,1)}, u32[]{:S(2)}, u32[]{:S(2)}) async-start(bf16[4,512,128]{2,1,0:T(8,128)(2,1)} %pad_maximum_fusion.11), calls=%async_computation | async-start | bytes 1048576 | tf_op jit(solution)/shard_map/all_to_all | solution.py:375
  15.1 51.3 %collective-permute-start = (bf16[256,2048]{1,0:T(8,128)(2,1)}, bf16[256,2048]{1,0:T(8,128)(2,1)}, u32[]{:S(2)}, u32[]{:S(2)}) collective-permute-start(bf16[256,2048]{1,0:T(8,128)(2,1)} %pad_maximum_fusion.2.refs_0_), channel_id=1, source_target_pairs={{0,1},{1,0},{2,3},{3,2},{4,5},{5,4},{6,7},{7,6},{8,9},{9,8},{10,11... | collective-permute-start | bytes 3145736 | tf_op jit(solution)/shard_map/ppermute | solution.py:351
  16.6 72.2 %collective-permute-start.1 = (bf16[256,2048]{1,0:T(8,128)(2,1)}, bf16[256,2048]{1,0:T(8,128)(2,1)}, u32[]{:S(2)}, u32[]{:S(2)}) collective-permute-start(bf16[256,2048]{1,0:T(8,128)(2,1)} %pad_maximum_fusion.2.refs_0_), channel_id=1, source_target_pairs={{0,2},{1,3},{2,0},{3,1},{4,6},{5,7},{6,4},{7,5},{8,10},{9,11},{10,... | collective-permute-start | bytes 3145736 | tf_op jit(solution)/shard_map/ppermute | solution.py:351
  16.8 56.7 %collective-permute-start.3 = (bf16[256,2048]{1,0:T(8,128)(2,1)}, bf16[256,2048]{1,0:T(8,128)(2,1)}, u32[]{:S(2)}, u32[]{:S(2)}) collective-permute-start(bf16[256,2048]{1,0:T(8,128)(2,1)} %pad_maximum_fusion.2.refs_0_), channel_id=1, source_target_pairs={{0,4},{1,5},{2,6},{3,7},{4,0},{5,1},{6,2},{7,3},{8,12},{9,13},{10,... | collective-permute-start | bytes 3145736 | tf_op jit(solution)/shard_map/ppermute | solution.py:351
  21.4 19.5 %collective-permute-start.16 = (bf16[4,512,128]{2,1,0:T(8,128)(2,1)}, bf16[4,512,128]{2,1,0:T(8,128)(2,1)}, u32[]{:S(2)}, u32[]{:S(2)}) collective-permute-start(bf16[4,512,128]{2,1,0:T(8,128)(2,1)} %all-to-all-done.refs_18_), channel_id=1, source_target_pairs={{0,8},{1,9},{2,10},{3,11},{4,12},{5,13},{6,14},{7,15},{8,0},{9,1},... | collective-permute-start | bytes 1572872 | tf_op jit(solution)/shard_map/ppermute | solution.py:351
  21.8 16.9 %collective-permute-start.17 = (bf16[4,512,128]{2,1,0:T(8,128)(2,1)}, bf16[4,512,128]{2,1,0:T(8,128)(2,1)}, u32[]{:S(2)}, u32[]{:S(2)}) collective-permute-start(bf16[4,512,128]{2,1,0:T(8,128)(2,1)} %all-to-all-done.refs_18_), channel_id=1, source_target_pairs={{8,16},{9,17},{10,18},{11,19},{12,20},{13,21},{14,22},{15,23},{16,... | collective-permute-start | bytes 1572872 | tf_op jit(solution)/shard_map/ppermute | solution.py:351
  26.4 33.0 %all-to-all-start.2 = ((bf16[4,1536,128]{2,1,0:T(8,128)(2,1)}), bf16[4,1536,128]{2,1,0:T(8,128)(2,1)S(1)}, u32[]{:S(2)}, u32[]{:S(2)}) async-start(bf16[4,1536,128]{2,1,0:T(8,128)(2,1)} %pad_maximum_fusion.1), calls=%async_computation.2 | async-start | bytes 3145728 | tf_op jit(solution)/shard_map/all_to_all | solution.py:375
  38.8 17.5 %collective-permute-start.19 = (bf16[4,512,128]{2,1,0:T(8,128)(2,1)}, bf16[4,512,128]{2,1,0:T(8,128)(2,1)}, u32[]{:S(2)}, u32[]{:S(2)}) collective-permute-start(bf16[4,512,128]{2,1,0:T(8,128)(2,1)} %collective-permute-done.17.refs_20_), channel_id=1, source_target_pairs={{8,0},{9,1},{10,2},{11,3},{12,4},{13,5},{14,6},{15,7},{16,24},{17,... | collective-permute-start | bytes 1572872 | tf_op jit(solution)/shard_map/ppermute | solution.py:351
  56.3 21.3 %collective-permute-start.20 = (bf16[4,512,128]{2,1,0:T(8,128)(2,1)}, bf16[4,512,128]{2,1,0:T(8,128)(2,1)}, u32[]{:S(2)}, u32[]{:S(2)}) collective-permute-start(bf16[4,512,128]{2,1,0:T(8,128)(2,1)} %collective-permute-done.18.refs_21_), channel_id=1, source_target_pairs={{8,0},{9,1},{10,2},{11,3},{12,4},{13,5},{14,6},{15,7},{16,24},{17,... | collective-permute-start | bytes 1572872 | tf_op jit(solution)/shard_map/ppermute | solution.py:351
  66.1 18.3 %collective-permute-start.21 = (bf16[4,512,128]{2,1,0:T(8,128)(2,1)S(1)}, bf16[4,512,128]{2,1,0:T(8,128)(2,1)}, u32[]{:S(2)}, u32[]{:S(2)}) collective-permute-start(bf16[4,512,128]{2,1,0:T(8,128)(2,1)S(1)} %slice.598.refs_18_), channel_id=1, source_target_pairs={{0,8},{1,9},{2,10},{3,11},{4,12},{5,13},{6,14},{7,15},{8,0},{9,1},... | collective-permute-start | bytes 1572872 | tf_op jit(solution)/shard_map/ppermute | solution.py:351
  73.5 29.6 %collective-permute-start.9 = (bf16[256,2048]{1,0:T(8,128)(2,1)}, bf16[256,2048]{1,0:T(8,128)(2,1)}, u32[]{:S(2)}, u32[]{:S(2)}) collective-permute-start(bf16[256,2048]{1,0:T(8,128)(2,1)} %pad_maximum_fusion.3.refs_10_), channel_id=1, source_target_pairs={{0,1},{1,0},{2,3},{3,2},{4,5},{5,4},{6,7},{7,6},{8,9},{9,8},{10,11... | collective-permute-start | bytes 3145736 | tf_op jit(solution)/shard_map/ppermute | solution.py:351
  77.6 27.0 %collective-permute-start.10 = (bf16[256,2048]{1,0:T(8,128)(2,1)}, bf16[256,2048]{1,0:T(8,128)(2,1)}, u32[]{:S(2)}, u32[]{:S(2)}) collective-permute-start(bf16[256,2048]{1,0:T(8,128)(2,1)} %pad_maximum_fusion.3.refs_10_), channel_id=1, source_target_pairs={{0,2},{1,3},{2,0},{3,1},{4,6},{5,7},{6,4},{7,5},{8,10},{9,11},{10,... | collective-permute-start | bytes 3145736 | tf_op jit(solution)/shard_map/ppermute | solution.py:351
  88.9 26.2 %collective-permute-start.12 = (bf16[256,2048]{1,0:T(8,128)(2,1)S(1)}, bf16[256,2048]{1,0:T(8,128)(2,1)}, u32[]{:S(2)}, u32[]{:S(2)}) collective-permute-start(bf16[256,2048]{1,0:T(8,128)(2,1)S(1)} %copy-done.15), channel_id=1, source_target_pairs={{0,4},{1,5},{2,6},{3,7},{4,0},{5,1},{6,2},{7,3},{8,12},{9,13},{10,... | collective-permute-start | bytes 3145736 | tf_op jit(solution)/shard_map/ppermute | solution.py:351
  99.7 24.9 %collective-permute-start.26 = (bf16[4,1024,128]{2,1,0:T(8,128)(2,1)}, bf16[4,1024,128]{2,1,0:T(8,128)(2,1)}, u32[]{:S(2)}, u32[]{:S(2)}) collective-permute-start(bf16[4,1024,128]{2,1,0:T(8,128)(2,1)} %slice.600.refs_18_), channel_id=1, source_target_pairs={{0,8},{1,9},{2,10},{3,11},{4,12},{5,13},{6,14},{7,15},{8,0},{9,1},... | collective-permute-start | bytes 3145736 | tf_op jit(solution)/shard_map/ppermute | solution.py:351
  99.7 25.8 %collective-permute-start.27 = (bf16[4,1024,128]{2,1,0:T(8,128)(2,1)}, bf16[4,1024,128]{2,1,0:T(8,128)(2,1)}, u32[]{:S(2)}, u32[]{:S(2)}) collective-permute-start(bf16[4,1024,128]{2,1,0:T(8,128)(2,1)} %slice.600.refs_18_), channel_id=1, source_target_pairs={{8,16},{9,17},{10,18},{11,19},{12,20},{13,21},{14,22},{15,23},{16,... | collective-permute-start | bytes 3145736 | tf_op jit(solution)/shard_map/ppermute | solution.py:351
  103.1 21.5 %collective-permute-start.4 = (bf16[256,1024]{1,0:T(8,128)(2,1)}, bf16[256,1024]{1,0:T(8,128)(2,1)S(1)}, u32[]{:S(2)}, u32[]{:S(2)}) collective-permute-start(bf16[256,1024]{1,0:T(8,128)(2,1)} %slice.591), channel_id=1, source_target_pairs={{0,4},{1,5},{2,6},{3,7},{4,0},{5,1},{6,2},{7,3},{8,12},{9,13},{10,... | collective-permute-start | bytes 1572872 | tf_op jit(solution)/shard_map/ppermute | solution.py:351
  104.6 27.9 %collective-permute-start.25 = (bf16[4,512,128]{2,1,0:T(8,128)(2,1)S(1)}, bf16[4,512,128]{2,1,0:T(8,128)(2,1)}, u32[]{:S(2)}, u32[]{:S(2)}) collective-permute-start(bf16[4,512,128]{2,1,0:T(8,128)(2,1)S(1)} %collective-permute-done.23.refs_21_), channel_id=1, source_target_pairs={{8,0},{9,1},{10,2},{11,3},{12,4},{13,5},{14,6},{15,7},{16,24},{17,... | collective-permute-start | bytes 1572872 | tf_op jit(solution)/shard_map/ppermute | solution.py:351
  115.1 20.4 %collective-permute-start.5 = (bf16[256,1024]{1,0:T(8,128)(2,1)}, bf16[256,1024]{1,0:T(8,128)(2,1)}, u32[]{:S(2)}, u32[]{:S(2)}) collective-permute-start(bf16[256,1024]{1,0:T(8,128)(2,1)} %slice.592), channel_id=1, source_target_pairs={{0,1},{1,0},{2,3},{3,2},{4,5},{5,4},{6,7},{7,6},{8,9},{9,8},{10,11... | collective-permute-start | bytes 1572872 | tf_op jit(solution)/shard_map/ppermute | solution.py:351
  116.7 49.4 %all-to-all-start.3 = ((bf16[4,1024,128]{2,1,0:T(8,128)(2,1)}), bf16[4,1024,128]{2,1,0:T(8,128)(2,1)S(1)}, u32[]{:S(2)}, u32[]{:S(2)}) async-start(bf16[4,1024,128]{2,1,0:T(8,128)(2,1)} %pad_maximum_fusion.4), calls=%async_computation.3 | async-start | bytes 2097152 | tf_op jit(solution)/shard_map/all_to_all | solution.py:375
  124.6 19.1 %collective-permute-start.2 = (bf16[256,2048]{1,0:T(8,128)(2,1)}, bf16[256,2048]{1,0:T(8,128)(2,1)S(1)}, u32[]{:S(2)}, u32[]{:S(2)}) collective-permute-start(bf16[256,2048]{1,0:T(8,128)(2,1)} %collective-permute-done.refs_1_), channel_id=1, source_target_pairs={{0,2},{1,3},{2,0},{3,1},{4,6},{5,7},{6,4},{7,5},{8,10},{9,11},{10,... | collective-permute-start | bytes 3145736 | tf_op jit(solution)/shard_map/ppermute | solution.py:351
  124.6 19.2 %collective-permute-start.6 = (bf16[256,2048]{1,0:T(8,128)(2,1)}, bf16[256,2048]{1,0:T(8,128)(2,1)S(1)}, u32[]{:S(2)}, u32[]{:S(2)}) collective-permute-start(bf16[256,2048]{1,0:T(8,128)(2,1)} %collective-permute-done.3.refs_4_), channel_id=1, source_target_pairs={{0,2},{1,3},{2,0},{3,1},{4,6},{5,7},{6,4},{7,5},{8,10},{9,11},{10,... | collective-permute-start | bytes 3145736 | tf_op jit(solution)/shard_map/ppermute | solution.py:351
  125.5 25.6 %collective-permute-start.13 = (bf16[256,2048]{1,0:T(8,128)(2,1)}, bf16[256,2048]{1,0:T(8,128)(2,1)}, u32[]{:S(2)}, u32[]{:S(2)}) collective-permute-start(bf16[256,2048]{1,0:T(8,128)(2,1)} %collective-permute-done.12.refs_14_), channel_id=1, source_target_pairs={{0,1},{1,0},{2,3},{3,2},{4,5},{5,4},{6,7},{7,6},{8,9},{9,8},{10,11... | collective-permute-start | bytes 3145736 | tf_op jit(solution)/shard_map/ppermute | solution.py:351
  132.5 25.0 %collective-permute-start.28 = (bf16[4,1024,128]{2,1,0:T(8,128)(2,1)}, bf16[4,1024,128]{2,1,0:T(8,128)(2,1)S(1)}, u32[]{:S(2)}, u32[]{:S(2)}) collective-permute-start(bf16[4,1024,128]{2,1,0:T(8,128)(2,1)} %collective-permute-done.26.refs_19_), channel_id=1, source_target_pairs={{8,16},{9,17},{10,18},{11,19},{12,20},{13,21},{14,22},{15,23},{16,... | collective-permute-start | bytes 3145736 | tf_op jit(solution)/shard_map/ppermute | solution.py:351
  135.5 23.0 %collective-permute-start.29 = (bf16[4,1024,128]{2,1,0:T(8,128)(2,1)}, bf16[4,1024,128]{2,1,0:T(8,128)(2,1)S(1)}, u32[]{:S(2)}, u32[]{:S(2)}) collective-permute-start(bf16[4,1024,128]{2,1,0:T(8,128)(2,1)} %collective-permute-done.27.refs_20_), channel_id=1, source_target_pairs={{8,0},{9,1},{10,2},{11,3},{12,4},{13,5},{14,6},{15,7},{16,24},{17,... | collective-permute-start | bytes 3145736 | tf_op jit(solution)/shard_map/ppermute | solution.py:351
  143.7 25.4 %collective-permute-start.14 = (bf16[256,2048]{1,0:T(8,128)(2,1)}, bf16[256,2048]{1,0:T(8,128)(2,1)}, u32[]{:S(2)}, u32[]{:S(2)}) collective-permute-start(bf16[256,2048]{1,0:T(8,128)(2,1)} %collective-permute-done.12.refs_14_), channel_id=1, source_target_pairs={{0,2},{1,3},{2,0},{3,1},{4,6},{5,7},{6,4},{7,5},{8,10},{9,11},{10,... | collective-permute-start | bytes 3145736 | tf_op jit(solution)/shard_map/ppermute | solution.py:351
  143.8 22.5 %collective-permute-start.11 = (bf16[256,2048]{1,0:T(8,128)(2,1)}, bf16[256,2048]{1,0:T(8,128)(2,1)}, u32[]{:S(2)}, u32[]{:S(2)}) collective-permute-start(bf16[256,2048]{1,0:T(8,128)(2,1)} %collective-permute-done.9.refs_11_), channel_id=1, source_target_pairs={{0,2},{1,3},{2,0},{3,1},{4,6},{5,7},{6,4},{7,5},{8,10},{9,11},{10,... | collective-permute-start | bytes 3145736 | tf_op jit(solution)/shard_map/ppermute | solution.py:351
  160.8 43.1 %collective-permute-start.30 = (bf16[4,1024,128]{2,1,0:T(8,128)(2,1)}, bf16[4,1024,128]{2,1,0:T(8,128)(2,1)}, u32[]{:S(2)}, u32[]{:S(2)}) collective-permute-start(bf16[4,1024,128]{2,1,0:T(8,128)(2,1)} %copy-done.53), channel_id=1, source_target_pairs={{8,0},{9,1},{10,2},{11,3},{12,4},{13,5},{14,6},{15,7},{16,24},{17,... | collective-permute-start | bytes 3145736 | tf_op jit(solution)/shard_map/ppermute | solution.py:351
  166.2 32.5 %collective-permute-start.31 = (bf16[4,512,128]{2,1,0:T(8,128)(2,1)S(1)}, bf16[4,512,128]{2,1,0:T(8,128)(2,1)S(1)}, u32[]{:S(2)}, u32[]{:S(2)}) collective-permute-start(bf16[4,512,128]{2,1,0:T(8,128)(2,1)S(1)} %get-tuple-element.105.refs_18_), channel_id=1, source_target_pairs={{0,8},{1,9},{2,10},{3,11},{4,12},{5,13},{6,14},{7,15},{8,0},{9,1},... | collective-permute-start | bytes 1572872 | tf_op jit(solution)/shard_map/ppermute | solution.py:351
  166.3 37.6 %collective-permute-start.32 = (bf16[4,512,128]{2,1,0:T(8,128)(2,1)S(1)}, bf16[4,512,128]{2,1,0:T(8,128)(2,1)S(1)}, u32[]{:S(2)}, u32[]{:S(2)}) collective-permute-start(bf16[4,512,128]{2,1,0:T(8,128)(2,1)S(1)} %get-tuple-element.105.refs_18_), channel_id=1, source_target_pairs={{8,16},{9,17},{10,18},{11,19},{12,20},{13,21},{14,22},{15,23},{16,... | collective-permute-start | bytes 1572872 | tf_op jit(solution)/shard_map/ppermute | solution.py:351
  187.8 96.0 %collective-permute-start.54 = (bf16[12,512,128]{2,1,0:T(8,128)(2,1)}, bf16[12,512,128]{2,1,0:T(8,128)(2,1)}, u32[]{:S(2)}, u32[]{:S(2)}) collective-permute-start(bf16[12,512,128]{2,1,0:T(8,128)(2,1)} %get-tuple-element.140), channel_id=1, source_target_pairs={{0,8},{1,9},{2,10},{3,11},{4,12},{5,13},{6,14},{7,15},{24,16},{25,... | collective-permute-start | bytes 4718600 | tf_op jit(solution)/shard_map/ppermute | solution.py:351
  198.7 39.9 %collective-permute-start.36 = (bf16[4,512,128]{2,1,0:T(8,128)(2,1)S(1)}, bf16[4,512,128]{2,1,0:T(8,128)(2,1)}, u32[]{:S(2)}, u32[]{:S(2)}) collective-permute-start(bf16[4,512,128]{2,1,0:T(8,128)(2,1)S(1)} %get-tuple-element.111.refs_18_), channel_id=1, source_target_pairs={{0,8},{1,9},{2,10},{3,11},{4,12},{5,13},{6,14},{7,15},{8,0},{9,1},... | collective-permute-start | bytes 1572872 | tf_op jit(solution)/shard_map/ppermute | solution.py:351
  201.2 24.0 %collective-permute-start.33 = (bf16[4,512,128]{2,1,0:T(8,128)(2,1)S(1)}, bf16[4,512,128]{2,1,0:T(8,128)(2,1)}, u32[]{:S(2)}, u32[]{:S(2)}) collective-permute-start(bf16[4,512,128]{2,1,0:T(8,128)(2,1)S(1)} %collective-permute-done.31.refs_19_), channel_id=1, source_target_pairs={{8,16},{9,17},{10,18},{11,19},{12,20},{13,21},{14,22},{15,23},{16,... | collective-permute-start | bytes 1572872 | tf_op jit(solution)/shard_map/ppermute | solution.py:351
  203.9 37.9 %collective-permute-start.34 = (bf16[4,512,128]{2,1,0:T(8,128)(2,1)S(1)}, bf16[4,512,128]{2,1,0:T(8,128)(2,1)S(1)}, u32[]{:S(2)}, u32[]{:S(2)}) collective-permute-start(bf16[4,512,128]{2,1,0:T(8,128)(2,1)S(1)} %collective-permute-done.32.refs_20_), channel_id=1, source_target_pairs={{8,0},{9,1},{10,2},{11,3},{12,4},{13,5},{14,6},{15,7},{16,24},{17,... | collective-permute-start | bytes 1572872 | tf_op jit(solution)/shard_map/ppermute | solution.py:351
  223.9 89.9 %collective-permute-start.57 = (bf16[12,512,128]{2,1,0:T(8,128)(2,1)}, bf16[12,512,128]{2,1,0:T(8,128)(2,1)S(1)}, u32[]{:S(2)}, u32[]{:S(2)}) collective-permute-start(bf16[12,512,128]{2,1,0:T(8,128)(2,1)} %get-tuple-element.145), channel_id=1, source_target_pairs={{0,8},{1,9},{2,10},{3,11},{4,12},{5,13},{6,14},{7,15},{24,16},{25,... | collective-permute-start | bytes 4718600 | tf_op jit(solution)/shard_map/ppermute | solution.py:351
  225.2 62.7 %collective-permute-start.37 = (bf16[4,512,128]{2,1,0:T(8,128)(2,1)S(1)}, bf16[4,512,128]{2,1,0:T(8,128)(2,1)}, u32[]{:S(2)}, u32[]{:S(2)}) collective-permute-start(bf16[4,512,128]{2,1,0:T(8,128)(2,1)S(1)} %get-tuple-element.111.refs_18_), channel_id=1, source_target_pairs={{8,16},{9,17},{10,18},{11,19},{12,20},{13,21},{14,22},{15,23},{16,... | collective-permute-start | bytes 1572872 | tf_op jit(solution)/shard_map/ppermute | solution.py:351
  238.6 76.5 %collective-permute-start.38 = (bf16[4,512,128]{2,1,0:T(8,128)(2,1)}, bf16[4,512,128]{2,1,0:T(8,128)(2,1)}, u32[]{:S(2)}, u32[]{:S(2)}) collective-permute-start(bf16[4,512,128]{2,1,0:T(8,128)(2,1)} %collective-permute-done.36.refs_19_), channel_id=1, source_target_pairs={{8,16},{9,17},{10,18},{11,19},{12,20},{13,21},{14,22},{15,23},{16,... | collective-permute-start | bytes 1572872 | tf_op jit(solution)/shard_map/ppermute | solution.py:351
  241.8 48.8 %collective-permute-start.35 = (bf16[4,512,128]{2,1,0:T(8,128)(2,1)}, bf16[4,512,128]{2,1,0:T(8,128)(2,1)}, u32[]{:S(2)}, u32[]{:S(2)}) collective-permute-start(bf16[4,512,128]{2,1,0:T(8,128)(2,1)} %collective-permute-done.33.refs_21_), channel_id=1, source_target_pairs={{8,0},{9,1},{10,2},{11,3},{12,4},{13,5},{14,6},{15,7},{16,24},{17,... | collective-permute-start | bytes 1572872 | tf_op jit(solution)/shard_map/ppermute | solution.py:351
  283.8 134.4 %collective-permute-start.51 = (bf16[12,1024,128]{2,1,0:T(8,128)(2,1)}, bf16[12,1024,128]{2,1,0:T(8,128)(2,1)}, u32[]{:S(2)}, u32[]{:S(2)}) collective-permute-start(bf16[12,1024,128]{2,1,0:T(8,128)(2,1)} %get-tuple-element.137), channel_id=1, source_target_pairs={{0,8},{1,9},{2,10},{3,11},{4,12},{5,13},{6,14},{7,15},{24,16},{25,... | collective-permute-start | bytes 9437192 | tf_op jit(solution)/shard_map/ppermute | solution.py:351
  287.9 36.7 %collective-permute-start.55 = (bf16[8,512,128]{2,1,0:T(8,128)(2,1)}, bf16[8,512,128]{2,1,0:T(8,128)(2,1)S(1)}, u32[]{:S(2)}, u32[]{:S(2)}) collective-permute-start(bf16[8,512,128]{2,1,0:T(8,128)(2,1)} %add_convert_fusion.4), channel_id=1, source_target_pairs={{8,16},{9,17},{10,18},{11,19},{12,20},{13,21},{14,22},{15,23},{16,... | collective-permute-start | bytes 3145736 | tf_op jit(solution)/shard_map/ppermute | solution.py:351
  290.6 24.5 %collective-permute-start.39 = (bf16[4,512,128]{2,1,0:T(8,128)(2,1)}, bf16[4,512,128]{2,1,0:T(8,128)(2,1)S(1)}, u32[]{:S(2)}, u32[]{:S(2)}) collective-permute-start(bf16[4,512,128]{2,1,0:T(8,128)(2,1)} %collective-permute-done.37.refs_20_), channel_id=1, source_target_pairs={{8,0},{9,1},{10,2},{11,3},{12,4},{13,5},{14,6},{15,7},{16,24},{17,... | collective-permute-start | bytes 1572872 | tf_op jit(solution)/shard_map/ppermute | solution.py:351
  313.8 93.2 %collective-permute-start.60 = (bf16[12,512,128]{2,1,0:T(8,128)(2,1)}, bf16[12,512,128]{2,1,0:T(8,128)(2,1)}, u32[]{:S(2)}, u32[]{:S(2)}) collective-permute-start(bf16[12,512,128]{2,1,0:T(8,128)(2,1)} %get-tuple-element.149), channel_id=1, source_target_pairs={{0,8},{1,9},{2,10},{3,11},{4,12},{5,13},{6,14},{7,15},{24,16},{25,... | collective-permute-start | bytes 4718600 | tf_op jit(solution)/shard_map/ppermute | solution.py:351
  315.1 16.9 %collective-permute-start.40 = (bf16[4,512,128]{2,1,0:T(8,128)(2,1)}, bf16[4,512,128]{2,1,0:T(8,128)(2,1)}, u32[]{:S(2)}, u32[]{:S(2)}) collective-permute-start(bf16[4,512,128]{2,1,0:T(8,128)(2,1)} %collective-permute-done.38.refs_21_), channel_id=1, source_target_pairs={{8,0},{9,1},{10,2},{11,3},{12,4},{13,5},{14,6},{15,7},{16,24},{17,... | collective-permute-start | bytes 1572872 | tf_op jit(solution)/shard_map/ppermute | solution.py:351
  321.9 66.7 %collective-permute-start.58 = (bf16[8,512,128]{2,1,0:T(8,128)(2,1)S(1)}, bf16[8,512,128]{2,1,0:T(8,128)(2,1)S(1)}, u32[]{:S(2)}, u32[]{:S(2)}) collective-permute-start(bf16[8,512,128]{2,1,0:T(8,128)(2,1)S(1)} %add_convert_fusion.3), channel_id=1, source_target_pairs={{8,16},{9,17},{10,18},{11,19},{12,20},{13,21},{14,22},{15,23},{16,... | collective-permute-start | bytes 3145736 | tf_op jit(solution)/shard_map/ppermute | solution.py:351
  327.0 73.3 %collective-permute-start.56 = (bf16[4,512,128]{2,1,0:T(8,128)(2,1)}, bf16[4,512,128]{2,1,0:T(8,128)(2,1)}, u32[]{:S(2)}, u32[]{:S(2)}) collective-permute-start(bf16[4,512,128]{2,1,0:T(8,128)(2,1)} %add_convert_fusion.14), channel_id=1, source_target_pairs={{8,0},{9,1},{10,2},{11,3},{12,4},{13,5},{14,6},{15,7},{16,24},{17,... | collective-permute-start | bytes 1572872 | tf_op jit(solution)/shard_map/ppermute | solution.py:351
  350.6 68.8 %collective-permute-start.63 = (bf16[12,512,128]{2,1,0:T(8,128)(2,1)}, bf16[12,512,128]{2,1,0:T(8,128)(2,1)}, u32[]{:S(2)}, u32[]{:S(2)}) collective-permute-start(bf16[12,512,128]{2,1,0:T(8,128)(2,1)} %get-tuple-element.151), channel_id=1, source_target_pairs={{0,8},{1,9},{2,10},{3,11},{4,12},{5,13},{6,14},{7,15},{24,16},{25,... | collective-permute-start | bytes 4718600 | tf_op jit(solution)/shard_map/ppermute | solution.py:351
  388.6 124.4 %collective-permute-start.46 = (bf16[1024,2048]{1,0:T(8,128)(2,1)}, bf16[1024,2048]{1,0:T(8,128)(2,1)}, u32[]{:S(2)}, u32[]{:S(2)}) collective-permute-start(bf16[1024,2048]{1,0:T(8,128)(2,1)} %join.7), channel_id=1, source_target_pairs={{0,2},{1,3},{2,0},{3,1},{4,6},{5,7},{6,4},{7,5},{8,10},{9,11},{10,... | collective-permute-start | bytes 12582920 | tf_op jit(solution)/shard_map/ppermute | solution.py:351
  400.3 39.6 %collective-permute-start.59 = (bf16[4,512,128]{2,1,0:T(8,128)(2,1)}, bf16[4,512,128]{2,1,0:T(8,128)(2,1)}, u32[]{:S(2)}, u32[]{:S(2)}) collective-permute-start(bf16[4,512,128]{2,1,0:T(8,128)(2,1)} %add_convert_fusion.12), channel_id=1, source_target_pairs={{8,0},{9,1},{10,2},{11,3},{12,4},{13,5},{14,6},{15,7},{16,24},{17,... | collective-permute-start | bytes 1572872 | tf_op jit(solution)/shard_map/ppermute | solution.py:351
  409.5 28.3 %collective-permute-start.61 = (bf16[8,512,128]{2,1,0:T(8,128)(2,1)}, bf16[8,512,128]{2,1,0:T(8,128)(2,1)}, u32[]{:S(2)}, u32[]{:S(2)}) collective-permute-start(bf16[8,512,128]{2,1,0:T(8,128)(2,1)} %add_convert_fusion.2), channel_id=1, source_target_pairs={{8,16},{9,17},{10,18},{11,19},{12,20},{13,21},{14,22},{15,23},{16,... | collective-permute-start | bytes 3145736 | tf_op jit(solution)/shard_map/ppermute | solution.py:351
  414.1 17.0 %all-to-all-start.6 = ((bf16[4,512,128]{2,1,0:T(8,128)(2,1)}), bf16[4,512,128]{2,1,0:T(8,128)(2,1)}, u32[]{:S(2)}, u32[]{:S(2)}) async-start(bf16[4,512,128]{2,1,0:T(8,128)(2,1)} %add_convert_fusion.13), calls=%async_computation.6 | async-start | bytes 1048576 | tf_op jit(solution)/shard_map/all_to_all | solution.py:375
  421.8 38.5 %collective-permute-start.64 = (bf16[8,512,128]{2,1,0:T(8,128)(2,1)}, bf16[8,512,128]{2,1,0:T(8,128)(2,1)}, u32[]{:S(2)}, u32[]{:S(2)}) collective-permute-start(bf16[8,512,128]{2,1,0:T(8,128)(2,1)} %add_convert_fusion.1), channel_id=1, source_target_pairs={{8,16},{9,17},{10,18},{11,19},{12,20},{13,21},{14,22},{15,23},{16,... | collective-permute-start | bytes 3145736 | tf_op jit(solution)/shard_map/ppermute | solution.py:351
  428.1 76.1 %collective-permute-start.52 = (bf16[8,1024,128]{2,1,0:T(8,128)(2,1)}, bf16[8,1024,128]{2,1,0:T(8,128)(2,1)S(1)}, u32[]{:S(2)}, u32[]{:S(2)}) collective-permute-start(bf16[8,1024,128]{2,1,0:T(8,128)(2,1)} %add_convert_fusion), channel_id=1, source_target_pairs={{8,16},{9,17},{10,18},{11,19},{12,20},{13,21},{14,22},{15,23},{16,... | collective-permute-start | bytes 6291464 | tf_op jit(solution)/shard_map/ppermute | solution.py:351
  437.8 100.3 %collective-permute-start.41 = (bf16[1024,2048]{1,0:T(8,128)(2,1)}, bf16[1024,2048]{1,0:T(8,128)(2,1)}, u32[]{:S(2)}, u32[]{:S(2)}) collective-permute-start(bf16[1024,2048]{1,0:T(8,128)(2,1)} %join.5), channel_id=1, source_target_pairs={{0,2},{1,3},{2,0},{3,1},{4,6},{5,7},{6,4},{7,5},{8,10},{9,11},{10,... | collective-permute-start | bytes 12582920 | tf_op jit(solution)/shard_map/ppermute | solution.py:351
  440.0 24.5 %collective-permute-start.62 = (bf16[4,512,128]{2,1,0:T(8,128)(2,1)}, bf16[4,512,128]{2,1,0:T(8,128)(2,1)}, u32[]{:S(2)}, u32[]{:S(2)}) collective-permute-start(bf16[4,512,128]{2,1,0:T(8,128)(2,1)} %add_convert_fusion.10), channel_id=1, source_target_pairs={{8,0},{9,1},{10,2},{11,3},{12,4},{13,5},{14,6},{15,7},{16,24},{17,... | collective-permute-start | bytes 1572872 | tf_op jit(solution)/shard_map/ppermute | solution.py:351
  444.3 22.7 %all-to-all-start.7 = ((bf16[4,512,128]{2,1,0:T(8,128)(2,1)}), bf16[4,512,128]{2,1,0:T(8,128)(2,1)}, u32[]{:S(2)}, u32[]{:S(2)}) async-start(bf16[4,512,128]{2,1,0:T(8,128)(2,1)} %add_convert_fusion.11), calls=%async_computation.7 | async-start | bytes 1048576 | tf_op jit(solution)/shard_map/all_to_all | solution.py:375
  480.1 29.9 %all-to-all-start.9 = ((bf16[4,512,128]{2,1,0:T(8,128)(2,1)}), bf16[4,512,128]{2,1,0:T(8,128)(2,1)}, u32[]{:S(2)}, u32[]{:S(2)}) async-start(bf16[4,512,128]{2,1,0:T(8,128)(2,1)} %add_convert_fusion.7), calls=%async_computation.9 | async-start | bytes 1048576 | tf_op jit(solution)/shard_map/all_to_all | solution.py:375
  507.5 23.7 %collective-permute-start.53 = (bf16[4,1024,128]{2,1,0:T(8,128)(2,1)}, bf16[4,1024,128]{2,1,0:T(8,128)(2,1)}, u32[]{:S(2)}, u32[]{:S(2)}) collective-permute-start(bf16[4,1024,128]{2,1,0:T(8,128)(2,1)} %add_convert_fusion.6), channel_id=1, source_target_pairs={{8,0},{9,1},{10,2},{11,3},{12,4},{13,5},{14,6},{15,7},{16,24},{17,... | collective-permute-start | bytes 3145736 | tf_op jit(solution)/shard_map/ppermute | solution.py:351
  515.9 27.1 %collective-permute-start.47 = (bf16[256,2048]{1,0:T(8,128)(2,1)}, bf16[256,2048]{1,0:T(8,128)(2,1)}, u32[]{:S(2)}, u32[]{:S(2)}) collective-permute-start(bf16[256,2048]{1,0:T(8,128)(2,1)} %pad_maximum_fusion.7), channel_id=1, source_target_pairs={{0,4},{1,5},{2,6},{3,7},{4,0},{5,1},{6,2},{7,3},{8,12},{9,13},{10,... | collective-permute-start | bytes 3145736 | tf_op jit(solution)/shard_map/ppermute | solution.py:351
  534.5 18.4 %all-to-all-start.5 = ((bf16[4,1024,128]{2,1,0:T(8,128)(2,1)}), bf16[4,1024,128]{2,1,0:T(8,128)(2,1)S(1)}, u32[]{:S(2)}, u32[]{:S(2)}) async-start(bf16[4,1024,128]{2,1,0:T(8,128)(2,1)} %add_convert_fusion.5), calls=%async_computation.5 | async-start | bytes 2097152 | tf_op jit(solution)/shard_map/all_to_all | solution.py:375
  541.1 34.0 %collective-permute-start.42 = (bf16[256,2048]{1,0:T(8,128)(2,1)}, bf16[256,2048]{1,0:T(8,128)(2,1)}, u32[]{:S(2)}, u32[]{:S(2)}) collective-permute-start(bf16[256,2048]{1,0:T(8,128)(2,1)} %pad_maximum_fusion.5), channel_id=1, source_target_pairs={{0,4},{1,5},{2,6},{3,7},{4,0},{5,1},{6,2},{7,3},{8,12},{9,13},{10,... | collective-permute-start | bytes 3145736 | tf_op jit(solution)/shard_map/ppermute | solution.py:351
  547.7 37.5 %collective-permute-start.49 = (bf16[256,2048]{1,0:T(8,128)(2,1)}, bf16[256,2048]{1,0:T(8,128)(2,1)}, u32[]{:S(2)}, u32[]{:S(2)}) collective-permute-start(bf16[256,2048]{1,0:T(8,128)(2,1)} %pad_maximum_fusion.8), channel_id=1, source_target_pairs={{0,1},{1,0},{2,3},{3,2},{4,5},{5,4},{6,7},{7,6},{8,9},{9,8},{10,11... | collective-permute-start | bytes 3145736 | tf_op jit(solution)/shard_map/ppermute | solution.py:351
  553.0 32.2 %collective-permute-start.48 = (bf16[256,1024]{1,0:T(8,128)(2,1)}, bf16[256,1024]{1,0:T(8,128)(2,1)S(1)}, u32[]{:S(2)}, u32[]{:S(2)}) collective-permute-start(bf16[256,1024]{1,0:T(8,128)(2,1)} %get-tuple-element.173), channel_id=1, source_target_pairs={{0,1},{1,0},{2,3},{3,2},{4,5},{5,4},{6,7},{7,6},{8,9},{9,8},{10,11... | collective-permute-start | bytes 1572872 | tf_op jit(solution)/shard_map/ppermute | solution.py:351
  578.8 17.7 %collective-permute-start.43 = (bf16[256,1024]{1,0:T(8,128)(2,1)}, bf16[256,1024]{1,0:T(8,128)(2,1)}, u32[]{:S(2)}, u32[]{:S(2)}) collective-permute-start(bf16[256,1024]{1,0:T(8,128)(2,1)} %get-tuple-element.180), channel_id=1, source_target_pairs={{0,1},{1,0},{2,3},{3,2},{4,5},{5,4},{6,7},{7,6},{8,9},{9,8},{10,11... | collective-permute-start | bytes 1572872 | tf_op jit(solution)/shard_map/ppermute | solution.py:351
  581.3 36.5 %collective-permute-start.44 = (bf16[256,2048]{1,0:T(8,128)(2,1)}, bf16[256,2048]{1,0:T(8,128)(2,1)}, u32[]{:S(2)}, u32[]{:S(2)}) collective-permute-start(bf16[256,2048]{1,0:T(8,128)(2,1)} %pad_maximum_fusion.6), channel_id=1, source_target_pairs={{0,1},{1,0},{2,3},{3,2},{4,5},{5,4},{6,7},{7,6},{8,9},{9,8},{10,11... | collective-permute-start | bytes 3145736 | tf_op jit(solution)/shard_map/ppermute | solution.py:351
  588.9 32.2 %collective-permute-start.50 = (bf16[256,1024]{1,0:T(8,128)(2,1)}, bf16[256,1024]{1,0:T(8,128)(2,1)}, u32[]{:S(2)}, u32[]{:S(2)}) collective-permute-start(bf16[256,1024]{1,0:T(8,128)(2,1)} %get-tuple-element.172), channel_id=1, source_target_pairs={{0,4},{1,5},{2,6},{3,7},{4,0},{5,1},{6,2},{7,3},{8,12},{9,13},{10,... | collective-permute-start | bytes 1572872 | tf_op jit(solution)/shard_map/ppermute | solution.py:351
  (79 other events, 1285.5 us)

commit v2 on v1

v2 whole, which is shorter than its diff:
```python
import functools
import math

import jax
import jax.numpy as jnp
from jax import lax
from jax.experimental import pallas as pl
from jax.experimental.pallas import tpu as pltpu
from jax.sharding import PartitionSpec as P

HD = 256
ROT = 64
DOCS = 3
EPSILON = 1e-05
INNER = 4
LANES = 128
AXES = ("dp", "tensor")
BF = jnp.bfloat16
F32 = jnp.float32
NT = ((1,), (1,))
NN = ((1,), (0,))
TN = ((0,), (0,))
VMEM_LIMIT = 56 * 2**20
STEPS = 4


ORDER = (
    "p1", "p0", "g1", "p2", "g0", "p3", "g2", "own", "g3", "h1", "h0", "sm", "p4", "h2", "i1", "h3", "xt", "c",
    "i0", "j1", "g4", "vec", "i2", "j0", "i3", "b", "tc", "h4", "bc", "K0", "r0", "K1", "i4", "j3", "j2", "r1",
    "KA", "r2", "u0", "j4", "u1", "K4", "r3", "r4", "v0", "JB", "v1", "JO", "u2", "kB", "w0", "CB", "kO", "u3",
    "z0", "v2", "CO", "DB", "tail", "v3", "u4", "w2", "tz", "w1", "DO", "z2", "EO", "v4", "w3", "EB", "z1", "w4",
    "z3", "z4",
)

NOTHING = pl.CostEstimate(flops=0, bytes_accessed=0, transcendentals=0)
SCALARS = pl.BlockSpec(memory_space=pltpu.SMEM)
ANYWHERE = pl.BlockSpec(memory_space=pl.ANY)
VECTORS = pl.BlockSpec(memory_space=pltpu.VMEM)

OUTER, INSIDE, SIDE, SPOT, DOC_ROW = 0, 1, 2, 3, 7


def dot(a, b, dims):
    return lax.dot_general(a, b, (dims, ((), ())), preferred_element_type=F32)


def shaped(shape, dtype=BF):
    return jax.ShapeDtypeStruct(shape, dtype)


def whole(shape):
    return pl.BlockSpec(shape, lambda *_: (0,) * len(shape), pipeline_mode=pl.Buffered(1))


def run_kernel(kernel, outs, in_specs, out_specs, args, name, grid=(), scratch=(), aliases=None, vmem=None):
    return pl.pallas_call(
        kernel,
        grid=grid,
        out_shape=outs,
        in_specs=in_specs,
        out_specs=out_specs,
        scratch_shapes=scratch,
        input_output_aliases=aliases or {},
        compiler_params=pltpu.CompilerParams(vmem_limit_bytes=vmem),
        cost_estimate=NOTHING,
        name=name,
    )(*args)


def gate_kernel(*refs):
    pass


class Line:
    def __init__(self):
        self.mark = jnp.zeros((8, LANES), F32)

    def __call__(self, *arrays):
        held = (*arrays, self.mark)
        *held, self.mark = run_kernel(
            gate_kernel, [shaped(v.shape, v.dtype) for v in held], [ANYWHERE] * len(held), [ANYWHERE] * len(held),
            held, "gate", aliases={n: n for n in range(len(held))},
        )
        return held[0] if len(held) == 1 else held


def spot(place, b, width):
    return pl.ds(pl.multiple_of(place[SPOT + b] * width, width), width)


def places(axis, shape, count, shift):
    at = lax.broadcasted_iota(jnp.int32, shape, axis) + shift
    return jnp.where(at >= count, at - count, at)


def full_lanes(n):
    return n + -n % LANES


def take_weights(parts, gain_ref, dests):
    both, far, passed = parts
    for b in range(16):
        lanes = slice(b * LANES, (b + 1) * LANES)
        block = both[b].astype(F32) if b < 8 else far[b - 8].astype(F32) + passed[b - 8].astype(F32)
        for lo, hi, to, at, gained in dests:
            rows = block[lo:hi]
            to[at : at + hi - lo, lanes] = (rows * gain_ref[:, lanes] if gained else rows).astype(BF)


def give_grads(acc1, acc2, col, gain_ref, shift_ref, w1, to1, to2, norm_ref):
    for b in range(16):
        lanes = slice(b * LANES, (b + 1) * LANES)
        gain = gain_ref[:, lanes]
        m = acc1[:, lanes]
        w = w1[:, lanes].astype(F32)
        for (own, rest, at), v in ((to1, m * gain + col[...] * shift_ref[:, lanes]), (to2, acc2[:, lanes])):
            to, k = (own, b) if b < 4 else (rest, b - 4)
            to[k, at : at + v.shape[0]] = v.astype(BF)
        norm_ref[0:1, lanes] = jnp.sum(w * m, axis=0, keepdims=True) / gain
        norm_ref[1:2, lanes] = jnp.sum(w * col[...], axis=0, keepdims=True) / gain


def stream(step, pieces, unit_buf, cot_buf, sems):
    rows = pieces[0].shape[1]
    steps = len(pieces) // 2

    def copies(s):
        made = []
        for k in (2 * s, 2 * s + 1):
            for n, buffer in enumerate((unit_buf, cot_buf)):
                to = buffer.at[s % 2, pl.ds((k % 2) * rows, rows)]
                made.append(pltpu.make_async_copy(pieces[k].at[n], to, sems.at[s % 2, len(made)]))
        return made

    def begin(s):
        for c in copies(s):
            c.start()

    def arrive():
        for s in range(steps):
            @pl.when(step == s)
            def _(s=s):
                if s + 1 < steps:
                    begin(s + 1)
                for c in copies(s):
                    c.wait()

    return begin, arrive


def stream_scratch(rows, width):
    return [pltpu.VMEM((2, rows, width), BF), pltpu.VMEM((2, rows, width), BF), pltpu.SemaphoreType.DMA((2, 4))]


def feed_kernel(cols, split, *refs):
    pieces, parts, refs = refs[:8], refs[8:11], refs[11:]
    gain_ref, shift_ref, ratio_ref, bias_ref = refs[:4]
    hidden_ref, pre_grad_ref, w1, w2, norm_ref, sum_ref = refs[4:10]
    grads, refs = refs[10 : 10 + 2 * split], refs[10 + 2 * split :]
    acc1, acc2, col, row, unit_buf, cot_buf, sems = refs
    step = pl.program_id(0)
    begin, arrive = stream(step, pieces, unit_buf, cot_buf, sems)

    @pl.when(step == 0)
    def _():
        begin(0)
        take_weights(parts, gain_ref, ((0, cols, w1, 0, True), (cols, 2 * cols, w2, 0, False)))
        row[...] = jnp.sum(dot(ratio_ref[...], w1[...], NT), axis=0, keepdims=True) + bias_ref[...]
        acc1[...] = jnp.zeros_like(acc1)
        acc2[...] = jnp.zeros_like(acc2)
        col[...] = jnp.zeros_like(col)
        sum_ref[...] = jnp.zeros_like(sum_ref)

    arrive()
    slot = lax.rem(step, 2)
    unit = unit_buf[slot]
    cot = cot_buf[slot]
    pre = dot(unit, w1[...], NT) + row[...]
    back = dot(cot, w2[...], NT)
    phi = 0.5 * (1.0 + lax.erf(pre * (1.0 / math.sqrt(2.0))))
    slope = phi + pre * (jnp.exp(-0.5 * pre * pre) * (1.0 / math.sqrt(2.0 * math.pi)))
    hidden = (pre * phi).astype(BF)
    pre_grad = (back * slope).astype(BF)
    hidden_ref[...] = hidden
    pre_grad_ref[...] = pre_grad
    acc1[...] += dot(pre_grad, unit, TN)
    acc2[...] += dot(hidden, cot, TN)
    col[...] += dot(pre_grad, jnp.ones((pre_grad.shape[0], LANES), BF), TN)
    sum_ref[...] += jnp.sum(pre_grad.astype(F32), axis=0, keepdims=True)

    @pl.when(step == pl.num_programs(0) - 1)
    def _():
        to1 = (*grads[:2], 0)
        to2 = (*grads[2:], 0) if split == 2 else (*grads[:2], cols)
        give_grads(acc1, acc2, col, gain_ref, shift_ref, w1, to1, to2, norm_ref)


def chunk_call(kernel, name, pieces, extra_in, extra_specs, sets, vectors, cols, others, split):
    _, part, width = pieces[0].shape
    block, rows = 2 * part, 8 * part
    per_row = lambda n: pl.BlockSpec((block, n), lambda r: (r, 0))
    shapes = [
        shaped((rows, others)), shaped((rows, cols)), shaped((cols, width)), shaped((others, width)),
        shaped((2, width), F32), shaped((1, cols), F32),
    ]
    specs = [per_row(others), per_row(cols)] + [whole(s.shape) for s in shapes[2:]]
    for n in (cols, others) if split == 2 else (cols + others,):
        shapes += [shaped((4, n, LANES)), shaped((12, n, LANES))]
    specs += [whole(s.shape) for s in shapes[6:]]
    weights = [w for s in sets for w in s]
    return run_kernel(
        kernel, shapes,
        [ANYWHERE] * 8 + [whole(w.shape) for w in weights] + [whole(v.shape) for v in vectors] + extra_specs,
        specs, (*pieces, *weights, *vectors, *extra_in), name, grid=(rows // block,),
        scratch=[
            pltpu.VMEM((cols, width), F32), pltpu.VMEM((others, width), F32), pltpu.VMEM((cols, LANES), F32),
            pltpu.VMEM((1, cols), F32),
        ]
        + stream_scratch(block, width),
        vmem=VMEM_LIMIT,
    )


def attention_kernel(cols, *refs):
    pieces, refs = refs[:8], refs[8:]
    set_one, set_two, refs = refs[:3], refs[3:6], refs[6:]
    gain_ref, shift_ref, ratio_ref, bias_ref, lengths, place, cos_ref, sin_up_ref, sin_down_ref = refs[:9]
    mixed_ref, qkv_grad_ref, w1, w2, norm_ref, sum_ref, own_ref, rest_ref = refs[9:17]
    acc1, acc2, col, row, unit_buf, cot_buf, sems = refs[17:]
    group = pl.program_id(0)
    begin, arrive = stream(group, pieces, unit_buf, cot_buf, sems)

    @pl.when(group == 0)
    def _():
        begin(0)
        take_weights(set_one, gain_ref, ((0, 2 * HD, w1, 0, True),))
        take_weights(set_two, gain_ref, ((0, HD, w1, 2 * HD, True), (HD, 2 * HD, w2, 0, False)))
        row[...] = jnp.sum(dot(ratio_ref[...], w1[...], NT), axis=0, keepdims=True) + bias_ref[...]
        acc1[...] = jnp.zeros_like(acc1)
        acc2[...] = jnp.zeros_like(acc2)
        col[...] = jnp.zeros_like(col)
        sum_ref[...] = jnp.zeros_like(sum_ref)

    arrive()
    slot = lax.rem(group, 2)
    unit = unit_buf[slot]
    cot = cot_buf[slot]
    count = unit.shape[0]
    cosine, sin_up, sin_down = cos_ref[...], sin_up_ref[...], sin_down_ref[...]
    half = ROT // 2

    def turn(u):
        p = u[:, :LANES]
        p = p * cosine + pltpu.roll(p, LANES - half, 1) * sin_up + pltpu.roll(p, half, 1) * sin_down
        return jnp.concatenate([p, u[:, LANES:]], axis=1)

    def unturn(u):
        p = u[:, :LANES]
        p = p * cosine + pltpu.roll(p * sin_up, half, 1) + pltpu.roll(p * sin_down, LANES - half, 1)
        return jnp.concatenate([p, u[:, LANES:]], axis=1)

    qkv = dot(unit, w1[...], NT) + row[...]
    query = turn(qkv[:, :HD]).astype(BF)
    key = turn(qkv[:, HD : 2 * HD]).astype(BF)
    value = qkv[:, 2 * HD :].astype(BF)
    back = dot(cot, w2[...], NT).astype(BF)

    shift = place[SIDE] * (count // 2)
    at = places(0, (count, 1), count, shift)
    to = places(1, (1, count), count, shift)
    end, seg_at, seg_to = 0, jnp.zeros_like(at), jnp.zeros_like(to)
    for k in range(DOCS):
        end = end + lengths[group, k]
        seg_at = seg_at + jnp.where(at >= end, 1, 0)
        seg_to = seg_to + jnp.where(to >= end, 1, 0)
    seg_at = jnp.where(seg_at == DOCS, DOCS + at, seg_at)
    seg_to = jnp.where(seg_to == DOCS, DOCS + to, seg_to)
    visible = (seg_at == seg_to) & (to <= at)

    scale = 1.0 / math.sqrt(HD)
    scores = jnp.where(visible, dot(query, key, NT) * scale, -1e30)
    expo = jnp.exp(scores - jnp.max(scores, axis=1, keepdims=True))
    probs = expo / jnp.sum(expo, axis=1, keepdims=True)
    low = probs.astype(BF)
    mixed = dot(low, value, NN).astype(BF)
    value_grad = dot(low, back, TN)
    probs_grad = dot(back, value, NT)
    inner = jnp.sum(probs * probs_grad, axis=1, keepdims=True)
    score_grad = (probs * (probs_grad - inner)).astype(BF)
    query_grad = unturn(dot(score_grad, key, NN) * scale)
    key_grad = unturn(dot(score_grad, query, TN) * scale)
    qkv_grad = jnp.concatenate([query_grad, key_grad, value_grad], axis=1).astype(BF)
    mixed_ref[...] = mixed
    qkv_grad_ref[...] = qkv_grad
    acc1[...] += dot(qkv_grad, unit, TN)
    acc2[...] += dot(mixed, cot, TN)
    col[...] += dot(qkv_grad, jnp.ones((count, LANES), BF), TN)
    sum_ref[...] += jnp.sum(qkv_grad.astype(F32), axis=0, keepdims=True)

    @pl.when(group == pl.num_programs(0) - 1)
    def _():
        give_grads(acc1, acc2, col, gain_ref, shift_ref, w1, (own_ref, rest_ref, 0), (own_ref, rest_ref, cols), norm_ref)


def join_kernel(n, *refs):
    total = dot(refs[0][...], refs[n][...], NN)
    for j in range(1, n):
        total += dot(refs[j][...], refs[n + j][...], NN)
    refs[2 * n][...] = total.astype(BF)


def join_call(acts, weights, sent):
    rows, width = acts[0].shape[0], weights[0].shape[1]
    block = rows // 8
    first = 2 if sent else 0
    return run_kernel(
        functools.partial(join_kernel, len(acts)),
        shaped((rows // 2, width)),
        [pl.BlockSpec((block, a.shape[1]), lambda r: (4 * (r // 2) + r % 2 + first, 0)) for a in acts]
        + [whole(w.shape) for w in weights],
        pl.BlockSpec((block, width), lambda r: (r, 0)),
        (*acts, *weights),
        "join",
        grid=(4,),
        vmem=VMEM_LIMIT,
    )


def own_kernel(place, x_ref, cot_ref, out_ref, sum_ref):
    x = x_ref[...].astype(F32)
    centred = x - jnp.mean(x, axis=1, keepdims=True)
    spread = jnp.mean(centred * centred, axis=1, keepdims=True)
    unit = (centred * lax.rsqrt(spread + EPSILON)).astype(BF)
    width = x.shape[1] // 4
    for b in range(4):
        out_ref[0, :, spot(place, b, width)] = unit[:, b * width : (b + 1) * width]
        out_ref[1, :, spot(place, b, width)] = cot_ref[:, b * width : (b + 1) * width]

    @pl.when(pl.program_id(0) == 0)
    def _():
        sum_ref[...] = jnp.zeros_like(sum_ref)

    sum_ref[...] += jnp.sum(cot_ref[...].astype(F32), axis=0, keepdims=True)


def own_call(place, x, cot):
    rows, width = x.shape
    spec = pl.BlockSpec((rows // STEPS, width), lambda r: (r, 0))
    return run_kernel(
        own_kernel, [shaped((2, rows, width)), shaped((1, width), F32)], [SCALARS, spec, spec],
        [pl.BlockSpec((2, rows // STEPS, width), lambda r: (0, r, 0)), pl.BlockSpec((1, width), lambda r: (0, 0))],
        (place, x, cot), "own", grid=(STEPS,),
    )


def part_specs(parts, strip):
    specs = []
    for cross, n, first, every in parts:
        if cross:
            specs.append(pl.BlockSpec((strip, n), functools.partial(lambda f, e, k: (0, k * e + f), first, every)))
        else:
            specs.append(pl.BlockSpec((n, strip), functools.partial(lambda f, e, k: (k * e + f, 0), first, every)))
    return specs


def piece_kernel(parts, *refs):
    out_ref, at = refs[-1], 0
    for (cross, n, *_), ref in zip(parts, refs):
        out_ref[0, at : at + n] = ref[...].astype(F32).T.astype(BF) if cross else ref[...]
        at += n


def piece_call(arrays, parts, strip):
    n = sum(p[1] for p in parts)
    return run_kernel(
        functools.partial(piece_kernel, parts), shaped((INNER, n, strip)), part_specs(parts, strip),
        pl.BlockSpec((1, n, strip), lambda k: (k, 0, 0)), arrays, "piece", grid=(INNER,),
    )


def unpiece_kernel(parts, *refs):
    v_ref, outs, at = refs[0], refs[-len(parts) :], 0
    for (cross, n, *_), ref in zip(parts, outs):
        v = v_ref[0, at : at + n].astype(F32)
        ref[...] = v.T if cross else v
        at += n


def unpiece_call(v, shapes, parts, held):
    _, n, strip = v.shape
    held = [h for h in held if h is not None]
    return run_kernel(
        functools.partial(unpiece_kernel, parts), [shaped(s, F32) for s in shapes],
        [pl.BlockSpec((1, n, strip), lambda k: (k, 0, 0))] + [ANYWHERE] * len(held),
        part_specs(parts, strip), (v, *held), "unpiece", grid=(INNER,),
        aliases={1 + k: k for k in range(len(held))},
    )


def cat_kernel(a, b, out):
    out[0] = a[...]
    out[1] = b[...]


def cat_call(a, b):
    n = a.shape[0] // 2
    spec = pl.BlockSpec((n,) + a.shape[1:], lambda k: (k, 0, 0))
    out = run_kernel(
        cat_kernel, shaped((2,) + a.shape), [spec, spec],
        pl.BlockSpec((2, n) + a.shape[1:], lambda k: (0, k, 0, 0)), (a, b), "cat", grid=(2,),
    )
    return out.reshape((8,) + a.shape[1:])


def vectors_kernel(piece, nq, nf, share, tensor, place, small, g1, s1, g2, s2, r1, r2, out_bias, bq, bf, lengths):
    total = small.shape[0]
    per = total // 4
    width = per * piece

    def lay(to, b, k, where):
        part = small[b * per : (b + 1) * per, k * piece : (k + 1) * piece]
        to[:, where] = jnp.concatenate([part[r : r + 1] for r in range(per)], axis=1)

    for b in range(4):
        for k, to in enumerate((g1, s1, g2, s2)):
            lay(to, b, k, spot(place, b, width))
        lay(out_bias, b, 4, slice(b * width, (b + 1) * width))
    for gain, shift, ratio in ((g1, s1, r1), (g2, s2, r2)):
        v = shift[...] / gain[...]
        high = v.astype(BF).astype(F32)
        ratio[...] = jnp.concatenate([high, v - high, jnp.zeros((14, v.shape[1]), F32)], axis=0).astype(BF)
    at = 5 * piece
    for k in range(share):
        row = small[pl.ds((place[INSIDE] * share + k) * tensor + place[SIDE], 1), :]
        bq[:, k * nq : (k + 1) * nq] = row[:, at : at + nq]
        bf[:, k * nf : (k + 1) * nf] = row[:, at + nq : at + nq + nf]
    for g in range(INNER):
        row = small[pl.ds(place[DOC_ROW + g], 1), :]
        docs = row[:, at + nq + nf : at + nq + nf + LANES]
        lengths[g : g + 1] = (docs + 0.5).astype(jnp.int32)


def turns_kernel(own_rows, place, lengths, cos_ref, up_ref, down_ref):
    count = cos_ref.shape[0]
    group = pl.program_id(0)
    at = places(0, (count, 1), count, place[SIDE] * own_rows)
    end, begin = 0, jnp.zeros_like(at)
    for k in range(DOCS):
        end = end + lengths[group, k]
        begin = jnp.where(at >= end, end, begin)
    half = ROT // 2
    lane = lax.broadcasted_iota(jnp.int32, (1, LANES), 1)
    step = jnp.where(lane >= half, lane - half, lane).astype(F32)
    freq = jnp.exp(step * (-2.0 * math.log(10000.0) / ROT))
    angle = (at - begin).astype(F32) * freq
    sine = jnp.sin(angle)
    cos_ref[...] = jnp.where(lane < ROT, jnp.cos(angle), 1.0)
    up_ref[...] = jnp.where(lane < half, -sine, 0.0)
    down_ref[...] = jnp.where((lane >= half) & (lane < ROT), sine, 0.0)


def sum_kernel(*refs):
    total = refs[0][...].astype(F32)
    for r in refs[1:-1]:
        total += r[...].astype(F32)
    refs[-1][...] = total.astype(BF)


def sum_call(parts, firsts, count):
    shape = (4,) + parts[0].shape[1:]
    return run_kernel(
        sum_kernel,
        shaped((count,) + shape[1:]),
        [pl.BlockSpec(shape, functools.partial(lambda f, k: (k + f, 0, 0), f // 4)) for f in firsts],
        pl.BlockSpec(shape, lambda k: (k, 0, 0)),
        parts,
        "sum",
        grid=(count // 4,),
        vmem=VMEM_LIMIT,
    )


def core_kernel(kt, kx, kb, ot, ox, ob, x1, t1):
    half = kt.shape[1] // 2
    add = lambda a, b, cut: (a[:, cut].astype(F32) + b[:, cut].astype(F32)).astype(BF)
    left, right = slice(0, half), slice(half, 2 * half)
    x1[:, left] = add(kb, ob, left)
    x1[:, right] = add(kx, ox, left)
    t1[:, left] = add(kb, ob, right)
    t1[:, right] = add(kt, ot, right)


def cross_kernel(kt, kx, ot, ox, x1, t1, t2, x2):
    half = kt.shape[1] // 2
    left, right = slice(0, half), slice(half, 2 * half)
    add = lambda a, b, c: (a.astype(F32) + b.astype(F32) + c.astype(F32)).astype(BF)
    t2[...] = add(kt[:, left], ot[:, left], x1[:, left])
    x2[...] = add(kx[:, right], ox[:, right], t1[:, left])


def face_sum(place, kept, other, x1, t1, t2, x2, natural):
    half = kept.shape[1] // 2
    left, right = slice(0, half), slice(half, 2 * half)
    natural[:, left] = kept[:, left].astype(F32) + other[:, left].astype(F32) + x1[:, right].astype(F32) + t2[...].astype(F32)
    natural[:, right] = (
        kept[:, right].astype(F32) + other[:, right].astype(F32) + t1[:, right].astype(F32) + x2[...].astype(F32)
    )
    return jnp.concatenate([natural[:, spot(place, b, half // 2)] for b in range(4)], axis=1)


def output_kernel(place, x_ref, bias_ref, kept, other, x1, t1, t2, x2, out_ref, natural):
    total = face_sum(place, kept, other, x1, t1, t2, x2, natural) + bias_ref[...] + x_ref[...].astype(F32)
    out_ref[...] = total.astype(BF)


def input_grad_kernel(place, x_ref, cot_ref, kept, other, x1, t1, t2, x2, out_ref, natural):
    pulled = face_sum(place, kept, other, x1, t1, t2, x2, natural)
    x = x_ref[...].astype(F32)
    centred = x - jnp.mean(x, axis=1, keepdims=True)
    rstd = lax.rsqrt(jnp.mean(centred * centred, axis=1, keepdims=True) + EPSILON)
    unit = centred * rstd
    along = jnp.mean(pulled * unit, axis=1, keepdims=True)
    level = jnp.mean(pulled, axis=1, keepdims=True)
    out_ref[...] = (cot_ref[...].astype(F32) + rstd * (pulled - level - unit * along)).astype(BF)


def own_rows_call(kernel, place, rows_in, row_in, sums, name):
    rows, width = rows_in[0].shape
    block = rows // STEPS
    spec = pl.BlockSpec((block, width), lambda r: (r, 0))
    half = pl.BlockSpec((block, width // 2), lambda r: (r, 0))
    vector = pl.BlockSpec((1, width), lambda r: (0, 0))
    return run_kernel(
        kernel, shaped((rows, width)),
        [SCALARS] + [spec] * len(rows_in) + [vector] * len(row_in) + [spec] * 4 + [half] * 2,
        spec, (place, *rows_in, *row_in, *sums), name, grid=(STEPS,), scratch=[pltpu.VMEM((block, width), F32)],
    )


def tail_kernel(piece, nq, nf, share, tensor, place, n_attn, n0, n1, n2, sum_q, f0, f1, f2, cot_sum, tail):
    total = tail.shape[0]
    per = total // 4
    width = per * piece
    tail[...] = jnp.zeros_like(tail)

    def lay(k, b, row):
        rows = jnp.concatenate([row[:, r * piece : (r + 1) * piece] for r in range(per)], axis=0)
        tail[b * per : (b + 1) * per, k * piece : (k + 1) * piece] = rows

    for b in range(4):
        at = spot(place, b, width)
        attn = n_attn[:, at]
        feeds = n0[:, at] + n1[:, at] + n2[:, at]
        for k, row in enumerate((attn[0:1], attn[1:2], feeds[0:1], feeds[1:2])):
            lay(k, b, row)
        lay(4, b, cot_sum[:, b * width : (b + 1) * width])
    hidden = jnp.concatenate([f0[...], f1[...], f2[...]], axis=1)
    query = sum_q[...]
    at = full_lanes(5 * piece)
    rest = jnp.zeros((1, full_lanes(nq + nf) - nq - nf), F32)
    line = lax.broadcasted_iota(jnp.int32, (total, 1), 0)
    below = jnp.zeros((total, full_lanes(nq + nf)), F32)
    for k in range(share):
        row = (place[INSIDE] * share + k) * tensor + place[SIDE]
        both = [query[:, k * nq : (k + 1) * nq], hidden[:, k * nf : (k + 1) * nf]]
        both = jnp.concatenate(both + [rest] if rest.shape[1] else both, axis=1)
        below = jnp.where(line == row, both, below)
    tail[:, at:] = below


def make(dp, tensor):
    outer = dp // INNER
    face = INNER * tensor
    total = dp * tensor
    short = outer == 4

    def permute(v, pairs):
        return lax.ppermute(v, AXES, pairs)

    def flip(v, k):
        return permute(v, [(l, l ^ k) for l in range(total)])

    def hop(v, moves):
        return permute(v, [(a * face + f, b * face + f) for a, b in moves for f in range(face)])

    column_groups = [[o * face + f for o in range(outer)] for f in range(face)]
    ring_groups = [[o * face + i * tensor + t for i in range(INNER)] for o in range(outer) for t in range(tensor)]
    towards_middle = [(0, 1), (3, 2)]
    across_middle = [(1, 2), (2, 1)]
    towards_ends = [(1, 0), (2, 3)]

    back_table = [[0, 1, 2, 3], [1, 0, 2, 3], [3, 2, 0, 1], [3, 2, 1, 0]]

    def swap_ring(v):
        return lax.all_to_all(v, AXES, split_axis=0, concat_axis=0, tiled=True, axis_index_groups=ring_groups)

    def swap_all(v):
        return lax.all_to_all(v, AXES, split_axis=0, concat_axis=0, tiled=True)

    class Gather:
        def __init__(self, v):
            if not short:
                every = lax.all_gather(v, AXES, axis=0, tiled=True, axis_index_groups=column_groups)
                n = v.shape[1]
                every = every.transpose(1, 0, 2).reshape(n, 16, LANES).transpose(1, 0, 2)
                self.parts = [every[:8], every[8:], jnp.zeros_like(every[8:])]
                return
            self.own = v
            self.near = flip(v, face)

        def near_came(self, line):
            if short:
                self.own, near = line(self.own, self.near)
                self.both = line(cat_call(self.own, near))
                self.far = hop(self.both, across_middle)

        def far_came(self, line):
            if short:
                self.far = line(self.far)
                self.passed = hop(self.far, towards_ends)

        def passed_came(self, line):
            if short:
                self.parts = list(line(self.both, self.far, self.passed))

    class Reduce:
        def __init__(self, line, own, rest):
            if not short:
                v = jnp.concatenate([own, rest], axis=0)
                v = v.transpose(1, 0, 2).reshape(v.shape[1], dp, -1).transpose(1, 0, 2)
                self.total = lax.psum_scatter(
                    v, AXES, scatter_dimension=0, tiled=True, axis_index_groups=column_groups
                )
                return
            self.own, self.rest = line(own, rest)
            self.first = hop(self.rest, towards_middle)

        def first_came(self, line):
            if short:
                self.rest, self.first = line(self.rest, self.first)
                far = line(sum_call((self.rest, self.first), (4, 4), 8))
                self.second = hop(far, across_middle)

        def second_came(self, line):
            if short:
                self.rest, self.second = line(self.rest, self.second)
                near = line(sum_call((self.rest, self.second), (0, 4), 4))
                self.third = hop(near, towards_ends)

        def third_came(self, line):
            if short:
                self.third = line(self.third)
                self.total = sum_call((self.own, self.first, self.second, self.third), (0, 0, 0, 0), 4)
            self.total = line(self.total)
            self.final = swap_ring(self.total)

    class FaceReduce:
        def __init__(self, sent):
            self.other = flip(sent, 2)

        def core_came(self, line):
            self.kept, self.other = line(self.kept, self.other)
            self.rows, self.width = self.kept.shape[0] // 4, self.kept.shape[1]
            spec = pl.BlockSpec((self.rows // STEPS, self.width), lambda r: (r, 0))
            x1, t1 = run_kernel(
                core_kernel, [shaped((self.rows, self.width))] * 2, self.block_specs(1, 2, 3) * 2, [spec] * 2,
                (self.kept,) * 3 + (self.other,) * 3, "core", grid=(STEPS,),
            )
            x1, t1 = line(x1, t1)
            self.x1, self.t1 = flip(x1, 4), flip(t1, 1)

        def block_specs(self, *blocks):
            block = self.rows // STEPS
            return [
                pl.BlockSpec((block, self.width), functools.partial(lambda k, r: (k * STEPS + r, 0), k)) for k in blocks
            ]

        def first_came(self, line):
            self.x1, self.t1 = line(self.x1, self.t1)
            rows, width = self.rows, self.width
            spec = pl.BlockSpec((rows // STEPS, width), lambda r: (r, 0))
            half = pl.BlockSpec((rows // STEPS, width // 2), lambda r: (r, 0))
            t2, x2 = run_kernel(
                cross_kernel, [shaped((rows, width // 2))] * 2, self.block_specs(1, 2) * 2 + [spec] * 2, [half] * 2,
                (self.kept, self.kept, self.other, self.other, self.x1, self.t1), "cross", grid=(STEPS,),
            )
            t2, x2 = line(t2, x2)
            self.t2, self.x2 = flip(t2, 1), flip(x2, 4)

        def second_came(self, line):
            self.t2, self.x2 = line(self.t2, self.x2)
            return self.kept, self.other, self.x1, self.t1, self.t2, self.x2

    def per_device(
        layer_input, doc_lengths, ln1_gain, ln1_bias, ln2_gain, ln2_bias, w_qkv, b_qkv, w_dense, b_dense,
        w_fc1, b_fc1, w_fc2, b_fc2, cotangent,
    ):
        d, t = lax.axis_index("dp"), lax.axis_index("tensor")
        o, i = d // INNER, d % INNER
        own_rows, width = layer_input.shape
        rows, group_rows = own_rows * face, own_rows * tensor
        strip = width // dp
        hidden_own = w_fc1.shape[1] // INNER
        qkv_own = w_qkv.shape[1] // INNER
        quarter = hidden_own // 4
        piece, nq, nf = width // total, b_qkv.shape[0], b_fc1.shape[0]
        share = dp // INNER
        line = Line()
        if short:
            spots = jnp.array(back_table, jnp.int32)[o]
        else:
            spots = jnp.arange(4, dtype=jnp.int32)
        doc_rows = (o * INNER + (i ^ jnp.arange(INNER, dtype=jnp.int32))) * tensor
        place = jnp.concatenate([jnp.stack([o, i, t]).astype(jnp.int32), spots, doc_rows.astype(jnp.int32)])

        forms = [
            ((w_fc1, w_fc2), ((True, quarter, 0, 4), (False, quarter, 0, 4))),
            ((w_fc1, w_fc2), ((True, quarter, 1, 4), (False, quarter, 1, 4))),
            ((w_qkv, w_qkv), ((True, HD, 0, 3), (True, HD, 1, 3))),
            ((w_qkv, w_dense), ((True, HD, 2, 3), (False, HD, 0, 1))),
            ((w_fc1, w_fc2), ((True, 2 * quarter, 1, 2), (False, 2 * quarter, 1, 2))),
        ]
        s = {}
        steps = {}

        def own():
            s["own"], s["cot_sum"] = own_call(place, *line(layer_input, cotangent))
            s["own"] = line(s["own"])
            s["t"], s["x"], s["c"] = flip(s["own"], 1), flip(s["own"], 4), flip(s["own"], 2)

        def own_c():
            s["c"] = line(s["c"])

        def own_xt():
            s["x"], s["t"] = line(s["x"], s["t"])
            s["b"], s["tc"], s["xc"] = flip(s["x"], 1), flip(s["t"], 2), flip(s["x"], 2)

        def own_tc():
            s["tc"], s["xc"] = line(s["tc"], s["xc"])

        def own_b():
            s["b"] = line(s["b"])
            s["bc"] = flip(s["b"], 2)

        def own_bc():
            s["bc"] = line(s["bc"])

        steps.update({"own": own, "c": own_c, "xt": own_xt, "tc": own_tc, "b": own_b, "bc": own_bc})

        def small():
            v = jnp.concatenate(
                [ln1_gain, ln1_bias, ln2_gain, ln2_bias, b_dense + b_fc2, b_qkv.astype(F32), b_fc1.astype(F32),
                 doc_lengths[0].astype(F32), jnp.zeros((LANES - DOCS,), F32)]
            )
            s["small"] = swap_all(line(jnp.broadcast_to(v[None], (total, v.shape[0]))))

        def vectors():
            v = line(s["small"]).reshape(total, -1)
            row, fine = shaped((1, width), F32), shaped((16, width))
            *s["vec"], s["bias_q"], s["bias_f"], s["lengths"] = run_kernel(
                functools.partial(vectors_kernel, piece, nq, nf, share, tensor),
                [row] * 4 + [fine] * 2 + [row, shaped((1, qkv_own), F32), shaped((1, hidden_own), F32),
                                          shaped((INNER, LANES), jnp.int32)],
                [SCALARS, VECTORS], [VECTORS] * 10, (place, v), "vectors",
            )
            turn_spec = pl.BlockSpec((group_rows, LANES), lambda g: (g, 0))
            turns = run_kernel(
                functools.partial(turns_kernel, own_rows), [shaped((rows, LANES), F32)] * 3, [SCALARS] * 2,
                [turn_spec] * 3, (place, s["lengths"]), "turns", grid=(INNER,),
            )
            s["turns"] = line(*turns)

        steps.update({"sm": small, "vec": vectors})
        gathers, done, sums = {}, {}, {}

        def gather_steps(k):
            def p():
                arrays, parts = forms[k]
                s[f"ring{k}"] = swap_ring(line(piece_call(arrays, parts, strip)))

            def g():
                gathers[k] = Gather(line(s[f"ring{k}"]))

            steps.update({
                f"p{k}": p, f"g{k}": g, f"h{k}": lambda: gathers[k].near_came(line),
                f"i{k}": lambda: gathers[k].far_came(line), f"j{k}": lambda: gathers[k].passed_came(line),
            })

        for k in range(5):
            gather_steps(k)

        def pieces():
            return [s[n] for n in ("own", "t", "c", "tc", "x", "b", "xc", "bc")]

        def feed(k, first, count):
            def run():
                gain, shift, ratio = s["vec"][2], s["vec"][3], s["vec"][5]
                bias = s["bias_f"][:, first * quarter : (first + count) * quarter]
                cols, split = count * quarter, count
                parts = gathers[k].parts
                parts[0] = line(parts[0])
                done[k] = list(chunk_call(
                    functools.partial(feed_kernel, cols, split), "feed", pieces(), (), [], [parts],
                    (gain, shift, ratio, bias), cols, cols, split,
                ))
                done[k][5] = line(done[k][5])

            return run

        def attention():
            gain, shift, ratio = s["vec"][0], s["vec"][1], s["vec"][4]
            one, two = gathers[2].parts, gathers[3].parts
            one[0] = line(one[0])
            turn_spec = pl.BlockSpec((group_rows, LANES), lambda r: (r, 0))
            done[2] = list(chunk_call(
                functools.partial(attention_kernel, qkv_own), "attention", pieces(),
                (s["lengths"], place, *s["turns"]), [SCALARS, SCALARS] + [turn_spec] * 3, [one, two],
                (gain, shift, ratio, s["bias_q"]), qkv_own, HD, 1,
            ))
            done[2][5] = line(done[2][5])

        steps.update({"K0": feed(0, 0, 1), "K1": feed(1, 1, 1), "KA": attention, "K4": feed(4, 2, 2)})

        def reduce_steps(k, chunk, at):
            def r():
                sums[k] = Reduce(line, *done[chunk][at : at + 2])

            def z():
                final = line(sums[k].final)
                if k == 2:
                    s["qkv"], s["dense"] = line(*unpiece_call(
                        final, (w_qkv.shape, w_dense.shape), ((True, qkv_own, 0, 1), (False, HD, 0, 1)), ()
                    ))
                elif k < 2:
                    s["fc1"], s["fc2"] = line(*unpiece_call(
                        final, (w_fc1.shape, w_fc2.shape), forms[k][1], (s.get("fc1"), s.get("fc2"))
                    ))
                else:
                    name, w, form = (("fc1", w_fc1, 0), ("fc2", w_fc2, 1))[k - 3]
                    s[name] = line(*unpiece_call(final, (w.shape,), forms[4][1][form : form + 1], (s[name],)))

            steps.update({
                f"r{k}": r, f"u{k}": lambda: sums[k].first_came(line), f"v{k}": lambda: sums[k].second_came(line),
                f"w{k}": lambda: sums[k].third_came(line), f"z{k}": z,
            })

        for k, chunk, at in ((0, 0, 6), (1, 1, 6), (2, 2, 6), (3, 4, 6), (4, 4, 8)):
            reduce_steps(k, chunk, at)

        def face_steps(name, act, weight, finish):
            def parts():
                chunks = [done[k] for k in (0, 1, 2, 4)]
                return [c[act] for c in chunks], [c[weight] for c in chunks]

            def sent():
                acts, weights = parts()
                acts[0] = line(acts[0])
                s["face" + name] = FaceReduce(line(join_call(acts, weights, True)))

            def kept():
                acts, weights = parts()
                acts[0] = line(acts[0])
                s["face" + name].kept = line(join_call(acts, weights, False))

            steps.update({
                "J" + name: sent, "k" + name: kept, "C" + name: lambda: s["face" + name].core_came(line),
                "D" + name: lambda: s["face" + name].first_came(line),
                "E" + name: lambda: finish(s["face" + name].second_came(line)),
            })

        def finish_back(sums_in):
            s["input_grad"] = line(
                own_rows_call(input_grad_kernel, place, (layer_input, cotangent), (), sums_in, "input_grad")
            )

        def finish_out(sums_in):
            s["output"] = line(own_rows_call(output_kernel, place, (layer_input,), (s["vec"][6],), sums_in, "output"))

        face_steps("B", 1, 2, finish_back)
        face_steps("O", 0, 3, finish_out)

        def tail():
            feeds = [done[k] for k in (0, 1, 4)]
            v = run_kernel(
                functools.partial(tail_kernel, piece, nq, nf, share, tensor),
                shaped((total, full_lanes(5 * piece) + full_lanes(nq + nf)), F32), [SCALARS] + [VECTORS] * 9, VECTORS,
                (place, done[2][4], *[p[4] for p in feeds], done[2][5], *[p[5] for p in feeds], s["cot_sum"]), "tail",
            )
            s["tail"] = swap_all(line(v))

        def tail_came():
            s["tail"] = jnp.sum(line(s["tail"]), axis=0)

        steps.update({"tail": tail, "tz": tail_came})
        for name in ORDER:
            steps[name]()

        tail_row = s["tail"]
        cuts = [tail_row[j * piece : (j + 1) * piece] for j in range(5)]
        at = full_lanes(5 * piece)
        return (
            s["output"], s["input_grad"], cuts[0], cuts[1], cuts[2], cuts[3], s["qkv"], tail_row[at : at + nq],
            s["dense"], cuts[4], s["fc1"], tail_row[at + nq : at + nq + nf], s["fc2"], cuts[4],
        )

    return per_device


def solution(mesh):
    rows = P(("dp", "tensor"), None)
    vector = P(("dp", "tensor"))
    crossed = P(("tensor", "dp"))
    wide = P("dp", "tensor")
    tall = P("tensor", "dp")
    return jax.shard_map(
        make(mesh.shape["dp"], mesh.shape["tensor"]),
        mesh=mesh,
        in_specs=(rows, P("dp", None), vector, vector, vector, vector, wide, crossed, tall, vector, wide, crossed,
                  tall, vector, rows),
        out_specs=(rows, rows, vector, vector, vector, vector, wide, crossed, tall, vector, wide, crossed, tall,
                   vector),
        check_vma=False,
    )
```

time: 665 us -> 565 us (0.85)
  Pallas kernels: 160 us -> 278 us
  waiting for transfers between devices: 198 us -> 90 us
  other arithmetic: 86.4 us -> 0.03 us
  starting transfers between devices: 168 us -> 134 us
  blocking collectives: 0 us -> 23.9 us
  local copies, waits for them, and re-layouts: 33.7 us -> 26 us
    ppermute x66 -> x47, waiting for transfers between devices: 186 us -> 59.4 us  [permute(): return lax.ppermute(v, AXES, pairs)]
    pallas_call x9 -> x163, Pallas kernels: 160 us -> 278 us  [run_kernel(): pl.pallas_call(kernel, grid=grid, out_shape=outs, in_specs=in_specs, out_...]
    convert_element_type x29 -> x1, other arithmetic: 47.1 us -> 0.01 us  [small(): doc_lengths[0].astype(F32)]
    ppermute x66 -> x47, starting transfers between devices: 126 us -> 94.4 us  [permute(): return lax.ppermute(v, AXES, pairs)]
    all_to_all x0 -> x1, blocking collectives: none -> 23.9 us  [swap_all(): return lax.all_to_all(v, AXES, split_axis=0, concat_axis=0, tiled=True)]
    all_to_all x8 -> x10, waiting for transfers between devices: 6.97 us -> 30.6 us  [swap_ring(): lax.all_to_all(v, AXES, split_axis=0, concat_axis=0, tiled=True, axis_ind...]
    unnamed x143 -> x89, local copies, waits for them, and re-layouts: 4.13 us -> 18.7 us
    slice x24 -> x5, local copies, waits for them, and re-layouts: 17 us -> 2.93 us  [the longest x2 1.14 us: run(): bias = s['bias_f'][:, first * quarter:(first + count) * quarter]]
  transfers between devices with their start and end apart: 76 -> 58, of which waited for: 29 -> 17; matrix products, arithmetic and copies ran while one was open for 16% -> 3% of each run, Pallas kernels for 24% -> 49%
where the time goes in v2:
time: 565 us; the launch traced here: 554 us
  Pallas kernels  278 us (49%)
  starting transfers between devices  134 us (24%)
  waiting for transfers between devices  90 us (16%)
  local copies, waits for them, and re-layouts  26 us (5%)
  blocking collectives  23.9 us (4%)
    pallas_call x163, Pallas kernels, run_kernel(): pl.pallas_call(kernel, grid=grid, out_shape=outs, in_specs=in_specs, out_...  278 us
    ppermute x47, starting transfers between devices, permute(): return lax.ppermute(v, AXES, pairs)  94.4 us
    ppermute x47, waiting for transfers between devices, permute(): return lax.ppermute(v, AXES, pairs)  59.4 us
    all_to_all x10, starting transfers between devices, swap_ring(): lax.all_to_all(v, AXES, split_axis=0, concat_axis=0, tiled=True, axis_ind...  36.9 us
    all_to_all x10, waiting for transfers between devices, swap_ring(): lax.all_to_all(v, AXES, split_axis=0, concat_axis=0, tiled=True, axis_ind...  30.6 us
    all_to_all x1, blocking collectives, swap_all(): return lax.all_to_all(v, AXES, split_axis=0, concat_axis=0, tiled=True)  23.9 us
    unnamed x89, local copies, waits for them, and re-layouts  18.7 us
  transfers between devices with their start and end apart: 58, of which 17 were waited for; matrix products, arithmetic and copies ran while one was open for 3% of the time, Pallas kernels for 49%

profile of v2, /device:TPU:8, one launch (start us, length us, event | category | flops | bytes accessed | tf_op | source)
XLA Modules:
  0.0 554.0 jit_solution(4038409399626159951)
XLA Ops:
  0.6 3.3 piece.6.refs_0_
  4.5 3.5 all-to-all-start.1
  8.0 3.3 piece.5.refs_0_
  11.3 5.5 all-to-all-done.1.refs_0_
  16.8 3.5 all-to-all-start
  20.3 3.3 piece.7.refs_0_
  23.6 5.5 all-to-all-done.refs_0_
  29.1 3.5 all-to-all-start.3
  34.7 3.3 piece.8.refs_0_
  38.0 3.4 all-to-all-done.3.refs_0_
  41.4 4.1 all-to-all-start.2
  48.8 4.5 own.1
  59.5 4.7 collective-permute-start.2
  64.2 7.1 %collective-permute-done.3.refs_1_ = bf16[4,512,128]{2,1,0:T(8,128)(2,1)} collective-permute-done((bf16[4,512,128]{2,1,0:T(8,128)(2,1)S(1)}, bf16[4,512,128]{2,1,0:T(8,128)(2,1)}, u32[]{:S(2)}, u32[]{:S(2)}) %collective-permute-start.3) | collective-permute-done | bytes 524320 | tf_op jit(solution)/shard_map/ppermute | solution.py:578
  71.8 3.6 piece.9.refs_0_
  80.4 4.8 collective-permute-done.9.refs_1_
  85.2 3.5 collective-permute-start.5
  88.7 3.0 collective-permute-start.15
  93.8 7.8 %collective-permute-done.7.refs_0_ = bf16[2,256,2048]{2,1,0:T(8,128)(2,1)} collective-permute-done((bf16[2,256,2048]{2,1,0:T(8,128)(2,1)}, bf16[2,256,2048]{2,1,0:T(8,128)(2,1)}, u32[]{:S(2)}, u32[]{:S(2)}) %collective-permute-start.7) | collective-permute-done | bytes 2097184 | tf_op jit(solution)/shard_map/ppermute | solution.py:578
  107.8 5.5 collective-permute-done.5.refs_0_
  113.3 20.3 %collective-permute-done.15.refs_0_ = bf16[8,512,128]{2,1,0:T(8,128)(2,1)} collective-permute-done((bf16[8,512,128]{2,1,0:T(8,128)(2,1)}, bf16[8,512,128]{2,1,0:T(8,128)(2,1)}, u32[]{:S(2)}, u32[]{:S(2)}) %collective-permute-start.15) | collective-permute-done | bytes 1048608 | tf_op jit(solution)/shard_map/ppermute | solution.py:578
  135.8 4.3 all-to-all-start.5
  140.1 3.5 collective-permute-start.13
  143.6 11.0 %all-to-all-done.5.refs_0_ = bf16[4,1024,128]{2,1,0:T(8,128)(2,1)} async-done(((bf16[4,1024,128]{2,1,0:T(8,128)(2,1)}), bf16[4,1024,128]{2,1,0:T(8,128)(2,1)}, u32[]{:S(2)}, u32[]{:S(2)}) %all-to-all-start.5) | async-done | bytes 1048608 | tf_op jit(solution)/shard_map/all_to_all | solution.py:595
  158.5 23.9 %all_to_all.72 = f32[32,1,896]{2,1,0:T(1,128)S(1)} all-to-all(f32[32,1,896]{2,1,0:T(1,128)S(1)} %copy.312), channel_id=1, replica_groups=mesh['dp'=16,'tensor'=2] {'dp','tensor'}, dimensions={0} | all-to-all | bytes 229376 | tf_op jit(solution)/shard_map/all_to_all | solution.py:598
  184.8 6.0 %turns.1 = (f32[2048,128]{1,0:T(8,128)}, f32[2048,128]{1,0:T(8,128)}, f32[2048,128]{1,0:T(8,128)}) custom-call(s32[11]{0:T(128)} %concatenate.6.place.refs_19_, s32[4,128]{1,0:T(4,128)} %get-tuple-element.413.lengths.refs_18_), custom_call_target="tpu_custom_call" | custom-call | tf_op jit(solution)/shard_map/turns/pallas_call | solution.py:56
  202.0 18.5 %feed.3 = (bf16[2048,256]{1,0:T(8,128)(2,1)}, bf16[2048,256]{1,0:T(8,128)(2,1)}, bf16[256,2048]{1,0:T(8,128)(2,1)}, bf16[256,2048]{1,0:T(8,128)(2,1)}, f32[2,204...) custom-call(bf16[2,256,2048]{2,1,0:T(8,128)(2,1)} %get-tuple-element.393.refs_0_, ...), custom_call_target="tpu_custom_call" | custom-call | tf_op jit(solution)/shard_map/feed/pallas_call | solution.py:56
  222.3 18.5 %feed.4 = (bf16[2048,256]{1,0:T(8,128)(2,1)}, bf16[2048,256]{1,0:T(8,128)(2,1)}, bf16[256,2048]{1,0:T(8,128)(2,1)}, bf16[256,2048]{1,0:T(8,128)(2,1)}, f32[2,204...) custom-call(bf16[2,256,2048]{2,1,0:T(8,128)(2,1)} %get-tuple-element.393.refs_0_, ...), custom_call_target="tpu_custom_call" | custom-call | tf_op jit(solution)/shard_map/feed/pallas_call | solution.py:56
  240.9 4.2 collective-permute-done.20.refs_0_
  246.5 2.8 collective-permute-start.23
  251.5 38.6 %attention.1 = (bf16[2048,256]{1,0:T(8,128)(2,1)}, bf16[2048,768]{1,0:T(8,128)(2,1)}, bf16[768,2048]{1,0:T(8,128)(2,1)}, bf16[256,2048]{1,0:T(8,128)(2,1)}, f32[...) custom-call(bf16[2,256,2048]{2,1,0:T(8,128)(2,1)} %get-tuple-element.393.refs_, ...), custom_call_target="tpu_custom_call" | custom-call | tf_op jit(solution)/shard_map/attention/pallas_call | solution.py:56
  292.8 3.0 collective-permute-start.26
  299.6 3.0 collective-permute-start.25
  305.5 30.8 %feed.5 = (bf16[2048,512]{1,0:T(8,128)(2,1)}, bf16[2048,512]{1,0:T(8,128)(2,1)}, bf16[512,2048]{1,0:T(8,128)(2,1)}, bf16[512,2048]{1,0:T(8,128)(2,1)}, f32[2,204...) custom-call(bf16[2,256,2048]{2,1,0:T(8,128)(2,1)} %get-tuple-element, ...), custom_call_target="tpu_custom_call" | custom-call | tf_op jit(solution)/shard_map/feed/pallas_call | solution.py:56
  338.4 13.0 %join.4.refs_0_ = bf16[1024,2048]{1,0:T(8,128)(2,1)} custom-call(bf16[2048,256]{1,0:T(8,128)(2,1)} %get-tuple-element.518.refs_0_, bf16[2048,256]{1,0:T(8,128)(2,1)} %get-tuple-element.519.refs_1_, bf16[2048,768]{1,0:T(8,128)(2,1)} %get-tuple-element.520.refs_2_, bf16[2048,512]{1,0:T(8,128)(2,1)} %get-tuple-element.521.refs_3_, ...), custom_call_target="tpu_custom_call" | custom-call | tf_op jit(solution)/shard_map/join/pallas_call | solution.py:56
  355.8 10.2 %join.5.refs_0_ = bf16[1024,2048]{1,0:T(8,128)(2,1)} custom-call(bf16[2048,256]{1,0:T(8,128)(2,1)} %get-tuple-element.532.refs_0_, bf16[2048,256]{1,0:T(8,128)(2,1)} %get-tuple-element.533.refs_1_, bf16[2048,256]{1,0:T(8,128)(2,1)} %get-tuple-element.534.refs_2_, bf16[2048,512]{1,0:T(8,128)(2,1)} %get-tuple-element.535.refs_3_, ...), custom_call_target="tpu_custom_call" | custom-call | tf_op jit(solution)/shard_map/join/pallas_call | solution.py:56
  367.2 3.4 sum.19.refs_0_
  370.6 3.1 collective-permute-start.30
  375.1 5.9 %collective-permute-start.28 = (bf16[4,512,128]{2,1,0:T(8,128)(2,1)S(1)}, bf16[4,512,128]{2,1,0:T(8,128)(2,1)S(1)}, u32[]{:S(2)}, u32[]{:S(2)}) collective-permute-start(bf16[4,512,128]{2,1,0:T(8,128)(2,1)S(1)} %copy-done.24), channel_id=1, source_target_pairs={{8,0},{9,1},{10,2},{11,3},{12,4},{13,5},{14,6},{15,7},{16,24},{17,... | collective-permute-start | bytes 1572872 | tf_op jit(solution)/shard_map/ppermute | solution.py:578
  381.0 13.0 %join.6.refs_0_ = bf16[1024,2048]{1,0:T(8,128)(2,1)} custom-call(bf16[2048,256]{1,0:T(8,128)(2,1)} %get-tuple-element.546.refs_0_, bf16[2048,256]{1,0:T(8,128)(2,1)} %get-tuple-element.519.refs_1_, bf16[2048,768]{1,0:T(8,128)(2,1)} %get-tuple-element.520.refs_2_, bf16[2048,512]{1,0:T(8,128)(2,1)} %get-tuple-element.521.refs_3_, ...), custom_call_target="tpu_custom_call" | custom-call | tf_op jit(solution)/shard_map/join/pallas_call | solution.py:56
  397.4 4.6 core.2
  405.0 6.1 %collective-permute-done.31.refs_1_ = bf16[12,512,128]{2,1,0:T(8,128)(2,1)} collective-permute-done((bf16[12,512,128]{2,1,0:T(8,128)(2,1)S(1)}, bf16[12,512,128]{2,1,0:T(8,128)(2,1)}, u32[]{:S(2)}, u32[]{:S(2)}) %collective-permute-start.31) | collective-permute-done | bytes 1572896 | tf_op jit(solution)/shard_map/ppermute | solution.py:578
  412.4 4.2 all-to-all-start.6
  416.6 10.1 %join.7.refs_0_ = bf16[1024,2048]{1,0:T(8,128)(2,1)} custom-call(bf16[2048,256]{1,0:T(8,128)(2,1)} %get-tuple-element.562.refs_0_, bf16[2048,256]{1,0:T(8,128)(2,1)} %get-tuple-element.533.refs_1_, bf16[2048,256]{1,0:T(8,128)(2,1)} %get-tuple-element.534.refs_2_, bf16[2048,512]{1,0:T(8,128)(2,1)} %get-tuple-element.535.refs_3_, ...), custom_call_target="tpu_custom_call" | custom-call | tf_op jit(solution)/shard_map/join/pallas_call | solution.py:56
  429.1 2.8 collective-permute-start.39
  432.0 3.4 unpiece.5
  438.1 4.4 collective-permute-start.37
  442.5 4.6 core.3
  452.1 4.4 cross.2
  460.7 3.0 collective-permute-start.34
  469.4 4.6 collective-permute-start.45
  474.0 3.7 sum.25.refs_0_
  477.7 3.5 all-to-all-start.8
  484.5 4.3 cross.3
  496.1 3.5 all-to-all-start.10
  501.2 3.7 unpiece.6
  507.5 4.9 output.1.refs_0_
  519.3 3.5 all-to-all-start.9
  524.5 5.5 %input_grad.1.refs_0_ = bf16[256,2048]{1,0:T(8,128)(2,1)} custom-call(s32[11]{0:T(128)} %concatenate.6.place.refs_19_, bf16[256,2048]{1,0:T(8,128)(2,1)} %x_ref.3, bf16[256,2048]{1,0:T(8,128)(2,1)} %cot_ref.1, bf16[1024,2048]{1,0:T(8,128)(2,1)} %get-tuple-element.556.kt.kx.kb.kept, bf16[1024,2048]{1,0:T(8,128)(2,1)} %get-tuple-element.557.ot.ox.ob.other, ...), custom_call_target="tpu_custom_call" | custom-call | tf_op jit(solution)/shard_map/input_grad/pallas_call | solution.py:56
  530.1 3.4 unpiece.7
  536.9 3.5 all-to-all-start.11
  542.2 3.5 unpiece.8.refs_0_
  545.7 3.5 all-to-all-done.11.refs_0_
  550.0 3.3 unpiece.9.refs_0_
  (322 shorter events, 126.8 us)
Async XLA Ops:
  4.5 12.3 %all-to-all-start.1 = ((bf16[4,512,128]{2,1,0:T(8,128)(2,1)}), bf16[4,512,128]{2,1,0:T(8,128)(2,1)S(1)}, u32[]{:S(2)}, u32[]{:S(2)}) async-start(bf16[4,512,128]{2,1,0:T(8,128)(2,1)} %get-tuple-element.356), calls=%async_computation.1 | async-start | bytes 1048576 | tf_op jit(solution)/shard_map/all_to_all | solution.py:595
  16.8 12.3 %all-to-all-start = ((bf16[4,512,128]{2,1,0:T(8,128)(2,1)}), bf16[4,512,128]{2,1,0:T(8,128)(2,1)S(1)}, u32[]{:S(2)}, u32[]{:S(2)}) async-start(bf16[4,512,128]{2,1,0:T(8,128)(2,1)} %get-tuple-element.355), calls=%async_computation | async-start | bytes 1048576 | tf_op jit(solution)/shard_map/all_to_all | solution.py:595
  29.1 12.3 %all-to-all-start.3 = ((bf16[4,512,128]{2,1,0:T(8,128)(2,1)}), bf16[4,512,128]{2,1,0:T(8,128)(2,1)S(1)}, u32[]{:S(2)}, u32[]{:S(2)}) async-start(bf16[4,512,128]{2,1,0:T(8,128)(2,1)} %get-tuple-element.364), calls=%async_computation.3 | async-start | bytes 1048576 | tf_op jit(solution)/shard_map/all_to_all | solution.py:595
  32.6 24.2 %collective-permute-start.1 = (bf16[4,512,128]{2,1,0:T(8,128)(2,1)}, bf16[4,512,128]{2,1,0:T(8,128)(2,1)}, u32[]{:S(2)}, u32[]{:S(2)}) collective-permute-start(bf16[4,512,128]{2,1,0:T(8,128)(2,1)} %get-tuple-element.361.refs_0_), channel_id=1, source_target_pairs={{0,8},{1,9},{2,10},{3,11},{4,12},{5,13},{6,14},{7,15},{8,0},{9,1},... | collective-permute-start | bytes 1572872 | tf_op jit(solution)/shard_map/ppermute | solution.py:578
  32.7 26.7 %collective-permute-start = (bf16[4,512,128]{2,1,0:T(8,128)(2,1)}, bf16[4,512,128]{2,1,0:T(8,128)(2,1)S(1)}, u32[]{:S(2)}, u32[]{:S(2)}) collective-permute-start(bf16[4,512,128]{2,1,0:T(8,128)(2,1)} %get-tuple-element.360.refs_0_), channel_id=1, source_target_pairs={{0,8},{1,9},{2,10},{3,11},{4,12},{5,13},{6,14},{7,15},{8,0},{9,1},... | collective-permute-start | bytes 1572872 | tf_op jit(solution)/shard_map/ppermute | solution.py:578
  41.4 15.4 %all-to-all-start.2 = ((bf16[4,512,128]{2,1,0:T(8,128)(2,1)}), bf16[4,512,128]{2,1,0:T(8,128)(2,1)}, u32[]{:S(2)}, u32[]{:S(2)}) async-start(bf16[4,512,128]{2,1,0:T(8,128)(2,1)} %get-tuple-element.363), calls=%async_computation.2 | async-start | bytes 1048576 | tf_op jit(solution)/shard_map/all_to_all | solution.py:595
  53.3 48.3 %collective-permute-start.7 = (bf16[2,256,2048]{2,1,0:T(8,128)(2,1)}, bf16[2,256,2048]{2,1,0:T(8,128)(2,1)}, u32[]{:S(2)}, u32[]{:S(2)}) collective-permute-start(bf16[2,256,2048]{2,1,0:T(8,128)(2,1)} %get-tuple-element.393.refs_0_), channel_id=1, source_target_pairs={{0,4},{1,5},{2,6},{3,7},{4,0},{5,1},{6,2},{7,3},{8,12},{9,13},{10,... | collective-permute-start | bytes 6291464 | tf_op jit(solution)/shard_map/ppermute | solution.py:578
  55.3 49.0 %collective-permute-start.8 = (bf16[2,256,2048]{2,1,0:T(8,128)(2,1)}, bf16[2,256,2048]{2,1,0:T(8,128)(2,1)}, u32[]{:S(2)}, u32[]{:S(2)}) collective-permute-start(bf16[2,256,2048]{2,1,0:T(8,128)(2,1)} %get-tuple-element.393.refs_0_), channel_id=1, source_target_pairs={{0,1},{1,0},{2,3},{3,2},{4,5},{5,4},{6,7},{7,6},{8,9},{9,8},{10,11... | collective-permute-start | bytes 6291464 | tf_op jit(solution)/shard_map/ppermute | solution.py:578
  56.8 49.7 %collective-permute-start.6 = (bf16[2,256,2048]{2,1,0:T(8,128)(2,1)}, bf16[2,256,2048]{2,1,0:T(8,128)(2,1)S(1)}, u32[]{:S(2)}, u32[]{:S(2)}) collective-permute-start(bf16[2,256,2048]{2,1,0:T(8,128)(2,1)} %get-tuple-element.393.refs_0_), channel_id=1, source_target_pairs={{0,2},{1,3},{2,0},{3,1},{4,6},{5,7},{6,4},{7,5},{8,10},{9,11},{10,... | collective-permute-start | bytes 6291464 | tf_op jit(solution)/shard_map/ppermute | solution.py:578
  56.8 14.5 %collective-permute-start.3 = (bf16[4,512,128]{2,1,0:T(8,128)(2,1)S(1)}, bf16[4,512,128]{2,1,0:T(8,128)(2,1)}, u32[]{:S(2)}, u32[]{:S(2)}) collective-permute-start(bf16[4,512,128]{2,1,0:T(8,128)(2,1)S(1)} %copy-done.13), channel_id=1, source_target_pairs={{0,8},{1,9},{2,10},{3,11},{4,12},{5,13},{6,14},{7,15},{8,0},{9,1},... | collective-permute-start | bytes 1572872 | tf_op jit(solution)/shard_map/ppermute | solution.py:578
  59.4 16.0 %copy-start.31 = (f32[64]{0:T(128)S(1)}, f32[64]{0:T(128)}, u32[]{:S(2)}) copy-start(f32[64]{0:T(128)} %param.18) | copy-start | bytes 772
  59.4 16.0 %copy-start.32 = (f32[64]{0:T(128)S(1)}, f32[64]{0:T(128)}, u32[]{:S(2)}) copy-start(f32[64]{0:T(128)} %param.19) | copy-start | bytes 772
  59.4 16.0 %copy-start.33 = (f32[64]{0:T(128)S(1)}, f32[64]{0:T(128)}, u32[]{:S(2)}) copy-start(f32[64]{0:T(128)} %param.20) | copy-start | bytes 772
  59.4 16.0 %copy-start.34 = (f32[64]{0:T(128)S(1)}, f32[64]{0:T(128)}, u32[]{:S(2)}) copy-start(f32[64]{0:T(128)} %param.21) | copy-start | bytes 772
  59.5 16.1 %copy-start.23 = (bf16[4,512,128]{2,1,0:T(8,128)(2,1)}, bf16[4,512,128]{2,1,0:T(8,128)(2,1)S(1)}, u32[]{:S(2)}) copy-start(bf16[4,512,128]{2,1,0:T(8,128)(2,1)S(1)} %collective-permute-done.refs_1_) | copy-start | bytes 1572868
  59.5 29.2 %collective-permute-start.2 = (bf16[8,512,128]{2,1,0:T(8,128)(2,1)}, bf16[8,512,128]{2,1,0:T(8,128)(2,1)}, u32[]{:S(2)}, u32[]{:S(2)}) collective-permute-start(bf16[8,512,128]{2,1,0:T(8,128)(2,1)} %get-tuple-element.384.refs_0_), channel_id=1, source_target_pairs={{8,16},{9,17},{10,18},{11,19},{12,20},{13,21},{14,22},{15,23},{16,... | collective-permute-start | bytes 3145736 | tf_op jit(solution)/shard_map/ppermute | solution.py:578
  71.3 13.9 %collective-permute-start.9 = (bf16[4,512,128]{2,1,0:T(8,128)(2,1)}, bf16[4,512,128]{2,1,0:T(8,128)(2,1)}, u32[]{:S(2)}, u32[]{:S(2)}) collective-permute-start(bf16[4,512,128]{2,1,0:T(8,128)(2,1)} %get-tuple-element.394.refs_0_), channel_id=1, source_target_pairs={{0,8},{1,9},{2,10},{3,11},{4,12},{5,13},{6,14},{7,15},{8,0},{9,1},... | collective-permute-start | bytes 1572872 | tf_op jit(solution)/shard_map/ppermute | solution.py:578
  85.2 28.1 %collective-permute-start.5 = (bf16[8,512,128]{2,1,0:T(8,128)(2,1)S(1)}, bf16[8,512,128]{2,1,0:T(8,128)(2,1)}, u32[]{:S(2)}, u32[]{:S(2)}) collective-permute-start(bf16[8,512,128]{2,1,0:T(8,128)(2,1)S(1)} %copy-done.5), channel_id=1, source_target_pairs={{8,16},{9,17},{10,18},{11,19},{12,20},{13,21},{14,22},{15,23},{16,... | collective-permute-start | bytes 3145736 | tf_op jit(solution)/shard_map/ppermute | solution.py:578
  88.7 44.9 %collective-permute-start.15 = (bf16[8,512,128]{2,1,0:T(8,128)(2,1)}, bf16[8,512,128]{2,1,0:T(8,128)(2,1)}, u32[]{:S(2)}, u32[]{:S(2)}) collective-permute-start(bf16[8,512,128]{2,1,0:T(8,128)(2,1)} %get-tuple-element.412.refs_0_), channel_id=1, source_target_pairs={{8,16},{9,17},{10,18},{11,19},{12,20},{13,21},{14,22},{15,23},{16,... | collective-permute-start | bytes 3145736 | tf_op jit(solution)/shard_map/ppermute | solution.py:578
  101.6 38.5 %collective-permute-start.4 = (bf16[8,512,128]{2,1,0:T(8,128)(2,1)}, bf16[8,512,128]{2,1,0:T(8,128)(2,1)}, u32[]{:S(2)}, u32[]{:S(2)}) collective-permute-start(bf16[8,512,128]{2,1,0:T(8,128)(2,1)} %get-tuple-element.391.refs_1_), channel_id=1, source_target_pairs={{8,0},{9,1},{10,2},{11,3},{12,4},{13,5},{14,6},{15,7},{16,24},{17,... | collective-permute-start | bytes 3145736 | tf_op jit(solution)/shard_map/ppermute | solution.py:578
  104.3 86.6 %collective-permute-start.12 = (bf16[2,256,2048]{2,1,0:T(8,128)(2,1)}, bf16[2,256,2048]{2,1,0:T(8,128)(2,1)}, u32[]{:S(2)}, u32[]{:S(2)}) collective-permute-start(bf16[2,256,2048]{2,1,0:T(8,128)(2,1)} %get-tuple-element.409.refs_4_), channel_id=1, source_target_pairs={{0,1},{1,0},{2,3},{3,2},{4,5},{5,4},{6,7},{7,6},{8,9},{9,8},{10,11... | collective-permute-start | bytes 6291464 | tf_op jit(solution)/shard_map/ppermute | solution.py:578
  106.5 84.5 %collective-permute-start.11 = (bf16[2,256,2048]{2,1,0:T(8,128)(2,1)}, bf16[2,256,2048]{2,1,0:T(8,128)(2,1)}, u32[]{:S(2)}, u32[]{:S(2)}) collective-permute-start(bf16[2,256,2048]{2,1,0:T(8,128)(2,1)} %get-tuple-element.409.refs_4_), channel_id=1, source_target_pairs={{0,2},{1,3},{2,0},{3,1},{4,6},{5,7},{6,4},{7,5},{8,10},{9,11},{10,... | collective-permute-start | bytes 6291464 | tf_op jit(solution)/shard_map/ppermute | solution.py:578
  113.3 26.8 %copy-start.7 = (bf16[8,512,128]{2,1,0:T(8,128)(2,1)S(1)}, bf16[8,512,128]{2,1,0:T(8,128)(2,1)}, u32[]{:S(2)}) copy-start(bf16[8,512,128]{2,1,0:T(8,128)(2,1)} %get-tuple-element.410.refs_0_) | copy-start | bytes 3145732
  113.3 77.7 %collective-permute-start.10 = (bf16[2,256,2048]{2,1,0:T(8,128)(2,1)}, bf16[2,256,2048]{2,1,0:T(8,128)(2,1)S(1)}, u32[]{:S(2)}, u32[]{:S(2)}) collective-permute-start(bf16[2,256,2048]{2,1,0:T(8,128)(2,1)} %get-tuple-element.407.refs_1_), channel_id=1, source_target_pairs={{0,2},{1,3},{2,0},{3,1},{4,6},{5,7},{6,4},{7,5},{8,10},{9,11},{10,... | collective-permute-start | bytes 6291464 | tf_op jit(solution)/shard_map/ppermute | solution.py:578
  133.5 22.4 %collective-permute-start.14 = (bf16[8,512,128]{2,1,0:T(8,128)(2,1)}, bf16[8,512,128]{2,1,0:T(8,128)(2,1)}, u32[]{:S(2)}, u32[]{:S(2)}) collective-permute-start(bf16[8,512,128]{2,1,0:T(8,128)(2,1)} %get-tuple-element.411.refs_1_), channel_id=1, source_target_pairs={{8,0},{9,1},{10,2},{11,3},{12,4},{13,5},{14,6},{15,7},{16,24},{17,... | collective-permute-start | bytes 3145736 | tf_op jit(solution)/shard_map/ppermute | solution.py:578
  135.8 18.8 %all-to-all-start.5 = ((bf16[4,1024,128]{2,1,0:T(8,128)(2,1)}), bf16[4,1024,128]{2,1,0:T(8,128)(2,1)}, u32[]{:S(2)}, u32[]{:S(2)}) async-start(bf16[4,1024,128]{2,1,0:T(8,128)(2,1)} %get-tuple-element.383), calls=%async_computation.5 | async-start | bytes 2097152 | tf_op jit(solution)/shard_map/all_to_all | solution.py:595
  140.1 50.7 %collective-permute-start.13 = (bf16[8,512,128]{2,1,0:T(8,128)(2,1)S(1)}, bf16[8,512,128]{2,1,0:T(8,128)(2,1)}, u32[]{:S(2)}, u32[]{:S(2)}) collective-permute-start(bf16[8,512,128]{2,1,0:T(8,128)(2,1)S(1)} %copy-done.7), channel_id=1, source_target_pairs={{8,16},{9,17},{10,18},{11,19},{12,20},{13,21},{14,22},{15,23},{16,... | collective-permute-start | bytes 3145736 | tf_op jit(solution)/shard_map/ppermute | solution.py:578
  155.9 36.4 %collective-permute-start.17 = (bf16[4,1024,128]{2,1,0:T(8,128)(2,1)}, bf16[4,1024,128]{2,1,0:T(8,128)(2,1)}, u32[]{:S(2)}, u32[]{:S(2)}) collective-permute-start(bf16[4,1024,128]{2,1,0:T(8,128)(2,1)} %get-tuple-element.426.refs_0_), channel_id=1, source_target_pairs={{0,8},{1,9},{2,10},{3,11},{4,12},{5,13},{6,14},{7,15},{8,0},{9,1},... | collective-permute-start | bytes 3145736 | tf_op jit(solution)/shard_map/ppermute | solution.py:578
  190.8 11.2 %collective-permute-start.16 = (bf16[2,256,2048]{2,1,0:T(8,128)(2,1)}, bf16[2,256,2048]{2,1,0:T(8,128)(2,1)}, u32[]{:S(2)}, u32[]{:S(2)}) collective-permute-start(bf16[2,256,2048]{2,1,0:T(8,128)(2,1)} %get-tuple-element.424.refs_5_), channel_id=1, source_target_pairs={{0,2},{1,3},{2,0},{3,1},{4,6},{5,7},{6,4},{7,5},{8,10},{9,11},{10,... | collective-permute-start | bytes 6291464 | tf_op jit(solution)/shard_map/ppermute | solution.py:578
  194.9 50.2 %collective-permute-start.20 = (bf16[8,1024,128]{2,1,0:T(8,128)(2,1)}, bf16[8,1024,128]{2,1,0:T(8,128)(2,1)S(1)}, u32[]{:S(2)}, u32[]{:S(2)}) collective-permute-start(bf16[8,1024,128]{2,1,0:T(8,128)(2,1)} %get-tuple-element.446.refs_0_), channel_id=1, source_target_pairs={{8,16},{9,17},{10,18},{11,19},{12,20},{13,21},{14,22},{15,23},{16,... | collective-permute-start | bytes 6291464 | tf_op jit(solution)/shard_map/ppermute | solution.py:578
  197.5 51.8 %collective-permute-start.19 = (bf16[8,512,128]{2,1,0:T(8,128)(2,1)}, bf16[8,512,128]{2,1,0:T(8,128)(2,1)}, u32[]{:S(2)}, u32[]{:S(2)}) collective-permute-start(bf16[8,512,128]{2,1,0:T(8,128)(2,1)} %get-tuple-element.445.refs_1_), channel_id=1, source_target_pairs={{8,0},{9,1},{10,2},{11,3},{12,4},{13,5},{14,6},{15,7},{16,24},{17,... | collective-permute-start | bytes 3145736 | tf_op jit(solution)/shard_map/ppermute | solution.py:578
  200.1 49.2 %collective-permute-start.18 = (bf16[8,512,128]{2,1,0:T(8,128)(2,1)}, bf16[8,512,128]{2,1,0:T(8,128)(2,1)S(1)}, u32[]{:S(2)}, u32[]{:S(2)}) collective-permute-start(bf16[8,512,128]{2,1,0:T(8,128)(2,1)} %get-tuple-element.444.refs_1_), channel_id=1, source_target_pairs={{8,0},{9,1},{10,2},{11,3},{12,4},{13,5},{14,6},{15,7},{16,24},{17,... | collective-permute-start | bytes 3145736 | tf_op jit(solution)/shard_map/ppermute | solution.py:578
  220.5 69.6 %collective-permute-start.24 = (bf16[12,512,128]{2,1,0:T(8,128)(2,1)}, bf16[12,512,128]{2,1,0:T(8,128)(2,1)}, u32[]{:S(2)}, u32[]{:S(2)}) collective-permute-start(bf16[12,512,128]{2,1,0:T(8,128)(2,1)} %get-tuple-element.488.refs_0_), channel_id=1, source_target_pairs={{0,8},{1,9},{2,10},{3,11},{4,12},{5,13},{6,14},{7,15},{24,16},{25,... | collective-permute-start | bytes 4718600 | tf_op jit(solution)/shard_map/ppermute | solution.py:578
  246.5 50.6 %collective-permute-start.23 = (bf16[8,1024,128]{2,1,0:T(8,128)(2,1)}, bf16[8,1024,128]{2,1,0:T(8,128)(2,1)}, u32[]{:S(2)}, u32[]{:S(2)}) collective-permute-start(bf16[8,1024,128]{2,1,0:T(8,128)(2,1)} %get-tuple-element.487.refs_1_), channel_id=1, source_target_pairs={{8,0},{9,1},{10,2},{11,3},{12,4},{13,5},{14,6},{15,7},{16,24},{17,... | collective-permute-start | bytes 6291464 | tf_op jit(solution)/shard_map/ppermute | solution.py:578
  250.2 46.9 %collective-permute-start.22 = (bf16[12,512,128]{2,1,0:T(8,128)(2,1)}, bf16[12,512,128]{2,1,0:T(8,128)(2,1)}, u32[]{:S(2)}, u32[]{:S(2)}) collective-permute-start(bf16[12,512,128]{2,1,0:T(8,128)(2,1)} %get-tuple-element.486.refs_0_), channel_id=1, source_target_pairs={{0,8},{1,9},{2,10},{3,11},{4,12},{5,13},{6,14},{7,15},{24,16},{25,... | collective-permute-start | bytes 4718600 | tf_op jit(solution)/shard_map/ppermute | solution.py:578
  292.8 43.5 %collective-permute-start.26 = (bf16[8,512,128]{2,1,0:T(8,128)(2,1)}, bf16[8,512,128]{2,1,0:T(8,128)(2,1)}, u32[]{:S(2)}, u32[]{:S(2)}) collective-permute-start(bf16[8,512,128]{2,1,0:T(8,128)(2,1)} %get-tuple-element.499), channel_id=1, source_target_pairs={{8,16},{9,17},{10,18},{11,19},{12,20},{13,21},{14,22},{15,23},{16,... | collective-permute-start | bytes 3145736 | tf_op jit(solution)/shard_map/ppermute | solution.py:578
  295.8 71.4 %collective-permute-start.21 = (bf16[12,1024,128]{2,1,0:T(8,128)(2,1)S(1)}, bf16[12,1024,128]{2,1,0:T(8,128)(2,1)}, u32[]{:S(2)}, u32[]{:S(2)}) collective-permute-start(bf16[12,1024,128]{2,1,0:T(8,128)(2,1)S(1)} %copy-done), channel_id=1, source_target_pairs={{0,8},{1,9},{2,10},{3,11},{4,12},{5,13},{6,14},{7,15},{24,16},{25,... | collective-permute-start | bytes 9437192 | tf_op jit(solution)/shard_map/ppermute | solution.py:578
  299.6 54.1 %collective-permute-start.25 = (bf16[8,512,128]{2,1,0:T(8,128)(2,1)}, bf16[8,512,128]{2,1,0:T(8,128)(2,1)}, u32[]{:S(2)}, u32[]{:S(2)}) collective-permute-start(bf16[8,512,128]{2,1,0:T(8,128)(2,1)} %get-tuple-element.498), channel_id=1, source_target_pairs={{8,16},{9,17},{10,18},{11,19},{12,20},{13,21},{14,22},{15,23},{16,... | collective-permute-start | bytes 3145736 | tf_op jit(solution)/shard_map/ppermute | solution.py:578
  351.4 46.0 %collective-permute-start.27 = (bf16[1024,2048]{1,0:T(8,128)(2,1)}, bf16[1024,2048]{1,0:T(8,128)(2,1)}, u32[]{:S(2)}, u32[]{:S(2)}) collective-permute-start(bf16[1024,2048]{1,0:T(8,128)(2,1)} %get-tuple-element.549), channel_id=1, source_target_pairs={{0,2},{1,3},{2,0},{3,1},{4,6},{5,7},{6,4},{7,5},{8,10},{9,11},{10,... | collective-permute-start | bytes 12582920 | tf_op jit(solution)/shard_map/ppermute | solution.py:578
  366.0 72.1 %collective-permute-start.29 = (bf16[1024,2048]{1,0:T(8,128)(2,1)}, bf16[1024,2048]{1,0:T(8,128)(2,1)}, u32[]{:S(2)}, u32[]{:S(2)}) collective-permute-start(bf16[1024,2048]{1,0:T(8,128)(2,1)} %get-tuple-element.565), channel_id=1, source_target_pairs={{0,2},{1,3},{2,0},{3,1},{4,6},{5,7},{6,4},{7,5},{8,10},{9,11},{10,... | collective-permute-start | bytes 12582920 | tf_op jit(solution)/shard_map/ppermute | solution.py:578
  370.6 58.5 %collective-permute-start.30 = (bf16[8,1024,128]{2,1,0:T(8,128)(2,1)}, bf16[8,1024,128]{2,1,0:T(8,128)(2,1)}, u32[]{:S(2)}, u32[]{:S(2)}) collective-permute-start(bf16[8,1024,128]{2,1,0:T(8,128)(2,1)} %get-tuple-element.566), channel_id=1, source_target_pairs={{8,16},{9,17},{10,18},{11,19},{12,20},{13,21},{14,22},{15,23},{16,... | collective-permute-start | bytes 6291464 | tf_op jit(solution)/shard_map/ppermute | solution.py:578
  373.8 37.3 %collective-permute-start.31 = (bf16[12,512,128]{2,1,0:T(8,128)(2,1)S(1)}, bf16[12,512,128]{2,1,0:T(8,128)(2,1)}, u32[]{:S(2)}, u32[]{:S(2)}) collective-permute-start(bf16[12,512,128]{2,1,0:T(8,128)(2,1)S(1)} %copy-done.4), channel_id=1, source_target_pairs={{0,8},{1,9},{2,10},{3,11},{4,12},{5,13},{6,14},{7,15},{24,16},{25,... | collective-permute-start | bytes 4718600 | tf_op jit(solution)/shard_map/ppermute | solution.py:578
  375.1 19.0 %collective-permute-start.28 = (bf16[4,512,128]{2,1,0:T(8,128)(2,1)S(1)}, bf16[4,512,128]{2,1,0:T(8,128)(2,1)S(1)}, u32[]{:S(2)}, u32[]{:S(2)}) collective-permute-start(bf16[4,512,128]{2,1,0:T(8,128)(2,1)S(1)} %copy-done.24), channel_id=1, source_target_pairs={{8,0},{9,1},{10,2},{11,3},{12,4},{13,5},{14,6},{15,7},{16,24},{17,... | collective-permute-start | bytes 1572872 | tf_op jit(solution)/shard_map/ppermute | solution.py:578
  402.0 45.0 %collective-permute-start.35 = (bf16[256,2048]{1,0:T(8,128)(2,1)}, bf16[256,2048]{1,0:T(8,128)(2,1)}, u32[]{:S(2)}, u32[]{:S(2)}) collective-permute-start(bf16[256,2048]{1,0:T(8,128)(2,1)} %get-tuple-element.601), channel_id=1, source_target_pairs={{0,4},{1,5},{2,6},{3,7},{4,0},{5,1},{6,2},{7,3},{8,12},{9,13},{10,... | collective-permute-start | bytes 3145736 | tf_op jit(solution)/shard_map/ppermute | solution.py:578
  403.1 45.9 %collective-permute-start.36 = (bf16[256,2048]{1,0:T(8,128)(2,1)}, bf16[256,2048]{1,0:T(8,128)(2,1)}, u32[]{:S(2)}, u32[]{:S(2)}) collective-permute-start(bf16[256,2048]{1,0:T(8,128)(2,1)} %get-tuple-element.602), channel_id=1, source_target_pairs={{0,1},{1,0},{2,3},{3,2},{4,5},{5,4},{6,7},{7,6},{8,9},{9,8},{10,11... | collective-permute-start | bytes 3145736 | tf_op jit(solution)/shard_map/ppermute | solution.py:578
  411.1 54.7 %collective-permute-start.38 = (bf16[12,512,128]{2,1,0:T(8,128)(2,1)S(1)}, bf16[12,512,128]{2,1,0:T(8,128)(2,1)S(1)}, u32[]{:S(2)}, u32[]{:S(2)}) collective-permute-start(bf16[12,512,128]{2,1,0:T(8,128)(2,1)S(1)} %copy-done.3), channel_id=1, source_target_pairs={{0,8},{1,9},{2,10},{3,11},{4,12},{5,13},{6,14},{7,15},{24,16},{25,... | collective-permute-start | bytes 4718600 | tf_op jit(solution)/shard_map/ppermute | solution.py:578
  412.4 19.6 %all-to-all-start.6 = ((bf16[4,512,128]{2,1,0:T(8,128)(2,1)}), bf16[4,512,128]{2,1,0:T(8,128)(2,1)}, u32[]{:S(2)}, u32[]{:S(2)}) async-start(bf16[4,512,128]{2,1,0:T(8,128)(2,1)} %get-tuple-element.567), calls=%async_computation.6 | async-start | bytes 1048576 | tf_op jit(solution)/shard_map/all_to_all | solution.py:595
  429.1 31.6 %collective-permute-start.39 = (bf16[8,512,128]{2,1,0:T(8,128)(2,1)}, bf16[8,512,128]{2,1,0:T(8,128)(2,1)}, u32[]{:S(2)}, u32[]{:S(2)}) collective-permute-start(bf16[8,512,128]{2,1,0:T(8,128)(2,1)} %get-tuple-element.614), channel_id=1, source_target_pairs={{8,16},{9,17},{10,18},{11,19},{12,20},{13,21},{14,22},{15,23},{16,... | collective-permute-start | bytes 3145736 | tf_op jit(solution)/shard_map/ppermute | solution.py:578
  438.1 35.9 %collective-permute-start.37 = (bf16[4,1024,128]{2,1,0:T(8,128)(2,1)}, bf16[4,1024,128]{2,1,0:T(8,128)(2,1)}, u32[]{:S(2)}, u32[]{:S(2)}) collective-permute-start(bf16[4,1024,128]{2,1,0:T(8,128)(2,1)} %get-tuple-element.612), channel_id=1, source_target_pairs={{8,0},{9,1},{10,2},{11,3},{12,4},{13,5},{14,6},{15,7},{16,24},{17,... | collective-permute-start | bytes 3145736 | tf_op jit(solution)/shard_map/ppermute | solution.py:578
  447.0 37.5 %collective-permute-start.32 = (bf16[256,2048]{1,0:T(8,128)(2,1)}, bf16[256,2048]{1,0:T(8,128)(2,1)}, u32[]{:S(2)}, u32[]{:S(2)}) collective-permute-start(bf16[256,2048]{1,0:T(8,128)(2,1)} %get-tuple-element.588), channel_id=1, source_target_pairs={{0,4},{1,5},{2,6},{3,7},{4,0},{5,1},{6,2},{7,3},{8,12},{9,13},{10,... | collective-permute-start | bytes 3145736 | tf_op jit(solution)/shard_map/ppermute | solution.py:578
  449.0 35.5 %collective-permute-start.33 = (bf16[256,2048]{1,0:T(8,128)(2,1)}, bf16[256,2048]{1,0:T(8,128)(2,1)}, u32[]{:S(2)}, u32[]{:S(2)}) collective-permute-start(bf16[256,2048]{1,0:T(8,128)(2,1)} %get-tuple-element.589), channel_id=1, source_target_pairs={{0,1},{1,0},{2,3},{3,2},{4,5},{5,4},{6,7},{7,6},{8,9},{9,8},{10,11... | collective-permute-start | bytes 3145736 | tf_op jit(solution)/shard_map/ppermute | solution.py:578
  458.1 19.6 %all-to-all-start.7 = ((f32[32,1,896]{2,1,0:T(1,128)}), f32[32,1,896]{2,1,0:T(1,128)S(1)}, u32[]{:S(2)}, u32[]{:S(2)}) async-start(f32[32,1,896]{2,1,0:T(1,128)} %copy.313), calls=%async_computation.7 | async-start | bytes 229376 | tf_op jit(solution)/shard_map/all_to_all | solution.py:598
  460.7 21.2 %collective-permute-start.34 = (bf16[4,512,128]{2,1,0:T(8,128)(2,1)}, bf16[4,512,128]{2,1,0:T(8,128)(2,1)}, u32[]{:S(2)}, u32[]{:S(2)}) collective-permute-start(bf16[4,512,128]{2,1,0:T(8,128)(2,1)} %get-tuple-element.591), channel_id=1, source_target_pairs={{8,0},{9,1},{10,2},{11,3},{12,4},{13,5},{14,6},{15,7},{16,24},{17,... | collective-permute-start | bytes 1572872 | tf_op jit(solution)/shard_map/ppermute | solution.py:578
  469.4 42.9 %collective-permute-start.45 = (bf16[8,512,128]{2,1,0:T(8,128)(2,1)}, bf16[8,512,128]{2,1,0:T(8,128)(2,1)S(1)}, u32[]{:S(2)}, u32[]{:S(2)}) collective-permute-start(bf16[8,512,128]{2,1,0:T(8,128)(2,1)} %get-tuple-element.653), channel_id=1, source_target_pairs={{8,16},{9,17},{10,18},{11,19},{12,20},{13,21},{14,22},{15,23},{16,... | collective-permute-start | bytes 3145736 | tf_op jit(solution)/shard_map/ppermute | solution.py:578
  477.7 18.4 %all-to-all-start.8 = ((bf16[4,1024,128]{2,1,0:T(8,128)(2,1)}), bf16[4,1024,128]{2,1,0:T(8,128)(2,1)S(1)}, u32[]{:S(2)}, u32[]{:S(2)}) async-start(bf16[4,1024,128]{2,1,0:T(8,128)(2,1)} %get-tuple-element.638), calls=%async_computation.8 | async-start | bytes 2097152 | tf_op jit(solution)/shard_map/all_to_all | solution.py:595
  488.9 16.1 %collective-permute-start.40 = (bf16[256,1024]{1,0:T(8,128)(2,1)}, bf16[256,1024]{1,0:T(8,128)(2,1)}, u32[]{:S(2)}, u32[]{:S(2)}) collective-permute-start(bf16[256,1024]{1,0:T(8,128)(2,1)} %get-tuple-element.636), channel_id=1, source_target_pairs={{0,1},{1,0},{2,3},{3,2},{4,5},{5,4},{6,7},{7,6},{8,9},{9,8},{10,11... | collective-permute-start | bytes 1572872 | tf_op jit(solution)/shard_map/ppermute | solution.py:578
  490.4 17.1 %collective-permute-start.41 = (bf16[256,1024]{1,0:T(8,128)(2,1)}, bf16[256,1024]{1,0:T(8,128)(2,1)}, u32[]{:S(2)}, u32[]{:S(2)}) collective-permute-start(bf16[256,1024]{1,0:T(8,128)(2,1)} %get-tuple-element.637), channel_id=1, source_target_pairs={{0,4},{1,5},{2,6},{3,7},{4,0},{5,1},{6,2},{7,3},{8,12},{9,13},{10,... | collective-permute-start | bytes 1572872 | tf_op jit(solution)/shard_map/ppermute | solution.py:578
  492.4 24.4 %collective-permute-start.44 = (bf16[4,512,128]{2,1,0:T(8,128)(2,1)}, bf16[4,512,128]{2,1,0:T(8,128)(2,1)}, u32[]{:S(2)}, u32[]{:S(2)}) collective-permute-start(bf16[4,512,128]{2,1,0:T(8,128)(2,1)} %get-tuple-element.652), channel_id=1, source_target_pairs={{8,0},{9,1},{10,2},{11,3},{12,4},{13,5},{14,6},{15,7},{16,24},{17,... | collective-permute-start | bytes 1572872 | tf_op jit(solution)/shard_map/ppermute | solution.py:578
  496.1 23.2 %all-to-all-start.10 = ((bf16[4,512,128]{2,1,0:T(8,128)(2,1)}), bf16[4,512,128]{2,1,0:T(8,128)(2,1)S(1)}, u32[]{:S(2)}, u32[]{:S(2)}) async-start(bf16[4,512,128]{2,1,0:T(8,128)(2,1)} %get-tuple-element.672), calls=%async_computation.10 | async-start | bytes 1048576 | tf_op jit(solution)/shard_map/all_to_all | solution.py:595
  499.6 23.2 %collective-permute-start.42 = (bf16[256,1024]{1,0:T(8,128)(2,1)}, bf16[256,1024]{1,0:T(8,128)(2,1)S(1)}, u32[]{:S(2)}, u32[]{:S(2)}) collective-permute-start(bf16[256,1024]{1,0:T(8,128)(2,1)} %get-tuple-element.649), channel_id=1, source_target_pairs={{0,1},{1,0},{2,3},{3,2},{4,5},{5,4},{6,7},{7,6},{8,9},{9,8},{10,11... | collective-permute-start | bytes 1572872 | tf_op jit(solution)/shard_map/ppermute | solution.py:578
  504.9 18.8 %collective-permute-start.43 = (bf16[256,1024]{1,0:T(8,128)(2,1)S(1)}, bf16[256,1024]{1,0:T(8,128)(2,1)S(1)}, u32[]{:S(2)}, u32[]{:S(2)}) collective-permute-start(bf16[256,1024]{1,0:T(8,128)(2,1)S(1)} %copy-done.29), channel_id=1, source_target_pairs={{0,4},{1,5},{2,6},{3,7},{4,0},{5,1},{6,2},{7,3},{8,12},{9,13},{10,... | collective-permute-start | bytes 1572872 | tf_op jit(solution)/shard_map/ppermute | solution.py:578
  515.4 18.0 %collective-permute-start.46 = (bf16[4,512,128]{2,1,0:T(8,128)(2,1)}, bf16[4,512,128]{2,1,0:T(8,128)(2,1)S(1)}, u32[]{:S(2)}, u32[]{:S(2)}) collective-permute-start(bf16[4,512,128]{2,1,0:T(8,128)(2,1)} %get-tuple-element.671), channel_id=1, source_target_pairs={{8,0},{9,1},{10,2},{11,3},{12,4},{13,5},{14,6},{15,7},{16,24},{17,... | collective-permute-start | bytes 1572872 | tf_op jit(solution)/shard_map/ppermute | solution.py:578
  519.3 17.6 %all-to-all-start.9 = ((bf16[4,512,128]{2,1,0:T(8,128)(2,1)}), bf16[4,512,128]{2,1,0:T(8,128)(2,1)S(1)}, u32[]{:S(2)}, u32[]{:S(2)}) async-start(bf16[4,512,128]{2,1,0:T(8,128)(2,1)} %get-tuple-element.669), calls=%async_computation.9 | async-start | bytes 1048576 | tf_op jit(solution)/shard_map/all_to_all | solution.py:595
  536.9 12.3 %all-to-all-start.11 = ((bf16[4,512,128]{2,1,0:T(8,128)(2,1)}), bf16[4,512,128]{2,1,0:T(8,128)(2,1)S(1)}, u32[]{:S(2)}, u32[]{:S(2)}) async-start(bf16[4,512,128]{2,1,0:T(8,128)(2,1)} %get-tuple-element.688), calls=%async_computation.11 | async-start | bytes 1048576 | tf_op jit(solution)/shard_map/all_to_all | solution.py:595
  (35 other events, 229.8 us)

commit v3 on v2

--- a/solution.py
+++ b/solution.py
@@ -20,16 +20,15 @@
 NT = ((1,), (1,))
 NN = ((1,), (0,))
 TN = ((0,), (0,))
-VMEM_LIMIT = 56 * 2**20
+VMEM = 63 * 2**20
 STEPS = 4
 
 
 ORDER = (
-    "p1", "p0", "g1", "p2", "g0", "p3", "g2", "own", "g3", "h1", "h0", "sm", "p4", "h2", "i1", "h3", "xt", "c",
-    "i0", "j1", "g4", "vec", "i2", "j0", "i3", "b", "tc", "h4", "bc", "K0", "r0", "K1", "i4", "j3", "j2", "r1",
-    "KA", "r2", "u0", "j4", "u1", "K4", "r3", "r4", "v0", "JB", "v1", "JO", "u2", "kB", "w0", "CB", "kO", "u3",
-    "z0", "v2", "CO", "DB", "tail", "v3", "u4", "w2", "tz", "w1", "DO", "z2", "EO", "v4", "w3", "EB", "z1", "w4",
-    "z3", "z4",
+    "p0", "p2", "g0", "g2", "own", "h0", "h1", "sm", "i0", "c", "h2", "h3", "sw", "xt", "i1", "vec", "j0", "p4",
+    "b", "j1", "i2", "g4", "bc", "tc", "K0", "r0", "i3", "h4", "K1", "i4", "j2", "j3", "r1", "KA", "r2", "u0", "j4",
+    "u1", "K4", "r3", "r4", "v0", "JB", "v1", "JO", "u2", "kB", "w0", "CB", "kO", "u3", "z0", "v2", "CO", "DB",
+    "tail", "v3", "u4", "w2", "tz", "w1", "DO", "z2", "EO", "v4", "w3", "EB", "z1", "w4", "z3", "z4",
 )
 
 NOTHING = pl.CostEstimate(flops=0, bytes_accessed=0, transcendentals=0)
@@ -52,19 +51,38 @@
     return pl.BlockSpec(shape, lambda *_: (0,) * len(shape), pipeline_mode=pl.Buffered(1))
 
 
-def run_kernel(kernel, outs, in_specs, out_specs, args, name, grid=(), scratch=(), aliases=None, vmem=None):
-    return pl.pallas_call(
-        kernel,
+def run_kernel(
+    kernel, outs, in_specs, out_specs, args, name, grid=(), scratch=(), aliases=None, line=None
+):
+    one = not isinstance(outs, (list, tuple))
+    outs, out_specs = ([outs], [out_specs]) if one else (list(outs), list(out_specs))
+    in_specs, args, aliases, inner = list(in_specs), list(args), dict(aliases or {}), kernel
+    if line is not None:
+        n, m = len(args), len(outs)
+        aliases[n] = m
+        in_specs.append(ANYWHERE)
+        out_specs.append(ANYWHERE)
+        args.append(line.mark)
+        outs.append(shaped(line.mark.shape, line.mark.dtype))
+
+        def inner(*refs):
+            kernel(*refs[:n], *refs[n + 1 : n + 1 + m], *refs[n + 2 + m :])
+
+    got = pl.pallas_call(
+        inner,
         grid=grid,
         out_shape=outs,
         in_specs=in_specs,
         out_specs=out_specs,
         scratch_shapes=scratch,
-        input_output_aliases=aliases or {},
-        compiler_params=pltpu.CompilerParams(vmem_limit_bytes=vmem),
+        input_output_aliases=aliases,
+        compiler_params=pltpu.CompilerParams(vmem_limit_bytes=VMEM),
         cost_estimate=NOTHING,
         name=name,
     )(*args)
+    if line is not None:
+        *got, line.mark = got
+    return got[0] if one else got
 
 
 def gate_kernel(*refs):
@@ -107,8 +125,8 @@
             to[at : at + hi - lo, lanes] = (rows * gain_ref[:, lanes] if gained else rows).astype(BF)
 
 
-def give_grads(acc1, acc2, col, gain_ref, shift_ref, w1, to1, to2, norm_ref):
-    for b in range(16):
+def give_grads(blocks, acc1, acc2, col, gain_ref, shift_ref, w1, to1, to2, norm_ref):
+    for b in blocks:
         lanes = slice(b * LANES, (b + 1) * LANES)
         gain = gain_ref[:, lanes]
         m = acc1[:, lanes]
@@ -120,16 +138,38 @@
         norm_ref[1:2, lanes] = jnp.sum(w * col[...], axis=0, keepdims=True) / gain
 
 
+def add_grads(step, grad, unit, act, cot, acc1, acc2, col, sum_ref, finish):
+    col[...] += dot(grad, jnp.ones((grad.shape[0], LANES), BF), TN)
+    sum_ref[...] += jnp.sum(grad.astype(F32), axis=0, keepdims=True)
+    last = pl.num_programs(0) - 1
+
+    @pl.when(step < last)
+    def _():
+        acc1[...] += dot(grad, unit, TN)
+        acc2[...] += dot(act, cot, TN)
+
+    @pl.when(step == last)
+    def _():
+        width = unit.shape[1] // 4
+        for part in range(4):
+            lanes = slice(part * width, (part + 1) * width)
+            acc1[:, lanes] += dot(grad, unit[:, lanes], TN)
+            acc2[:, lanes] += dot(act, cot[:, lanes], TN)
+            finish(range(4 * part, 4 * part + 4))
+
+
 def stream(step, pieces, unit_buf, cot_buf, sems):
+    blocks = [(p.at[0], p.at[1]) for p in pieces[:6]] + [(pieces[6], pieces[7]), (pieces[8], pieces[9])]
+    blocks = [blocks[k] for k in (0, 1, 2, 3, 4, 6, 5, 7)]
     rows = pieces[0].shape[1]
-    steps = len(pieces) // 2
+    steps = len(blocks) // 2
 
     def copies(s):
         made = []
         for k in (2 * s, 2 * s + 1):
             for n, buffer in enumerate((unit_buf, cot_buf)):
                 to = buffer.at[s % 2, pl.ds((k % 2) * rows, rows)]
-                made.append(pltpu.make_async_copy(pieces[k].at[n], to, sems.at[s % 2, len(made)]))
+                made.append(pltpu.make_async_copy(blocks[k][n], to, sems.at[s % 2, len(made)]))
         return made
 
     def begin(s):
@@ -152,8 +192,8 @@
     return [pltpu.VMEM((2, rows, width), BF), pltpu.VMEM((2, rows, width), BF), pltpu.SemaphoreType.DMA((2, 4))]
 
 
-def feed_kernel(cols, split, *refs):
-    pieces, parts, refs = refs[:8], refs[8:11], refs[11:]
+def feed_kernel(cols, split, sets, *refs):
+    pieces, parts, refs = refs[:10], refs[10 : 10 + 3 * sets], refs[10 + 3 * sets :]
     gain_ref, shift_ref, ratio_ref, bias_ref = refs[:4]
     hidden_ref, pre_grad_ref, w1, w2, norm_ref, sum_ref = refs[4:10]
     grads, refs = refs[10 : 10 + 2 * split], refs[10 + 2 * split :]
@@ -164,7 +204,9 @@
     @pl.when(step == 0)
     def _():
         begin(0)
-        take_weights(parts, gain_ref, ((0, cols, w1, 0, True), (cols, 2 * cols, w2, 0, False)))
+        n = cols // sets
+        for k in range(sets):
+            take_weights(parts[3 * k : 3 * k + 3], gain_ref, ((0, n, w1, k * n, True), (n, 2 * n, w2, k * n, False)))
         row[...] = jnp.sum(dot(ratio_ref[...], w1[...], NT), axis=0, keepdims=True) + bias_ref[...]
         acc1[...] = jnp.zeros_like(acc1)
         acc2[...] = jnp.zeros_like(acc2)
@@ -183,19 +225,13 @@
     pre_grad = (back * slope).astype(BF)
     hidden_ref[...] = hidden
     pre_grad_ref[...] = pre_grad
-    acc1[...] += dot(pre_grad, unit, TN)
-    acc2[...] += dot(hidden, cot, TN)
-    col[...] += dot(pre_grad, jnp.ones((pre_grad.shape[0], LANES), BF), TN)
-    sum_ref[...] += jnp.sum(pre_grad.astype(F32), axis=0, keepdims=True)
-
-    @pl.when(step == pl.num_programs(0) - 1)
-    def _():
-        to1 = (*grads[:2], 0)
-        to2 = (*grads[2:], 0) if split == 2 else (*grads[:2], cols)
-        give_grads(acc1, acc2, col, gain_ref, shift_ref, w1, to1, to2, norm_ref)
-
-
-def chunk_call(kernel, name, pieces, extra_in, extra_specs, sets, vectors, cols, others, split):
+    to1 = (*grads[:2], 0)
+    to2 = (*grads[2:], 0) if split == 2 else (*grads[:2], cols)
+    finish = lambda blocks: give_grads(blocks, acc1, acc2, col, gain_ref, shift_ref, w1, to1, to2, norm_ref)
+    add_grads(step, pre_grad, unit, hidden, cot, acc1, acc2, col, sum_ref, finish)
+
+
+def chunk_call(line, kernel, name, pieces, extra_in, extra_specs, sets, vectors, cols, others, split):
     _, part, width = pieces[0].shape
     block, rows = 2 * part, 8 * part
     per_row = lambda n: pl.BlockSpec((block, n), lambda r: (r, 0))
@@ -210,19 +246,19 @@
     weights = [w for s in sets for w in s]
     return run_kernel(
         kernel, shapes,
-        [ANYWHERE] * 8 + [whole(w.shape) for w in weights] + [whole(v.shape) for v in vectors] + extra_specs,
+        [ANYWHERE] * 10 + [whole(w.shape) for w in weights] + [whole(v.shape) for v in vectors] + extra_specs,
         specs, (*pieces, *weights, *vectors, *extra_in), name, grid=(rows // block,),
         scratch=[
             pltpu.VMEM((cols, width), F32), pltpu.VMEM((others, width), F32), pltpu.VMEM((cols, LANES), F32),
             pltpu.VMEM((1, cols), F32),
         ]
         + stream_scratch(block, width),
-        vmem=VMEM_LIMIT,
+        line=line,
     )
 
 
 def attention_kernel(cols, *refs):
-    pieces, refs = refs[:8], refs[8:]
+    pieces, refs = refs[:10], refs[10:]
     set_one, set_two, refs = refs[:3], refs[3:6], refs[6:]
     gain_ref, shift_ref, ratio_ref, bias_ref, lengths, place, cos_ref, sin_up_ref, sin_down_ref = refs[:9]
     mixed_ref, qkv_grad_ref, w1, w2, norm_ref, sum_ref, own_ref, rest_ref = refs[9:17]
@@ -292,14 +328,9 @@
     qkv_grad = jnp.concatenate([query_grad, key_grad, value_grad], axis=1).astype(BF)
     mixed_ref[...] = mixed
     qkv_grad_ref[...] = qkv_grad
-    acc1[...] += dot(qkv_grad, unit, TN)
-    acc2[...] += dot(mixed, cot, TN)
-    col[...] += dot(qkv_grad, jnp.ones((count, LANES), BF), TN)
-    sum_ref[...] += jnp.sum(qkv_grad.astype(F32), axis=0, keepdims=True)
-
-    @pl.when(group == pl.num_programs(0) - 1)
-    def _():
-        give_grads(acc1, acc2, col, gain_ref, shift_ref, w1, (own_ref, rest_ref, 0), (own_ref, rest_ref, cols), norm_ref)
+    to1, to2 = (own_ref, rest_ref, 0), (own_ref, rest_ref, cols)
+    finish = lambda blocks: give_grads(blocks, acc1, acc2, col, gain_ref, shift_ref, w1, to1, to2, norm_ref)
+    add_grads(group, qkv_grad, unit, mixed, cot, acc1, acc2, col, sum_ref, finish)
 
 
 def join_kernel(n, *refs):
@@ -309,20 +340,20 @@
     refs[2 * n][...] = total.astype(BF)
 
 
-def join_call(acts, weights, sent):
+def join_call(line, acts, weights, sent):
     rows, width = acts[0].shape[0], weights[0].shape[1]
-    block = rows // 8
-    first = 2 if sent else 0
+    block = rows // 4
+    first = 1 if sent else 0
     return run_kernel(
         functools.partial(join_kernel, len(acts)),
         shaped((rows // 2, width)),
-        [pl.BlockSpec((block, a.shape[1]), lambda r: (4 * (r // 2) + r % 2 + first, 0)) for a in acts]
+        [pl.BlockSpec((block, a.shape[1]), lambda r: (2 * r + first, 0)) for a in acts]
         + [whole(w.shape) for w in weights],
         pl.BlockSpec((block, width), lambda r: (r, 0)),
         (*acts, *weights),
         "join",
-        grid=(4,),
-        vmem=VMEM_LIMIT,
+        grid=(2,),
+        line=line,
     )
 
 
@@ -343,13 +374,13 @@
     sum_ref[...] += jnp.sum(cot_ref[...].astype(F32), axis=0, keepdims=True)
 
 
-def own_call(place, x, cot):
+def own_call(line, place, x, cot):
     rows, width = x.shape
     spec = pl.BlockSpec((rows // STEPS, width), lambda r: (r, 0))
     return run_kernel(
         own_kernel, [shaped((2, rows, width)), shaped((1, width), F32)], [SCALARS, spec, spec],
         [pl.BlockSpec((2, rows // STEPS, width), lambda r: (0, r, 0)), pl.BlockSpec((1, width), lambda r: (0, 0))],
-        (place, x, cot), "own", grid=(STEPS,),
+        (place, x, cot), "own", grid=(STEPS,), line=line,
     )
 
 
@@ -370,30 +401,46 @@
         at += n
 
 
-def piece_call(arrays, parts, strip):
+def piece_call(line, arrays, parts, strip):
     n = sum(p[1] for p in parts)
     return run_kernel(
         functools.partial(piece_kernel, parts), shaped((INNER, n, strip)), part_specs(parts, strip),
         pl.BlockSpec((1, n, strip), lambda k: (k, 0, 0)), arrays, "piece", grid=(INNER,),
+        line=line,
     )
 
 
 def unpiece_kernel(parts, *refs):
-    v_ref, outs, at = refs[0], refs[-len(parts) :], 0
-    for (cross, n, *_), ref in zip(parts, outs):
-        v = v_ref[0, at : at + n].astype(F32)
-        ref[...] = v.T if cross else v
-        at += n
-
-
-def unpiece_call(v, shapes, parts, held):
-    _, n, strip = v.shape
+    count = len(parts)
+    v_ref, refs = refs[0], refs[-2 * count - 3 :]
+    outs, helds, buffer, sems, into = refs[:count], refs[count : 2 * count], refs[-3], refs[-2], refs[-1]
+    copies = []
+    loads = [pltpu.make_async_copy(v_ref.at[k], buffer.at[k], into.at[k]) for k in range(INNER)]
+    for load in loads:
+        load.start()
+    for k in range(INNER):
+        at = 0
+        loads[k].wait()
+        for c, ((cross, n, first, every), out, held) in enumerate(zip(parts, outs, helds)):
+            v = buffer[k, at : at + n].astype(F32)
+            held[k] = v.T if cross else v
+            where = pl.ds((k * every + first) * n, n)
+            copies.append(pltpu.make_async_copy(held.at[k], out.at[:, where] if cross else out.at[where], sems.at[c, k]))
+            copies[-1].start()
+            at += n
+    for c in copies:
+        c.wait()
+
+
+def unpiece_call(line, v, shapes, parts, held):
+    strip = v.shape[2]
     held = [h for h in held if h is not None]
     return run_kernel(
         functools.partial(unpiece_kernel, parts), [shaped(s, F32) for s in shapes],
-        [pl.BlockSpec((1, n, strip), lambda k: (k, 0, 0))] + [ANYWHERE] * len(held),
-        part_specs(parts, strip), (v, *held), "unpiece", grid=(INNER,),
-        aliases={1 + k: k for k in range(len(held))},
+        [ANYWHERE] * (1 + len(held)), [ANYWHERE] * len(shapes), (v, *held), "unpiece",
+        scratch=[pltpu.VMEM((INNER, strip, n) if cross else (INNER, n, strip), F32) for cross, n, _, _ in parts]
+        + [pltpu.VMEM(v.shape, BF), pltpu.SemaphoreType.DMA((len(parts), INNER)), pltpu.SemaphoreType.DMA((INNER,))],
+        aliases={1 + k: k for k in range(len(held))}, line=line,
     )
 
 
@@ -402,14 +449,15 @@
     out[1] = b[...]
 
 
-def cat_call(a, b):
+def cat_call(line, a, b, cols, at):
     n = a.shape[0] // 2
-    spec = pl.BlockSpec((n,) + a.shape[1:], lambda k: (k, 0, 0))
+    shape = a.shape[:1] + (cols,) + a.shape[2:]
+    spec = pl.BlockSpec((n,) + shape[1:], lambda k: (k, at, 0))
     out = run_kernel(
-        cat_kernel, shaped((2,) + a.shape), [spec, spec],
-        pl.BlockSpec((2, n) + a.shape[1:], lambda k: (0, k, 0, 0)), (a, b), "cat", grid=(2,),
+        cat_kernel, shaped((2,) + shape), [spec, spec],
+        pl.BlockSpec((2, n) + shape[1:], lambda k: (0, k, 0, 0)), (a, b), "cat", grid=(2,), line=line,
     )
-    return out.reshape((8,) + a.shape[1:])
+    return out.reshape((8,) + shape[1:])
 
 
 def vectors_kernel(piece, nq, nf, share, tensor, place, small, g1, s1, g2, s2, r1, r2, out_bias, bq, bf, lengths):
@@ -466,17 +514,13 @@
     refs[-1][...] = total.astype(BF)
 
 
-def sum_call(parts, firsts, count):
-    shape = (4,) + parts[0].shape[1:]
+def sum_call(line, parts, firsts, count):
+    n = count // 2
+    shape = (n,) + parts[0].shape[1:]
     return run_kernel(
-        sum_kernel,
-        shaped((count,) + shape[1:]),
-        [pl.BlockSpec(shape, functools.partial(lambda f, k: (k + f, 0, 0), f // 4)) for f in firsts],
-        pl.BlockSpec(shape, lambda k: (k, 0, 0)),
-        parts,
-        "sum",
-        grid=(count // 4,),
-        vmem=VMEM_LIMIT,
+        sum_kernel, shaped((count,) + shape[1:]),
+        [pl.BlockSpec(shape, functools.partial(lambda f, k: (k + f, 0, 0), f // n)) for f in firsts],
+        pl.BlockSpec(shape, lambda k: (k, 0, 0)), parts, "sum", grid=(2,), line=line,
     )
 
 
@@ -524,7 +568,7 @@
     out_ref[...] = (cot_ref[...].astype(F32) + rstd * (pulled - level - unit * along)).astype(BF)
 
 
-def own_rows_call(kernel, place, rows_in, row_in, sums, name):
+def own_rows_call(line, kernel, place, rows_in, row_in, sums, name):
     rows, width = rows_in[0].shape
     block = rows // STEPS
     spec = pl.BlockSpec((block, width), lambda r: (r, 0))
@@ -534,6 +578,7 @@
         kernel, shaped((rows, width)),
         [SCALARS] + [spec] * len(rows_in) + [vector] * len(row_in) + [spec] * 4 + [half] * 2,
         spec, (place, *rows_in, *row_in, *sums), name, grid=(STEPS,), scratch=[pltpu.VMEM((block, width), F32)],
+        line=line,
     )
 
 
@@ -575,7 +620,7 @@
     short = outer == 4
 
     def permute(v, pairs):
-        return lax.ppermute(v, AXES, pairs)
+        return lax.ppermute(v.reshape(-1, v.shape[-1]), AXES, pairs).reshape(v.shape)
 
     def flip(v, k):
         return permute(v, [(l, l ^ k) for l in range(total)])
@@ -597,22 +642,21 @@
     def swap_all(v):
         return lax.all_to_all(v, AXES, split_axis=0, concat_axis=0, tiled=True)
 
+    class Near:
+        def __init__(self, v):
+            self.own = v
+            self.near = flip(v, face) if short else None
+
     class Gather:
-        def __init__(self, v):
+        def __init__(self, line, v, cols, at):
             if not short:
-                every = lax.all_gather(v, AXES, axis=0, tiled=True, axis_index_groups=column_groups)
-                n = v.shape[1]
-                every = every.transpose(1, 0, 2).reshape(n, 16, LANES).transpose(1, 0, 2)
+                own = v.own[:, at * cols : (at + 1) * cols]
+                every = lax.all_gather(own, AXES, axis=0, tiled=True, axis_index_groups=column_groups)
+                every = every.transpose(1, 0, 2).reshape(cols, 16, LANES).transpose(1, 0, 2)
                 self.parts = [every[:8], every[8:], jnp.zeros_like(every[8:])]
                 return
-            self.own = v
-            self.near = flip(v, face)
-
-        def near_came(self, line):
-            if short:
-                self.own, near = line(self.own, self.near)
-                self.both = line(cat_call(self.own, near))
-                self.far = hop(self.both, across_middle)
+            self.both = cat_call(line, v.own, v.near, cols, at)
+            self.far = hop(self.both, across_middle)
 
         def far_came(self, line):
             if short:
@@ -621,7 +665,8 @@
 
         def passed_came(self, line):
             if short:
-                self.parts = list(line(self.both, self.far, self.passed))
+                self.passed = line(self.passed)
+                self.parts = [self.both, self.far, self.passed]
 
     class Reduce:
         def __init__(self, line, own, rest):
@@ -632,26 +677,22 @@
                     v, AXES, scatter_dimension=0, tiled=True, axis_index_groups=column_groups
                 )
                 return
-            self.own, self.rest = line(own, rest)
+            self.own, self.rest = own, line(rest)
             self.first = hop(self.rest, towards_middle)
 
         def first_came(self, line):
             if short:
-                self.rest, self.first = line(self.rest, self.first)
-                far = line(sum_call((self.rest, self.first), (4, 4), 8))
+                far = sum_call(line, (self.rest, self.first), (4, 4), 8)
                 self.second = hop(far, across_middle)
 
         def second_came(self, line):
             if short:
-                self.rest, self.second = line(self.rest, self.second)
-                near = line(sum_call((self.rest, self.second), (0, 4), 4))
+                near = sum_call(line, (self.rest, self.second), (0, 4), 4)
                 self.third = hop(near, towards_ends)
 
         def third_came(self, line):
             if short:
-                self.third = line(self.third)
-                self.total = sum_call((self.own, self.first, self.second, self.third), (0, 0, 0, 0), 4)
-            self.total = line(self.total)
+                self.total = sum_call(line, (self.own, self.first, self.second, self.third), (0, 0, 0, 0), 4)
             self.final = swap_ring(self.total)
 
     class FaceReduce:
@@ -659,14 +700,12 @@
             self.other = flip(sent, 2)
 
         def core_came(self, line):
-            self.kept, self.other = line(self.kept, self.other)
             self.rows, self.width = self.kept.shape[0] // 4, self.kept.shape[1]
             spec = pl.BlockSpec((self.rows // STEPS, self.width), lambda r: (r, 0))
             x1, t1 = run_kernel(
                 core_kernel, [shaped((self.rows, self.width))] * 2, self.block_specs(1, 2, 3) * 2, [spec] * 2,
-                (self.kept,) * 3 + (self.other,) * 3, "core", grid=(STEPS,),
+                (self.kept,) * 3 + (self.other,) * 3, "core", grid=(STEPS,), line=line,
             )
-            x1, t1 = line(x1, t1)
             self.x1, self.t1 = flip(x1, 4), flip(t1, 1)
 
         def block_specs(self, *blocks):
@@ -676,19 +715,16 @@
             ]
 
         def first_came(self, line):
-            self.x1, self.t1 = line(self.x1, self.t1)
             rows, width = self.rows, self.width
             spec = pl.BlockSpec((rows // STEPS, width), lambda r: (r, 0))
             half = pl.BlockSpec((rows // STEPS, width // 2), lambda r: (r, 0))
             t2, x2 = run_kernel(
                 cross_kernel, [shaped((rows, width // 2))] * 2, self.block_specs(1, 2) * 2 + [spec] * 2, [half] * 2,
-                (self.kept, self.kept, self.other, self.other, self.x1, self.t1), "cross", grid=(STEPS,),
+                (self.kept, self.kept, self.other, self.other, self.x1, self.t1), "cross", grid=(STEPS,), line=line,
             )
-            t2, x2 = line(t2, x2)
             self.t2, self.x2 = flip(t2, 1), flip(x2, 4)
 
-        def second_came(self, line):
-            self.t2, self.x2 = line(self.t2, self.x2)
+        def second_came(self):
             return self.kept, self.other, self.x1, self.t1, self.t2, self.x2
 
     def per_device(
@@ -713,19 +749,17 @@
         doc_rows = (o * INNER + (i ^ jnp.arange(INNER, dtype=jnp.int32))) * tensor
         place = jnp.concatenate([jnp.stack([o, i, t]).astype(jnp.int32), spots, doc_rows.astype(jnp.int32)])
 
-        forms = [
-            ((w_fc1, w_fc2), ((True, quarter, 0, 4), (False, quarter, 0, 4))),
-            ((w_fc1, w_fc2), ((True, quarter, 1, 4), (False, quarter, 1, 4))),
-            ((w_qkv, w_qkv), ((True, HD, 0, 3), (True, HD, 1, 3))),
-            ((w_qkv, w_dense), ((True, HD, 2, 3), (False, HD, 0, 1))),
-            ((w_fc1, w_fc2), ((True, 2 * quarter, 1, 2), (False, 2 * quarter, 1, 2))),
-        ]
+        forms = {
+            0: ((w_fc1, w_fc2) * 2, tuple((cross, quarter, k, 4) for k in (0, 1) for cross in (True, False))),
+            2: ((w_qkv,) * 3 + (w_dense,), tuple((True, HD, k, 3) for k in (0, 1, 2)) + ((False, HD, 0, 1),)),
+            4: ((w_fc1, w_fc2), ((True, 2 * quarter, 1, 2), (False, 2 * quarter, 1, 2))),
+        }
+        cuts_of = {0: (0, 2 * quarter, 0), 1: (0, 2 * quarter, 1), 2: (2, 2 * HD, 0), 3: (2, 2 * HD, 1), 4: (4, 4 * quarter, 0)}
         s = {}
         steps = {}
 
         def own():
-            s["own"], s["cot_sum"] = own_call(place, *line(layer_input, cotangent))
-            s["own"] = line(s["own"])
+            s["own"], s["cot_sum"] = own_call(line, place, layer_input, cotangent)
             s["t"], s["x"], s["c"] = flip(s["own"], 1), flip(s["own"], 4), flip(s["own"], 2)
 
         def own_c():
@@ -733,17 +767,18 @@
 
         def own_xt():
             s["x"], s["t"] = line(s["x"], s["t"])
-            s["b"], s["tc"], s["xc"] = flip(s["x"], 1), flip(s["t"], 2), flip(s["x"], 2)
+            s["bu"], s["bv"] = flip(s["x"][0], 1), flip(s["t"][1], 4)
+            s["tc"], s["xc"] = flip(s["t"], 2), flip(s["x"], 2)
 
         def own_tc():
             s["tc"], s["xc"] = line(s["tc"], s["xc"])
 
         def own_b():
-            s["b"] = line(s["b"])
-            s["bc"] = flip(s["b"], 2)
+            s["bu"], s["bv"] = line(s["bu"], s["bv"])
+            s["buc"], s["bvc"] = flip(s["bu"], 2), flip(s["bv"], 2)
 
         def own_bc():
-            s["bc"] = line(s["bc"])
+            s["buc"], s["bvc"] = line(s["buc"], s["bvc"])
 
         steps.update({"own": own, "c": own_c, "xt": own_xt, "tc": own_tc, "b": own_b, "bc": own_bc})
 
@@ -754,90 +789,95 @@
             )
             s["small"] = swap_all(line(jnp.broadcast_to(v[None], (total, v.shape[0]))))
 
+        def small_came():
+            s["small"] = line(s["small"])
+
         def vectors():
-            v = line(s["small"]).reshape(total, -1)
+            v = s["small"].reshape(total, -1)
             row, fine = shaped((1, width), F32), shaped((16, width))
             *s["vec"], s["bias_q"], s["bias_f"], s["lengths"] = run_kernel(
                 functools.partial(vectors_kernel, piece, nq, nf, share, tensor),
                 [row] * 4 + [fine] * 2 + [row, shaped((1, qkv_own), F32), shaped((1, hidden_own), F32),
                                           shaped((INNER, LANES), jnp.int32)],
-                [SCALARS, VECTORS], [VECTORS] * 10, (place, v), "vectors",
+                [SCALARS, VECTORS], [VECTORS] * 10, (place, v), "vectors", line=line,
             )
             turn_spec = pl.BlockSpec((group_rows, LANES), lambda g: (g, 0))
-            turns = run_kernel(
+            s["turns"] = run_kernel(
                 functools.partial(turns_kernel, own_rows), [shaped((rows, LANES), F32)] * 3, [SCALARS] * 2,
-                [turn_spec] * 3, (place, s["lengths"]), "turns", grid=(INNER,),
+                [turn_spec] * 3, (place, s["lengths"]), "turns", grid=(INNER,), line=line,
             )
-            s["turns"] = line(*turns)
-
-        steps.update({"sm": small, "vec": vectors})
-        gathers, done, sums = {}, {}, {}
-
-        def gather_steps(k):
+
+        steps.update({"sm": small, "sw": small_came, "vec": vectors})
+        nears, gathers, done, sums = {}, {}, {}, {}
+
+        def near_steps(k):
             def p():
                 arrays, parts = forms[k]
-                s[f"ring{k}"] = swap_ring(line(piece_call(arrays, parts, strip)))
+                s[f"ring{k}"] = swap_ring(piece_call(line, arrays, parts, strip))
 
             def g():
-                gathers[k] = Gather(line(s[f"ring{k}"]))
+                nears[k] = Near(line(s[f"ring{k}"]))
+
+            steps.update({f"p{k}": p, f"g{k}": g})
+
+        def gather_steps(k):
+            def h():
+                of, cols, at = cuts_of[k]
+                gathers[k] = Gather(line, nears[of], cols, at)
 
             steps.update({
-                f"p{k}": p, f"g{k}": g, f"h{k}": lambda: gathers[k].near_came(line),
-                f"i{k}": lambda: gathers[k].far_came(line), f"j{k}": lambda: gathers[k].passed_came(line),
+                f"h{k}": h, f"i{k}": lambda: gathers[k].far_came(line), f"j{k}": lambda: gathers[k].passed_came(line),
             })
 
-        for k in range(5):
+        for k in forms:
+            near_steps(k)
+        for k in cuts_of:
             gather_steps(k)
 
         def pieces():
-            return [s[n] for n in ("own", "t", "c", "tc", "x", "b", "xc", "bc")]
-
-        def feed(k, first, count):
+            return [s[n] for n in ("own", "t", "c", "tc", "x", "xc", "bu", "bv", "buc", "bvc")]
+
+        def feed(k, first, split, sets):
             def run():
                 gain, shift, ratio = s["vec"][2], s["vec"][3], s["vec"][5]
-                bias = s["bias_f"][:, first * quarter : (first + count) * quarter]
-                cols, split = count * quarter, count
-                parts = gathers[k].parts
-                parts[0] = line(parts[0])
-                done[k] = list(chunk_call(
-                    functools.partial(feed_kernel, cols, split), "feed", pieces(), (), [], [parts],
-                    (gain, shift, ratio, bias), cols, cols, split,
-                ))
-                done[k][5] = line(done[k][5])
+                cols = split * quarter
+                bias = s["bias_f"][:, first * quarter : first * quarter + cols]
+                done[k] = chunk_call(
+                    line, functools.partial(feed_kernel, cols, split, len(sets)), "feed", pieces(), (), [],
+                    [gathers[j].parts for j in sets], (gain, shift, ratio, bias), cols, cols, split,
+                )
 
             return run
 
         def attention():
             gain, shift, ratio = s["vec"][0], s["vec"][1], s["vec"][4]
             one, two = gathers[2].parts, gathers[3].parts
-            one[0] = line(one[0])
             turn_spec = pl.BlockSpec((group_rows, LANES), lambda r: (r, 0))
-            done[2] = list(chunk_call(
-                functools.partial(attention_kernel, qkv_own), "attention", pieces(),
+            done[2] = chunk_call(
+                line, functools.partial(attention_kernel, qkv_own), "attention", pieces(),
                 (s["lengths"], place, *s["turns"]), [SCALARS, SCALARS] + [turn_spec] * 3, [one, two],
                 (gain, shift, ratio, s["bias_q"]), qkv_own, HD, 1,
-            ))
-            done[2][5] = line(done[2][5])
-
-        steps.update({"K0": feed(0, 0, 1), "K1": feed(1, 1, 1), "KA": attention, "K4": feed(4, 2, 2)})
+            )
+
+        steps.update({"K0": feed(0, 0, 1, (0,)), "K1": feed(1, 1, 1, (1,)), "KA": attention, "K4": feed(4, 2, 2, (4,))})
 
         def reduce_steps(k, chunk, at):
             def r():
                 sums[k] = Reduce(line, *done[chunk][at : at + 2])
 
             def z():
-                final = line(sums[k].final)
+                final = sums[k].final
                 if k == 2:
-                    s["qkv"], s["dense"] = line(*unpiece_call(
-                        final, (w_qkv.shape, w_dense.shape), ((True, qkv_own, 0, 1), (False, HD, 0, 1)), ()
-                    ))
+                    s["qkv"], s["dense"] = unpiece_call(
+                        line, final, (w_qkv.shape, w_dense.shape), ((True, qkv_own, 0, 1), (False, HD, 0, 1)), ()
+                    )
                 elif k < 2:
-                    s["fc1"], s["fc2"] = line(*unpiece_call(
-                        final, (w_fc1.shape, w_fc2.shape), forms[k][1], (s.get("fc1"), s.get("fc2"))
-                    ))
+                    s["fc1"], s["fc2"] = unpiece_call(
+                        line, final, (w_fc1.shape, w_fc2.shape), forms[0][1][2 * k : 2 * k + 2], (s.get("fc1"), s.get("fc2"))
+                    )
                 else:
                     name, w, form = (("fc1", w_fc1, 0), ("fc2", w_fc2, 1))[k - 3]
-                    s[name] = line(*unpiece_call(final, (w.shape,), forms[4][1][form : form + 1], (s[name],)))
+                    s[name], = unpiece_call(line, final, (w.shape,), forms[4][1][form : form + 1], (s[name],))
 
             steps.update({
                 f"r{k}": r, f"u{k}": lambda: sums[k].first_came(line), f"v{k}": lambda: sums[k].second_came(line),
@@ -853,28 +893,24 @@
                 return [c[act] for c in chunks], [c[weight] for c in chunks]
 
             def sent():
-                acts, weights = parts()
-                acts[0] = line(acts[0])
-                s["face" + name] = FaceReduce(line(join_call(acts, weights, True)))
+                s["face" + name] = FaceReduce(join_call(line, *parts(), True))
 
             def kept():
-                acts, weights = parts()
-                acts[0] = line(acts[0])
-                s["face" + name].kept = line(join_call(acts, weights, False))
+                s["face" + name].kept = join_call(line, *parts(), False)
 
             steps.update({
                 "J" + name: sent, "k" + name: kept, "C" + name: lambda: s["face" + name].core_came(line),
                 "D" + name: lambda: s["face" + name].first_came(line),
-                "E" + name: lambda: finish(s["face" + name].second_came(line)),
+                "E" + name: lambda: finish(s["face" + name].second_came()),
             })
 
         def finish_back(sums_in):
-            s["input_grad"] = line(
-                own_rows_call(input_grad_kernel, place, (layer_input, cotangent), (), sums_in, "input_grad")
+            s["input_grad"] = own_rows_call(
+                line, input_grad_kernel, place, (layer_input, cotangent), (), sums_in, "input_grad"
             )
 
         def finish_out(sums_in):
-            s["output"] = line(own_rows_call(output_kernel, place, (layer_input,), (s["vec"][6],), sums_in, "output"))
+            s["output"] = own_rows_call(line, output_kernel, place, (layer_input,), (s["vec"][6],), sums_in, "output")
 
         face_steps("B", 1, 2, finish_back)
         face_steps("O", 0, 3, finish_out)
@@ -884,9 +920,9 @@
             v = run_kernel(
                 functools.partial(tail_kernel, piece, nq, nf, share, tensor),
                 shaped((total, full_lanes(5 * piece) + full_lanes(nq + nf)), F32), [SCALARS] + [VECTORS] * 9, VECTORS,
-                (place, done[2][4], *[p[4] for p in feeds], done[2][5], *[p[5] for p in feeds], s["cot_sum"]), "tail",
+                (place, done[2][4], *[p[4] for p in feeds], done[2][5], *[p[5] for p in feeds], s["cot_sum"]), "tail", line=line,
             )
-            s["tail"] = swap_all(line(v))
+            s["tail"] = swap_all(v)
 
         def tail_came():
             s["tail"] = jnp.sum(line(s["tail"]), axis=0)

time: 565 us -> 554 us (0.981)
  Pallas kernels: 278 us -> 263 us
  blocking collectives: 23.9 us -> 33.7 us
  waiting for transfers between devices: 90 us -> 99.3 us
  local copies, waits for them, and re-layouts: 26 us -> 17.9 us
  starting transfers between devices: 134 us -> 128 us
    pallas_call x163 -> x72, Pallas kernels: 278 us -> 263 us  [run_kernel(): pl.pallas_call(inner, grid=grid, out_shape=outs, in_specs=in_specs, out_s...]
    unnamed x89 -> x37, local copies, waits for them, and re-layouts: 18.7 us -> 5.04 us
    all_to_all x1, blocking collectives: 23.9 us -> 33.7 us  [swap_all(): return lax.all_to_all(v, AXES, split_axis=0, concat_axis=0, tiled=True)]
    ppermute x47, waiting for transfers between devices: 59.4 us -> 68.9 us  [permute(): lax.ppermute(v.reshape(-1, v.shape[-1]), AXES, pairs).reshape(v.shape)]
    all_to_all x10 -> x8, starting transfers between devices: 36.9 us -> 31.8 us  [swap_ring(): lax.all_to_all(v, AXES, split_axis=0, concat_axis=0, tiled=True, axis_ind...]
    all_to_all x10 -> x8, waiting for transfers between devices: 30.6 us -> 30.4 us  [swap_ring(): lax.all_to_all(v, AXES, split_axis=0, concat_axis=0, tiled=True, axis_ind...]
  transfers between devices with their start and end apart: 58 -> 56, of which waited for: 17 -> 15; matrix products, arithmetic and copies ran while one was open for 3% -> 3% of each run, Pallas kernels for 49% -> 47%
where the time goes in v3:
time: 554 us; the launch traced here: 544 us
  Pallas kernels  263 us (47%)
  starting transfers between devices  128 us (23%)
  waiting for transfers between devices  99.3 us (18%)
  blocking collectives  33.7 us (6%)
  local copies, waits for them, and re-layouts  17.9 us (3%)
    pallas_call x72, Pallas kernels, run_kernel(): pl.pallas_call(inner, grid=grid, out_shape=outs, in_specs=in_specs, out_s...  263 us
    ppermute x47, starting transfers between devices, permute(): lax.ppermute(v.reshape(-1, v.shape[-1]), AXES, pairs).reshape(v.shape)  93.4 us
    ppermute x47, waiting for transfers between devices, permute(): lax.ppermute(v.reshape(-1, v.shape[-1]), AXES, pairs).reshape(v.shape)  68.9 us
    all_to_all x1, blocking collectives, swap_all(): return lax.all_to_all(v, AXES, split_axis=0, concat_axis=0, tiled=True)  33.7 us
    all_to_all x8, starting transfers between devices, swap_ring(): lax.all_to_all(v, AXES, split_axis=0, concat_axis=0, tiled=True, axis_ind...  31.8 us
    all_to_all x8, waiting for transfers between devices, swap_ring(): lax.all_to_all(v, AXES, split_axis=0, concat_axis=0, tiled=True, axis_ind...  30.4 us
  transfers between devices with their start and end apart: 56, of which 15 were waited for; matrix products, arithmetic and copies ran while one was open for 3% of the time, Pallas kernels for 47%

profile of v3, /device:TPU:8, one launch (start us, length us, event | category | flops | bytes accessed | tf_op | source)
XLA Modules:
  0.0 543.9 jit_solution(8018632208102195192)
XLA Ops:
  1.2 3.5 piece.3
  4.7 4.3 all-to-all-start
  9.0 3.6 piece.4
  12.6 10.9 %all-to-all-done.refs_0_ = bf16[4,1024,128]{2,1,0:T(8,128)(2,1)} async-done(((bf16[4,1024,128]{2,1,0:T(8,128)(2,1)}), bf16[4,1024,128]{2,1,0:T(8,128)(2,1)}, u32[]{:S(2)}, u32[]{:S(2)}) %all-to-all-start) | async-done | bytes 1048608 | tf_op jit(solution)/shard_map/all_to_all | solution.py:640
  23.5 4.2 all-to-all-start.1
  29.1 13.2 %all-to-all-done.1.refs_0_ = bf16[4,1024,128]{2,1,0:T(8,128)(2,1)} async-done(((bf16[4,1024,128]{2,1,0:T(8,128)(2,1)}), bf16[4,1024,128]{2,1,0:T(8,128)(2,1)}, u32[]{:S(2)}, u32[]{:S(2)}) %all-to-all-start.1) | async-done | bytes 1048608 | tf_op jit(solution)/shard_map/all_to_all | solution.py:640
  42.4 4.5 own.1
  48.8 5.5 %collective-permute-done = bf16[4096,128]{1,0:T(8,128)(2,1)} collective-permute-done((bf16[4096,128]{1,0:T(8,128)(2,1)}, bf16[4096,128]{1,0:T(8,128)(2,1)}, u32[]{:S(2)}, u32[]{:S(2)}) %collective-permute-start) | collective-permute-done | bytes 1048608 | tf_op jit(solution)/shard_map/ppermute | solution.py:623
  56.4 3.5 collective-permute-start.3
  63.8 33.7 %all_to_all.62 = f32[32,1,896]{2,1,0:T(1,128)S(1)} all-to-all(f32[32,1,896]{2,1,0:T(1,128)S(1)} %copy.136), channel_id=1, replica_groups=mesh['dp'=16,'tensor'=2] {'dp','tensor'}, dimensions={0} | all-to-all | bytes 229376 | tf_op jit(solution)/shard_map/all_to_all | solution.py:643
  98.2 3.5 collective-permute-start.4
  114.6 11.0 %collective-permute-done.4 = bf16[4096,128]{1,0:T(8,128)(2,1)} collective-permute-done((bf16[4096,128]{1,0:T(8,128)(2,1)}, bf16[4096,128]{1,0:T(8,128)(2,1)}, u32[]{:S(2)}, u32[]{:S(2)}) %collective-permute-start.4) | collective-permute-done | bytes 1048608 | tf_op jit(solution)/shard_map/ppermute | solution.py:623
  130.1 6.0 %turns.1 = (f32[2048,128]{1,0:T(8,128)}, f32[2048,128]{1,0:T(8,128)}, f32[2048,128]{1,0:T(8,128)}, f32[8,128]{1,0:T(8,128)}) custom-call(s32[11]{0:T(128)} %concatenate.6.refs_0_.refs_21_, s32[4,128]{1,0:T(4,128)} %get-tuple-element.239.refs_1_.refs_20_, f32[8,128]{1,0:T(8,128)} %get-tuple-element.240.refs_2_), custom_call_target="tpu_custom_call", output_to_operand_aliasing={{3}: (2, {})} | custom-call | tf_op jit(solution)/shard_map/turns/pallas_call | solution.py:71
  136.2 3.5 collective-permute-start.14
  139.7 3.6 piece.5
  143.3 4.3 all-to-all-start.3
  149.3 14.1 %collective-permute-done.14 = bf16[4096,128]{1,0:T(8,128)(2,1)} collective-permute-done((bf16[4096,128]{1,0:T(8,128)(2,1)}, bf16[4096,128]{1,0:T(8,128)(2,1)}, u32[]{:S(2)}, u32[]{:S(2)}) %collective-permute-start.14) | collective-permute-done | bytes 1048608 | tf_op jit(solution)/shard_map/ppermute | solution.py:623
  163.4 3.5 collective-permute-start.17
  167.6 18.9 %feed.3 = (bf16[2048,256]{1,0:T(8,128)(2,1)}, bf16[2048,256]{1,0:T(8,128)(2,1)}, bf16[256,2048]{1,0:T(8,128)(2,1)}, bf16[256,2048]{1,0:T(8,128)(2,1)}, f32[2,204...) custom-call(bf16[2,256,2048]{2,1,0:T(8,128)(2,1)} %get-tuple-element, ...), custom_call_target="tpu_custom_call", output_to_operand_aliasing={{8}: (17, {})} | custom-call | tf_op jit(solution)/shard_map/feed/pallas_call | solution.py:71
  186.5 3.3 collective-permute-done.17
  191.3 2.6 cat.9
  193.9 2.3 collective-permute-start.19
  196.2 2.8 collective-permute-start.18
  202.8 18.9 %feed.4 = (bf16[2048,256]{1,0:T(8,128)(2,1)}, bf16[2048,256]{1,0:T(8,128)(2,1)}, bf16[256,2048]{1,0:T(8,128)(2,1)}, bf16[256,2048]{1,0:T(8,128)(2,1)}, f32[2,204...) custom-call(bf16[2,256,2048]{2,1,0:T(8,128)(2,1)} %get-tuple-element, ...), custom_call_target="tpu_custom_call", output_to_operand_aliasing={{8}: (17, {})} | custom-call | tf_op jit(solution)/shard_map/feed/pallas_call | solution.py:71
  221.7 19.9 %collective-permute-done.19 = bf16[8192,128]{1,0:T(8,128)(2,1)} collective-permute-done((bf16[8192,128]{1,0:T(8,128)(2,1)}, bf16[8192,128]{1,0:T(8,128)(2,1)}, u32[]{:S(2)}, u32[]{:S(2)}) %collective-permute-start.19) | collective-permute-done | bytes 2097184 | tf_op jit(solution)/shard_map/ppermute | solution.py:623
  241.5 2.6 collective-permute-start.21
  245.5 37.9 %attention.1 = (bf16[2048,256]{1,0:T(8,128)(2,1)}, bf16[2048,768]{1,0:T(8,128)(2,1)}, bf16[768,2048]{1,0:T(8,128)(2,1)}, bf16[256,2048]{1,0:T(8,128)(2,1)}, f32[...) custom-call(bf16[2,256,2048]{2,1,0:T(8,128)(2,1)} %get-tuple-element, ...), custom_call_target="tpu_custom_call", output_to_operand_aliasing={{8}: (25, {})} | custom-call | tf_op jit(solution)/shard_map/attention/pallas_call | solution.py:71
  283.5 2.5 sum.15
  285.9 2.3 collective-permute-start.26
  289.6 2.4 sum.16
  292.1 12.1 %collective-permute-start.25 = (bf16[4096,128]{1,0:T(8,128)(2,1)}, bf16[4096,128]{1,0:T(8,128)(2,1)}, u32[]{:S(2)}, u32[]{:S(2)}) collective-permute-start(bf16[4096,128]{1,0:T(8,128)(2,1)} %bitcast.117), channel_id=1, source_target_pairs={{8,16},{9,17},{10,18},{11,19},{12,20},{13,21},{14,22},{15,23},{16,... | collective-permute-start | bytes 3145736 | tf_op jit(solution)/shard_map/ppermute | solution.py:623
  304.7 29.8 %feed.5 = (bf16[2048,512]{1,0:T(8,128)(2,1)}, bf16[2048,512]{1,0:T(8,128)(2,1)}, bf16[512,2048]{1,0:T(8,128)(2,1)}, bf16[512,2048]{1,0:T(8,128)(2,1)}, f32[2,204...) custom-call(bf16[2,256,2048]{2,1,0:T(8,128)(2,1)} %get-tuple-element, ...), custom_call_target="tpu_custom_call", output_to_operand_aliasing={{10}: (17, {})} | custom-call | tf_op jit(solution)/shard_map/feed/pallas_call | solution.py:71
  336.6 13.1 %join.4 = (bf16[1024,2048]{1,0:T(8,128)(2,1)}, f32[8,128]{1,0:T(8,128)}) custom-call(bf16[2048,256]{1,0:T(8,128)(2,1)} %get-tuple-element.308.refs_0_, bf16[2048,256]{1,0:T(8,128)(2,1)} %get-tuple-element.309.refs_1_, bf16[2048,768]{1,0:T(8,128)(2,1)} %get-tuple-element.310.refs_2_, ...), custom_call_target="tpu_custom_call", output_to_operand_aliasing={{1}: (8, {})} | custom-call | tf_op jit(solution)/shard_map/join/pallas_call | solution.py:71
  351.7 10.4 %join.5 = (bf16[1024,2048]{1,0:T(8,128)(2,1)}, f32[8,128]{1,0:T(8,128)}) custom-call(bf16[2048,256]{1,0:T(8,128)(2,1)} %get-tuple-element.264.refs_0_, bf16[2048,256]{1,0:T(8,128)(2,1)} %get-tuple-element.273.refs_1_, bf16[2048,256]{1,0:T(8,128)(2,1)} %get-tuple-element.292.refs_2_, ...), custom_call_target="tpu_custom_call", output_to_operand_aliasing={{1}: (8, {})} | custom-call | tf_op jit(solution)/shard_map/join/pallas_call | solution.py:71
  362.6 3.4 sum.19
  366.0 2.3 collective-permute-start.30
  369.6 5.7 %collective-permute-start.28 = (bf16[2048,128]{1,0:T(8,128)(2,1)}, bf16[2048,128]{1,0:T(8,128)(2,1)S(1)}, u32[]{:S(2)}, u32[]{:S(2)}) collective-permute-start(bf16[2048,128]{1,0:T(8,128)(2,1)} %bitcast.119), channel_id=1, source_target_pairs={{8,0},{9,1},{10,2},{11,3},{12,4},{13,5},{14,6},{15,7},{16,24},{17,... | collective-permute-start | bytes 1572872 | tf_op jit(solution)/shard_map/ppermute | solution.py:623
  375.3 13.1 %join.6 = (bf16[1024,2048]{1,0:T(8,128)(2,1)}, f32[8,128]{1,0:T(8,128)}) custom-call(bf16[2048,256]{1,0:T(8,128)(2,1)} %get-tuple-element.308.refs_0_, bf16[2048,256]{1,0:T(8,128)(2,1)} %get-tuple-element.309.refs_1_, bf16[2048,768]{1,0:T(8,128)(2,1)} %get-tuple-element.310.refs_2_, ...), custom_call_target="tpu_custom_call", output_to_operand_aliasing={{1}: (8, {})} | custom-call | tf_op jit(solution)/shard_map/join/pallas_call | solution.py:71
  389.3 2.3 sum.20
  391.6 4.5 core.2
  397.7 9.1 %collective-permute-done.31 = bf16[6144,128]{1,0:T(8,128)(2,1)} collective-permute-done((bf16[6144,128]{1,0:T(8,128)(2,1)}, bf16[6144,128]{1,0:T(8,128)(2,1)}, u32[]{:S(2)}, u32[]{:S(2)}) %collective-permute-start.31) | collective-permute-done | bytes 1572896 | tf_op jit(solution)/shard_map/ppermute | solution.py:623
  408.1 3.5 all-to-all-start.4
  411.5 10.2 %join.7 = (bf16[1024,2048]{1,0:T(8,128)(2,1)}, f32[8,128]{1,0:T(8,128)}) custom-call(bf16[2048,256]{1,0:T(8,128)(2,1)} %get-tuple-element.264.refs_0_, bf16[2048,256]{1,0:T(8,128)(2,1)} %get-tuple-element.273.refs_1_, bf16[2048,256]{1,0:T(8,128)(2,1)} %get-tuple-element.292.refs_2_, ...), custom_call_target="tpu_custom_call", output_to_operand_aliasing={{1}: (8, {})} | custom-call | tf_op jit(solution)/shard_map/join/pallas_call | solution.py:71
  421.7 2.4 sum.21
  424.2 3.3 collective-permute-start.39
  430.4 2.5 sum.22
  432.9 5.0 collective-permute-start.37
  437.9 4.5 core.3
  445.8 4.3 cross.2
  453.5 3.0 all-to-all-start.5
  460.7 2.4 sum.24
  463.1 4.6 collective-permute-start.45
  467.8 3.2 sum.25
  471.0 4.5 all-to-all-start.6
  479.3 4.3 cross.3
  490.2 3.5 all-to-all-start.8
  495.3 2.5 unpiece.6
  501.5 4.8 output.1
  510.4 2.4 sum.28
  513.5 3.5 all-to-all-start.7
  517.8 5.5 %input_grad.1 = (bf16[256,2048]{1,0:T(8,128)(2,1)}, f32[8,128]{1,0:T(8,128)}) custom-call(s32[11]{0:T(128)} %concatenate.6.refs_0_.refs_21_, bf16[256,2048]{1,0:T(8,128)(2,1)} %refs_1_.11, bf16[256,2048]{1,0:T(8,128)(2,1)} %refs_2_.7, bf16[1024,2048]{1,0:T(8,128)(2,1)} %get-tuple-element.329.refs_0_.refs_1_.refs_2_.refs_3_, ...), custom_call_target="tpu_custom_call", output_to_operand_aliasing={{1}: (9, {})} | custom-call | tf_op jit(solution)/shard_map/input_grad/pallas_call | solution.py:71
  525.5 2.4 sum.29
  527.9 4.2 all-to-all-start.9
  536.0 5.0 all-to-all-done.9.refs_0_
  (177 shorter events, 91.7 us)
Async XLA Ops:
  4.7 18.8 %all-to-all-start = ((bf16[4,1024,128]{2,1,0:T(8,128)(2,1)}), bf16[4,1024,128]{2,1,0:T(8,128)(2,1)}, u32[]{:S(2)}, u32[]{:S(2)}) async-start(bf16[4,1024,128]{2,1,0:T(8,128)(2,1)} %get-tuple-element.210), calls=%async_computation | async-start | bytes 2097152 | tf_op jit(solution)/shard_map/all_to_all | solution.py:640
  23.5 18.8 %all-to-all-start.1 = ((bf16[4,1024,128]{2,1,0:T(8,128)(2,1)}), bf16[4,1024,128]{2,1,0:T(8,128)(2,1)}, u32[]{:S(2)}, u32[]{:S(2)}) async-start(bf16[4,1024,128]{2,1,0:T(8,128)(2,1)} %get-tuple-element.214), calls=%async_computation.1 | async-start | bytes 2097152 | tf_op jit(solution)/shard_map/all_to_all | solution.py:640
  28.5 25.8 %collective-permute-start = (bf16[4096,128]{1,0:T(8,128)(2,1)}, bf16[4096,128]{1,0:T(8,128)(2,1)}, u32[]{:S(2)}, u32[]{:S(2)}) collective-permute-start(bf16[4096,128]{1,0:T(8,128)(2,1)} %bitcast.5), channel_id=1, source_target_pairs={{0,8},{1,9},{2,10},{3,11},{4,12},{5,13},{6,14},{7,15},{8,0},{9,1},... | collective-permute-start | bytes 3145736 | tf_op jit(solution)/shard_map/ppermute | solution.py:623
  42.3 17.6 %copy-start.16 = (s32[1,3]{1,0:T(1,128)S(1)}, s32[1,3]{1,0:T(1,128)}, u32[]{:S(2)}) copy-start(s32[1,3]{1,0:T(1,128)} %param.17) | copy-start | bytes 40
  42.3 17.7 %copy-start.7 = (f32[64]{0:T(128)S(1)}, f32[64]{0:T(128)}, u32[]{:S(2)}) copy-start(f32[64]{0:T(128)} %param.18) | copy-start | bytes 772
  42.3 17.7 %copy-start.8 = (f32[64]{0:T(128)S(1)}, f32[64]{0:T(128)}, u32[]{:S(2)}) copy-start(f32[64]{0:T(128)} %param.19) | copy-start | bytes 772
  42.3 17.7 %copy-start.9 = (f32[64]{0:T(128)S(1)}, f32[64]{0:T(128)}, u32[]{:S(2)}) copy-start(f32[64]{0:T(128)} %param.20) | copy-start | bytes 772
  42.3 17.7 %copy-start.10 = (f32[64]{0:T(128)S(1)}, f32[64]{0:T(128)}, u32[]{:S(2)}) copy-start(f32[64]{0:T(128)} %param.21) | copy-start | bytes 772
  42.4 17.7 %copy-start.11 = (bf16[192]{0:T(256)(128)(2,1)S(1)}, bf16[192]{0:T(256)(128)(2,1)}, u32[]{:S(2)}) copy-start(bf16[192]{0:T(256)(128)(2,1)} %param.23) | copy-start | bytes 1156
  42.4 17.7 %copy-start.12 = (bf16[256]{0:T(256)(128)(2,1)S(1)}, bf16[256]{0:T(256)(128)(2,1)}, u32[]{:S(2)}) copy-start(bf16[256]{0:T(256)(128)(2,1)} %param.27) | copy-start | bytes 1540
  46.9 54.9 %collective-permute-start.2 = (bf16[512,2048]{1,0:T(8,128)(2,1)}, bf16[512,2048]{1,0:T(8,128)(2,1)}, u32[]{:S(2)}, u32[]{:S(2)}) collective-permute-start(bf16[512,2048]{1,0:T(8,128)(2,1)} %bitcast.88), channel_id=1, source_target_pairs={{0,2},{1,3},{2,0},{3,1},{4,6},{5,7},{6,4},{7,5},{8,10},{9,11},{10,... | collective-permute-start | bytes 6291464 | tf_op jit(solution)/shard_map/ppermute | solution.py:623
  46.9 61.3 %collective-permute-start.6 = (bf16[512,2048]{1,0:T(8,128)(2,1)}, bf16[512,2048]{1,0:T(8,128)(2,1)}, u32[]{:S(2)}, u32[]{:S(2)}) collective-permute-start(bf16[512,2048]{1,0:T(8,128)(2,1)} %bitcast.89), channel_id=1, source_target_pairs={{0,1},{1,0},{2,3},{3,2},{4,5},{5,4},{6,7},{7,6},{8,9},{9,8},{10,11... | collective-permute-start | bytes 6291464 | tf_op jit(solution)/shard_map/ppermute | solution.py:623
  48.4 59.7 %collective-permute-start.5 = (bf16[512,2048]{1,0:T(8,128)(2,1)}, bf16[512,2048]{1,0:T(8,128)(2,1)}, u32[]{:S(2)}, u32[]{:S(2)}) collective-permute-start(bf16[512,2048]{1,0:T(8,128)(2,1)} %bitcast.90), channel_id=1, source_target_pairs={{0,4},{1,5},{2,6},{3,7},{4,0},{5,1},{6,2},{7,3},{8,12},{9,13},{10,... | collective-permute-start | bytes 6291464 | tf_op jit(solution)/shard_map/ppermute | solution.py:623
  56.4 41.9 %collective-permute-start.3 = (bf16[4096,128]{1,0:T(8,128)(2,1)}, bf16[4096,128]{1,0:T(8,128)(2,1)}, u32[]{:S(2)}, u32[]{:S(2)}) collective-permute-start(bf16[4096,128]{1,0:T(8,128)(2,1)} %bitcast.104), channel_id=1, source_target_pairs={{8,16},{9,17},{10,18},{11,19},{12,20},{13,21},{14,22},{15,23},{16,... | collective-permute-start | bytes 3145736 | tf_op jit(solution)/shard_map/ppermute | solution.py:623
  59.8 44.2 %collective-permute-start.1 = (bf16[4096,128]{1,0:T(8,128)(2,1)}, bf16[4096,128]{1,0:T(8,128)(2,1)}, u32[]{:S(2)}, u32[]{:S(2)}) collective-permute-start(bf16[4096,128]{1,0:T(8,128)(2,1)} %bitcast.8), channel_id=1, source_target_pairs={{0,8},{1,9},{2,10},{3,11},{4,12},{5,13},{6,14},{7,15},{8,0},{9,1},... | collective-permute-start | bytes 3145736 | tf_op jit(solution)/shard_map/ppermute | solution.py:623
  98.2 27.4 %collective-permute-start.4 = (bf16[4096,128]{1,0:T(8,128)(2,1)}, bf16[4096,128]{1,0:T(8,128)(2,1)}, u32[]{:S(2)}, u32[]{:S(2)}) collective-permute-start(bf16[4096,128]{1,0:T(8,128)(2,1)} %bitcast.102), channel_id=1, source_target_pairs={{8,16},{9,17},{10,18},{11,19},{12,20},{13,21},{14,22},{15,23},{16,... | collective-permute-start | bytes 3145736 | tf_op jit(solution)/shard_map/ppermute | solution.py:623
  101.7 26.2 %collective-permute-start.11 = (bf16[4096,128]{1,0:T(8,128)(2,1)}, bf16[4096,128]{1,0:T(8,128)(2,1)}, u32[]{:S(2)}, u32[]{:S(2)}) collective-permute-start(bf16[4096,128]{1,0:T(8,128)(2,1)} %bitcast.24), channel_id=1, source_target_pairs={{8,0},{9,1},{10,2},{11,3},{12,4},{13,5},{14,6},{15,7},{16,24},{17,... | collective-permute-start | bytes 3145736 | tf_op jit(solution)/shard_map/ppermute | solution.py:623
  110.5 25.7 %collective-permute-start.9 = (bf16[256,2048]{1,0:T(8,128)(2,1)}, bf16[256,2048]{1,0:T(8,128)(2,1)}, u32[]{:S(2)}, u32[]{:S(2)}) collective-permute-start(bf16[256,2048]{1,0:T(8,128)(2,1)} %slice_bitcast_fusion.1), channel_id=1, source_target_pairs={{0,1},{1,0},{2,3},{3,2},{4,5},{5,4},{6,7},{7,6},{8,9},{9,8},{10,11... | collective-permute-start | bytes 3145736 | tf_op jit(solution)/shard_map/ppermute | solution.py:623
  114.1 29.1 %collective-permute-start.10 = (bf16[256,2048]{1,0:T(8,128)(2,1)}, bf16[256,2048]{1,0:T(8,128)(2,1)}, u32[]{:S(2)}, u32[]{:S(2)}) collective-permute-start(bf16[256,2048]{1,0:T(8,128)(2,1)} %slice_bitcast_fusion), channel_id=1, source_target_pairs={{0,4},{1,5},{2,6},{3,7},{4,0},{5,1},{6,2},{7,3},{8,12},{9,13},{10,... | collective-permute-start | bytes 3145736 | tf_op jit(solution)/shard_map/ppermute | solution.py:623
  125.6 23.7 %collective-permute-start.15 = (bf16[4096,128]{1,0:T(8,128)(2,1)}, bf16[4096,128]{1,0:T(8,128)(2,1)}, u32[]{:S(2)}, u32[]{:S(2)}) collective-permute-start(bf16[4096,128]{1,0:T(8,128)(2,1)} %bitcast.28), channel_id=1, source_target_pairs={{8,0},{9,1},{10,2},{11,3},{12,4},{13,5},{14,6},{15,7},{16,24},{17,... | collective-permute-start | bytes 3145736 | tf_op jit(solution)/shard_map/ppermute | solution.py:623
  127.9 39.7 %collective-permute-start.8 = (bf16[512,2048]{1,0:T(8,128)(2,1)}, bf16[512,2048]{1,0:T(8,128)(2,1)}, u32[]{:S(2)}, u32[]{:S(2)}) collective-permute-start(bf16[512,2048]{1,0:T(8,128)(2,1)} %bitcast.20), channel_id=1, source_target_pairs={{0,2},{1,3},{2,0},{3,1},{4,6},{5,7},{6,4},{7,5},{8,10},{9,11},{10,... | collective-permute-start | bytes 6291464 | tf_op jit(solution)/shard_map/ppermute | solution.py:623
  127.9 39.7 %collective-permute-start.7 = (bf16[512,2048]{1,0:T(8,128)(2,1)}, bf16[512,2048]{1,0:T(8,128)(2,1)}, u32[]{:S(2)}, u32[]{:S(2)}) collective-permute-start(bf16[512,2048]{1,0:T(8,128)(2,1)} %bitcast.18), channel_id=1, source_target_pairs={{0,2},{1,3},{2,0},{3,1},{4,6},{5,7},{6,4},{7,5},{8,10},{9,11},{10,... | collective-permute-start | bytes 6291464 | tf_op jit(solution)/shard_map/ppermute | solution.py:623
  136.2 27.3 %collective-permute-start.14 = (bf16[4096,128]{1,0:T(8,128)(2,1)}, bf16[4096,128]{1,0:T(8,128)(2,1)}, u32[]{:S(2)}, u32[]{:S(2)}) collective-permute-start(bf16[4096,128]{1,0:T(8,128)(2,1)} %bitcast.98), channel_id=1, source_target_pairs={{8,16},{9,17},{10,18},{11,19},{12,20},{13,21},{14,22},{15,23},{16,... | collective-permute-start | bytes 3145736 | tf_op jit(solution)/shard_map/ppermute | solution.py:623
  143.3 23.7 %collective-permute-start.12 = (bf16[256,2048]{1,0:T(8,128)(2,1)}, bf16[256,2048]{1,0:T(8,128)(2,1)}, u32[]{:S(2)}, u32[]{:S(2)}) collective-permute-start(bf16[256,2048]{1,0:T(8,128)(2,1)} %get-tuple-element.244.refs_6_), channel_id=1, source_target_pairs={{0,2},{1,3},{2,0},{3,1},{4,6},{5,7},{6,4},{7,5},{8,10},{9,11},{10,... | collective-permute-start | bytes 3145736 | tf_op jit(solution)/shard_map/ppermute | solution.py:623
  143.3 23.7 %all-to-all-start.3 = ((bf16[4,1024,128]{2,1,0:T(8,128)(2,1)}), bf16[4,1024,128]{2,1,0:T(8,128)(2,1)}, u32[]{:S(2)}, u32[]{:S(2)}) async-start(bf16[4,1024,128]{2,1,0:T(8,128)(2,1)} %get-tuple-element.246), calls=%async_computation.3 | async-start | bytes 2097152 | tf_op jit(solution)/shard_map/all_to_all | solution.py:640
  147.5 19.5 %copy-start.6 = (f32[1,1024]{1,0:T(1,128)S(1)}, f32[1,1024]{1,0:T(1,128)}, u32[]{:S(2)}) copy-start(f32[1,1024]{1,0:T(1,128)} %get-tuple-element.262) | copy-start | bytes 12292
  149.3 18.3 %collective-permute-start.13 = (bf16[256,2048]{1,0:T(8,128)(2,1)}, bf16[256,2048]{1,0:T(8,128)(2,1)}, u32[]{:S(2)}, u32[]{:S(2)}) collective-permute-start(bf16[256,2048]{1,0:T(8,128)(2,1)} %get-tuple-element.245.refs_7_), channel_id=1, source_target_pairs={{0,2},{1,3},{2,0},{3,1},{4,6},{5,7},{6,4},{7,5},{8,10},{9,11},{10,... | collective-permute-start | bytes 3145736 | tf_op jit(solution)/shard_map/ppermute | solution.py:623
  163.4 26.4 %collective-permute-start.17 = (bf16[4096,128]{1,0:T(8,128)(2,1)}, bf16[4096,128]{1,0:T(8,128)(2,1)}, u32[]{:S(2)}, u32[]{:S(2)}) collective-permute-start(bf16[4096,128]{1,0:T(8,128)(2,1)} %bitcast.100), channel_id=1, source_target_pairs={{8,16},{9,17},{10,18},{11,19},{12,20},{13,21},{14,22},{15,23},{16,... | collective-permute-start | bytes 3145736 | tf_op jit(solution)/shard_map/ppermute | solution.py:623
  167.0 24.3 %collective-permute-start.16 = (bf16[4096,128]{1,0:T(8,128)(2,1)}, bf16[4096,128]{1,0:T(8,128)(2,1)}, u32[]{:S(2)}, u32[]{:S(2)}) collective-permute-start(bf16[4096,128]{1,0:T(8,128)(2,1)} %bitcast.32), channel_id=1, source_target_pairs={{0,8},{1,9},{2,10},{3,11},{4,12},{5,13},{6,14},{7,15},{8,0},{9,1},... | collective-permute-start | bytes 3145736 | tf_op jit(solution)/shard_map/ppermute | solution.py:623
  193.9 47.7 %collective-permute-start.19 = (bf16[8192,128]{1,0:T(8,128)(2,1)}, bf16[8192,128]{1,0:T(8,128)(2,1)}, u32[]{:S(2)}, u32[]{:S(2)}) collective-permute-start(bf16[8192,128]{1,0:T(8,128)(2,1)} %bitcast.96), channel_id=1, source_target_pairs={{8,16},{9,17},{10,18},{11,19},{12,20},{13,21},{14,22},{15,23},{16,... | collective-permute-start | bytes 6291464 | tf_op jit(solution)/shard_map/ppermute | solution.py:623
  196.2 48.0 %collective-permute-start.18 = (bf16[4096,128]{1,0:T(8,128)(2,1)}, bf16[4096,128]{1,0:T(8,128)(2,1)}, u32[]{:S(2)}, u32[]{:S(2)}) collective-permute-start(bf16[4096,128]{1,0:T(8,128)(2,1)} %bitcast.37), channel_id=1, source_target_pairs={{8,0},{9,1},{10,2},{11,3},{12,4},{13,5},{14,6},{15,7},{16,24},{17,... | collective-permute-start | bytes 3145736 | tf_op jit(solution)/shard_map/ppermute | solution.py:623
  199.0 45.2 %collective-permute-start.20 = (bf16[4096,128]{1,0:T(8,128)(2,1)}, bf16[4096,128]{1,0:T(8,128)(2,1)}, u32[]{:S(2)}, u32[]{:S(2)}) collective-permute-start(bf16[4096,128]{1,0:T(8,128)(2,1)} %bitcast.42), channel_id=1, source_target_pairs={{8,0},{9,1},{10,2},{11,3},{12,4},{13,5},{14,6},{15,7},{16,24},{17,... | collective-permute-start | bytes 3145736 | tf_op jit(solution)/shard_map/ppermute | solution.py:623
  201.3 82.2 %collective-permute-start.22 = (bf16[6144,128]{1,0:T(8,128)(2,1)}, bf16[6144,128]{1,0:T(8,128)(2,1)}, u32[]{:S(2)}, u32[]{:S(2)}) collective-permute-start(bf16[6144,128]{1,0:T(8,128)(2,1)} %bitcast.95), channel_id=1, source_target_pairs={{0,8},{1,9},{2,10},{3,11},{4,12},{5,13},{6,14},{7,15},{24,16},{25,... | collective-permute-start | bytes 4718600 | tf_op jit(solution)/shard_map/ppermute | solution.py:623
  241.5 48.0 %collective-permute-start.21 = (bf16[8192,128]{1,0:T(8,128)(2,1)}, bf16[8192,128]{1,0:T(8,128)(2,1)}, u32[]{:S(2)}, u32[]{:S(2)}) collective-permute-start(bf16[8192,128]{1,0:T(8,128)(2,1)} %bitcast.45), channel_id=1, source_target_pairs={{8,0},{9,1},{10,2},{11,3},{12,4},{13,5},{14,6},{15,7},{16,24},{17,... | collective-permute-start | bytes 6291464 | tf_op jit(solution)/shard_map/ppermute | solution.py:623
  244.2 45.4 %collective-permute-start.23 = (bf16[6144,128]{1,0:T(8,128)(2,1)}, bf16[6144,128]{1,0:T(8,128)(2,1)}, u32[]{:S(2)}, u32[]{:S(2)}) collective-permute-start(bf16[6144,128]{1,0:T(8,128)(2,1)} %bitcast.92), channel_id=1, source_target_pairs={{0,8},{1,9},{2,10},{3,11},{4,12},{5,13},{6,14},{7,15},{24,16},{25,... | collective-permute-start | bytes 4718600 | tf_op jit(solution)/shard_map/ppermute | solution.py:623
  285.9 48.7 %collective-permute-start.26 = (bf16[4096,128]{1,0:T(8,128)(2,1)}, bf16[4096,128]{1,0:T(8,128)(2,1)}, u32[]{:S(2)}, u32[]{:S(2)}) collective-permute-start(bf16[4096,128]{1,0:T(8,128)(2,1)} %bitcast.116), channel_id=1, source_target_pairs={{8,16},{9,17},{10,18},{11,19},{12,20},{13,21},{14,22},{15,23},{16,... | collective-permute-start | bytes 3145736 | tf_op jit(solution)/shard_map/ppermute | solution.py:623
  288.3 74.3 %collective-permute-start.24 = (bf16[12288,128]{1,0:T(8,128)(2,1)}, bf16[12288,128]{1,0:T(8,128)(2,1)}, u32[]{:S(2)}, u32[]{:S(2)}) collective-permute-start(bf16[12288,128]{1,0:T(8,128)(2,1)} %bitcast.91), channel_id=1, source_target_pairs={{0,8},{1,9},{2,10},{3,11},{4,12},{5,13},{6,14},{7,15},{24,16},{25,... | collective-permute-start | bytes 9437192 | tf_op jit(solution)/shard_map/ppermute | solution.py:623
  292.1 57.7 %collective-permute-start.25 = (bf16[4096,128]{1,0:T(8,128)(2,1)}, bf16[4096,128]{1,0:T(8,128)(2,1)}, u32[]{:S(2)}, u32[]{:S(2)}) collective-permute-start(bf16[4096,128]{1,0:T(8,128)(2,1)} %bitcast.117), channel_id=1, source_target_pairs={{8,16},{9,17},{10,18},{11,19},{12,20},{13,21},{14,22},{15,23},{16,... | collective-permute-start | bytes 3145736 | tf_op jit(solution)/shard_map/ppermute | solution.py:623
  349.7 41.9 %collective-permute-start.27 = (bf16[1024,2048]{1,0:T(8,128)(2,1)}, bf16[1024,2048]{1,0:T(8,128)(2,1)}, u32[]{:S(2)}, u32[]{:S(2)}) collective-permute-start(bf16[1024,2048]{1,0:T(8,128)(2,1)} %get-tuple-element.330), channel_id=1, source_target_pairs={{0,2},{1,3},{2,0},{3,1},{4,6},{5,7},{6,4},{7,5},{8,10},{9,11},{10,... | collective-permute-start | bytes 12582920 | tf_op jit(solution)/shard_map/ppermute | solution.py:623
  362.1 70.8 %collective-permute-start.29 = (bf16[1024,2048]{1,0:T(8,128)(2,1)}, bf16[1024,2048]{1,0:T(8,128)(2,1)}, u32[]{:S(2)}, u32[]{:S(2)}) collective-permute-start(bf16[1024,2048]{1,0:T(8,128)(2,1)} %get-tuple-element.337), channel_id=1, source_target_pairs={{0,2},{1,3},{2,0},{3,1},{4,6},{5,7},{6,4},{7,5},{8,10},{9,11},{10,... | collective-permute-start | bytes 12582920 | tf_op jit(solution)/shard_map/ppermute | solution.py:623
  366.0 58.2 %collective-permute-start.30 = (bf16[8192,128]{1,0:T(8,128)(2,1)}, bf16[8192,128]{1,0:T(8,128)(2,1)}, u32[]{:S(2)}, u32[]{:S(2)}) collective-permute-start(bf16[8192,128]{1,0:T(8,128)(2,1)} %bitcast.112), channel_id=1, source_target_pairs={{8,16},{9,17},{10,18},{11,19},{12,20},{13,21},{14,22},{15,23},{16,... | collective-permute-start | bytes 6291464 | tf_op jit(solution)/shard_map/ppermute | solution.py:623
  368.3 38.5 %collective-permute-start.31 = (bf16[6144,128]{1,0:T(8,128)(2,1)}, bf16[6144,128]{1,0:T(8,128)(2,1)}, u32[]{:S(2)}, u32[]{:S(2)}) collective-permute-start(bf16[6144,128]{1,0:T(8,128)(2,1)} %bitcast.94), channel_id=1, source_target_pairs={{0,8},{1,9},{2,10},{3,11},{4,12},{5,13},{6,14},{7,15},{24,16},{25,... | collective-permute-start | bytes 4718600 | tf_op jit(solution)/shard_map/ppermute | solution.py:623
  369.6 18.9 %collective-permute-start.28 = (bf16[2048,128]{1,0:T(8,128)(2,1)}, bf16[2048,128]{1,0:T(8,128)(2,1)S(1)}, u32[]{:S(2)}, u32[]{:S(2)}) collective-permute-start(bf16[2048,128]{1,0:T(8,128)(2,1)} %bitcast.119), channel_id=1, source_target_pairs={{8,0},{9,1},{10,2},{11,3},{12,4},{13,5},{14,6},{15,7},{16,24},{17,... | collective-permute-start | bytes 1572872 | tf_op jit(solution)/shard_map/ppermute | solution.py:623
  396.2 46.3 %collective-permute-start.35 = (bf16[256,2048]{1,0:T(8,128)(2,1)}, bf16[256,2048]{1,0:T(8,128)(2,1)}, u32[]{:S(2)}, u32[]{:S(2)}) collective-permute-start(bf16[256,2048]{1,0:T(8,128)(2,1)} %get-tuple-element.358), channel_id=1, source_target_pairs={{0,4},{1,5},{2,6},{3,7},{4,0},{5,1},{6,2},{7,3},{8,12},{9,13},{10,... | collective-permute-start | bytes 3145736 | tf_op jit(solution)/shard_map/ppermute | solution.py:623
  396.5 47.9 %collective-permute-start.36 = (bf16[256,2048]{1,0:T(8,128)(2,1)}, bf16[256,2048]{1,0:T(8,128)(2,1)}, u32[]{:S(2)}, u32[]{:S(2)}) collective-permute-start(bf16[256,2048]{1,0:T(8,128)(2,1)} %get-tuple-element.359), channel_id=1, source_target_pairs={{0,1},{1,0},{2,3},{3,2},{4,5},{5,4},{6,7},{7,6},{8,9},{9,8},{10,11... | collective-permute-start | bytes 3145736 | tf_op jit(solution)/shard_map/ppermute | solution.py:623
  406.8 53.9 %collective-permute-start.38 = (bf16[6144,128]{1,0:T(8,128)(2,1)}, bf16[6144,128]{1,0:T(8,128)(2,1)}, u32[]{:S(2)}, u32[]{:S(2)}) collective-permute-start(bf16[6144,128]{1,0:T(8,128)(2,1)} %bitcast.93), channel_id=1, source_target_pairs={{0,8},{1,9},{2,10},{3,11},{4,12},{5,13},{6,14},{7,15},{24,16},{25,... | collective-permute-start | bytes 4718600 | tf_op jit(solution)/shard_map/ppermute | solution.py:623
  408.1 19.4 %all-to-all-start.4 = ((bf16[4,512,128]{2,1,0:T(8,128)(2,1)}), bf16[4,512,128]{2,1,0:T(8,128)(2,1)S(1)}, u32[]{:S(2)}, u32[]{:S(2)}) async-start(bf16[4,512,128]{2,1,0:T(8,128)(2,1)} %get-tuple-element.339), calls=%async_computation.4 | async-start | bytes 1048576 | tf_op jit(solution)/shard_map/all_to_all | solution.py:640
  424.2 32.3 %collective-permute-start.39 = (bf16[4096,128]{1,0:T(8,128)(2,1)}, bf16[4096,128]{1,0:T(8,128)(2,1)}, u32[]{:S(2)}, u32[]{:S(2)}) collective-permute-start(bf16[4096,128]{1,0:T(8,128)(2,1)} %bitcast.115), channel_id=1, source_target_pairs={{8,16},{9,17},{10,18},{11,19},{12,20},{13,21},{14,22},{15,23},{16,... | collective-permute-start | bytes 3145736 | tf_op jit(solution)/shard_map/ppermute | solution.py:623
  432.9 34.9 %collective-permute-start.37 = (bf16[4096,128]{1,0:T(8,128)(2,1)}, bf16[4096,128]{1,0:T(8,128)(2,1)}, u32[]{:S(2)}, u32[]{:S(2)}) collective-permute-start(bf16[4096,128]{1,0:T(8,128)(2,1)} %bitcast.114), channel_id=1, source_target_pairs={{8,0},{9,1},{10,2},{11,3},{12,4},{13,5},{14,6},{15,7},{16,24},{17,... | collective-permute-start | bytes 3145736 | tf_op jit(solution)/shard_map/ppermute | solution.py:623
  442.4 36.8 %collective-permute-start.32 = (bf16[256,2048]{1,0:T(8,128)(2,1)}, bf16[256,2048]{1,0:T(8,128)(2,1)}, u32[]{:S(2)}, u32[]{:S(2)}) collective-permute-start(bf16[256,2048]{1,0:T(8,128)(2,1)} %get-tuple-element.345), channel_id=1, source_target_pairs={{0,4},{1,5},{2,6},{3,7},{4,0},{5,1},{6,2},{7,3},{8,12},{9,13},{10,... | collective-permute-start | bytes 3145736 | tf_op jit(solution)/shard_map/ppermute | solution.py:623
  444.4 34.8 %collective-permute-start.33 = (bf16[256,2048]{1,0:T(8,128)(2,1)}, bf16[256,2048]{1,0:T(8,128)(2,1)}, u32[]{:S(2)}, u32[]{:S(2)}) collective-permute-start(bf16[256,2048]{1,0:T(8,128)(2,1)} %get-tuple-element.346), channel_id=1, source_target_pairs={{0,1},{1,0},{2,3},{3,2},{4,5},{5,4},{6,7},{7,6},{8,9},{9,8},{10,11... | collective-permute-start | bytes 3145736 | tf_op jit(solution)/shard_map/ppermute | solution.py:623
  453.5 17.5 %all-to-all-start.5 = ((f32[32,1,896]{2,1,0:T(1,128)}), f32[32,1,896]{2,1,0:T(1,128)S(1)}, u32[]{:S(2)}, u32[]{:S(2)}) async-start(f32[32,1,896]{2,1,0:T(1,128)} %copy.137), calls=%async_computation.5 | async-start | bytes 229376 | tf_op jit(solution)/shard_map/all_to_all | solution.py:643
  456.5 19.6 %collective-permute-start.34 = (bf16[2048,128]{1,0:T(8,128)(2,1)}, bf16[2048,128]{1,0:T(8,128)(2,1)S(1)}, u32[]{:S(2)}, u32[]{:S(2)}) collective-permute-start(bf16[2048,128]{1,0:T(8,128)(2,1)} %bitcast.118), channel_id=1, source_target_pairs={{8,0},{9,1},{10,2},{11,3},{12,4},{13,5},{14,6},{15,7},{16,24},{17,... | collective-permute-start | bytes 1572872 | tf_op jit(solution)/shard_map/ppermute | solution.py:623
  463.1 43.2 %collective-permute-start.45 = (bf16[4096,128]{1,0:T(8,128)(2,1)}, bf16[4096,128]{1,0:T(8,128)(2,1)}, u32[]{:S(2)}, u32[]{:S(2)}) collective-permute-start(bf16[4096,128]{1,0:T(8,128)(2,1)} %bitcast.113), channel_id=1, source_target_pairs={{8,16},{9,17},{10,18},{11,19},{12,20},{13,21},{14,22},{15,23},{16,... | collective-permute-start | bytes 3145736 | tf_op jit(solution)/shard_map/ppermute | solution.py:623
  471.0 19.2 %all-to-all-start.6 = ((bf16[4,1024,128]{2,1,0:T(8,128)(2,1)}), bf16[4,1024,128]{2,1,0:T(8,128)(2,1)}, u32[]{:S(2)}, u32[]{:S(2)}) async-start(bf16[4,1024,128]{2,1,0:T(8,128)(2,1)} %get-tuple-element.375), calls=%async_computation.6 | async-start | bytes 2097152 | tf_op jit(solution)/shard_map/all_to_all | solution.py:640
  483.6 15.1 %collective-permute-start.40 = (bf16[256,1024]{1,0:T(8,128)(2,1)}, bf16[256,1024]{1,0:T(8,128)(2,1)}, u32[]{:S(2)}, u32[]{:S(2)}) collective-permute-start(bf16[256,1024]{1,0:T(8,128)(2,1)} %get-tuple-element.373), channel_id=1, source_target_pairs={{0,1},{1,0},{2,3},{3,2},{4,5},{5,4},{6,7},{7,6},{8,9},{9,8},{10,11... | collective-permute-start | bytes 1572872 | tf_op jit(solution)/shard_map/ppermute | solution.py:623
  485.1 16.4 %collective-permute-start.41 = (bf16[256,1024]{1,0:T(8,128)(2,1)}, bf16[256,1024]{1,0:T(8,128)(2,1)}, u32[]{:S(2)}, u32[]{:S(2)}) collective-permute-start(bf16[256,1024]{1,0:T(8,128)(2,1)} %get-tuple-element.374), channel_id=1, source_target_pairs={{0,4},{1,5},{2,6},{3,7},{4,0},{5,1},{6,2},{7,3},{8,12},{9,13},{10,... | collective-permute-start | bytes 1572872 | tf_op jit(solution)/shard_map/ppermute | solution.py:623
  486.8 23.6 %collective-permute-start.44 = (bf16[2048,128]{1,0:T(8,128)(2,1)}, bf16[2048,128]{1,0:T(8,128)(2,1)}, u32[]{:S(2)}, u32[]{:S(2)}) collective-permute-start(bf16[2048,128]{1,0:T(8,128)(2,1)} %bitcast.72), channel_id=1, source_target_pairs={{8,0},{9,1},{10,2},{11,3},{12,4},{13,5},{14,6},{15,7},{16,24},{17,... | collective-permute-start | bytes 1572872 | tf_op jit(solution)/shard_map/ppermute | solution.py:623
  490.2 22.5 %all-to-all-start.8 = ((bf16[4,512,128]{2,1,0:T(8,128)(2,1)}), bf16[4,512,128]{2,1,0:T(8,128)(2,1)S(1)}, u32[]{:S(2)}, u32[]{:S(2)}) async-start(bf16[4,512,128]{2,1,0:T(8,128)(2,1)} %get-tuple-element.392), calls=%async_computation.8 | async-start | bytes 1048576 | tf_op jit(solution)/shard_map/all_to_all | solution.py:640
  493.7 23.3 %collective-permute-start.42 = (bf16[256,1024]{1,0:T(8,128)(2,1)}, bf16[256,1024]{1,0:T(8,128)(2,1)}, u32[]{:S(2)}, u32[]{:S(2)}) collective-permute-start(bf16[256,1024]{1,0:T(8,128)(2,1)} %get-tuple-element.379), channel_id=1, source_target_pairs={{0,1},{1,0},{2,3},{3,2},{4,5},{5,4},{6,7},{7,6},{8,9},{9,8},{10,11... | collective-permute-start | bytes 1572872 | tf_op jit(solution)/shard_map/ppermute | solution.py:623
  498.7 19.2 %collective-permute-start.43 = (bf16[256,1024]{1,0:T(8,128)(2,1)}, bf16[256,1024]{1,0:T(8,128)(2,1)}, u32[]{:S(2)}, u32[]{:S(2)}) collective-permute-start(bf16[256,1024]{1,0:T(8,128)(2,1)} %get-tuple-element.380), channel_id=1, source_target_pairs={{0,4},{1,5},{2,6},{3,7},{4,0},{5,1},{6,2},{7,3},{8,12},{9,13},{10,... | collective-permute-start | bytes 1572872 | tf_op jit(solution)/shard_map/ppermute | solution.py:623
  508.3 17.2 %collective-permute-start.46 = (bf16[2048,128]{1,0:T(8,128)(2,1)}, bf16[2048,128]{1,0:T(8,128)(2,1)}, u32[]{:S(2)}, u32[]{:S(2)}) collective-permute-start(bf16[2048,128]{1,0:T(8,128)(2,1)} %bitcast.120), channel_id=1, source_target_pairs={{8,0},{9,1},{10,2},{11,3},{12,4},{13,5},{14,6},{15,7},{16,24},{17,... | collective-permute-start | bytes 1572872 | tf_op jit(solution)/shard_map/ppermute | solution.py:623
  513.5 14.4 %all-to-all-start.7 = ((bf16[4,512,128]{2,1,0:T(8,128)(2,1)}), bf16[4,512,128]{2,1,0:T(8,128)(2,1)S(1)}, u32[]{:S(2)}, u32[]{:S(2)}) async-start(bf16[4,512,128]{2,1,0:T(8,128)(2,1)} %get-tuple-element.391), calls=%async_computation.7 | async-start | bytes 1048576 | tf_op jit(solution)/shard_map/all_to_all | solution.py:640
  527.9 13.1 %all-to-all-start.9 = ((bf16[4,512,128]{2,1,0:T(8,128)(2,1)}), bf16[4,512,128]{2,1,0:T(8,128)(2,1)}, u32[]{:S(2)}, u32[]{:S(2)}) async-start(bf16[4,512,128]{2,1,0:T(8,128)(2,1)} %get-tuple-element.402), calls=%async_computation.9 | async-start | bytes 1048576 | tf_op jit(solution)/shard_map/all_to_all | solution.py:640
  (9 other events, 60.1 us)

commit v4 on v3

--- a/solution.py
+++ b/solution.py
@@ -334,25 +334,27 @@
 
 
 def join_kernel(n, *refs):
-    total = dot(refs[0][...], refs[n][...], NN)
+    acts = [r[...].reshape(-1, r.shape[-1]) for r in refs[:n]]
+    total = dot(acts[0], refs[n][...], NN)
     for j in range(1, n):
-        total += dot(refs[j][...], refs[n + j][...], NN)
+        total += dot(acts[j], refs[n + j][...], NN)
     refs[2 * n][...] = total.astype(BF)
 
 
 def join_call(line, acts, weights, sent):
     rows, width = acts[0].shape[0], weights[0].shape[1]
-    block = rows // 4
+    block, part = rows // 4, width // 4
     first = 1 if sent else 0
+    acts = [a.reshape(2, 2, block, a.shape[1]) for a in acts]
     return run_kernel(
         functools.partial(join_kernel, len(acts)),
         shaped((rows // 2, width)),
-        [pl.BlockSpec((block, a.shape[1]), lambda r: (2 * r + first, 0)) for a in acts]
-        + [whole(w.shape) for w in weights],
-        pl.BlockSpec((block, width), lambda r: (r, 0)),
+        [pl.BlockSpec((2, None) + a.shape[2:], lambda c: (0, first, 0, 0), pipeline_mode=pl.Buffered(1)) for a in acts]
+        + [pl.BlockSpec((w.shape[0], part), lambda c: (0, c)) for w in weights],
+        pl.BlockSpec((rows // 2, part), lambda c: (0, c)),
         (*acts, *weights),
         "join",
-        grid=(2,),
+        grid=(4,),
         line=line,
     )
 
@@ -525,30 +527,25 @@
 
 
 def core_kernel(kt, kx, kb, ot, ox, ob, x1, t1):
-    half = kt.shape[1] // 2
-    add = lambda a, b, cut: (a[:, cut].astype(F32) + b[:, cut].astype(F32)).astype(BF)
-    left, right = slice(0, half), slice(half, 2 * half)
-    x1[:, left] = add(kb, ob, left)
-    x1[:, right] = add(kx, ox, left)
-    t1[:, left] = add(kb, ob, right)
-    t1[:, right] = add(kt, ot, right)
+    half = kb.shape[1] // 2
+    add = lambda a, b: (a.astype(F32) + b.astype(F32)).astype(BF)
+    x1[:, :half] = add(kb[:, :half], ob[:, :half])
+    x1[:, half:] = add(kx[...], ox[...])
+    t1[:, :half] = add(kb[:, half:], ob[:, half:])
+    t1[:, half:] = add(kt[...], ot[...])
 
 
 def cross_kernel(kt, kx, ot, ox, x1, t1, t2, x2):
-    half = kt.shape[1] // 2
-    left, right = slice(0, half), slice(half, 2 * half)
-    add = lambda a, b, c: (a.astype(F32) + b.astype(F32) + c.astype(F32)).astype(BF)
-    t2[...] = add(kt[:, left], ot[:, left], x1[:, left])
-    x2[...] = add(kx[:, right], ox[:, right], t1[:, left])
+    add = lambda a, b, c: (a[...].astype(F32) + b[...].astype(F32) + c[...].astype(F32)).astype(BF)
+    t2[...] = add(kt, ot, x1)
+    x2[...] = add(kx, ox, t1)
 
 
 def face_sum(place, kept, other, x1, t1, t2, x2, natural):
     half = kept.shape[1] // 2
     left, right = slice(0, half), slice(half, 2 * half)
-    natural[:, left] = kept[:, left].astype(F32) + other[:, left].astype(F32) + x1[:, right].astype(F32) + t2[...].astype(F32)
-    natural[:, right] = (
-        kept[:, right].astype(F32) + other[:, right].astype(F32) + t1[:, right].astype(F32) + x2[...].astype(F32)
-    )
+    natural[:, left] = kept[:, left].astype(F32) + other[:, left].astype(F32) + x1[...].astype(F32) + t2[...].astype(F32)
+    natural[:, right] = kept[:, right].astype(F32) + other[:, right].astype(F32) + t1[...].astype(F32) + x2[...].astype(F32)
     return jnp.concatenate([natural[:, spot(place, b, half // 2)] for b in range(4)], axis=1)
 
 
@@ -573,10 +570,11 @@
     block = rows // STEPS
     spec = pl.BlockSpec((block, width), lambda r: (r, 0))
     half = pl.BlockSpec((block, width // 2), lambda r: (r, 0))
+    second = pl.BlockSpec((block, width // 2), lambda r: (r, 1))
     vector = pl.BlockSpec((1, width), lambda r: (0, 0))
     return run_kernel(
         kernel, shaped((rows, width)),
-        [SCALARS] + [spec] * len(rows_in) + [vector] * len(row_in) + [spec] * 4 + [half] * 2,
+        [SCALARS] + [spec] * len(rows_in) + [vector] * len(row_in) + [spec] * 2 + [second] * 2 + [half] * 2,
         spec, (place, *rows_in, *row_in, *sums), name, grid=(STEPS,), scratch=[pltpu.VMEM((block, width), F32)],
         line=line,
     )
@@ -703,7 +701,7 @@
             self.rows, self.width = self.kept.shape[0] // 4, self.kept.shape[1]
             spec = pl.BlockSpec((self.rows // STEPS, self.width), lambda r: (r, 0))
             x1, t1 = run_kernel(
-                core_kernel, [shaped((self.rows, self.width))] * 2, self.block_specs(1, 2, 3) * 2, [spec] * 2,
+                core_kernel, [shaped((self.rows, self.width))] * 2, self.block_specs((1, 1), (2, 0), (3, None)) * 2, [spec] * 2,
                 (self.kept,) * 3 + (self.other,) * 3, "core", grid=(STEPS,), line=line,
             )
             self.x1, self.t1 = flip(x1, 4), flip(t1, 1)
@@ -711,15 +709,18 @@
         def block_specs(self, *blocks):
             block = self.rows // STEPS
             return [
-                pl.BlockSpec((block, self.width), functools.partial(lambda k, r: (k * STEPS + r, 0), k)) for k in blocks
+                pl.BlockSpec(
+                    (block, self.width if half is None else self.width // 2),
+                    functools.partial(lambda k, h, r: (k * STEPS + r, h), k, half or 0),
+                )
+                for k, half in blocks
             ]
 
         def first_came(self, line):
             rows, width = self.rows, self.width
-            spec = pl.BlockSpec((rows // STEPS, width), lambda r: (r, 0))
             half = pl.BlockSpec((rows // STEPS, width // 2), lambda r: (r, 0))
             t2, x2 = run_kernel(
-                cross_kernel, [shaped((rows, width // 2))] * 2, self.block_specs(1, 2) * 2 + [spec] * 2, [half] * 2,
+                cross_kernel, [shaped((rows, width // 2))] * 2, self.block_specs((1, 0), (2, 1)) * 2 + [half] * 2, [half] * 2,
                 (self.kept, self.kept, self.other, self.other, self.x1, self.t1), "cross", grid=(STEPS,), line=line,
             )
             self.t2, self.x2 = flip(t2, 1), flip(x2, 4)

time: 554 us -> 545 us (0.984)
  waiting for transfers between devices: 99.3 us -> 90.9 us
  Pallas kernels: 263 us -> 257 us
    ppermute x47, waiting for transfers between devices: 68.9 us -> 60.4 us  [permute(): lax.ppermute(v.reshape(-1, v.shape[-1]), AXES, pairs).reshape(v.shape)]
  transfers between devices with their start and end apart: 56 -> 56, of which waited for: 15 -> 17; matrix products, arithmetic and copies ran while one was open for 3% -> 3% of each run, Pallas kernels for 47% -> 47%
where the time goes in v4:
time: 545 us; the launch traced here: 534 us
  Pallas kernels  257 us (47%)
  starting transfers between devices  132 us (24%)
  waiting for transfers between devices  90.9 us (17%)
  blocking collectives  33.7 us (6%)
  local copies, waits for them, and re-layouts  17.9 us (3%)
    pallas_call x72, Pallas kernels, run_kernel(): pl.pallas_call(inner, grid=grid, out_shape=outs, in_specs=in_specs, out_s...  257 us
    ppermute x47, starting transfers between devices, permute(): lax.ppermute(v.reshape(-1, v.shape[-1]), AXES, pairs).reshape(v.shape)  98.1 us
    ppermute x47, waiting for transfers between devices, permute(): lax.ppermute(v.reshape(-1, v.shape[-1]), AXES, pairs).reshape(v.shape)  60.4 us
    all_to_all x1, blocking collectives, swap_all(): return lax.all_to_all(v, AXES, split_axis=0, concat_axis=0, tiled=True)  33.7 us
    all_to_all x8, starting transfers between devices, swap_ring(): lax.all_to_all(v, AXES, split_axis=0, concat_axis=0, tiled=True, axis_ind...  31.6 us
    all_to_all x8, waiting for transfers between devices, swap_ring(): lax.all_to_all(v, AXES, split_axis=0, concat_axis=0, tiled=True, axis_ind...  30.1 us
  transfers between devices with their start and end apart: 56, of which 17 were waited for; matrix products, arithmetic and copies ran while one was open for 3% of the time, Pallas kernels for 47%

profile of v4, /device:TPU:8, one launch (start us, length us, event | category | flops | bytes accessed | tf_op | source)
XLA Modules:
  0.0 534.0 jit_solution(10839646763378519376)
XLA Ops:
  1.2 3.5 piece.3
  4.7 4.3 all-to-all-start
  9.0 3.6 piece.4
  12.6 10.9 %all-to-all-done.refs_0_ = bf16[4,1024,128]{2,1,0:T(8,128)(2,1)} async-done(((bf16[4,1024,128]{2,1,0:T(8,128)(2,1)}), bf16[4,1024,128]{2,1,0:T(8,128)(2,1)}, u32[]{:S(2)}, u32[]{:S(2)}) %all-to-all-start) | async-done | bytes 1048608 | tf_op jit(solution)/shard_map/all_to_all | solution.py:638
  23.5 4.2 all-to-all-start.1
  29.1 13.2 %all-to-all-done.1.refs_0_ = bf16[4,1024,128]{2,1,0:T(8,128)(2,1)} async-done(((bf16[4,1024,128]{2,1,0:T(8,128)(2,1)}), bf16[4,1024,128]{2,1,0:T(8,128)(2,1)}, u32[]{:S(2)}, u32[]{:S(2)}) %all-to-all-start.1) | async-done | bytes 1048608 | tf_op jit(solution)/shard_map/all_to_all | solution.py:638
  42.4 4.5 own.1
  48.8 5.5 %collective-permute-done = bf16[4096,128]{1,0:T(8,128)(2,1)} collective-permute-done((bf16[4096,128]{1,0:T(8,128)(2,1)}, bf16[4096,128]{1,0:T(8,128)(2,1)}, u32[]{:S(2)}, u32[]{:S(2)}) %collective-permute-start) | collective-permute-done | bytes 1048608 | tf_op jit(solution)/shard_map/ppermute | solution.py:621
  56.4 3.5 collective-permute-start.3
  63.8 33.7 %all_to_all.62 = f32[32,1,896]{2,1,0:T(1,128)S(1)} all-to-all(f32[32,1,896]{2,1,0:T(1,128)S(1)} %copy.136), channel_id=1, replica_groups=mesh['dp'=16,'tensor'=2] {'dp','tensor'}, dimensions={0} | all-to-all | bytes 229376 | tf_op jit(solution)/shard_map/all_to_all | solution.py:641
  98.2 3.5 collective-permute-start.4
  114.6 11.0 %collective-permute-done.4 = bf16[4096,128]{1,0:T(8,128)(2,1)} collective-permute-done((bf16[4096,128]{1,0:T(8,128)(2,1)}, bf16[4096,128]{1,0:T(8,128)(2,1)}, u32[]{:S(2)}, u32[]{:S(2)}) %collective-permute-start.4) | collective-permute-done | bytes 1048608 | tf_op jit(solution)/shard_map/ppermute | solution.py:621
  130.1 6.0 %turns.1 = (f32[2048,128]{1,0:T(8,128)}, f32[2048,128]{1,0:T(8,128)}, f32[2048,128]{1,0:T(8,128)}, f32[8,128]{1,0:T(8,128)}) custom-call(s32[11]{0:T(128)} %concatenate.6.refs_0_.refs_21_, s32[4,128]{1,0:T(4,128)} %get-tuple-element.239.refs_1_.refs_20_, f32[8,128]{1,0:T(8,128)} %get-tuple-element.240.refs_2_), custom_call_target="tpu_custom_call", output_to_operand_aliasing={{3}: (2, {})} | custom-call | tf_op jit(solution)/shard_map/turns/pallas_call | solution.py:71
  136.2 3.5 collective-permute-start.14
  139.7 3.6 piece.5
  143.3 4.3 all-to-all-start.3
  149.3 14.1 %collective-permute-done.14 = bf16[4096,128]{1,0:T(8,128)(2,1)} collective-permute-done((bf16[4096,128]{1,0:T(8,128)(2,1)}, bf16[4096,128]{1,0:T(8,128)(2,1)}, u32[]{:S(2)}, u32[]{:S(2)}) %collective-permute-start.14) | collective-permute-done | bytes 1048608 | tf_op jit(solution)/shard_map/ppermute | solution.py:621
  163.4 3.5 collective-permute-start.17
  167.6 18.9 %feed.3 = (bf16[2048,256]{1,0:T(8,128)(2,1)}, bf16[2048,256]{1,0:T(8,128)(2,1)}, bf16[256,2048]{1,0:T(8,128)(2,1)}, bf16[256,2048]{1,0:T(8,128)(2,1)}, f32[2,204...) custom-call(bf16[2,256,2048]{2,1,0:T(8,128)(2,1)} %get-tuple-element, ...), custom_call_target="tpu_custom_call", output_to_operand_aliasing={{8}: (17, {})} | custom-call | tf_op jit(solution)/shard_map/feed/pallas_call | solution.py:71
  186.5 3.3 collective-permute-done.17
  191.3 2.6 cat.9
  196.2 2.8 collective-permute-start.18
  201.3 12.9 %collective-permute-start.22 = (bf16[6144,128]{1,0:T(8,128)(2,1)}, bf16[6144,128]{1,0:T(8,128)(2,1)}, u32[]{:S(2)}, u32[]{:S(2)}) collective-permute-start(bf16[6144,128]{1,0:T(8,128)(2,1)} %bitcast.103), channel_id=1, source_target_pairs={{0,8},{1,9},{2,10},{3,11},{4,12},{5,13},{6,14},{7,15},{24,16},{25,... | collective-permute-start | bytes 4718600 | tf_op jit(solution)/shard_map/ppermute | solution.py:621
  214.1 18.9 %feed.4 = (bf16[2048,256]{1,0:T(8,128)(2,1)}, bf16[2048,256]{1,0:T(8,128)(2,1)}, bf16[256,2048]{1,0:T(8,128)(2,1)}, bf16[256,2048]{1,0:T(8,128)(2,1)}, f32[2,204...) custom-call(bf16[2,256,2048]{2,1,0:T(8,128)(2,1)} %get-tuple-element, ...), custom_call_target="tpu_custom_call", output_to_operand_aliasing={{8}: (17, {})} | custom-call | tf_op jit(solution)/shard_map/feed/pallas_call | solution.py:71
  233.0 8.5 %collective-permute-done.19 = bf16[8192,128]{1,0:T(8,128)(2,1)} collective-permute-done((bf16[8192,128]{1,0:T(8,128)(2,1)}, bf16[8192,128]{1,0:T(8,128)(2,1)}, u32[]{:S(2)}, u32[]{:S(2)}) %collective-permute-start.19) | collective-permute-done | bytes 2097184 | tf_op jit(solution)/shard_map/ppermute | solution.py:621
  241.5 2.6 collective-permute-start.21
  245.5 37.9 %attention.1 = (bf16[2048,256]{1,0:T(8,128)(2,1)}, bf16[2048,768]{1,0:T(8,128)(2,1)}, bf16[768,2048]{1,0:T(8,128)(2,1)}, bf16[256,2048]{1,0:T(8,128)(2,1)}, f32[...) custom-call(bf16[2,256,2048]{2,1,0:T(8,128)(2,1)} %get-tuple-element, ...), custom_call_target="tpu_custom_call", output_to_operand_aliasing={{8}: (25, {})} | custom-call | tf_op jit(solution)/shard_map/attention/pallas_call | solution.py:71
  283.5 2.5 sum.15
  289.6 2.4 sum.16
  292.1 3.9 collective-permute-start.25
  296.5 29.8 %feed.5 = (bf16[2048,512]{1,0:T(8,128)(2,1)}, bf16[2048,512]{1,0:T(8,128)(2,1)}, bf16[512,2048]{1,0:T(8,128)(2,1)}, bf16[512,2048]{1,0:T(8,128)(2,1)}, f32[2,204...) custom-call(bf16[2,256,2048]{2,1,0:T(8,128)(2,1)} %get-tuple-element, ...), custom_call_target="tpu_custom_call", output_to_operand_aliasing={{10}: (17, {})} | custom-call | tf_op jit(solution)/shard_map/feed/pallas_call | solution.py:71
  328.4 12.0 %join.4 = (bf16[1024,2048]{1,0:T(8,128)(2,1)}, f32[8,128]{1,0:T(8,128)}) custom-call(bf16[2,2,512,256]{3,2,1,0:T(8,128)(2,1)} %bitcast.116, bf16[2,2,512,256]{3,2,1,0:T(8,128)(2,1)} %bitcast.118, bf16[2,2,512,768]{3,2,1,0:T(8,128)(2,1)} %bitcast.104, bf16[2,2,512,512]{3,2,1,0:T(8,128)(2,1)} %bitcast.108, ...), custom_call_target="tpu_custom_call", output_to_operand_aliasing={{1}: (8, {})} | custom-call | tf_op jit(solution)/shard_map/join/pallas_call | solution.py:71
  342.4 9.5 %join.5 = (bf16[1024,2048]{1,0:T(8,128)(2,1)}, f32[8,128]{1,0:T(8,128)}) custom-call(bf16[2,2,512,256]{3,2,1,0:T(8,128)(2,1)} %bitcast.110, bf16[2,2,512,256]{3,2,1,0:T(8,128)(2,1)} %bitcast.112, bf16[2,2,512,256]{3,2,1,0:T(8,128)(2,1)} %bitcast.114, bf16[2,2,512,512]{3,2,1,0:T(8,128)(2,1)} %bitcast.106, ...), custom_call_target="tpu_custom_call", output_to_operand_aliasing={{1}: (8, {})} | custom-call | tf_op jit(solution)/shard_map/join/pallas_call | solution.py:71
  352.4 5.5 %collective-permute-done.24 = bf16[12288,128]{1,0:T(8,128)(2,1)} collective-permute-done((bf16[12288,128]{1,0:T(8,128)(2,1)}, bf16[12288,128]{1,0:T(8,128)(2,1)}, u32[]{:S(2)}, u32[]{:S(2)}) %collective-permute-start.24) | collective-permute-done | bytes 3145760 | tf_op jit(solution)/shard_map/ppermute | solution.py:621
  357.9 3.4 sum.19
  361.3 2.8 collective-permute-start.30
  365.4 5.9 %collective-permute-start.28 = (bf16[2048,128]{1,0:T(8,128)(2,1)}, bf16[2048,128]{1,0:T(8,128)(2,1)S(1)}, u32[]{:S(2)}, u32[]{:S(2)}) collective-permute-start(bf16[2048,128]{1,0:T(8,128)(2,1)} %bitcast.143), channel_id=1, source_target_pairs={{8,0},{9,1},{10,2},{11,3},{12,4},{13,5},{14,6},{15,7},{16,24},{17,... | collective-permute-start | bytes 1572872 | tf_op jit(solution)/shard_map/ppermute | solution.py:621
  371.3 12.1 %join.6 = (bf16[1024,2048]{1,0:T(8,128)(2,1)}, f32[8,128]{1,0:T(8,128)}) custom-call(bf16[2,2,512,256]{3,2,1,0:T(8,128)(2,1)} %bitcast.117, bf16[2,2,512,256]{3,2,1,0:T(8,128)(2,1)} %bitcast.119, bf16[2,2,512,768]{3,2,1,0:T(8,128)(2,1)} %bitcast.105, bf16[2,2,512,512]{3,2,1,0:T(8,128)(2,1)} %bitcast.109, ...), custom_call_target="tpu_custom_call", output_to_operand_aliasing={{1}: (8, {})} | custom-call | tf_op jit(solution)/shard_map/join/pallas_call | solution.py:71
  386.6 4.2 core.2
  392.4 6.3 %collective-permute-done.31 = bf16[6144,128]{1,0:T(8,128)(2,1)} collective-permute-done((bf16[6144,128]{1,0:T(8,128)(2,1)}, bf16[6144,128]{1,0:T(8,128)(2,1)}, u32[]{:S(2)}, u32[]{:S(2)}) %collective-permute-start.31) | collective-permute-done | bytes 1572896 | tf_op jit(solution)/shard_map/ppermute | solution.py:621
  400.0 3.5 all-to-all-start.4
  403.5 9.5 %join.7 = (bf16[1024,2048]{1,0:T(8,128)(2,1)}, f32[8,128]{1,0:T(8,128)}) custom-call(bf16[2,2,512,256]{3,2,1,0:T(8,128)(2,1)} %bitcast.111, bf16[2,2,512,256]{3,2,1,0:T(8,128)(2,1)} %bitcast.113, bf16[2,2,512,256]{3,2,1,0:T(8,128)(2,1)} %bitcast.115, bf16[2,2,512,512]{3,2,1,0:T(8,128)(2,1)} %bitcast.107, ...), custom_call_target="tpu_custom_call", output_to_operand_aliasing={{1}: (8, {})} | custom-call | tf_op jit(solution)/shard_map/join/pallas_call | solution.py:71
  412.9 2.4 sum.21
  415.4 3.0 collective-permute-start.39
  421.3 2.5 sum.22
  423.8 5.3 collective-permute-start.37
  429.1 4.2 core.3
  436.8 3.9 cross.2
  444.0 2.7 all-to-all-start.5
  450.9 2.4 sum.24
  453.3 4.6 collective-permute-start.45
  458.0 3.2 sum.25
  461.5 4.2 all-to-all-start.6
  469.5 3.9 cross.3
  476.8 2.9 collective-permute-start.44
  480.7 3.5 all-to-all-start.8
  485.7 2.5 unpiece.6
  492.0 4.8 output.1
  500.8 2.4 sum.28
  504.0 3.5 all-to-all-start.7
  508.3 5.3 input_grad.1
  515.8 2.4 sum.29
  518.2 4.2 all-to-all-start.9
  526.3 5.0 all-to-all-done.9.refs_0_
  (177 shorter events, 95.4 us)
Async XLA Ops:
  4.7 18.8 %all-to-all-start = ((bf16[4,1024,128]{2,1,0:T(8,128)(2,1)}), bf16[4,1024,128]{2,1,0:T(8,128)(2,1)}, u32[]{:S(2)}, u32[]{:S(2)}) async-start(bf16[4,1024,128]{2,1,0:T(8,128)(2,1)} %get-tuple-element.210), calls=%async_computation | async-start | bytes 2097152 | tf_op jit(solution)/shard_map/all_to_all | solution.py:638
  23.5 18.8 %all-to-all-start.1 = ((bf16[4,1024,128]{2,1,0:T(8,128)(2,1)}), bf16[4,1024,128]{2,1,0:T(8,128)(2,1)}, u32[]{:S(2)}, u32[]{:S(2)}) async-start(bf16[4,1024,128]{2,1,0:T(8,128)(2,1)} %get-tuple-element.214), calls=%async_computation.1 | async-start | bytes 2097152 | tf_op jit(solution)/shard_map/all_to_all | solution.py:638
  28.5 25.8 %collective-permute-start = (bf16[4096,128]{1,0:T(8,128)(2,1)}, bf16[4096,128]{1,0:T(8,128)(2,1)}, u32[]{:S(2)}, u32[]{:S(2)}) collective-permute-start(bf16[4096,128]{1,0:T(8,128)(2,1)} %bitcast.5), channel_id=1, source_target_pairs={{0,8},{1,9},{2,10},{3,11},{4,12},{5,13},{6,14},{7,15},{8,0},{9,1},... | collective-permute-start | bytes 3145736 | tf_op jit(solution)/shard_map/ppermute | solution.py:621
  42.3 17.6 %copy-start.16 = (s32[1,3]{1,0:T(1,128)S(1)}, s32[1,3]{1,0:T(1,128)}, u32[]{:S(2)}) copy-start(s32[1,3]{1,0:T(1,128)} %param.17) | copy-start | bytes 40
  42.3 17.7 %copy-start.7 = (f32[64]{0:T(128)S(1)}, f32[64]{0:T(128)}, u32[]{:S(2)}) copy-start(f32[64]{0:T(128)} %param.18) | copy-start | bytes 772
  42.3 17.7 %copy-start.8 = (f32[64]{0:T(128)S(1)}, f32[64]{0:T(128)}, u32[]{:S(2)}) copy-start(f32[64]{0:T(128)} %param.19) | copy-start | bytes 772
  42.3 17.7 %copy-start.9 = (f32[64]{0:T(128)S(1)}, f32[64]{0:T(128)}, u32[]{:S(2)}) copy-start(f32[64]{0:T(128)} %param.20) | copy-start | bytes 772
  42.3 17.7 %copy-start.10 = (f32[64]{0:T(128)S(1)}, f32[64]{0:T(128)}, u32[]{:S(2)}) copy-start(f32[64]{0:T(128)} %param.21) | copy-start | bytes 772
  42.4 17.7 %copy-start.11 = (bf16[192]{0:T(256)(128)(2,1)S(1)}, bf16[192]{0:T(256)(128)(2,1)}, u32[]{:S(2)}) copy-start(bf16[192]{0:T(256)(128)(2,1)} %param.23) | copy-start | bytes 1156
  42.4 17.7 %copy-start.12 = (bf16[256]{0:T(256)(128)(2,1)S(1)}, bf16[256]{0:T(256)(128)(2,1)}, u32[]{:S(2)}) copy-start(bf16[256]{0:T(256)(128)(2,1)} %param.27) | copy-start | bytes 1540
  46.9 54.9 %collective-permute-start.2 = (bf16[512,2048]{1,0:T(8,128)(2,1)}, bf16[512,2048]{1,0:T(8,128)(2,1)}, u32[]{:S(2)}, u32[]{:S(2)}) collective-permute-start(bf16[512,2048]{1,0:T(8,128)(2,1)} %bitcast.96), channel_id=1, source_target_pairs={{0,2},{1,3},{2,0},{3,1},{4,6},{5,7},{6,4},{7,5},{8,10},{9,11},{10,... | collective-permute-start | bytes 6291464 | tf_op jit(solution)/shard_map/ppermute | solution.py:621
  46.9 61.3 %collective-permute-start.6 = (bf16[512,2048]{1,0:T(8,128)(2,1)}, bf16[512,2048]{1,0:T(8,128)(2,1)}, u32[]{:S(2)}, u32[]{:S(2)}) collective-permute-start(bf16[512,2048]{1,0:T(8,128)(2,1)} %bitcast.97), channel_id=1, source_target_pairs={{0,1},{1,0},{2,3},{3,2},{4,5},{5,4},{6,7},{7,6},{8,9},{9,8},{10,11... | collective-permute-start | bytes 6291464 | tf_op jit(solution)/shard_map/ppermute | solution.py:621
  48.4 59.7 %collective-permute-start.5 = (bf16[512,2048]{1,0:T(8,128)(2,1)}, bf16[512,2048]{1,0:T(8,128)(2,1)}, u32[]{:S(2)}, u32[]{:S(2)}) collective-permute-start(bf16[512,2048]{1,0:T(8,128)(2,1)} %bitcast.98), channel_id=1, source_target_pairs={{0,4},{1,5},{2,6},{3,7},{4,0},{5,1},{6,2},{7,3},{8,12},{9,13},{10,... | collective-permute-start | bytes 6291464 | tf_op jit(solution)/shard_map/ppermute | solution.py:621
  56.4 41.9 %collective-permute-start.3 = (bf16[4096,128]{1,0:T(8,128)(2,1)}, bf16[4096,128]{1,0:T(8,128)(2,1)}, u32[]{:S(2)}, u32[]{:S(2)}) collective-permute-start(bf16[4096,128]{1,0:T(8,128)(2,1)} %bitcast.128), channel_id=1, source_target_pairs={{8,16},{9,17},{10,18},{11,19},{12,20},{13,21},{14,22},{15,23},{16,... | collective-permute-start | bytes 3145736 | tf_op jit(solution)/shard_map/ppermute | solution.py:621
  59.8 44.2 %collective-permute-start.1 = (bf16[4096,128]{1,0:T(8,128)(2,1)}, bf16[4096,128]{1,0:T(8,128)(2,1)}, u32[]{:S(2)}, u32[]{:S(2)}) collective-permute-start(bf16[4096,128]{1,0:T(8,128)(2,1)} %bitcast.8), channel_id=1, source_target_pairs={{0,8},{1,9},{2,10},{3,11},{4,12},{5,13},{6,14},{7,15},{8,0},{9,1},... | collective-permute-start | bytes 3145736 | tf_op jit(solution)/shard_map/ppermute | solution.py:621
  98.2 27.4 %collective-permute-start.4 = (bf16[4096,128]{1,0:T(8,128)(2,1)}, bf16[4096,128]{1,0:T(8,128)(2,1)}, u32[]{:S(2)}, u32[]{:S(2)}) collective-permute-start(bf16[4096,128]{1,0:T(8,128)(2,1)} %bitcast.126), channel_id=1, source_target_pairs={{8,16},{9,17},{10,18},{11,19},{12,20},{13,21},{14,22},{15,23},{16,... | collective-permute-start | bytes 3145736 | tf_op jit(solution)/shard_map/ppermute | solution.py:621
  101.7 26.2 %collective-permute-start.11 = (bf16[4096,128]{1,0:T(8,128)(2,1)}, bf16[4096,128]{1,0:T(8,128)(2,1)}, u32[]{:S(2)}, u32[]{:S(2)}) collective-permute-start(bf16[4096,128]{1,0:T(8,128)(2,1)} %bitcast.24), channel_id=1, source_target_pairs={{8,0},{9,1},{10,2},{11,3},{12,4},{13,5},{14,6},{15,7},{16,24},{17,... | collective-permute-start | bytes 3145736 | tf_op jit(solution)/shard_map/ppermute | solution.py:621
  110.5 25.7 %collective-permute-start.9 = (bf16[256,2048]{1,0:T(8,128)(2,1)}, bf16[256,2048]{1,0:T(8,128)(2,1)}, u32[]{:S(2)}, u32[]{:S(2)}) collective-permute-start(bf16[256,2048]{1,0:T(8,128)(2,1)} %slice_bitcast_fusion.1), channel_id=1, source_target_pairs={{0,1},{1,0},{2,3},{3,2},{4,5},{5,4},{6,7},{7,6},{8,9},{9,8},{10,11... | collective-permute-start | bytes 3145736 | tf_op jit(solution)/shard_map/ppermute | solution.py:621
  114.1 29.1 %collective-permute-start.10 = (bf16[256,2048]{1,0:T(8,128)(2,1)}, bf16[256,2048]{1,0:T(8,128)(2,1)}, u32[]{:S(2)}, u32[]{:S(2)}) collective-permute-start(bf16[256,2048]{1,0:T(8,128)(2,1)} %slice_bitcast_fusion), channel_id=1, source_target_pairs={{0,4},{1,5},{2,6},{3,7},{4,0},{5,1},{6,2},{7,3},{8,12},{9,13},{10,... | collective-permute-start | bytes 3145736 | tf_op jit(solution)/shard_map/ppermute | solution.py:621
  125.6 23.7 %collective-permute-start.15 = (bf16[4096,128]{1,0:T(8,128)(2,1)}, bf16[4096,128]{1,0:T(8,128)(2,1)}, u32[]{:S(2)}, u32[]{:S(2)}) collective-permute-start(bf16[4096,128]{1,0:T(8,128)(2,1)} %bitcast.28), channel_id=1, source_target_pairs={{8,0},{9,1},{10,2},{11,3},{12,4},{13,5},{14,6},{15,7},{16,24},{17,... | collective-permute-start | bytes 3145736 | tf_op jit(solution)/shard_map/ppermute | solution.py:621
  127.9 39.7 %collective-permute-start.8 = (bf16[512,2048]{1,0:T(8,128)(2,1)}, bf16[512,2048]{1,0:T(8,128)(2,1)}, u32[]{:S(2)}, u32[]{:S(2)}) collective-permute-start(bf16[512,2048]{1,0:T(8,128)(2,1)} %bitcast.20), channel_id=1, source_target_pairs={{0,2},{1,3},{2,0},{3,1},{4,6},{5,7},{6,4},{7,5},{8,10},{9,11},{10,... | collective-permute-start | bytes 6291464 | tf_op jit(solution)/shard_map/ppermute | solution.py:621
  127.9 39.7 %collective-permute-start.7 = (bf16[512,2048]{1,0:T(8,128)(2,1)}, bf16[512,2048]{1,0:T(8,128)(2,1)}, u32[]{:S(2)}, u32[]{:S(2)}) collective-permute-start(bf16[512,2048]{1,0:T(8,128)(2,1)} %bitcast.18), channel_id=1, source_target_pairs={{0,2},{1,3},{2,0},{3,1},{4,6},{5,7},{6,4},{7,5},{8,10},{9,11},{10,... | collective-permute-start | bytes 6291464 | tf_op jit(solution)/shard_map/ppermute | solution.py:621
  136.2 27.3 %collective-permute-start.14 = (bf16[4096,128]{1,0:T(8,128)(2,1)}, bf16[4096,128]{1,0:T(8,128)(2,1)}, u32[]{:S(2)}, u32[]{:S(2)}) collective-permute-start(bf16[4096,128]{1,0:T(8,128)(2,1)} %bitcast.122), channel_id=1, source_target_pairs={{8,16},{9,17},{10,18},{11,19},{12,20},{13,21},{14,22},{15,23},{16,... | collective-permute-start | bytes 3145736 | tf_op jit(solution)/shard_map/ppermute | solution.py:621
  143.3 23.7 %collective-permute-start.12 = (bf16[256,2048]{1,0:T(8,128)(2,1)}, bf16[256,2048]{1,0:T(8,128)(2,1)}, u32[]{:S(2)}, u32[]{:S(2)}) collective-permute-start(bf16[256,2048]{1,0:T(8,128)(2,1)} %get-tuple-element.244.refs_6_), channel_id=1, source_target_pairs={{0,2},{1,3},{2,0},{3,1},{4,6},{5,7},{6,4},{7,5},{8,10},{9,11},{10,... | collective-permute-start | bytes 3145736 | tf_op jit(solution)/shard_map/ppermute | solution.py:621
  143.3 23.7 %all-to-all-start.3 = ((bf16[4,1024,128]{2,1,0:T(8,128)(2,1)}), bf16[4,1024,128]{2,1,0:T(8,128)(2,1)}, u32[]{:S(2)}, u32[]{:S(2)}) async-start(bf16[4,1024,128]{2,1,0:T(8,128)(2,1)} %get-tuple-element.246), calls=%async_computation.3 | async-start | bytes 2097152 | tf_op jit(solution)/shard_map/all_to_all | solution.py:638
  147.5 19.5 %copy-start.6 = (f32[1,1024]{1,0:T(1,128)S(1)}, f32[1,1024]{1,0:T(1,128)}, u32[]{:S(2)}) copy-start(f32[1,1024]{1,0:T(1,128)} %get-tuple-element.262) | copy-start | bytes 12292
  149.3 18.3 %collective-permute-start.13 = (bf16[256,2048]{1,0:T(8,128)(2,1)}, bf16[256,2048]{1,0:T(8,128)(2,1)}, u32[]{:S(2)}, u32[]{:S(2)}) collective-permute-start(bf16[256,2048]{1,0:T(8,128)(2,1)} %get-tuple-element.245.refs_7_), channel_id=1, source_target_pairs={{0,2},{1,3},{2,0},{3,1},{4,6},{5,7},{6,4},{7,5},{8,10},{9,11},{10,... | collective-permute-start | bytes 3145736 | tf_op jit(solution)/shard_map/ppermute | solution.py:621
  163.4 26.4 %collective-permute-start.17 = (bf16[4096,128]{1,0:T(8,128)(2,1)}, bf16[4096,128]{1,0:T(8,128)(2,1)}, u32[]{:S(2)}, u32[]{:S(2)}) collective-permute-start(bf16[4096,128]{1,0:T(8,128)(2,1)} %bitcast.124), channel_id=1, source_target_pairs={{8,16},{9,17},{10,18},{11,19},{12,20},{13,21},{14,22},{15,23},{16,... | collective-permute-start | bytes 3145736 | tf_op jit(solution)/shard_map/ppermute | solution.py:621
  167.0 24.3 %collective-permute-start.16 = (bf16[4096,128]{1,0:T(8,128)(2,1)}, bf16[4096,128]{1,0:T(8,128)(2,1)}, u32[]{:S(2)}, u32[]{:S(2)}) collective-permute-start(bf16[4096,128]{1,0:T(8,128)(2,1)} %bitcast.33), channel_id=1, source_target_pairs={{0,8},{1,9},{2,10},{3,11},{4,12},{5,13},{6,14},{7,15},{8,0},{9,1},... | collective-permute-start | bytes 3145736 | tf_op jit(solution)/shard_map/ppermute | solution.py:621
  193.9 47.7 %collective-permute-start.19 = (bf16[8192,128]{1,0:T(8,128)(2,1)}, bf16[8192,128]{1,0:T(8,128)(2,1)}, u32[]{:S(2)}, u32[]{:S(2)}) collective-permute-start(bf16[8192,128]{1,0:T(8,128)(2,1)} %bitcast.120), channel_id=1, source_target_pairs={{8,16},{9,17},{10,18},{11,19},{12,20},{13,21},{14,22},{15,23},{16,... | collective-permute-start | bytes 6291464 | tf_op jit(solution)/shard_map/ppermute | solution.py:621
  196.2 48.0 %collective-permute-start.18 = (bf16[4096,128]{1,0:T(8,128)(2,1)}, bf16[4096,128]{1,0:T(8,128)(2,1)}, u32[]{:S(2)}, u32[]{:S(2)}) collective-permute-start(bf16[4096,128]{1,0:T(8,128)(2,1)} %bitcast.39), channel_id=1, source_target_pairs={{8,0},{9,1},{10,2},{11,3},{12,4},{13,5},{14,6},{15,7},{16,24},{17,... | collective-permute-start | bytes 3145736 | tf_op jit(solution)/shard_map/ppermute | solution.py:621
  199.0 45.2 %collective-permute-start.20 = (bf16[4096,128]{1,0:T(8,128)(2,1)}, bf16[4096,128]{1,0:T(8,128)(2,1)}, u32[]{:S(2)}, u32[]{:S(2)}) collective-permute-start(bf16[4096,128]{1,0:T(8,128)(2,1)} %bitcast.44), channel_id=1, source_target_pairs={{8,0},{9,1},{10,2},{11,3},{12,4},{13,5},{14,6},{15,7},{16,24},{17,... | collective-permute-start | bytes 3145736 | tf_op jit(solution)/shard_map/ppermute | solution.py:621
  201.3 82.2 %collective-permute-start.22 = (bf16[6144,128]{1,0:T(8,128)(2,1)}, bf16[6144,128]{1,0:T(8,128)(2,1)}, u32[]{:S(2)}, u32[]{:S(2)}) collective-permute-start(bf16[6144,128]{1,0:T(8,128)(2,1)} %bitcast.103), channel_id=1, source_target_pairs={{0,8},{1,9},{2,10},{3,11},{4,12},{5,13},{6,14},{7,15},{24,16},{25,... | collective-permute-start | bytes 4718600 | tf_op jit(solution)/shard_map/ppermute | solution.py:621
  241.5 48.0 %collective-permute-start.21 = (bf16[8192,128]{1,0:T(8,128)(2,1)}, bf16[8192,128]{1,0:T(8,128)(2,1)}, u32[]{:S(2)}, u32[]{:S(2)}) collective-permute-start(bf16[8192,128]{1,0:T(8,128)(2,1)} %bitcast.48), channel_id=1, source_target_pairs={{8,0},{9,1},{10,2},{11,3},{12,4},{13,5},{14,6},{15,7},{16,24},{17,... | collective-permute-start | bytes 6291464 | tf_op jit(solution)/shard_map/ppermute | solution.py:621
  244.2 45.4 %collective-permute-start.23 = (bf16[6144,128]{1,0:T(8,128)(2,1)}, bf16[6144,128]{1,0:T(8,128)(2,1)}, u32[]{:S(2)}, u32[]{:S(2)}) collective-permute-start(bf16[6144,128]{1,0:T(8,128)(2,1)} %bitcast.100), channel_id=1, source_target_pairs={{0,8},{1,9},{2,10},{3,11},{4,12},{5,13},{6,14},{7,15},{24,16},{25,... | collective-permute-start | bytes 4718600 | tf_op jit(solution)/shard_map/ppermute | solution.py:621
  285.9 40.5 %collective-permute-start.26 = (bf16[4096,128]{1,0:T(8,128)(2,1)}, bf16[4096,128]{1,0:T(8,128)(2,1)}, u32[]{:S(2)}, u32[]{:S(2)}) collective-permute-start(bf16[4096,128]{1,0:T(8,128)(2,1)} %bitcast.140), channel_id=1, source_target_pairs={{8,16},{9,17},{10,18},{11,19},{12,20},{13,21},{14,22},{15,23},{16,... | collective-permute-start | bytes 3145736 | tf_op jit(solution)/shard_map/ppermute | solution.py:621
  288.3 69.6 %collective-permute-start.24 = (bf16[12288,128]{1,0:T(8,128)(2,1)}, bf16[12288,128]{1,0:T(8,128)(2,1)}, u32[]{:S(2)}, u32[]{:S(2)}) collective-permute-start(bf16[12288,128]{1,0:T(8,128)(2,1)} %bitcast.99), channel_id=1, source_target_pairs={{0,8},{1,9},{2,10},{3,11},{4,12},{5,13},{6,14},{7,15},{24,16},{25,... | collective-permute-start | bytes 9437192 | tf_op jit(solution)/shard_map/ppermute | solution.py:621
  292.1 48.4 %collective-permute-start.25 = (bf16[4096,128]{1,0:T(8,128)(2,1)}, bf16[4096,128]{1,0:T(8,128)(2,1)}, u32[]{:S(2)}, u32[]{:S(2)}) collective-permute-start(bf16[4096,128]{1,0:T(8,128)(2,1)} %bitcast.141), channel_id=1, source_target_pairs={{8,16},{9,17},{10,18},{11,19},{12,20},{13,21},{14,22},{15,23},{16,... | collective-permute-start | bytes 3145736 | tf_op jit(solution)/shard_map/ppermute | solution.py:621
  340.4 46.2 %collective-permute-start.27 = (bf16[1024,2048]{1,0:T(8,128)(2,1)}, bf16[1024,2048]{1,0:T(8,128)(2,1)}, u32[]{:S(2)}, u32[]{:S(2)}) collective-permute-start(bf16[1024,2048]{1,0:T(8,128)(2,1)} %get-tuple-element.330), channel_id=1, source_target_pairs={{0,2},{1,3},{2,0},{3,1},{4,6},{5,7},{6,4},{7,5},{8,10},{9,11},{10,... | collective-permute-start | bytes 12582920 | tf_op jit(solution)/shard_map/ppermute | solution.py:621
  351.9 71.9 %collective-permute-start.29 = (bf16[1024,2048]{1,0:T(8,128)(2,1)}, bf16[1024,2048]{1,0:T(8,128)(2,1)}, u32[]{:S(2)}, u32[]{:S(2)}) collective-permute-start(bf16[1024,2048]{1,0:T(8,128)(2,1)} %get-tuple-element.337), channel_id=1, source_target_pairs={{0,2},{1,3},{2,0},{3,1},{4,6},{5,7},{6,4},{7,5},{8,10},{9,11},{10,... | collective-permute-start | bytes 12582920 | tf_op jit(solution)/shard_map/ppermute | solution.py:621
  361.3 54.1 %collective-permute-start.30 = (bf16[8192,128]{1,0:T(8,128)(2,1)}, bf16[8192,128]{1,0:T(8,128)(2,1)}, u32[]{:S(2)}, u32[]{:S(2)}) collective-permute-start(bf16[8192,128]{1,0:T(8,128)(2,1)} %bitcast.136), channel_id=1, source_target_pairs={{8,16},{9,17},{10,18},{11,19},{12,20},{13,21},{14,22},{15,23},{16,... | collective-permute-start | bytes 6291464 | tf_op jit(solution)/shard_map/ppermute | solution.py:621
  364.1 34.6 %collective-permute-start.31 = (bf16[6144,128]{1,0:T(8,128)(2,1)}, bf16[6144,128]{1,0:T(8,128)(2,1)}, u32[]{:S(2)}, u32[]{:S(2)}) collective-permute-start(bf16[6144,128]{1,0:T(8,128)(2,1)} %bitcast.102), channel_id=1, source_target_pairs={{0,8},{1,9},{2,10},{3,11},{4,12},{5,13},{6,14},{7,15},{24,16},{25,... | collective-permute-start | bytes 4718600 | tf_op jit(solution)/shard_map/ppermute | solution.py:621
  365.4 18.0 %collective-permute-start.28 = (bf16[2048,128]{1,0:T(8,128)(2,1)}, bf16[2048,128]{1,0:T(8,128)(2,1)S(1)}, u32[]{:S(2)}, u32[]{:S(2)}) collective-permute-start(bf16[2048,128]{1,0:T(8,128)(2,1)} %bitcast.143), channel_id=1, source_target_pairs={{8,0},{9,1},{10,2},{11,3},{12,4},{13,5},{14,6},{15,7},{16,24},{17,... | collective-permute-start | bytes 1572872 | tf_op jit(solution)/shard_map/ppermute | solution.py:621
  390.8 42.5 %collective-permute-start.35 = (bf16[256,2048]{1,0:T(8,128)(2,1)}, bf16[256,2048]{1,0:T(8,128)(2,1)}, u32[]{:S(2)}, u32[]{:S(2)}) collective-permute-start(bf16[256,2048]{1,0:T(8,128)(2,1)} %get-tuple-element.358), channel_id=1, source_target_pairs={{0,4},{1,5},{2,6},{3,7},{4,0},{5,1},{6,2},{7,3},{8,12},{9,13},{10,... | collective-permute-start | bytes 3145736 | tf_op jit(solution)/shard_map/ppermute | solution.py:621
  391.2 44.2 %collective-permute-start.36 = (bf16[256,2048]{1,0:T(8,128)(2,1)}, bf16[256,2048]{1,0:T(8,128)(2,1)}, u32[]{:S(2)}, u32[]{:S(2)}) collective-permute-start(bf16[256,2048]{1,0:T(8,128)(2,1)} %get-tuple-element.359), channel_id=1, source_target_pairs={{0,1},{1,0},{2,3},{3,2},{4,5},{5,4},{6,7},{7,6},{8,9},{9,8},{10,11... | collective-permute-start | bytes 3145736 | tf_op jit(solution)/shard_map/ppermute | solution.py:621
  398.7 52.2 %collective-permute-start.38 = (bf16[6144,128]{1,0:T(8,128)(2,1)}, bf16[6144,128]{1,0:T(8,128)(2,1)}, u32[]{:S(2)}, u32[]{:S(2)}) collective-permute-start(bf16[6144,128]{1,0:T(8,128)(2,1)} %bitcast.101), channel_id=1, source_target_pairs={{0,8},{1,9},{2,10},{3,11},{4,12},{5,13},{6,14},{7,15},{24,16},{25,... | collective-permute-start | bytes 4718600 | tf_op jit(solution)/shard_map/ppermute | solution.py:621
  400.0 18.4 %all-to-all-start.4 = ((bf16[4,512,128]{2,1,0:T(8,128)(2,1)}), bf16[4,512,128]{2,1,0:T(8,128)(2,1)S(1)}, u32[]{:S(2)}, u32[]{:S(2)}) async-start(bf16[4,512,128]{2,1,0:T(8,128)(2,1)} %get-tuple-element.339), calls=%async_computation.4 | async-start | bytes 1048576 | tf_op jit(solution)/shard_map/all_to_all | solution.py:638
  415.4 31.3 %collective-permute-start.39 = (bf16[4096,128]{1,0:T(8,128)(2,1)}, bf16[4096,128]{1,0:T(8,128)(2,1)}, u32[]{:S(2)}, u32[]{:S(2)}) collective-permute-start(bf16[4096,128]{1,0:T(8,128)(2,1)} %bitcast.139), channel_id=1, source_target_pairs={{8,16},{9,17},{10,18},{11,19},{12,20},{13,21},{14,22},{15,23},{16,... | collective-permute-start | bytes 3145736 | tf_op jit(solution)/shard_map/ppermute | solution.py:621
  423.8 34.2 %collective-permute-start.37 = (bf16[4096,128]{1,0:T(8,128)(2,1)}, bf16[4096,128]{1,0:T(8,128)(2,1)}, u32[]{:S(2)}, u32[]{:S(2)}) collective-permute-start(bf16[4096,128]{1,0:T(8,128)(2,1)} %bitcast.138), channel_id=1, source_target_pairs={{8,0},{9,1},{10,2},{11,3},{12,4},{13,5},{14,6},{15,7},{16,24},{17,... | collective-permute-start | bytes 3145736 | tf_op jit(solution)/shard_map/ppermute | solution.py:621
  433.3 36.2 %collective-permute-start.32 = (bf16[256,2048]{1,0:T(8,128)(2,1)}, bf16[256,2048]{1,0:T(8,128)(2,1)}, u32[]{:S(2)}, u32[]{:S(2)}) collective-permute-start(bf16[256,2048]{1,0:T(8,128)(2,1)} %get-tuple-element.345), channel_id=1, source_target_pairs={{0,4},{1,5},{2,6},{3,7},{4,0},{5,1},{6,2},{7,3},{8,12},{9,13},{10,... | collective-permute-start | bytes 3145736 | tf_op jit(solution)/shard_map/ppermute | solution.py:621
  435.4 34.1 %collective-permute-start.33 = (bf16[256,2048]{1,0:T(8,128)(2,1)}, bf16[256,2048]{1,0:T(8,128)(2,1)}, u32[]{:S(2)}, u32[]{:S(2)}) collective-permute-start(bf16[256,2048]{1,0:T(8,128)(2,1)} %get-tuple-element.346), channel_id=1, source_target_pairs={{0,1},{1,0},{2,3},{3,2},{4,5},{5,4},{6,7},{7,6},{8,9},{9,8},{10,11... | collective-permute-start | bytes 3145736 | tf_op jit(solution)/shard_map/ppermute | solution.py:621
  444.0 17.5 %all-to-all-start.5 = ((f32[32,1,896]{2,1,0:T(1,128)}), f32[32,1,896]{2,1,0:T(1,128)S(1)}, u32[]{:S(2)}, u32[]{:S(2)}) async-start(f32[32,1,896]{2,1,0:T(1,128)} %copy.137), calls=%async_computation.5 | async-start | bytes 229376 | tf_op jit(solution)/shard_map/all_to_all | solution.py:641
  446.7 19.7 %collective-permute-start.34 = (bf16[2048,128]{1,0:T(8,128)(2,1)}, bf16[2048,128]{1,0:T(8,128)(2,1)S(1)}, u32[]{:S(2)}, u32[]{:S(2)}) collective-permute-start(bf16[2048,128]{1,0:T(8,128)(2,1)} %bitcast.142), channel_id=1, source_target_pairs={{8,0},{9,1},{10,2},{11,3},{12,4},{13,5},{14,6},{15,7},{16,24},{17,... | collective-permute-start | bytes 1572872 | tf_op jit(solution)/shard_map/ppermute | solution.py:621
  453.3 43.4 %collective-permute-start.45 = (bf16[4096,128]{1,0:T(8,128)(2,1)}, bf16[4096,128]{1,0:T(8,128)(2,1)}, u32[]{:S(2)}, u32[]{:S(2)}) collective-permute-start(bf16[4096,128]{1,0:T(8,128)(2,1)} %bitcast.137), channel_id=1, source_target_pairs={{8,16},{9,17},{10,18},{11,19},{12,20},{13,21},{14,22},{15,23},{16,... | collective-permute-start | bytes 3145736 | tf_op jit(solution)/shard_map/ppermute | solution.py:621
  461.5 19.2 %all-to-all-start.6 = ((bf16[4,1024,128]{2,1,0:T(8,128)(2,1)}), bf16[4,1024,128]{2,1,0:T(8,128)(2,1)}, u32[]{:S(2)}, u32[]{:S(2)}) async-start(bf16[4,1024,128]{2,1,0:T(8,128)(2,1)} %get-tuple-element.375), calls=%async_computation.6 | async-start | bytes 2097152 | tf_op jit(solution)/shard_map/all_to_all | solution.py:638
  473.4 14.9 %collective-permute-start.40 = (bf16[256,1024]{1,0:T(8,128)(2,1)}, bf16[256,1024]{1,0:T(8,128)(2,1)}, u32[]{:S(2)}, u32[]{:S(2)}) collective-permute-start(bf16[256,1024]{1,0:T(8,128)(2,1)} %get-tuple-element.373), channel_id=1, source_target_pairs={{0,1},{1,0},{2,3},{3,2},{4,5},{5,4},{6,7},{7,6},{8,9},{9,8},{10,11... | collective-permute-start | bytes 1572872 | tf_op jit(solution)/shard_map/ppermute | solution.py:621
  474.8 17.1 %collective-permute-start.41 = (bf16[256,1024]{1,0:T(8,128)(2,1)}, bf16[256,1024]{1,0:T(8,128)(2,1)}, u32[]{:S(2)}, u32[]{:S(2)}) collective-permute-start(bf16[256,1024]{1,0:T(8,128)(2,1)} %get-tuple-element.374), channel_id=1, source_target_pairs={{0,4},{1,5},{2,6},{3,7},{4,0},{5,1},{6,2},{7,3},{8,12},{9,13},{10,... | collective-permute-start | bytes 1572872 | tf_op jit(solution)/shard_map/ppermute | solution.py:621
  476.8 24.0 %collective-permute-start.44 = (bf16[2048,128]{1,0:T(8,128)(2,1)}, bf16[2048,128]{1,0:T(8,128)(2,1)}, u32[]{:S(2)}, u32[]{:S(2)}) collective-permute-start(bf16[2048,128]{1,0:T(8,128)(2,1)} %bitcast.80), channel_id=1, source_target_pairs={{8,0},{9,1},{10,2},{11,3},{12,4},{13,5},{14,6},{15,7},{16,24},{17,... | collective-permute-start | bytes 1572872 | tf_op jit(solution)/shard_map/ppermute | solution.py:621
  480.7 22.4 %all-to-all-start.8 = ((bf16[4,512,128]{2,1,0:T(8,128)(2,1)}), bf16[4,512,128]{2,1,0:T(8,128)(2,1)S(1)}, u32[]{:S(2)}, u32[]{:S(2)}) async-start(bf16[4,512,128]{2,1,0:T(8,128)(2,1)} %get-tuple-element.392), calls=%async_computation.8 | async-start | bytes 1048576 | tf_op jit(solution)/shard_map/all_to_all | solution.py:638
  484.2 23.2 %collective-permute-start.42 = (bf16[256,1024]{1,0:T(8,128)(2,1)}, bf16[256,1024]{1,0:T(8,128)(2,1)}, u32[]{:S(2)}, u32[]{:S(2)}) collective-permute-start(bf16[256,1024]{1,0:T(8,128)(2,1)} %get-tuple-element.379), channel_id=1, source_target_pairs={{0,1},{1,0},{2,3},{3,2},{4,5},{5,4},{6,7},{7,6},{8,9},{9,8},{10,11... | collective-permute-start | bytes 1572872 | tf_op jit(solution)/shard_map/ppermute | solution.py:621
  488.4 20.0 %collective-permute-start.43 = (bf16[256,1024]{1,0:T(8,128)(2,1)}, bf16[256,1024]{1,0:T(8,128)(2,1)}, u32[]{:S(2)}, u32[]{:S(2)}) collective-permute-start(bf16[256,1024]{1,0:T(8,128)(2,1)} %get-tuple-element.380), channel_id=1, source_target_pairs={{0,4},{1,5},{2,6},{3,7},{4,0},{5,1},{6,2},{7,3},{8,12},{9,13},{10,... | collective-permute-start | bytes 1572872 | tf_op jit(solution)/shard_map/ppermute | solution.py:621
  498.7 17.1 %collective-permute-start.46 = (bf16[2048,128]{1,0:T(8,128)(2,1)}, bf16[2048,128]{1,0:T(8,128)(2,1)}, u32[]{:S(2)}, u32[]{:S(2)}) collective-permute-start(bf16[2048,128]{1,0:T(8,128)(2,1)} %bitcast.144), channel_id=1, source_target_pairs={{8,0},{9,1},{10,2},{11,3},{12,4},{13,5},{14,6},{15,7},{16,24},{17,... | collective-permute-start | bytes 1572872 | tf_op jit(solution)/shard_map/ppermute | solution.py:621
  504.0 14.3 %all-to-all-start.7 = ((bf16[4,512,128]{2,1,0:T(8,128)(2,1)}), bf16[4,512,128]{2,1,0:T(8,128)(2,1)S(1)}, u32[]{:S(2)}, u32[]{:S(2)}) async-start(bf16[4,512,128]{2,1,0:T(8,128)(2,1)} %get-tuple-element.391), calls=%async_computation.7 | async-start | bytes 1048576 | tf_op jit(solution)/shard_map/all_to_all | solution.py:638
  518.2 13.1 %all-to-all-start.9 = ((bf16[4,512,128]{2,1,0:T(8,128)(2,1)}), bf16[4,512,128]{2,1,0:T(8,128)(2,1)}, u32[]{:S(2)}, u32[]{:S(2)}) async-start(bf16[4,512,128]{2,1,0:T(8,128)(2,1)} %get-tuple-element.402), calls=%async_computation.9 | async-start | bytes 1048576 | tf_op jit(solution)/shard_map/all_to_all | solution.py:638
  (9 other events, 60.1 us)

commit v5 on v4

--- a/solution.py
+++ b/solution.py
@@ -314,9 +314,10 @@
     visible = (seg_at == seg_to) & (to <= at)
 
     scale = 1.0 / math.sqrt(HD)
-    scores = jnp.where(visible, dot(query, key, NT) * scale, -1e30)
+    query = query * jnp.asarray(scale, BF)
+    scores = jnp.where(visible, dot(query, key, NT), -1e30)
     expo = jnp.exp(scores - jnp.max(scores, axis=1, keepdims=True))
-    probs = expo / jnp.sum(expo, axis=1, keepdims=True)
+    probs = expo * (1.0 / jnp.sum(expo, axis=1, keepdims=True))
     low = probs.astype(BF)
     mixed = dot(low, value, NN).astype(BF)
     value_grad = dot(low, back, TN)
@@ -324,7 +325,7 @@
     inner = jnp.sum(probs * probs_grad, axis=1, keepdims=True)
     score_grad = (probs * (probs_grad - inner)).astype(BF)
     query_grad = unturn(dot(score_grad, key, NN) * scale)
-    key_grad = unturn(dot(score_grad, query, TN) * scale)
+    key_grad = unturn(dot(score_grad, query, TN))
     qkv_grad = jnp.concatenate([query_grad, key_grad, value_grad], axis=1).astype(BF)
     mixed_ref[...] = mixed
     qkv_grad_ref[...] = qkv_grad

time: 545 us -> 545 us (level)
  no operation moved by 1% of the time
where the time goes in v5:
time: 545 us; the launch traced here: 534 us
  Pallas kernels  257 us (47%)
  starting transfers between devices  132 us (24%)
  waiting for transfers between devices  90.8 us (17%)
  blocking collectives  33.7 us (6%)
  local copies, waits for them, and re-layouts  17.9 us (3%)
    pallas_call x72, Pallas kernels, run_kernel(): pl.pallas_call(inner, grid=grid, out_shape=outs, in_specs=in_specs, out_s...  257 us
    ppermute x47, starting transfers between devices, permute(): lax.ppermute(v.reshape(-1, v.shape[-1]), AXES, pairs).reshape(v.shape)  98.2 us
    ppermute x47, waiting for transfers between devices, permute(): lax.ppermute(v.reshape(-1, v.shape[-1]), AXES, pairs).reshape(v.shape)  60.4 us
    all_to_all x1, blocking collectives, swap_all(): return lax.all_to_all(v, AXES, split_axis=0, concat_axis=0, tiled=True)  33.7 us
    all_to_all x8, starting transfers between devices, swap_ring(): lax.all_to_all(v, AXES, split_axis=0, concat_axis=0, tiled=True, axis_ind...  31.6 us
    all_to_all x8, waiting for transfers between devices, swap_ring(): lax.all_to_all(v, AXES, split_axis=0, concat_axis=0, tiled=True, axis_ind...  30.1 us
  transfers between devices with their start and end apart: 56, of which 17 were waited for; matrix products, arithmetic and copies ran while one was open for 3% of the time, Pallas kernels for 47%

profile of v5, /device:TPU:8, one launch (start us, length us, event | category | flops | bytes accessed | tf_op | source)
XLA Modules:
  0.0 533.9 jit_solution(9819527420974597399)
XLA Ops:
  1.2 3.5 piece.3
  4.7 4.3 all-to-all-start
  9.0 3.6 piece.4
  12.6 10.9 %all-to-all-done.refs_0_ = bf16[4,1024,128]{2,1,0:T(8,128)(2,1)} async-done(((bf16[4,1024,128]{2,1,0:T(8,128)(2,1)}), bf16[4,1024,128]{2,1,0:T(8,128)(2,1)}, u32[]{:S(2)}, u32[]{:S(2)}) %all-to-all-start) | async-done | bytes 1048608 | tf_op jit(solution)/shard_map/all_to_all | solution.py:639
  23.5 4.2 all-to-all-start.1
  29.1 13.2 %all-to-all-done.1.refs_0_ = bf16[4,1024,128]{2,1,0:T(8,128)(2,1)} async-done(((bf16[4,1024,128]{2,1,0:T(8,128)(2,1)}), bf16[4,1024,128]{2,1,0:T(8,128)(2,1)}, u32[]{:S(2)}, u32[]{:S(2)}) %all-to-all-start.1) | async-done | bytes 1048608 | tf_op jit(solution)/shard_map/all_to_all | solution.py:639
  42.4 4.5 own.1
  48.8 5.5 %collective-permute-done = bf16[4096,128]{1,0:T(8,128)(2,1)} collective-permute-done((bf16[4096,128]{1,0:T(8,128)(2,1)}, bf16[4096,128]{1,0:T(8,128)(2,1)}, u32[]{:S(2)}, u32[]{:S(2)}) %collective-permute-start) | collective-permute-done | bytes 1048608 | tf_op jit(solution)/shard_map/ppermute | solution.py:622
  56.4 3.5 collective-permute-start.3
  63.8 33.7 %all_to_all.62 = f32[32,1,896]{2,1,0:T(1,128)S(1)} all-to-all(f32[32,1,896]{2,1,0:T(1,128)S(1)} %copy.136), channel_id=1, replica_groups=mesh['dp'=16,'tensor'=2] {'dp','tensor'}, dimensions={0} | all-to-all | bytes 229376 | tf_op jit(solution)/shard_map/all_to_all | solution.py:642
  98.2 3.5 collective-permute-start.4
  114.6 11.0 %collective-permute-done.4 = bf16[4096,128]{1,0:T(8,128)(2,1)} collective-permute-done((bf16[4096,128]{1,0:T(8,128)(2,1)}, bf16[4096,128]{1,0:T(8,128)(2,1)}, u32[]{:S(2)}, u32[]{:S(2)}) %collective-permute-start.4) | collective-permute-done | bytes 1048608 | tf_op jit(solution)/shard_map/ppermute | solution.py:622
  130.1 6.0 %turns.1 = (f32[2048,128]{1,0:T(8,128)}, f32[2048,128]{1,0:T(8,128)}, f32[2048,128]{1,0:T(8,128)}, f32[8,128]{1,0:T(8,128)}) custom-call(s32[11]{0:T(128)} %concatenate.6.refs_0_.refs_21_, s32[4,128]{1,0:T(4,128)} %get-tuple-element.239.refs_1_.refs_20_, f32[8,128]{1,0:T(8,128)} %get-tuple-element.240.refs_2_), custom_call_target="tpu_custom_call", output_to_operand_aliasing={{3}: (2, {})} | custom-call | tf_op jit(solution)/shard_map/turns/pallas_call | solution.py:71
  136.2 3.5 collective-permute-start.14
  139.7 3.6 piece.5
  143.3 4.3 all-to-all-start.3
  149.3 14.1 %collective-permute-done.14 = bf16[4096,128]{1,0:T(8,128)(2,1)} collective-permute-done((bf16[4096,128]{1,0:T(8,128)(2,1)}, bf16[4096,128]{1,0:T(8,128)(2,1)}, u32[]{:S(2)}, u32[]{:S(2)}) %collective-permute-start.14) | collective-permute-done | bytes 1048608 | tf_op jit(solution)/shard_map/ppermute | solution.py:622
  163.4 3.5 collective-permute-start.17
  167.6 18.9 %feed.3 = (bf16[2048,256]{1,0:T(8,128)(2,1)}, bf16[2048,256]{1,0:T(8,128)(2,1)}, bf16[256,2048]{1,0:T(8,128)(2,1)}, bf16[256,2048]{1,0:T(8,128)(2,1)}, f32[2,204...) custom-call(bf16[2,256,2048]{2,1,0:T(8,128)(2,1)} %get-tuple-element, ...), custom_call_target="tpu_custom_call", output_to_operand_aliasing={{8}: (17, {})} | custom-call | tf_op jit(solution)/shard_map/feed/pallas_call | solution.py:71
  186.5 3.3 collective-permute-done.17
  191.3 2.6 cat.9
  196.2 2.8 collective-permute-start.18
  201.3 12.9 %collective-permute-start.22 = (bf16[6144,128]{1,0:T(8,128)(2,1)}, bf16[6144,128]{1,0:T(8,128)(2,1)}, u32[]{:S(2)}, u32[]{:S(2)}) collective-permute-start(bf16[6144,128]{1,0:T(8,128)(2,1)} %bitcast.103), channel_id=1, source_target_pairs={{0,8},{1,9},{2,10},{3,11},{4,12},{5,13},{6,14},{7,15},{24,16},{25,... | collective-permute-start | bytes 4718600 | tf_op jit(solution)/shard_map/ppermute | solution.py:622
  214.2 18.9 %feed.4 = (bf16[2048,256]{1,0:T(8,128)(2,1)}, bf16[2048,256]{1,0:T(8,128)(2,1)}, bf16[256,2048]{1,0:T(8,128)(2,1)}, bf16[256,2048]{1,0:T(8,128)(2,1)}, f32[2,204...) custom-call(bf16[2,256,2048]{2,1,0:T(8,128)(2,1)} %get-tuple-element, ...), custom_call_target="tpu_custom_call", output_to_operand_aliasing={{8}: (17, {})} | custom-call | tf_op jit(solution)/shard_map/feed/pallas_call | solution.py:71
  233.1 8.5 %collective-permute-done.19 = bf16[8192,128]{1,0:T(8,128)(2,1)} collective-permute-done((bf16[8192,128]{1,0:T(8,128)(2,1)}, bf16[8192,128]{1,0:T(8,128)(2,1)}, u32[]{:S(2)}, u32[]{:S(2)}) %collective-permute-start.19) | collective-permute-done | bytes 2097184 | tf_op jit(solution)/shard_map/ppermute | solution.py:622
  241.5 2.6 collective-permute-start.21
  245.5 37.9 %attention.1 = (bf16[2048,256]{1,0:T(8,128)(2,1)}, bf16[2048,768]{1,0:T(8,128)(2,1)}, bf16[768,2048]{1,0:T(8,128)(2,1)}, bf16[256,2048]{1,0:T(8,128)(2,1)}, f32[...) custom-call(bf16[2,256,2048]{2,1,0:T(8,128)(2,1)} %get-tuple-element, ...), custom_call_target="tpu_custom_call", output_to_operand_aliasing={{8}: (25, {})} | custom-call | tf_op jit(solution)/shard_map/attention/pallas_call | solution.py:71
  283.4 2.5 sum.15
  289.6 2.4 sum.16
  292.0 3.9 collective-permute-start.25
  296.5 29.8 %feed.5 = (bf16[2048,512]{1,0:T(8,128)(2,1)}, bf16[2048,512]{1,0:T(8,128)(2,1)}, bf16[512,2048]{1,0:T(8,128)(2,1)}, bf16[512,2048]{1,0:T(8,128)(2,1)}, f32[2,204...) custom-call(bf16[2,256,2048]{2,1,0:T(8,128)(2,1)} %get-tuple-element, ...), custom_call_target="tpu_custom_call", output_to_operand_aliasing={{10}: (17, {})} | custom-call | tf_op jit(solution)/shard_map/feed/pallas_call | solution.py:71
  328.3 12.0 %join.4 = (bf16[1024,2048]{1,0:T(8,128)(2,1)}, f32[8,128]{1,0:T(8,128)}) custom-call(bf16[2,2,512,256]{3,2,1,0:T(8,128)(2,1)} %bitcast.116, bf16[2,2,512,256]{3,2,1,0:T(8,128)(2,1)} %bitcast.118, bf16[2,2,512,768]{3,2,1,0:T(8,128)(2,1)} %bitcast.104, bf16[2,2,512,512]{3,2,1,0:T(8,128)(2,1)} %bitcast.108, ...), custom_call_target="tpu_custom_call", output_to_operand_aliasing={{1}: (8, {})} | custom-call | tf_op jit(solution)/shard_map/join/pallas_call | solution.py:71
  342.4 9.5 %join.5 = (bf16[1024,2048]{1,0:T(8,128)(2,1)}, f32[8,128]{1,0:T(8,128)}) custom-call(bf16[2,2,512,256]{3,2,1,0:T(8,128)(2,1)} %bitcast.110, bf16[2,2,512,256]{3,2,1,0:T(8,128)(2,1)} %bitcast.112, bf16[2,2,512,256]{3,2,1,0:T(8,128)(2,1)} %bitcast.114, bf16[2,2,512,512]{3,2,1,0:T(8,128)(2,1)} %bitcast.106, ...), custom_call_target="tpu_custom_call", output_to_operand_aliasing={{1}: (8, {})} | custom-call | tf_op jit(solution)/shard_map/join/pallas_call | solution.py:71
  352.3 5.5 %collective-permute-done.24 = bf16[12288,128]{1,0:T(8,128)(2,1)} collective-permute-done((bf16[12288,128]{1,0:T(8,128)(2,1)}, bf16[12288,128]{1,0:T(8,128)(2,1)}, u32[]{:S(2)}, u32[]{:S(2)}) %collective-permute-start.24) | collective-permute-done | bytes 3145760 | tf_op jit(solution)/shard_map/ppermute | solution.py:622
  357.9 3.4 sum.19
  361.2 2.8 collective-permute-start.30
  365.4 5.9 %collective-permute-start.28 = (bf16[2048,128]{1,0:T(8,128)(2,1)}, bf16[2048,128]{1,0:T(8,128)(2,1)S(1)}, u32[]{:S(2)}, u32[]{:S(2)}) collective-permute-start(bf16[2048,128]{1,0:T(8,128)(2,1)} %bitcast.143), channel_id=1, source_target_pairs={{8,0},{9,1},{10,2},{11,3},{12,4},{13,5},{14,6},{15,7},{16,24},{17,... | collective-permute-start | bytes 1572872 | tf_op jit(solution)/shard_map/ppermute | solution.py:622
  371.3 12.1 %join.6 = (bf16[1024,2048]{1,0:T(8,128)(2,1)}, f32[8,128]{1,0:T(8,128)}) custom-call(bf16[2,2,512,256]{3,2,1,0:T(8,128)(2,1)} %bitcast.117, bf16[2,2,512,256]{3,2,1,0:T(8,128)(2,1)} %bitcast.119, bf16[2,2,512,768]{3,2,1,0:T(8,128)(2,1)} %bitcast.105, bf16[2,2,512,512]{3,2,1,0:T(8,128)(2,1)} %bitcast.109, ...), custom_call_target="tpu_custom_call", output_to_operand_aliasing={{1}: (8, {})} | custom-call | tf_op jit(solution)/shard_map/join/pallas_call | solution.py:71
  386.5 4.2 core.2
  392.3 6.3 %collective-permute-done.31 = bf16[6144,128]{1,0:T(8,128)(2,1)} collective-permute-done((bf16[6144,128]{1,0:T(8,128)(2,1)}, bf16[6144,128]{1,0:T(8,128)(2,1)}, u32[]{:S(2)}, u32[]{:S(2)}) %collective-permute-start.31) | collective-permute-done | bytes 1572896 | tf_op jit(solution)/shard_map/ppermute | solution.py:622
  399.9 3.5 all-to-all-start.4
  403.4 9.5 %join.7 = (bf16[1024,2048]{1,0:T(8,128)(2,1)}, f32[8,128]{1,0:T(8,128)}) custom-call(bf16[2,2,512,256]{3,2,1,0:T(8,128)(2,1)} %bitcast.111, bf16[2,2,512,256]{3,2,1,0:T(8,128)(2,1)} %bitcast.113, bf16[2,2,512,256]{3,2,1,0:T(8,128)(2,1)} %bitcast.115, bf16[2,2,512,512]{3,2,1,0:T(8,128)(2,1)} %bitcast.107, ...), custom_call_target="tpu_custom_call", output_to_operand_aliasing={{1}: (8, {})} | custom-call | tf_op jit(solution)/shard_map/join/pallas_call | solution.py:71
  412.9 2.4 sum.21
  415.3 3.0 collective-permute-start.39
  421.3 2.5 sum.22
  423.8 5.3 collective-permute-start.37
  429.1 4.2 core.3
  436.7 3.9 cross.2
  443.9 2.7 all-to-all-start.5
  450.9 2.4 sum.24
  453.3 4.6 collective-permute-start.45
  457.9 3.2 sum.25
  461.5 4.2 all-to-all-start.6
  469.5 3.9 cross.3
  476.8 2.9 collective-permute-start.44
  480.7 3.5 all-to-all-start.8
  485.6 2.5 unpiece.6
  491.9 4.8 output.1
  500.8 2.4 sum.28
  503.9 3.5 all-to-all-start.7
  508.3 5.3 input_grad.1
  515.8 2.4 sum.29
  518.2 4.2 all-to-all-start.9
  526.3 5.0 all-to-all-done.9.refs_0_
  (177 shorter events, 95.4 us)
Async XLA Ops:
  4.7 18.8 %all-to-all-start = ((bf16[4,1024,128]{2,1,0:T(8,128)(2,1)}), bf16[4,1024,128]{2,1,0:T(8,128)(2,1)}, u32[]{:S(2)}, u32[]{:S(2)}) async-start(bf16[4,1024,128]{2,1,0:T(8,128)(2,1)} %get-tuple-element.210), calls=%async_computation | async-start | bytes 2097152 | tf_op jit(solution)/shard_map/all_to_all | solution.py:639
  23.5 18.8 %all-to-all-start.1 = ((bf16[4,1024,128]{2,1,0:T(8,128)(2,1)}), bf16[4,1024,128]{2,1,0:T(8,128)(2,1)}, u32[]{:S(2)}, u32[]{:S(2)}) async-start(bf16[4,1024,128]{2,1,0:T(8,128)(2,1)} %get-tuple-element.214), calls=%async_computation.1 | async-start | bytes 2097152 | tf_op jit(solution)/shard_map/all_to_all | solution.py:639
  28.5 25.8 %collective-permute-start = (bf16[4096,128]{1,0:T(8,128)(2,1)}, bf16[4096,128]{1,0:T(8,128)(2,1)}, u32[]{:S(2)}, u32[]{:S(2)}) collective-permute-start(bf16[4096,128]{1,0:T(8,128)(2,1)} %bitcast.5), channel_id=1, source_target_pairs={{0,8},{1,9},{2,10},{3,11},{4,12},{5,13},{6,14},{7,15},{8,0},{9,1},... | collective-permute-start | bytes 3145736 | tf_op jit(solution)/shard_map/ppermute | solution.py:622
  42.3 17.6 %copy-start.16 = (s32[1,3]{1,0:T(1,128)S(1)}, s32[1,3]{1,0:T(1,128)}, u32[]{:S(2)}) copy-start(s32[1,3]{1,0:T(1,128)} %param.17) | copy-start | bytes 40
  42.3 17.7 %copy-start.7 = (f32[64]{0:T(128)S(1)}, f32[64]{0:T(128)}, u32[]{:S(2)}) copy-start(f32[64]{0:T(128)} %param.18) | copy-start | bytes 772
  42.3 17.7 %copy-start.8 = (f32[64]{0:T(128)S(1)}, f32[64]{0:T(128)}, u32[]{:S(2)}) copy-start(f32[64]{0:T(128)} %param.19) | copy-start | bytes 772
  42.3 17.7 %copy-start.9 = (f32[64]{0:T(128)S(1)}, f32[64]{0:T(128)}, u32[]{:S(2)}) copy-start(f32[64]{0:T(128)} %param.20) | copy-start | bytes 772
  42.3 17.7 %copy-start.10 = (f32[64]{0:T(128)S(1)}, f32[64]{0:T(128)}, u32[]{:S(2)}) copy-start(f32[64]{0:T(128)} %param.21) | copy-start | bytes 772
  42.4 17.7 %copy-start.11 = (bf16[192]{0:T(256)(128)(2,1)S(1)}, bf16[192]{0:T(256)(128)(2,1)}, u32[]{:S(2)}) copy-start(bf16[192]{0:T(256)(128)(2,1)} %param.23) | copy-start | bytes 1156
  42.4 17.7 %copy-start.12 = (bf16[256]{0:T(256)(128)(2,1)S(1)}, bf16[256]{0:T(256)(128)(2,1)}, u32[]{:S(2)}) copy-start(bf16[256]{0:T(256)(128)(2,1)} %param.27) | copy-start | bytes 1540
  46.9 54.9 %collective-permute-start.2 = (bf16[512,2048]{1,0:T(8,128)(2,1)}, bf16[512,2048]{1,0:T(8,128)(2,1)}, u32[]{:S(2)}, u32[]{:S(2)}) collective-permute-start(bf16[512,2048]{1,0:T(8,128)(2,1)} %bitcast.96), channel_id=1, source_target_pairs={{0,2},{1,3},{2,0},{3,1},{4,6},{5,7},{6,4},{7,5},{8,10},{9,11},{10,... | collective-permute-start | bytes 6291464 | tf_op jit(solution)/shard_map/ppermute | solution.py:622
  46.9 61.3 %collective-permute-start.6 = (bf16[512,2048]{1,0:T(8,128)(2,1)}, bf16[512,2048]{1,0:T(8,128)(2,1)}, u32[]{:S(2)}, u32[]{:S(2)}) collective-permute-start(bf16[512,2048]{1,0:T(8,128)(2,1)} %bitcast.97), channel_id=1, source_target_pairs={{0,1},{1,0},{2,3},{3,2},{4,5},{5,4},{6,7},{7,6},{8,9},{9,8},{10,11... | collective-permute-start | bytes 6291464 | tf_op jit(solution)/shard_map/ppermute | solution.py:622
  48.4 59.7 %collective-permute-start.5 = (bf16[512,2048]{1,0:T(8,128)(2,1)}, bf16[512,2048]{1,0:T(8,128)(2,1)}, u32[]{:S(2)}, u32[]{:S(2)}) collective-permute-start(bf16[512,2048]{1,0:T(8,128)(2,1)} %bitcast.98), channel_id=1, source_target_pairs={{0,4},{1,5},{2,6},{3,7},{4,0},{5,1},{6,2},{7,3},{8,12},{9,13},{10,... | collective-permute-start | bytes 6291464 | tf_op jit(solution)/shard_map/ppermute | solution.py:622
  56.4 41.9 %collective-permute-start.3 = (bf16[4096,128]{1,0:T(8,128)(2,1)}, bf16[4096,128]{1,0:T(8,128)(2,1)}, u32[]{:S(2)}, u32[]{:S(2)}) collective-permute-start(bf16[4096,128]{1,0:T(8,128)(2,1)} %bitcast.128), channel_id=1, source_target_pairs={{8,16},{9,17},{10,18},{11,19},{12,20},{13,21},{14,22},{15,23},{16,... | collective-permute-start | bytes 3145736 | tf_op jit(solution)/shard_map/ppermute | solution.py:622
  59.8 44.2 %collective-permute-start.1 = (bf16[4096,128]{1,0:T(8,128)(2,1)}, bf16[4096,128]{1,0:T(8,128)(2,1)}, u32[]{:S(2)}, u32[]{:S(2)}) collective-permute-start(bf16[4096,128]{1,0:T(8,128)(2,1)} %bitcast.8), channel_id=1, source_target_pairs={{0,8},{1,9},{2,10},{3,11},{4,12},{5,13},{6,14},{7,15},{8,0},{9,1},... | collective-permute-start | bytes 3145736 | tf_op jit(solution)/shard_map/ppermute | solution.py:622
  98.2 27.4 %collective-permute-start.4 = (bf16[4096,128]{1,0:T(8,128)(2,1)}, bf16[4096,128]{1,0:T(8,128)(2,1)}, u32[]{:S(2)}, u32[]{:S(2)}) collective-permute-start(bf16[4096,128]{1,0:T(8,128)(2,1)} %bitcast.126), channel_id=1, source_target_pairs={{8,16},{9,17},{10,18},{11,19},{12,20},{13,21},{14,22},{15,23},{16,... | collective-permute-start | bytes 3145736 | tf_op jit(solution)/shard_map/ppermute | solution.py:622
  101.7 26.2 %collective-permute-start.11 = (bf16[4096,128]{1,0:T(8,128)(2,1)}, bf16[4096,128]{1,0:T(8,128)(2,1)}, u32[]{:S(2)}, u32[]{:S(2)}) collective-permute-start(bf16[4096,128]{1,0:T(8,128)(2,1)} %bitcast.24), channel_id=1, source_target_pairs={{8,0},{9,1},{10,2},{11,3},{12,4},{13,5},{14,6},{15,7},{16,24},{17,... | collective-permute-start | bytes 3145736 | tf_op jit(solution)/shard_map/ppermute | solution.py:622
  110.5 25.7 %collective-permute-start.9 = (bf16[256,2048]{1,0:T(8,128)(2,1)}, bf16[256,2048]{1,0:T(8,128)(2,1)}, u32[]{:S(2)}, u32[]{:S(2)}) collective-permute-start(bf16[256,2048]{1,0:T(8,128)(2,1)} %slice_bitcast_fusion.1), channel_id=1, source_target_pairs={{0,1},{1,0},{2,3},{3,2},{4,5},{5,4},{6,7},{7,6},{8,9},{9,8},{10,11... | collective-permute-start | bytes 3145736 | tf_op jit(solution)/shard_map/ppermute | solution.py:622
  114.1 29.1 %collective-permute-start.10 = (bf16[256,2048]{1,0:T(8,128)(2,1)}, bf16[256,2048]{1,0:T(8,128)(2,1)}, u32[]{:S(2)}, u32[]{:S(2)}) collective-permute-start(bf16[256,2048]{1,0:T(8,128)(2,1)} %slice_bitcast_fusion), channel_id=1, source_target_pairs={{0,4},{1,5},{2,6},{3,7},{4,0},{5,1},{6,2},{7,3},{8,12},{9,13},{10,... | collective-permute-start | bytes 3145736 | tf_op jit(solution)/shard_map/ppermute | solution.py:622
  125.6 23.7 %collective-permute-start.15 = (bf16[4096,128]{1,0:T(8,128)(2,1)}, bf16[4096,128]{1,0:T(8,128)(2,1)}, u32[]{:S(2)}, u32[]{:S(2)}) collective-permute-start(bf16[4096,128]{1,0:T(8,128)(2,1)} %bitcast.28), channel_id=1, source_target_pairs={{8,0},{9,1},{10,2},{11,3},{12,4},{13,5},{14,6},{15,7},{16,24},{17,... | collective-permute-start | bytes 3145736 | tf_op jit(solution)/shard_map/ppermute | solution.py:622
  127.9 39.7 %collective-permute-start.8 = (bf16[512,2048]{1,0:T(8,128)(2,1)}, bf16[512,2048]{1,0:T(8,128)(2,1)}, u32[]{:S(2)}, u32[]{:S(2)}) collective-permute-start(bf16[512,2048]{1,0:T(8,128)(2,1)} %bitcast.20), channel_id=1, source_target_pairs={{0,2},{1,3},{2,0},{3,1},{4,6},{5,7},{6,4},{7,5},{8,10},{9,11},{10,... | collective-permute-start | bytes 6291464 | tf_op jit(solution)/shard_map/ppermute | solution.py:622
  127.9 39.7 %collective-permute-start.7 = (bf16[512,2048]{1,0:T(8,128)(2,1)}, bf16[512,2048]{1,0:T(8,128)(2,1)}, u32[]{:S(2)}, u32[]{:S(2)}) collective-permute-start(bf16[512,2048]{1,0:T(8,128)(2,1)} %bitcast.18), channel_id=1, source_target_pairs={{0,2},{1,3},{2,0},{3,1},{4,6},{5,7},{6,4},{7,5},{8,10},{9,11},{10,... | collective-permute-start | bytes 6291464 | tf_op jit(solution)/shard_map/ppermute | solution.py:622
  136.2 27.3 %collective-permute-start.14 = (bf16[4096,128]{1,0:T(8,128)(2,1)}, bf16[4096,128]{1,0:T(8,128)(2,1)}, u32[]{:S(2)}, u32[]{:S(2)}) collective-permute-start(bf16[4096,128]{1,0:T(8,128)(2,1)} %bitcast.122), channel_id=1, source_target_pairs={{8,16},{9,17},{10,18},{11,19},{12,20},{13,21},{14,22},{15,23},{16,... | collective-permute-start | bytes 3145736 | tf_op jit(solution)/shard_map/ppermute | solution.py:622
  143.3 23.7 %collective-permute-start.12 = (bf16[256,2048]{1,0:T(8,128)(2,1)}, bf16[256,2048]{1,0:T(8,128)(2,1)}, u32[]{:S(2)}, u32[]{:S(2)}) collective-permute-start(bf16[256,2048]{1,0:T(8,128)(2,1)} %get-tuple-element.244.refs_6_), channel_id=1, source_target_pairs={{0,2},{1,3},{2,0},{3,1},{4,6},{5,7},{6,4},{7,5},{8,10},{9,11},{10,... | collective-permute-start | bytes 3145736 | tf_op jit(solution)/shard_map/ppermute | solution.py:622
  143.3 23.7 %all-to-all-start.3 = ((bf16[4,1024,128]{2,1,0:T(8,128)(2,1)}), bf16[4,1024,128]{2,1,0:T(8,128)(2,1)}, u32[]{:S(2)}, u32[]{:S(2)}) async-start(bf16[4,1024,128]{2,1,0:T(8,128)(2,1)} %get-tuple-element.246), calls=%async_computation.3 | async-start | bytes 2097152 | tf_op jit(solution)/shard_map/all_to_all | solution.py:639
  147.5 19.5 %copy-start.6 = (f32[1,1024]{1,0:T(1,128)S(1)}, f32[1,1024]{1,0:T(1,128)}, u32[]{:S(2)}) copy-start(f32[1,1024]{1,0:T(1,128)} %get-tuple-element.262) | copy-start | bytes 12292
  149.3 18.3 %collective-permute-start.13 = (bf16[256,2048]{1,0:T(8,128)(2,1)}, bf16[256,2048]{1,0:T(8,128)(2,1)}, u32[]{:S(2)}, u32[]{:S(2)}) collective-permute-start(bf16[256,2048]{1,0:T(8,128)(2,1)} %get-tuple-element.245.refs_7_), channel_id=1, source_target_pairs={{0,2},{1,3},{2,0},{3,1},{4,6},{5,7},{6,4},{7,5},{8,10},{9,11},{10,... | collective-permute-start | bytes 3145736 | tf_op jit(solution)/shard_map/ppermute | solution.py:622
  163.4 26.4 %collective-permute-start.17 = (bf16[4096,128]{1,0:T(8,128)(2,1)}, bf16[4096,128]{1,0:T(8,128)(2,1)}, u32[]{:S(2)}, u32[]{:S(2)}) collective-permute-start(bf16[4096,128]{1,0:T(8,128)(2,1)} %bitcast.124), channel_id=1, source_target_pairs={{8,16},{9,17},{10,18},{11,19},{12,20},{13,21},{14,22},{15,23},{16,... | collective-permute-start | bytes 3145736 | tf_op jit(solution)/shard_map/ppermute | solution.py:622
  167.0 24.3 %collective-permute-start.16 = (bf16[4096,128]{1,0:T(8,128)(2,1)}, bf16[4096,128]{1,0:T(8,128)(2,1)}, u32[]{:S(2)}, u32[]{:S(2)}) collective-permute-start(bf16[4096,128]{1,0:T(8,128)(2,1)} %bitcast.33), channel_id=1, source_target_pairs={{0,8},{1,9},{2,10},{3,11},{4,12},{5,13},{6,14},{7,15},{8,0},{9,1},... | collective-permute-start | bytes 3145736 | tf_op jit(solution)/shard_map/ppermute | solution.py:622
  193.9 47.7 %collective-permute-start.19 = (bf16[8192,128]{1,0:T(8,128)(2,1)}, bf16[8192,128]{1,0:T(8,128)(2,1)}, u32[]{:S(2)}, u32[]{:S(2)}) collective-permute-start(bf16[8192,128]{1,0:T(8,128)(2,1)} %bitcast.120), channel_id=1, source_target_pairs={{8,16},{9,17},{10,18},{11,19},{12,20},{13,21},{14,22},{15,23},{16,... | collective-permute-start | bytes 6291464 | tf_op jit(solution)/shard_map/ppermute | solution.py:622
  196.2 48.0 %collective-permute-start.18 = (bf16[4096,128]{1,0:T(8,128)(2,1)}, bf16[4096,128]{1,0:T(8,128)(2,1)}, u32[]{:S(2)}, u32[]{:S(2)}) collective-permute-start(bf16[4096,128]{1,0:T(8,128)(2,1)} %bitcast.39), channel_id=1, source_target_pairs={{8,0},{9,1},{10,2},{11,3},{12,4},{13,5},{14,6},{15,7},{16,24},{17,... | collective-permute-start | bytes 3145736 | tf_op jit(solution)/shard_map/ppermute | solution.py:622
  199.0 45.2 %collective-permute-start.20 = (bf16[4096,128]{1,0:T(8,128)(2,1)}, bf16[4096,128]{1,0:T(8,128)(2,1)}, u32[]{:S(2)}, u32[]{:S(2)}) collective-permute-start(bf16[4096,128]{1,0:T(8,128)(2,1)} %bitcast.44), channel_id=1, source_target_pairs={{8,0},{9,1},{10,2},{11,3},{12,4},{13,5},{14,6},{15,7},{16,24},{17,... | collective-permute-start | bytes 3145736 | tf_op jit(solution)/shard_map/ppermute | solution.py:622
  201.3 82.1 %collective-permute-start.22 = (bf16[6144,128]{1,0:T(8,128)(2,1)}, bf16[6144,128]{1,0:T(8,128)(2,1)}, u32[]{:S(2)}, u32[]{:S(2)}) collective-permute-start(bf16[6144,128]{1,0:T(8,128)(2,1)} %bitcast.103), channel_id=1, source_target_pairs={{0,8},{1,9},{2,10},{3,11},{4,12},{5,13},{6,14},{7,15},{24,16},{25,... | collective-permute-start | bytes 4718600 | tf_op jit(solution)/shard_map/ppermute | solution.py:622
  241.5 48.0 %collective-permute-start.21 = (bf16[8192,128]{1,0:T(8,128)(2,1)}, bf16[8192,128]{1,0:T(8,128)(2,1)}, u32[]{:S(2)}, u32[]{:S(2)}) collective-permute-start(bf16[8192,128]{1,0:T(8,128)(2,1)} %bitcast.48), channel_id=1, source_target_pairs={{8,0},{9,1},{10,2},{11,3},{12,4},{13,5},{14,6},{15,7},{16,24},{17,... | collective-permute-start | bytes 6291464 | tf_op jit(solution)/shard_map/ppermute | solution.py:622
  244.2 45.4 %collective-permute-start.23 = (bf16[6144,128]{1,0:T(8,128)(2,1)}, bf16[6144,128]{1,0:T(8,128)(2,1)}, u32[]{:S(2)}, u32[]{:S(2)}) collective-permute-start(bf16[6144,128]{1,0:T(8,128)(2,1)} %bitcast.100), channel_id=1, source_target_pairs={{0,8},{1,9},{2,10},{3,11},{4,12},{5,13},{6,14},{7,15},{24,16},{25,... | collective-permute-start | bytes 4718600 | tf_op jit(solution)/shard_map/ppermute | solution.py:622
  285.9 40.5 %collective-permute-start.26 = (bf16[4096,128]{1,0:T(8,128)(2,1)}, bf16[4096,128]{1,0:T(8,128)(2,1)}, u32[]{:S(2)}, u32[]{:S(2)}) collective-permute-start(bf16[4096,128]{1,0:T(8,128)(2,1)} %bitcast.140), channel_id=1, source_target_pairs={{8,16},{9,17},{10,18},{11,19},{12,20},{13,21},{14,22},{15,23},{16,... | collective-permute-start | bytes 3145736 | tf_op jit(solution)/shard_map/ppermute | solution.py:622
  288.2 69.6 %collective-permute-start.24 = (bf16[12288,128]{1,0:T(8,128)(2,1)}, bf16[12288,128]{1,0:T(8,128)(2,1)}, u32[]{:S(2)}, u32[]{:S(2)}) collective-permute-start(bf16[12288,128]{1,0:T(8,128)(2,1)} %bitcast.99), channel_id=1, source_target_pairs={{0,8},{1,9},{2,10},{3,11},{4,12},{5,13},{6,14},{7,15},{24,16},{25,... | collective-permute-start | bytes 9437192 | tf_op jit(solution)/shard_map/ppermute | solution.py:622
  292.0 48.4 %collective-permute-start.25 = (bf16[4096,128]{1,0:T(8,128)(2,1)}, bf16[4096,128]{1,0:T(8,128)(2,1)}, u32[]{:S(2)}, u32[]{:S(2)}) collective-permute-start(bf16[4096,128]{1,0:T(8,128)(2,1)} %bitcast.141), channel_id=1, source_target_pairs={{8,16},{9,17},{10,18},{11,19},{12,20},{13,21},{14,22},{15,23},{16,... | collective-permute-start | bytes 3145736 | tf_op jit(solution)/shard_map/ppermute | solution.py:622
  340.4 46.2 %collective-permute-start.27 = (bf16[1024,2048]{1,0:T(8,128)(2,1)}, bf16[1024,2048]{1,0:T(8,128)(2,1)}, u32[]{:S(2)}, u32[]{:S(2)}) collective-permute-start(bf16[1024,2048]{1,0:T(8,128)(2,1)} %get-tuple-element.330), channel_id=1, source_target_pairs={{0,2},{1,3},{2,0},{3,1},{4,6},{5,7},{6,4},{7,5},{8,10},{9,11},{10,... | collective-permute-start | bytes 12582920 | tf_op jit(solution)/shard_map/ppermute | solution.py:622
  351.9 71.9 %collective-permute-start.29 = (bf16[1024,2048]{1,0:T(8,128)(2,1)}, bf16[1024,2048]{1,0:T(8,128)(2,1)}, u32[]{:S(2)}, u32[]{:S(2)}) collective-permute-start(bf16[1024,2048]{1,0:T(8,128)(2,1)} %get-tuple-element.337), channel_id=1, source_target_pairs={{0,2},{1,3},{2,0},{3,1},{4,6},{5,7},{6,4},{7,5},{8,10},{9,11},{10,... | collective-permute-start | bytes 12582920 | tf_op jit(solution)/shard_map/ppermute | solution.py:622
  361.2 54.1 %collective-permute-start.30 = (bf16[8192,128]{1,0:T(8,128)(2,1)}, bf16[8192,128]{1,0:T(8,128)(2,1)}, u32[]{:S(2)}, u32[]{:S(2)}) collective-permute-start(bf16[8192,128]{1,0:T(8,128)(2,1)} %bitcast.136), channel_id=1, source_target_pairs={{8,16},{9,17},{10,18},{11,19},{12,20},{13,21},{14,22},{15,23},{16,... | collective-permute-start | bytes 6291464 | tf_op jit(solution)/shard_map/ppermute | solution.py:622
  364.1 34.6 %collective-permute-start.31 = (bf16[6144,128]{1,0:T(8,128)(2,1)}, bf16[6144,128]{1,0:T(8,128)(2,1)}, u32[]{:S(2)}, u32[]{:S(2)}) collective-permute-start(bf16[6144,128]{1,0:T(8,128)(2,1)} %bitcast.102), channel_id=1, source_target_pairs={{0,8},{1,9},{2,10},{3,11},{4,12},{5,13},{6,14},{7,15},{24,16},{25,... | collective-permute-start | bytes 4718600 | tf_op jit(solution)/shard_map/ppermute | solution.py:622
  365.4 18.0 %collective-permute-start.28 = (bf16[2048,128]{1,0:T(8,128)(2,1)}, bf16[2048,128]{1,0:T(8,128)(2,1)S(1)}, u32[]{:S(2)}, u32[]{:S(2)}) collective-permute-start(bf16[2048,128]{1,0:T(8,128)(2,1)} %bitcast.143), channel_id=1, source_target_pairs={{8,0},{9,1},{10,2},{11,3},{12,4},{13,5},{14,6},{15,7},{16,24},{17,... | collective-permute-start | bytes 1572872 | tf_op jit(solution)/shard_map/ppermute | solution.py:622
  390.8 42.5 %collective-permute-start.35 = (bf16[256,2048]{1,0:T(8,128)(2,1)}, bf16[256,2048]{1,0:T(8,128)(2,1)}, u32[]{:S(2)}, u32[]{:S(2)}) collective-permute-start(bf16[256,2048]{1,0:T(8,128)(2,1)} %get-tuple-element.358), channel_id=1, source_target_pairs={{0,4},{1,5},{2,6},{3,7},{4,0},{5,1},{6,2},{7,3},{8,12},{9,13},{10,... | collective-permute-start | bytes 3145736 | tf_op jit(solution)/shard_map/ppermute | solution.py:622
  391.1 44.2 %collective-permute-start.36 = (bf16[256,2048]{1,0:T(8,128)(2,1)}, bf16[256,2048]{1,0:T(8,128)(2,1)}, u32[]{:S(2)}, u32[]{:S(2)}) collective-permute-start(bf16[256,2048]{1,0:T(8,128)(2,1)} %get-tuple-element.359), channel_id=1, source_target_pairs={{0,1},{1,0},{2,3},{3,2},{4,5},{5,4},{6,7},{7,6},{8,9},{9,8},{10,11... | collective-permute-start | bytes 3145736 | tf_op jit(solution)/shard_map/ppermute | solution.py:622
  398.6 52.2 %collective-permute-start.38 = (bf16[6144,128]{1,0:T(8,128)(2,1)}, bf16[6144,128]{1,0:T(8,128)(2,1)}, u32[]{:S(2)}, u32[]{:S(2)}) collective-permute-start(bf16[6144,128]{1,0:T(8,128)(2,1)} %bitcast.101), channel_id=1, source_target_pairs={{0,8},{1,9},{2,10},{3,11},{4,12},{5,13},{6,14},{7,15},{24,16},{25,... | collective-permute-start | bytes 4718600 | tf_op jit(solution)/shard_map/ppermute | solution.py:622
  399.9 18.4 %all-to-all-start.4 = ((bf16[4,512,128]{2,1,0:T(8,128)(2,1)}), bf16[4,512,128]{2,1,0:T(8,128)(2,1)S(1)}, u32[]{:S(2)}, u32[]{:S(2)}) async-start(bf16[4,512,128]{2,1,0:T(8,128)(2,1)} %get-tuple-element.339), calls=%async_computation.4 | async-start | bytes 1048576 | tf_op jit(solution)/shard_map/all_to_all | solution.py:639
  415.3 31.3 %collective-permute-start.39 = (bf16[4096,128]{1,0:T(8,128)(2,1)}, bf16[4096,128]{1,0:T(8,128)(2,1)}, u32[]{:S(2)}, u32[]{:S(2)}) collective-permute-start(bf16[4096,128]{1,0:T(8,128)(2,1)} %bitcast.139), channel_id=1, source_target_pairs={{8,16},{9,17},{10,18},{11,19},{12,20},{13,21},{14,22},{15,23},{16,... | collective-permute-start | bytes 3145736 | tf_op jit(solution)/shard_map/ppermute | solution.py:622
  423.8 34.2 %collective-permute-start.37 = (bf16[4096,128]{1,0:T(8,128)(2,1)}, bf16[4096,128]{1,0:T(8,128)(2,1)}, u32[]{:S(2)}, u32[]{:S(2)}) collective-permute-start(bf16[4096,128]{1,0:T(8,128)(2,1)} %bitcast.138), channel_id=1, source_target_pairs={{8,0},{9,1},{10,2},{11,3},{12,4},{13,5},{14,6},{15,7},{16,24},{17,... | collective-permute-start | bytes 3145736 | tf_op jit(solution)/shard_map/ppermute | solution.py:622
  433.3 36.2 %collective-permute-start.32 = (bf16[256,2048]{1,0:T(8,128)(2,1)}, bf16[256,2048]{1,0:T(8,128)(2,1)}, u32[]{:S(2)}, u32[]{:S(2)}) collective-permute-start(bf16[256,2048]{1,0:T(8,128)(2,1)} %get-tuple-element.345), channel_id=1, source_target_pairs={{0,4},{1,5},{2,6},{3,7},{4,0},{5,1},{6,2},{7,3},{8,12},{9,13},{10,... | collective-permute-start | bytes 3145736 | tf_op jit(solution)/shard_map/ppermute | solution.py:622
  435.3 34.1 %collective-permute-start.33 = (bf16[256,2048]{1,0:T(8,128)(2,1)}, bf16[256,2048]{1,0:T(8,128)(2,1)}, u32[]{:S(2)}, u32[]{:S(2)}) collective-permute-start(bf16[256,2048]{1,0:T(8,128)(2,1)} %get-tuple-element.346), channel_id=1, source_target_pairs={{0,1},{1,0},{2,3},{3,2},{4,5},{5,4},{6,7},{7,6},{8,9},{9,8},{10,11... | collective-permute-start | bytes 3145736 | tf_op jit(solution)/shard_map/ppermute | solution.py:622
  443.9 17.5 %all-to-all-start.5 = ((f32[32,1,896]{2,1,0:T(1,128)}), f32[32,1,896]{2,1,0:T(1,128)S(1)}, u32[]{:S(2)}, u32[]{:S(2)}) async-start(f32[32,1,896]{2,1,0:T(1,128)} %copy.137), calls=%async_computation.5 | async-start | bytes 229376 | tf_op jit(solution)/shard_map/all_to_all | solution.py:642
  446.7 19.7 %collective-permute-start.34 = (bf16[2048,128]{1,0:T(8,128)(2,1)}, bf16[2048,128]{1,0:T(8,128)(2,1)S(1)}, u32[]{:S(2)}, u32[]{:S(2)}) collective-permute-start(bf16[2048,128]{1,0:T(8,128)(2,1)} %bitcast.142), channel_id=1, source_target_pairs={{8,0},{9,1},{10,2},{11,3},{12,4},{13,5},{14,6},{15,7},{16,24},{17,... | collective-permute-start | bytes 1572872 | tf_op jit(solution)/shard_map/ppermute | solution.py:622
  453.3 43.4 %collective-permute-start.45 = (bf16[4096,128]{1,0:T(8,128)(2,1)}, bf16[4096,128]{1,0:T(8,128)(2,1)}, u32[]{:S(2)}, u32[]{:S(2)}) collective-permute-start(bf16[4096,128]{1,0:T(8,128)(2,1)} %bitcast.137), channel_id=1, source_target_pairs={{8,16},{9,17},{10,18},{11,19},{12,20},{13,21},{14,22},{15,23},{16,... | collective-permute-start | bytes 3145736 | tf_op jit(solution)/shard_map/ppermute | solution.py:622
  461.5 19.2 %all-to-all-start.6 = ((bf16[4,1024,128]{2,1,0:T(8,128)(2,1)}), bf16[4,1024,128]{2,1,0:T(8,128)(2,1)}, u32[]{:S(2)}, u32[]{:S(2)}) async-start(bf16[4,1024,128]{2,1,0:T(8,128)(2,1)} %get-tuple-element.375), calls=%async_computation.6 | async-start | bytes 2097152 | tf_op jit(solution)/shard_map/all_to_all | solution.py:639
  473.4 14.9 %collective-permute-start.40 = (bf16[256,1024]{1,0:T(8,128)(2,1)}, bf16[256,1024]{1,0:T(8,128)(2,1)}, u32[]{:S(2)}, u32[]{:S(2)}) collective-permute-start(bf16[256,1024]{1,0:T(8,128)(2,1)} %get-tuple-element.373), channel_id=1, source_target_pairs={{0,1},{1,0},{2,3},{3,2},{4,5},{5,4},{6,7},{7,6},{8,9},{9,8},{10,11... | collective-permute-start | bytes 1572872 | tf_op jit(solution)/shard_map/ppermute | solution.py:622
  474.8 17.1 %collective-permute-start.41 = (bf16[256,1024]{1,0:T(8,128)(2,1)}, bf16[256,1024]{1,0:T(8,128)(2,1)}, u32[]{:S(2)}, u32[]{:S(2)}) collective-permute-start(bf16[256,1024]{1,0:T(8,128)(2,1)} %get-tuple-element.374), channel_id=1, source_target_pairs={{0,4},{1,5},{2,6},{3,7},{4,0},{5,1},{6,2},{7,3},{8,12},{9,13},{10,... | collective-permute-start | bytes 1572872 | tf_op jit(solution)/shard_map/ppermute | solution.py:622
  476.8 24.0 %collective-permute-start.44 = (bf16[2048,128]{1,0:T(8,128)(2,1)}, bf16[2048,128]{1,0:T(8,128)(2,1)}, u32[]{:S(2)}, u32[]{:S(2)}) collective-permute-start(bf16[2048,128]{1,0:T(8,128)(2,1)} %bitcast.80), channel_id=1, source_target_pairs={{8,0},{9,1},{10,2},{11,3},{12,4},{13,5},{14,6},{15,7},{16,24},{17,... | collective-permute-start | bytes 1572872 | tf_op jit(solution)/shard_map/ppermute | solution.py:622
  480.7 22.4 %all-to-all-start.8 = ((bf16[4,512,128]{2,1,0:T(8,128)(2,1)}), bf16[4,512,128]{2,1,0:T(8,128)(2,1)S(1)}, u32[]{:S(2)}, u32[]{:S(2)}) async-start(bf16[4,512,128]{2,1,0:T(8,128)(2,1)} %get-tuple-element.392), calls=%async_computation.8 | async-start | bytes 1048576 | tf_op jit(solution)/shard_map/all_to_all | solution.py:639
  484.2 23.2 %collective-permute-start.42 = (bf16[256,1024]{1,0:T(8,128)(2,1)}, bf16[256,1024]{1,0:T(8,128)(2,1)}, u32[]{:S(2)}, u32[]{:S(2)}) collective-permute-start(bf16[256,1024]{1,0:T(8,128)(2,1)} %get-tuple-element.379), channel_id=1, source_target_pairs={{0,1},{1,0},{2,3},{3,2},{4,5},{5,4},{6,7},{7,6},{8,9},{9,8},{10,11... | collective-permute-start | bytes 1572872 | tf_op jit(solution)/shard_map/ppermute | solution.py:622
  488.3 20.0 %collective-permute-start.43 = (bf16[256,1024]{1,0:T(8,128)(2,1)}, bf16[256,1024]{1,0:T(8,128)(2,1)}, u32[]{:S(2)}, u32[]{:S(2)}) collective-permute-start(bf16[256,1024]{1,0:T(8,128)(2,1)} %get-tuple-element.380), channel_id=1, source_target_pairs={{0,4},{1,5},{2,6},{3,7},{4,0},{5,1},{6,2},{7,3},{8,12},{9,13},{10,... | collective-permute-start | bytes 1572872 | tf_op jit(solution)/shard_map/ppermute | solution.py:622
  498.7 17.1 %collective-permute-start.46 = (bf16[2048,128]{1,0:T(8,128)(2,1)}, bf16[2048,128]{1,0:T(8,128)(2,1)}, u32[]{:S(2)}, u32[]{:S(2)}) collective-permute-start(bf16[2048,128]{1,0:T(8,128)(2,1)} %bitcast.144), channel_id=1, source_target_pairs={{8,0},{9,1},{10,2},{11,3},{12,4},{13,5},{14,6},{15,7},{16,24},{17,... | collective-permute-start | bytes 1572872 | tf_op jit(solution)/shard_map/ppermute | solution.py:622
  503.9 14.3 %all-to-all-start.7 = ((bf16[4,512,128]{2,1,0:T(8,128)(2,1)}), bf16[4,512,128]{2,1,0:T(8,128)(2,1)S(1)}, u32[]{:S(2)}, u32[]{:S(2)}) async-start(bf16[4,512,128]{2,1,0:T(8,128)(2,1)} %get-tuple-element.391), calls=%async_computation.7 | async-start | bytes 1048576 | tf_op jit(solution)/shard_map/all_to_all | solution.py:639
  518.2 13.1 %all-to-all-start.9 = ((bf16[4,512,128]{2,1,0:T(8,128)(2,1)}), bf16[4,512,128]{2,1,0:T(8,128)(2,1)}, u32[]{:S(2)}, u32[]{:S(2)}) async-start(bf16[4,512,128]{2,1,0:T(8,128)(2,1)} %get-tuple-element.402), calls=%async_computation.9 | async-start | bytes 1048576 | tf_op jit(solution)/shard_map/all_to_all | solution.py:639
  (9 other events, 60.1 us)
